TPU v7x, 256 devices: a whole 4x4x8 slice. The times are simulated.
256 devices in a mesh: depth: 8 (over y, core), row: 4 (over z_lo), col: 8 (over x, z_hi).
Axes of the slice: x: 4, y: 4, z: 8 (z_hi: 2, z_lo: 4; z = z_hi * 4 + z_lo), core: 2. Of those that a mesh axis runs over, the one named last changes fastest.
Arguments:
- inputs: bfloat16 [8, 512, 16384], P('col', None, ('depth', 'row')), may hold values from -6 to 6
- qweight: bfloat16 [16384, 9216], P(('depth', 'col'), 'row'), may hold values from -0.046875 to 0.046875
- scales: float32 [128, 72], P(('depth', 'col'), 'row'), may hold values from 0.25 to 4, as said below
- grad_out: bfloat16 [8, 512, 9216], P('col', 'depth', 'row'), may hold values from -0.796875 to 0.796875
Outputs:
- projected: bfloat16 [8, 512, 9216], P('col', 'depth', 'row')
- grad_inputs: bfloat16 [8, 512, 16384], P('col', None, ('depth', 'row'))
- grad_weight: bfloat16 [16384, 9216], P(('depth', 'col'), 'row')
Inputs may be any that keep to these rules, and one draw needn't show every extreme that they name: `scales`: every scale is a power of two.
All inputs are finite; a program needn't handle non-finite values.
Results may differ from a plain program's by a relative error of at most 0.019.
Values may be sent and summed in bfloat16 or wider, within the bound.
No kernel may reach another device: no remote copies, remote signals or barrier semaphores. Data moves between devices by JAX's collectives and lax.ppermute only.
A program may use at most 128 MiB of HBM per device.

v0:
```python
import jax
import jax.numpy as jnp
from jax import lax
from jax.sharding import PartitionSpec as P

BLOCK = 128


def transposed_product(left, right):
    return lax.dot_general(
        left, right, (((0,), (0,)), ((), ())), preferred_element_type=jnp.float32
    )


def against_rows(left, right):
    return lax.dot_general(
        left, right, (((1,), (1,)), ((), ())), preferred_element_type=jnp.float32
    )


def per_device(inputs, qweight, scales, grad_out):
    expand = jnp.repeat(jnp.repeat(scales, BLOCK, axis=0), BLOCK, axis=1)
    weight = (qweight.astype(jnp.float32) * expand).astype(jnp.bfloat16)
    panel = lax.all_gather(inputs[0], "row", axis=1, tiled=True)
    grad_rows = lax.all_gather(grad_out[0], "depth", axis=0, tiled=True)
    whole = lax.all_gather(weight, "col", axis=0, tiled=True)
    forward = jnp.dot(panel, whole, preferred_element_type=jnp.float32)
    backward = against_rows(grad_rows, whole)
    projected = lax.psum_scatter(
        forward.astype(jnp.bfloat16), "depth", scatter_dimension=0, tiled=True
    )
    grad_inputs = lax.psum_scatter(
        backward.astype(jnp.bfloat16), "row", scatter_dimension=1, tiled=True
    )
    grad_weight = lax.psum_scatter(
        transposed_product(panel, grad_rows).astype(jnp.bfloat16),
        "col",
        scatter_dimension=0,
        tiled=True,
    )
    return (projected[None], grad_inputs[None], grad_weight)


def solution(mesh):
    return jax.shard_map(
        per_device,
        mesh=mesh,
        in_specs=(
            P("col", None, ("depth", "row")),
            P(("depth", "col"), "row"),
            P(("depth", "col"), "row"),
            P("col", "depth", "row"),
        ),
        out_specs=(
            P("col", "depth", "row"),
            P("col", None, ("depth", "row")),
            P(("depth", "col"), "row"),
        ),
        check_vma=False,
    )
```

profile of v0, /device:TPU:32, one launch (start us, length us, event | category | flops | bytes accessed | tf_op | source)
XLA Modules:
  0.0 595.0 jit_solution(11013250619058486286)
XLA Ops:
  7.2 0.7 all-gather.10.cloned.1.call-update
  7.9 0.0 all-gather.6.cloned.1.call-start
  8.0 1.6 copy.13
  9.5 0.1 copy.14
  9.6 0.1 broadcast_bitcast_fusion
  9.8 1.3 fusion.4
  11.1 0.0 all-gather.8.cloned.1.call-start
  11.1 0.7 all-gather.8.cloned.1.call-update
  11.8 28.8 %all-gather.10.cloned.1.call-done = bf16[1,512,2304]{2,1,0:T(8,128)(2,1)} async-done(((bf16[1,64,2304]{2,1,0:T(8,128)(2,1)}), bf16[1,512,2304]{2,1,0:T(8,128)(2,1)}) %all-gather.10.cloned.1.call-update) | async-done | bytes 2359312 | tf_op jit(solution)/shard_map/all_gather | solution.py:25
  40.7 202.7 %all-gather.6.cloned.1.call-done = bf16[2048,2304]{0,1:T(8,128)(2,1)} async-done(((bf16[256,2304]{0,1:T(8,128)(2,1)}), bf16[2048,2304]{0,1:T(8,128)(2,1)}) %all-gather.6.cloned.1.call-update) | async-done | bytes 9437200 | tf_op jit(solution)/shard_map/all_gather | solution.py:26
  243.4 10.7 %fusion.1 = bf16[512,2048]{0,1:T(8,128)(2,1)} fusion(bf16[2048,2304]{0,1:T(8,128)(2,1)} %all-gather.6.cloned.1.call-done, bf16[1,512,2304]{2,1,0:T(8,128)(2,1)} %all-gather.10.cloned.1.call-done), kind=kOutput, calls=%fused_computation.4 | convolution fusion | flops 4832886784 | bytes 13893632 | tf_op jit(solution)/shard_map/dot_general | solution.py:16
  254.1 0.0 reduce-scatter.10.cloned.1.call-start
  254.1 37.7 %all-gather.8.cloned.1.call-done = bf16[1,512,2048]{2,1,0:T(8,128)(2,1)} async-done(((bf16[1,512,512]{2,1,0:T(8,128)(2,1)}), bf16[1,512,2048]{2,1,0:T(8,128)(2,1)}) %all-gather.8.cloned.1.call-update) | async-done | bytes 2097168 | tf_op jit(solution)/shard_map/all_gather | solution.py:24
  291.9 9.4 %fusion = bf16[512,2304]{0,1:T(8,128)(2,1)S(1)} fusion(bf16[2048,2304]{0,1:T(8,128)(2,1)} %all-gather.6.cloned.1.call-done, bf16[1,512,2048]{2,1,0:T(8,128)(2,1)} %all-gather.8.cloned.1.call-done), kind=kOutput, calls=%fused_computation.2 | convolution fusion | flops 4833017856 | bytes 13893632 | tf_op jit(solution)/shard_map/dot_general | solution.py:27
  301.3 2.6 copy.17
  303.8 0.0 reduce-scatter.8.cloned.1.call-start
  303.9 1.6 copy-done.1
  305.5 10.0 %convolution_convert_fusion = bf16[2048,2304]{1,0:T(8,128)(2,1)} fusion(bf16[1,512,2304]{2,1,0:T(8,128)(2,1)S(1)} %copy-done.1, bf16[1,512,2048]{2,1,0:T(8,128)(2,1)} %all-gather.8.cloned.1.call-done), kind=kOutput, calls=%fused_computation | convolution fusion | flops 4836556800 | bytes 13893632 | tf_op jit(solution)/shard_map/dot_general | solution.py:10
  315.5 25.9 %reduce-scatter.6.cloned.1.call-done = bf16[512,512]{0,1:T(8,128)(2,1)} async-done(((bf16[512,2048]{0,1:T(8,128)(2,1)}), bf16[512,512]{0,1:T(8,128)(2,1)}) %reduce-scatter.6.cloned.1.call-update) | async-done | bytes 524304 | tf_op jit(solution)/shard_map/reduce_scatter | solution.py:32
  341.4 2.0 copy.16
  343.5 39.3 %reduce-scatter.10.cloned.1.call-done = bf16[64,2304]{1,0:T(8,128)(2,1)} async-done(((bf16[512,2304]{1,0:T(8,128)(2,1)}), bf16[64,2304]{1,0:T(8,128)(2,1)}) %reduce-scatter.10.cloned.1.call-update) | async-done | bytes 294928
  382.7 1.3 copy.18
  384.0 1.0 copy.15
  385.0 203.2 %reduce-scatter.8.cloned.1.call-done = bf16[256,2304]{1,0:T(8,128)(2,1)} async-done(((bf16[2048,2304]{1,0:T(8,128)(2,1)}), bf16[256,2304]{1,0:T(8,128)(2,1)}) %reduce-scatter.8.cloned.1.call-update) | async-done | bytes 1179664 | tf_op jit(solution)/shard_map/reduce_scatter | solution.py:35
  (11 shorter events, 0.2 us)
Async XLA Ops:
  7.2 2.4 copy-start
  7.2 33.5 %all-gather.10.cloned.1.call-start = ((), (), s32[]{:S(2)}) async-start(), calls=%async_computation.7 | async-start | bytes 2654208 | tf_op jit(solution)/shard_map/all_gather | solution.py:25
  7.9 235.5 %all-gather.6.cloned.1.call-start = ((), (), s32[]{:S(2)}) async-start(), calls=%async_computation.3 | async-start | bytes 10616832 | tf_op jit(solution)/shard_map/all_gather | solution.py:26
  11.1 280.8 %all-gather.8.cloned.1.call-start = ((), (), s32[]{:S(2)}) async-start(), calls=%async_computation.6 | async-start | bytes 2621440 | tf_op jit(solution)/shard_map/all_gather | solution.py:24
  11.8 329.6 %reduce-scatter.6.cloned.1.call-start = ((), (), s32[]{:S(2)}) async-start(), calls=%async_computation.4 | async-start | bytes 2621440 | tf_op jit(solution)/shard_map/reduce_scatter | solution.py:32
  254.1 128.7 %reduce-scatter.10.cloned.1.call-start = ((), (), s32[]{:S(2)}) async-start(), calls=%async_computation.8 | async-start | bytes 2654208
  303.8 1.7 copy-start.1
  303.8 284.3 %reduce-scatter.8.cloned.1.call-start = ((), (), s32[]{:S(2)}) async-start(), calls=%async_computation.5 | async-start | bytes 10616832 | tf_op jit(solution)/shard_map/reduce_scatter | solution.py:35
Sparse Core Ops, SparseCore 0:
  9.8 30.7 all-gather.9
  43.7 199.6 all-gather.5
  245.2 46.6 all-gather.7
  294.3 47.1 reduce-scatter.5
  344.0 38.6 reduce-scatter.9
  387.9 200.1 reduce-scatter.7
where the time goes:
time: 597 us; the launch traced here: 595 us
  waiting for transfers between devices  539 us (90%)
  matrix products  30 us (5%)
  between operations  14.2 us (2%)
  local copies, waits for them, and re-layouts  10.2 us (2%)
    reduce_scatter x1, waiting for transfers between devices, per_device(): lax.psum_scatter(transposed_product(panel, grad_rows).astype(jnp.bfloat16...  203 us
    all_gather x1, waiting for transfers between devices, per_device(): whole = lax.all_gather(weight, 'col', axis=0, tiled=True)  203 us
    unnamed x7, waiting for transfers between devices  40.7 us
    all_gather x1, waiting for transfers between devices, per_device(): panel = lax.all_gather(inputs[0], 'row', axis=1, tiled=True)  37.7 us
    all_gather x1, waiting for transfers between devices, per_device(): grad_rows = lax.all_gather(grad_out[0], 'depth', axis=0, tiled=True)  28.8 us
    reduce_scatter x1, waiting for transfers between devices, per_device(): lax.psum_scatter(backward.astype(jnp.bfloat16), 'row', scatter_dimension=...  25.9 us
  transfers between devices with their start and end apart: 6, of which 6 were waited for; matrix products, arithmetic and copies ran while one was open for 7% of the time, Pallas kernels for 0%

commit v1 on v0

v1 whole, which is shorter than its diff:
```python
import jax
import jax.numpy as jnp
from jax import lax
from jax.experimental import pallas as pl
from jax.experimental.pallas import tpu as pltpu
from jax.sharding import Mesh, PartitionSpec as P

BLOCK = 128
BF = jnp.bfloat16
F32 = jnp.float32
VMEM_LIMIT = 56 * 1024 * 1024


def params():
    return pltpu.CompilerParams(vmem_limit_bytes=VMEM_LIMIT)


def cost(flops, moved):
    return pl.CostEstimate(flops=flops, bytes_accessed=moved, transcendentals=0)


def whole(shape):
    return pl.BlockSpec(shape, lambda *_: (0,) * len(shape))


SCALAR = pl.BlockSpec(memory_space=pltpu.SMEM)


def ring(size, step):
    return [(i, (i + step) % size) for i in range(size)]


def swapped(step):
    return [
        (zl * 2 + zh, ((zl + step) % 4) * 2 + 1 - zh)
        for zl in range(4)
        for zh in range(2)
    ]


def dequantize_kernel(scales, quantized, weight):
    for r in range(scales.shape[0]):
        for c in range(scales.shape[1]):
            at = (pl.ds(r * BLOCK, BLOCK), pl.ds(c * BLOCK, BLOCK))
            weight[at] = (quantized[at].astype(F32) * scales[r, c]).astype(BF)


def dequantize(quantized, scales):
    return pl.pallas_call(
        dequantize_kernel,
        out_shape=jax.ShapeDtypeStruct(quantized.shape, BF),
        in_specs=[SCALAR, whole(quantized.shape)],
        out_specs=whole(quantized.shape),
        compiler_params=params(),
        cost_estimate=cost(quantized.size, 4 * quantized.size),
    )(scales, quantized)


def forward_kernel(place, *refs):
    pieces, weights, (out, panel) = refs[:8], refs[8:12], refs[12:]
    turn, y, k = place[0], place[1], place[2]

    @pl.when(pl.program_id(0) == 0)
    def _():
        for s in range(2):
            for j in range(4):
                m = lax.rem(j + 4 - turn, 4)
                lanes = pl.ds(pl.multiple_of(m * 256, 256), 256)
                for b in range(8):
                    e = lax.rem(y - b // 2 + 4, 4)
                    kk = lax.rem(k + b % 2, 2)
                    row = kk * 512 + e * 128 + s * 64
                    rows = pl.ds(pl.multiple_of(row, 64), 64)
                    panel[rows, lanes] = pieces[s * 4 + j][b * 64 : b * 64 + 64, :]

    right = jnp.concatenate([w[...] for w in weights], axis=0)
    total = jnp.dot(panel[...], right, preferred_element_type=F32)
    out[...] = total.astype(BF)


def forward(place, pieces, weights):
    width = weights[0].shape[1]
    tile = 256
    return pl.pallas_call(
        forward_kernel,
        grid=(width // tile,),
        out_shape=jax.ShapeDtypeStruct((1024, width), BF),
        in_specs=[SCALAR]
        + [whole((512, 256))] * 8
        + [pl.BlockSpec((256, tile), lambda n: (0, n))] * 4,
        out_specs=pl.BlockSpec((1024, tile), lambda n: (0, n)),
        scratch_shapes=[pltpu.VMEM((1024, 1024), BF)],
        compiler_params=params(),
        cost_estimate=cost(2 * 1024 * 1024 * width, 2 * (1024 * 1024 + 2 * 1024 * width)),
    )(place, *pieces, *weights)


def weight_grad_kernel(place, *refs):
    pieces, grad, outs, panel = refs[:8], refs[8], refs[9:13], refs[13]
    turn = place[0]

    @pl.when(pl.program_id(0) == 0)
    def _():
        for s in range(2):
            for j in range(4):
                m = lax.rem(j + 4 - turn, 4)
                lanes = pl.ds(pl.multiple_of(m * 256, 256), 256)
                panel[s * 512 : s * 512 + 512, lanes] = pieces[s * 4 + j][...]

    total = lax.dot_general(
        panel[...], grad[...], (((0,), (0,)), ((), ())), preferred_element_type=F32
    )
    for m in range(4):
        outs[m][...] = total[m * 256 : m * 256 + 256, :].astype(BF)


def weight_grad(place, pieces, grad):
    width = grad.shape[1]
    tile = 256
    return pl.pallas_call(
        weight_grad_kernel,
        grid=(width // tile,),
        out_shape=[jax.ShapeDtypeStruct((256, width), BF)] * 4,
        in_specs=[SCALAR]
        + [whole((512, 256))] * 8
        + [pl.BlockSpec((1024, tile), lambda n: (0, n))],
        out_specs=[pl.BlockSpec((256, tile), lambda n: (0, n))] * 4,
        scratch_shapes=[pltpu.VMEM((1024, 1024), BF)],
        compiler_params=params(),
        cost_estimate=cost(2 * 1024 * 1024 * width, 2 * (1024 * 1024 + 2 * 1024 * width)),
    )(place, *pieces, grad)


def backward_kernel(place, grad, *refs):
    weights, outs = refs[:4], refs[4:12]
    turn = place[0]
    step = pl.program_id(0)
    half = pl.num_programs(0) // 2
    tile = grad.shape[0]
    rows = pl.ds(pl.multiple_of(lax.rem(step, half) * tile, tile), tile)
    for m in range(4):
        total = lax.dot_general(
            grad[...], weights[m][...], (((1,), (1,)), ((), ())),
            preferred_element_type=F32,
        ).astype(BF)
        target = lax.rem(turn + m, 4)
        for s in range(2):
            for j in range(4):
                @pl.when((step // half == s) & (target == j))
                def _():
                    outs[s * 4 + j][rows, :] = total


def backward(place, grad, weights):
    width = grad.shape[1]
    tile = 256
    return pl.pallas_call(
        backward_kernel,
        grid=(1024 // tile,),
        out_shape=[jax.ShapeDtypeStruct((512, 256), BF)] * 8,
        in_specs=[SCALAR, pl.BlockSpec((tile, width), lambda n: (n, 0))]
        + [whole((256, width))] * 4,
        out_specs=[whole((512, 256))] * 8,
        compiler_params=params(),
        cost_estimate=cost(2 * 1024 * 1024 * width, 2 * (1024 * 1024 + 2 * 1024 * width)),
    )(place, grad, *weights)


def added(*terms):
    total = terms[0].astype(F32)
    for term in terms[1:]:
        total = total + term.astype(F32)
    return total.astype(BF)


def per_device(inputs, qweight, scales, grad_out):
    y, k, zl = lax.axis_index("y"), lax.axis_index("k"), lax.axis_index("zl")
    x, zh = lax.axis_index("x"), lax.axis_index("zh")
    turn = lax.rem(zl - x + 4, 4)
    place = jnp.stack([turn, y, k, zh]).astype(jnp.int32)

    grad_own = grad_out[0]
    grad_other = lax.ppermute(grad_own, "zh", ring(2, 1))

    panel = inputs[0]
    half_own = lax.dynamic_slice(panel, (0, zh * 256), (512, 256))
    half_other = lax.dynamic_slice(panel, (0, (1 - zh) * 256), (512, 256))
    near = [half_own] + [lax.ppermute(half_own, "zl", ring(4, j)) for j in (1, 2, 3)]
    far = [lax.ppermute(half_other, ("zl", "zh"), swapped(j)) for j in range(4)]
    pieces = near + far

    weight = dequantize(qweight, scales)
    before = lax.ppermute(weight, "x", ring(4, 1))
    after = lax.ppermute(weight, "x", ring(4, -1))
    across = jnp.concatenate(
        [
            lax.ppermute(before[:128], "x", ring(4, 1)),
            lax.ppermute(after[128:], "x", ring(4, -1)),
        ],
        axis=0,
    )
    weights = [weight, before, across, after]

    both = jnp.stack([grad_own, grad_other])
    grads = lax.all_gather(both, ("y", "k"), axis=1, tiled=True).reshape(1024, -1)

    sums = backward(place, grads, weights)
    own = [sums[0]] + [lax.ppermute(sums[j], "zl", ring(4, -j)) for j in (1, 2, 3)]
    other = [lax.ppermute(sums[4 + j], ("zl", "zh"), swapped(-j)) for j in range(4)]
    own, other = added(*own), added(*other)
    low = jnp.where(zh == 0, own, other)
    high = jnp.where(zh == 0, other, own)
    grad_inputs = jnp.concatenate([low, high], axis=1)

    terms = weight_grad(place, pieces, grads)
    top = lax.ppermute(terms[2][:128], "x", ring(4, 1))
    bottom = lax.ppermute(terms[2][128:], "x", ring(4, -1))
    up = jnp.concatenate([added(terms[3][:128], top), terms[3][128:]], axis=0)
    down = jnp.concatenate([terms[1][:128], added(terms[1][128:], bottom)], axis=0)
    up = lax.ppermute(up, "x", ring(4, 1))
    down = lax.ppermute(down, "x", ring(4, -1))
    grad_weight = added(terms[0], up, down)

    product = forward(place, pieces, weights)
    mine = added(product[:512], lax.ppermute(product[512:], "k", ring(2, 1)))
    blocks = [mine[e * 128 : e * 128 + 128] for e in range(4)]
    top = lax.ppermute(blocks[2][:64], "y", ring(4, 1))
    bottom = lax.ppermute(blocks[2][64:], "y", ring(4, -1))
    up = jnp.concatenate([added(blocks[3][:64], top), blocks[3][64:]], axis=0)
    down = jnp.concatenate([blocks[1][:64], added(blocks[1][64:], bottom)], axis=0)
    up = lax.ppermute(up, "y", ring(4, 1))
    down = lax.ppermute(down, "y", ring(4, -1))
    last = added(blocks[0], up, down)
    projected = added(last[:64], lax.ppermute(last[64:], "zh", ring(2, 1)))

    return projected[None], grad_inputs[None], grad_weight


def solution(mesh):
    axes = Mesh(mesh.devices.reshape(4, 2, 4, 4, 2), ("y", "k", "zl", "x", "zh"))
    return jax.shard_map(
        per_device,
        mesh=axes,
        in_specs=(
            P(("x", "zh"), None, ("y", "k", "zl")),
            P(("y", "k", "x", "zh"), "zl"),
            P(("y", "k", "x", "zh"), "zl"),
            P(("x", "zh"), ("y", "k"), "zl"),
        ),
        out_specs=(
            P(("x", "zh"), ("y", "k"), "zl"),
            P(("x", "zh"), None, ("y", "k", "zl")),
            P(("y", "k", "x", "zh"), "zl"),
        ),
        check_vma=False,
    )
```

time: 597 us -> 267 us (0.45)
  waiting for transfers between devices: 539 us -> 123 us
  starting transfers between devices: 0.24 us -> 64 us
  Pallas kernels: 0 us -> 42.9 us
  matrix products: 30 us -> 0 us
  other arithmetic: 1.28 us -> 9.57 us
    all_gather x3 -> x1, waiting for transfers between devices: 269 us -> 0.01 us  [per_device(): lax.all_gather(both, ('y', 'k'), axis=1, tiled=True).reshape(1024, -1)]
    reduce_scatter x2 -> x0, waiting for transfers between devices: 229 us -> none  [the longest x1 203 us: per_device(): lax.psum_scatter(transposed_product(panel, grad_rows).astype(jnp.bfloat16...]
    ppermute x0 -> x29, waiting for transfers between devices: none -> 123 us  [the longest x3 24.3 us: per_device(): lax.ppermute(half_own, 'zl', ring(4, j))]
    ppermute x0 -> x29, starting transfers between devices: none -> 64 us  [the longest x4 17.6 us: per_device(): lax.ppermute(sums[4 + j], ('zl', 'zh'), swapped(-j))]
    pallas_call x0 -> x4, Pallas kernels: none -> 42.9 us  [the longest x1 17.4 us: backward(): pl.pallas_call(backward_kernel, grid=(1024 // tile,), out_shape=[jax.Shap...]
    unnamed x7 -> x1, waiting for transfers between devices: 40.7 us -> 0.02 us
    dot_general x3 -> x0, matrix products: 30 us -> none  [the longest x1 10.7 us: against_rows(): lax.dot_general(left, right, (((1,), (1,)), ((), ())), preferred_element_...]
    unnamed x13 -> x41, local copies, waits for them, and re-layouts: 10.2 us -> 3.81 us
  transfers between devices with their start and end apart: 6 -> 30, of which waited for: 6 -> 14; matrix products, arithmetic and copies ran while one was open for 7% -> 5% of each run, Pallas kernels for 0% -> 16%
where the time goes in v1:
time: 267 us; the launch traced here: 263 us
  waiting for transfers between devices  123 us (46%)
  starting transfers between devices  64 us (24%)
  Pallas kernels  42.9 us (16%)
  between operations  14.3 us (5%)
  other arithmetic  9.57 us (4%)
  local copies, waits for them, and re-layouts  9.35 us (4%)
    ppermute x3, waiting for transfers between devices, per_device(): lax.ppermute(half_own, 'zl', ring(4, j))  24.3 us
    ppermute x3, waiting for transfers between devices, per_device(): lax.ppermute(sums[j], 'zl', ring(4, -j))  20 us
    ppermute x4, waiting for transfers between devices, per_device(): far = [lax.ppermute(half_other, ('zl', 'zh'), swapped(j)) for j in range(4)]  17.8 us
    ppermute x4, starting transfers between devices, per_device(): lax.ppermute(sums[4 + j], ('zl', 'zh'), swapped(-j))  17.6 us
    pallas_call x1, Pallas kernels, backward(): pl.pallas_call(backward_kernel, grid=(1024 // tile,), out_shape=[jax.Shap...  17.4 us
    ppermute x1, waiting for transfers between devices, per_device(): before = lax.ppermute(weight, 'x', ring(4, 1))  16.8 us
    ppermute x1, waiting for transfers between devices, per_device(): up = lax.ppermute(up, 'x', ring(4, 1))  12.1 us
    pallas_call x1, Pallas kernels, forward(): pl.pallas_call(forward_kernel, grid=(width // tile,), out_shape=jax.Shape...  11.9 us
  transfers between devices with their start and end apart: 30, of which 14 were waited for; matrix products, arithmetic and copies ran while one was open for 5% of the time, Pallas kernels for 16%

profile of v1, /device:TPU:32, one launch (start us, length us, event | category | flops | bytes accessed | tf_op | source)
XLA Modules:
  0.0 263.4 jit_solution(16050996906933434514)
XLA Ops:
  7.2 6.4 %collective-permute-start.17 = (bf16[64,2304]{1,0:T(8,128)(2,1)}, bf16[64,2304]{1,0:T(8,128)(2,1)S(1)}, u32[]{:S(2)}, u32[]{:S(2)}) collective-permute-start(bf16[64,2304]{1,0:T(8,128)(2,1)} %bitcast.15), channel_id=1, source_target_pairs={{0,1},{1,0},{2,3},{3,2},{4,5},{5,4},{6,7},{7,6},{8,9},{9,8},{10,11... | collective-permute-start | bytes 884744 | tf_op jit(solution)/shard_map/ppermute | solution.py:183
  19.4 7.9 %collective-permute-done.17 = bf16[64,2304]{1,0:T(8,128)(2,1)S(1)} collective-permute-done((bf16[64,2304]{1,0:T(8,128)(2,1)}, bf16[64,2304]{1,0:T(8,128)(2,1)S(1)}, u32[]{:S(2)}, u32[]{:S(2)}) %collective-permute-start.17) | collective-permute-done | bytes 294944 | tf_op jit(solution)/shard_map/ppermute | solution.py:183
  28.1 16.8 %collective-permute-done.7.refs_9_.refs_1_ = bf16[256,2304]{1,0:T(8,128)(2,1)S(1)} collective-permute-done((bf16[256,2304]{1,0:T(8,128)(2,1)}, bf16[256,2304]{1,0:T(8,128)(2,1)S(1)}, u32[]{:S(2)}, u32[]{:S(2)}) %collective-permute-start.7) | collective-permute-done | bytes 1179680 | tf_op jit(solution)/shard_map/ppermute | solution.py:193
  53.8 6.4 %collective-permute-done.8 = bf16[128,2304]{1,0:T(8,128)(2,1)S(1)} collective-permute-done((bf16[128,2304]{1,0:T(8,128)(2,1)S(1)}, bf16[128,2304]{1,0:T(8,128)(2,1)S(1)}, u32[]{:S(2)}, u32[]{:S(2)}) %collective-permute-start.8) | collective-permute-done | bytes 589856 | tf_op jit(solution)/shard_map/ppermute | solution.py:197
  60.8 18.9 %collective-permute-done.refs_1_ = bf16[512,256]{1,0:T(8,128)(2,1)S(1)} collective-permute-done((bf16[512,256]{1,0:T(8,128)(2,1)S(1)}, bf16[512,256]{1,0:T(8,128)(2,1)S(1)}, u32[]{:S(2)}, u32[]{:S(2)}) %collective-permute-start) | collective-permute-done | bytes 262176 | tf_op jit(solution)/shard_map/ppermute | solution.py:188
  81.3 2.7 %collective-permute-done.1.refs_2_ = bf16[512,256]{1,0:T(8,128)(2,1)S(1)} collective-permute-done((bf16[512,256]{1,0:T(8,128)(2,1)S(1)}, bf16[512,256]{1,0:T(8,128)(2,1)S(1)}, u32[]{:S(2)}, u32[]{:S(2)}) %collective-permute-start.1) | collective-permute-done | bytes 262176 | tf_op jit(solution)/shard_map/ppermute | solution.py:188
  86.0 2.7 %collective-permute-done.2.refs_3_ = bf16[512,256]{1,0:T(8,128)(2,1)} collective-permute-done((bf16[512,256]{1,0:T(8,128)(2,1)S(1)}, bf16[512,256]{1,0:T(8,128)(2,1)}, u32[]{:S(2)}, u32[]{:S(2)}) %collective-permute-start.2) | collective-permute-done | bytes 262176 | tf_op jit(solution)/shard_map/ppermute | solution.py:188
  88.7 17.8 %collective-permute-done.4.refs_5_ = bf16[512,256]{1,0:T(8,128)(2,1)S(1)} collective-permute-done((bf16[512,256]{1,0:T(8,128)(2,1)S(1)}, bf16[512,256]{1,0:T(8,128)(2,1)S(1)}, u32[]{:S(2)}, u32[]{:S(2)}) %collective-permute-start.4) | collective-permute-done | bytes 262176 | tf_op jit(solution)/shard_map/ppermute | solution.py:189
  108.0 11.9 %shard_map.68 = bf16[1024,2304]{1,0:T(8,128)(2,1)} custom-call(s32[4]{0:T(128)} %pad_add_fusion.place, bf16[512,256]{1,0:T(8,128)(2,1)} %copy-done.8, bf16[512,256]{1,0:T(8,128)(2,1)} %copy-done.10, bf16[512,256]{1,0:T(8,128)(2,1)} %copy-done.11, bf16[512,256]{1,0:T(8,128)(2,1)} %collective-permute-done.2.refs_3_, bf16[512,256]{1,0:T(8,128)(2,1)} %copy-done.12, ...), custom_call_target="tpu_custom_call" | custom-call | flops 4831838208 | bytes 11534336 | tf_op jit(solution)/shard_map/pallas_call | solution.py:84
  121.9 4.5 %collective-permute-done.11 = bf16[512,2304]{1,0:T(8,128)(2,1)S(1)} collective-permute-done((bf16[512,2304]{1,0:T(8,128)(2,1)S(1)}, bf16[512,2304]{1,0:T(8,128)(2,1)S(1)}, u32[]{:S(2)}, u32[]{:S(2)}) %collective-permute-start.11) | collective-permute-done | bytes 2359328 | tf_op jit(solution)/shard_map/ppermute | solution.py:225
  130.9 7.1 %collective-permute-done.12 = bf16[64,2304]{1,0:T(8,128)(2,1)} collective-permute-done((bf16[64,2304]{1,0:T(8,128)(2,1)S(1)}, bf16[64,2304]{1,0:T(8,128)(2,1)}, u32[]{:S(2)}, u32[]{:S(2)}) %collective-permute-start.12) | collective-permute-done | bytes 294944 | tf_op jit(solution)/shard_map/ppermute | solution.py:227
  143.5 11.1 %shard_map.70 = (bf16[256,2304]{1,0:T(8,128)(2,1)}, bf16[256,2304]{1,0:T(8,128)(2,1)}, bf16[256,2304]{1,0:T(8,128)(2,1)}, bf16[256,2304]{1,0:T(8,128)(2,1)}) custom-call(s32[4]{0:T(128)} %pad_add_fusion.place, bf16[512,256]{1,0:T(8,128)(2,1)} %copy-done.8, bf16[512,256]{1,0:T(8,128)(2,1)} %copy-done.10, bf16[512,256]{1,0:T(8,128)(2,1)} %copy-done.11, ...), custom_call_target="tpu_custom_call" | custom-call | flops 4831838208 | bytes 11534336 | tf_op jit(solution)/shard_map/pallas_call | solution.py:120
  158.4 3.5 %collective-permute-start.16 = (bf16[64,2304]{1,0:T(8,128)(2,1)S(1)}, bf16[64,2304]{1,0:T(8,128)(2,1)S(1)}, u32[]{:S(2)}, u32[]{:S(2)}) collective-permute-start(bf16[64,2304]{1,0:T(8,128)(2,1)S(1)} %slice.97), channel_id=1, source_target_pairs={{0,1},{1,0},{2,3},{3,2},{4,5},{5,4},{6,7},{7,6},{8,9},{9,8},{10,11... | collective-permute-start | bytes 884744 | tf_op jit(solution)/shard_map/ppermute | solution.py:234
  162.0 3.1 %collective-permute-start.27 = (bf16[128,2304]{1,0:T(8,128)(2,1)S(1)}, bf16[128,2304]{1,0:T(8,128)(2,1)S(1)}, u32[]{:S(2)}, u32[]{:S(2)}) collective-permute-start(bf16[128,2304]{1,0:T(8,128)(2,1)S(1)} %get-tuple-element.37), channel_id=1, source_target_pairs={{0,6},{2,0},{4,2},{6,4},{1,7},{3,1},{5,3},{7,5},{8,14},{10,8},{12,... | collective-permute-start | bytes 1769480 | tf_op jit(solution)/shard_map/ppermute | solution.py:217
  165.1 17.4 %shard_map.69 = (bf16[512,256]{1,0:T(8,128)(2,1)}, bf16[512,256]{1,0:T(8,128)(2,1)}, bf16[512,256]{1,0:T(8,128)(2,1)}, bf16[512,256]{1,0:T(8,128)(2,1)}, bf16[51...) custom-call(s32[4]{0:T(128)} %pad_add_fusion.place, ...), custom_call_target="tpu_custom_call" | custom-call | flops 4831838208 | bytes 11534336 | tf_op jit(solution)/shard_map/pallas_call | solution.py:157
  182.5 2.6 %collective-permute-start.18 = (bf16[512,256]{1,0:T(8,128)(2,1)}, bf16[512,256]{1,0:T(8,128)(2,1)S(1)}, u32[]{:S(2)}, u32[]{:S(2)}) collective-permute-start(bf16[512,256]{1,0:T(8,128)(2,1)} %get-tuple-element.16), channel_id=1, source_target_pairs={{0,24},{8,0},{16,8},{24,16},{1,25},{9,1},{17,9},{25,17},{2,26},{10... | collective-permute-start | bytes 786440 | tf_op jit(solution)/shard_map/ppermute | solution.py:208
  185.1 3.8 %collective-permute-start.19 = (bf16[512,256]{1,0:T(8,128)(2,1)}, bf16[512,256]{1,0:T(8,128)(2,1)S(1)}, u32[]{:S(2)}, u32[]{:S(2)}) collective-permute-start(bf16[512,256]{1,0:T(8,128)(2,1)} %get-tuple-element.17), channel_id=1, source_target_pairs={{0,16},{8,24},{16,0},{24,8},{1,17},{9,25},{17,1},{25,9},{2,18},{10... | collective-permute-start | bytes 786440 | tf_op jit(solution)/shard_map/ppermute | solution.py:208
  189.0 2.8 %collective-permute-start.20 = (bf16[512,256]{1,0:T(8,128)(2,1)}, bf16[512,256]{1,0:T(8,128)(2,1)S(1)}, u32[]{:S(2)}, u32[]{:S(2)}) collective-permute-start(bf16[512,256]{1,0:T(8,128)(2,1)} %get-tuple-element.18), channel_id=1, source_target_pairs={{0,8},{8,16},{16,24},{24,0},{1,9},{9,17},{17,25},{25,1},{2,10},{10... | collective-permute-start | bytes 786440 | tf_op jit(solution)/shard_map/ppermute | solution.py:208
  199.6 13.3 %collective-permute-done.19 = bf16[512,256]{1,0:T(8,128)(2,1)S(1)} collective-permute-done((bf16[512,256]{1,0:T(8,128)(2,1)}, bf16[512,256]{1,0:T(8,128)(2,1)S(1)}, u32[]{:S(2)}, u32[]{:S(2)}) %collective-permute-start.19) | collective-permute-done | bytes 262176 | tf_op jit(solution)/shard_map/ppermute | solution.py:208
  212.9 11.9 %collective-permute-start.24 = (bf16[512,256]{1,0:T(8,128)(2,1)S(1)}, bf16[512,256]{1,0:T(8,128)(2,1)S(1)}, u32[]{:S(2)}, u32[]{:S(2)}) collective-permute-start(bf16[512,256]{1,0:T(8,128)(2,1)S(1)} %copy-done.15), channel_id=1, source_target_pairs={{0,9},{1,8},{8,17},{9,16},{16,25},{17,24},{24,1},{25,0},{2,11},{3,... | collective-permute-start | bytes 786440 | tf_op jit(solution)/shard_map/ppermute | solution.py:209
  224.8 6.7 %collective-permute-done.20 = bf16[512,256]{1,0:T(8,128)(2,1)S(1)} collective-permute-done((bf16[512,256]{1,0:T(8,128)(2,1)}, bf16[512,256]{1,0:T(8,128)(2,1)S(1)}, u32[]{:S(2)}, u32[]{:S(2)}) %collective-permute-start.20) | collective-permute-done | bytes 262176 | tf_op jit(solution)/shard_map/ppermute | solution.py:208
  231.5 3.2 %collective-permute-start.28 = (bf16[256,2304]{1,0:T(8,128)(2,1)S(1)}, bf16[256,2304]{1,0:T(8,128)(2,1)S(1)}, u32[]{:S(2)}, u32[]{:S(2)}) collective-permute-start(bf16[256,2304]{1,0:T(8,128)(2,1)S(1)} %pad_maximum_fusion.1), channel_id=1, source_target_pairs={{0,6},{2,0},{4,2},{6,4},{1,7},{3,1},{5,3},{7,5},{8,14},{10,8},{12,... | collective-permute-start | bytes 3538952 | tf_op jit(solution)/shard_map/ppermute | solution.py:221
  235.5 6.3 %collective-permute-done.24 = bf16[512,256]{1,0:T(8,128)(2,1)S(1)} collective-permute-done((bf16[512,256]{1,0:T(8,128)(2,1)S(1)}, bf16[512,256]{1,0:T(8,128)(2,1)S(1)}, u32[]{:S(2)}, u32[]{:S(2)}) %collective-permute-start.24) | collective-permute-done | bytes 262176 | tf_op jit(solution)/shard_map/ppermute | solution.py:209
  243.0 12.1 %collective-permute-done.26 = bf16[256,2304]{1,0:T(8,128)(2,1)S(1)} collective-permute-done((bf16[256,2304]{1,0:T(8,128)(2,1)S(1)}, bf16[256,2304]{1,0:T(8,128)(2,1)S(1)}, u32[]{:S(2)}, u32[]{:S(2)}) %collective-permute-start.26) | collective-permute-done | bytes 1179680 | tf_op jit(solution)/shard_map/ppermute | solution.py:220
  (108 shorter events, 48.1 us)
Async XLA Ops:
  7.2 136.4 %all-gather.2.cloned.1.call-start = ((), (), s32[]{:S(2)}) async-start(), calls=%async_computation | async-start | bytes 5308416 | tf_op jit(solution)/shard_map/all_gather | solution.py:205
  7.2 20.0 %collective-permute-start.17 = (bf16[64,2304]{1,0:T(8,128)(2,1)}, bf16[64,2304]{1,0:T(8,128)(2,1)S(1)}, u32[]{:S(2)}, u32[]{:S(2)}) collective-permute-start(bf16[64,2304]{1,0:T(8,128)(2,1)} %bitcast.15), channel_id=1, source_target_pairs={{0,1},{1,0},{2,3},{3,2},{4,5},{5,4},{6,7},{7,6},{8,9},{9,8},{10,11... | collective-permute-start | bytes 884744 | tf_op jit(solution)/shard_map/ppermute | solution.py:183
  16.1 28.8 %collective-permute-start.7 = (bf16[256,2304]{1,0:T(8,128)(2,1)}, bf16[256,2304]{1,0:T(8,128)(2,1)S(1)}, u32[]{:S(2)}, u32[]{:S(2)}) collective-permute-start(bf16[256,2304]{1,0:T(8,128)(2,1)} %shard_map.67.refs_8_.refs_0_), channel_id=1, source_target_pairs={{0,2},{2,4},{4,6},{6,0},{1,3},{3,5},{5,7},{7,1},{8,10},{10,12},{12... | collective-permute-start | bytes 3538952 | tf_op jit(solution)/shard_map/ppermute | solution.py:193
  17.6 28.4 %collective-permute-start.9 = (bf16[256,2304]{1,0:T(8,128)(2,1)}, bf16[256,2304]{1,0:T(8,128)(2,1)}, u32[]{:S(2)}, u32[]{:S(2)}) collective-permute-start(bf16[256,2304]{1,0:T(8,128)(2,1)} %shard_map.67.refs_8_.refs_0_), channel_id=1, source_target_pairs={{0,6},{2,0},{4,2},{6,4},{1,7},{3,1},{5,3},{7,5},{8,14},{10,8},{12,... | collective-permute-start | bytes 3538952 | tf_op jit(solution)/shard_map/ppermute | solution.py:194
  47.1 37.1 %collective-permute-start.10 = (bf16[128,2304]{1,0:T(8,128)(2,1)S(1)}, bf16[128,2304]{1,0:T(8,128)(2,1)S(1)}, u32[]{:S(2)}, u32[]{:S(2)}) collective-permute-start(bf16[128,2304]{1,0:T(8,128)(2,1)S(1)} %slice.86), channel_id=1, source_target_pairs={{0,6},{2,0},{4,2},{6,4},{1,7},{3,1},{5,3},{7,5},{8,14},{10,8},{12,... | collective-permute-start | bytes 1769480 | tf_op jit(solution)/shard_map/ppermute | solution.py:198
  49.6 30.2 %collective-permute-start = (bf16[512,256]{1,0:T(8,128)(2,1)S(1)}, bf16[512,256]{1,0:T(8,128)(2,1)S(1)}, u32[]{:S(2)}, u32[]{:S(2)}) collective-permute-start(bf16[512,256]{1,0:T(8,128)(2,1)S(1)} %get-tuple-element.39.refs_0_), channel_id=1, source_target_pairs={{0,8},{8,16},{16,24},{24,0},{1,9},{9,17},{17,25},{25,1},{2,10},{10... | collective-permute-start | bytes 786440 | tf_op jit(solution)/shard_map/ppermute | solution.py:188
  50.7 33.3 %collective-permute-start.1 = (bf16[512,256]{1,0:T(8,128)(2,1)S(1)}, bf16[512,256]{1,0:T(8,128)(2,1)S(1)}, u32[]{:S(2)}, u32[]{:S(2)}) collective-permute-start(bf16[512,256]{1,0:T(8,128)(2,1)S(1)} %get-tuple-element.39.refs_0_), channel_id=1, source_target_pairs={{0,16},{8,24},{16,0},{24,8},{1,17},{9,25},{17,1},{25,9},{2,18},{10... | collective-permute-start | bytes 786440 | tf_op jit(solution)/shard_map/ppermute | solution.py:188
  53.0 35.6 %collective-permute-start.2 = (bf16[512,256]{1,0:T(8,128)(2,1)S(1)}, bf16[512,256]{1,0:T(8,128)(2,1)}, u32[]{:S(2)}, u32[]{:S(2)}) collective-permute-start(bf16[512,256]{1,0:T(8,128)(2,1)S(1)} %get-tuple-element.39.refs_0_), channel_id=1, source_target_pairs={{0,24},{8,0},{16,8},{24,16},{1,25},{9,1},{17,9},{25,17},{2,26},{10... | collective-permute-start | bytes 786440 | tf_op jit(solution)/shard_map/ppermute | solution.py:188
  60.2 28.5 %collective-permute-start.3 = (bf16[512,256]{1,0:T(8,128)(2,1)S(1)}, bf16[512,256]{1,0:T(8,128)(2,1)S(1)}, u32[]{:S(2)}, u32[]{:S(2)}) collective-permute-start(bf16[512,256]{1,0:T(8,128)(2,1)S(1)} %get-tuple-element.38), channel_id=1, source_target_pairs={{0,1},{1,0},{8,9},{9,8},{16,17},{17,16},{24,25},{25,24},{2,3},{3,2... | collective-permute-start | bytes 786440 | tf_op jit(solution)/shard_map/ppermute | solution.py:189
  79.8 26.7 %collective-permute-start.4 = (bf16[512,256]{1,0:T(8,128)(2,1)S(1)}, bf16[512,256]{1,0:T(8,128)(2,1)S(1)}, u32[]{:S(2)}, u32[]{:S(2)}) collective-permute-start(bf16[512,256]{1,0:T(8,128)(2,1)S(1)} %get-tuple-element.38), channel_id=1, source_target_pairs={{0,9},{1,8},{8,17},{9,16},{16,25},{17,24},{24,1},{25,0},{2,11},{3,... | collective-permute-start | bytes 786440 | tf_op jit(solution)/shard_map/ppermute | solution.py:189
  84.0 22.5 %collective-permute-start.5 = (bf16[512,256]{1,0:T(8,128)(2,1)S(1)}, bf16[512,256]{1,0:T(8,128)(2,1)S(1)}, u32[]{:S(2)}, u32[]{:S(2)}) collective-permute-start(bf16[512,256]{1,0:T(8,128)(2,1)S(1)} %get-tuple-element.38), channel_id=1, source_target_pairs={{0,17},{1,16},{8,25},{9,24},{16,1},{17,0},{24,9},{25,8},{2,19},{3,... | collective-permute-start | bytes 786440 | tf_op jit(solution)/shard_map/ppermute | solution.py:189
  84.2 22.3 %collective-permute-start.6 = (bf16[512,256]{1,0:T(8,128)(2,1)S(1)}, bf16[512,256]{1,0:T(8,128)(2,1)S(1)}, u32[]{:S(2)}, u32[]{:S(2)}) collective-permute-start(bf16[512,256]{1,0:T(8,128)(2,1)S(1)} %get-tuple-element.38), channel_id=1, source_target_pairs={{0,25},{1,24},{8,1},{9,0},{16,9},{17,8},{24,17},{25,16},{2,27},{3,... | collective-permute-start | bytes 786440 | tf_op jit(solution)/shard_map/ppermute | solution.py:189
  139.3 17.5 %collective-permute-start.13 = (bf16[128,2304]{1,0:T(8,128)(2,1)S(1)}, bf16[128,2304]{1,0:T(8,128)(2,1)}, u32[]{:S(2)}, u32[]{:S(2)}) collective-permute-start(bf16[128,2304]{1,0:T(8,128)(2,1)S(1)} %pad_maximum_fusion.2), channel_id=1, source_target_pairs={{0,64},{64,128},{128,192},{192,0},{1,65},{65,129},{129,193},{193,1... | collective-permute-start | bytes 1769480 | tf_op jit(solution)/shard_map/ppermute | solution.py:231
  156.8 32.1 %collective-permute-start.25 = (bf16[128,2304]{1,0:T(8,128)(2,1)}, bf16[128,2304]{1,0:T(8,128)(2,1)S(1)}, u32[]{:S(2)}, u32[]{:S(2)}) collective-permute-start(bf16[128,2304]{1,0:T(8,128)(2,1)} %get-tuple-element.36), channel_id=1, source_target_pairs={{0,2},{2,4},{4,6},{6,0},{1,3},{3,5},{5,7},{7,1},{8,10},{10,12},{12... | collective-permute-start | bytes 1769480 | tf_op jit(solution)/shard_map/ppermute | solution.py:216
  158.4 36.5 %collective-permute-start.16 = (bf16[64,2304]{1,0:T(8,128)(2,1)S(1)}, bf16[64,2304]{1,0:T(8,128)(2,1)S(1)}, u32[]{:S(2)}, u32[]{:S(2)}) collective-permute-start(bf16[64,2304]{1,0:T(8,128)(2,1)S(1)} %slice.97), channel_id=1, source_target_pairs={{0,1},{1,0},{2,3},{3,2},{4,5},{5,4},{6,7},{7,6},{8,9},{9,8},{10,11... | collective-permute-start | bytes 884744 | tf_op jit(solution)/shard_map/ppermute | solution.py:234
  162.0 30.1 %collective-permute-start.27 = (bf16[128,2304]{1,0:T(8,128)(2,1)S(1)}, bf16[128,2304]{1,0:T(8,128)(2,1)S(1)}, u32[]{:S(2)}, u32[]{:S(2)}) collective-permute-start(bf16[128,2304]{1,0:T(8,128)(2,1)S(1)} %get-tuple-element.37), channel_id=1, source_target_pairs={{0,6},{2,0},{4,2},{6,4},{1,7},{3,1},{5,3},{7,5},{8,14},{10,8},{12,... | collective-permute-start | bytes 1769480 | tf_op jit(solution)/shard_map/ppermute | solution.py:217
  185.1 27.8 %collective-permute-start.19 = (bf16[512,256]{1,0:T(8,128)(2,1)}, bf16[512,256]{1,0:T(8,128)(2,1)S(1)}, u32[]{:S(2)}, u32[]{:S(2)}) collective-permute-start(bf16[512,256]{1,0:T(8,128)(2,1)} %get-tuple-element.17), channel_id=1, source_target_pairs={{0,16},{8,24},{16,0},{24,8},{1,17},{9,25},{17,1},{25,9},{2,18},{10... | collective-permute-start | bytes 786440 | tf_op jit(solution)/shard_map/ppermute | solution.py:208
  189.0 42.5 %collective-permute-start.20 = (bf16[512,256]{1,0:T(8,128)(2,1)}, bf16[512,256]{1,0:T(8,128)(2,1)S(1)}, u32[]{:S(2)}, u32[]{:S(2)}) collective-permute-start(bf16[512,256]{1,0:T(8,128)(2,1)} %get-tuple-element.18), channel_id=1, source_target_pairs={{0,8},{8,16},{16,24},{24,0},{1,9},{9,17},{17,25},{25,1},{2,10},{10... | collective-permute-start | bytes 786440 | tf_op jit(solution)/shard_map/ppermute | solution.py:208
  192.9 38.6 %collective-permute-start.21 = (bf16[512,256]{1,0:T(8,128)(2,1)S(1)}, bf16[512,256]{1,0:T(8,128)(2,1)S(1)}, u32[]{:S(2)}, u32[]{:S(2)}) collective-permute-start(bf16[512,256]{1,0:T(8,128)(2,1)S(1)} %copy-done.19), channel_id=1, source_target_pairs={{0,1},{1,0},{8,9},{9,8},{16,17},{17,16},{24,25},{25,24},{2,3},{3,2... | collective-permute-start | bytes 786440 | tf_op jit(solution)/shard_map/ppermute | solution.py:209
  195.7 39.8 %collective-permute-start.22 = (bf16[512,256]{1,0:T(8,128)(2,1)S(1)}, bf16[512,256]{1,0:T(8,128)(2,1)S(1)}, u32[]{:S(2)}, u32[]{:S(2)}) collective-permute-start(bf16[512,256]{1,0:T(8,128)(2,1)S(1)} %copy-done.18), channel_id=1, source_target_pairs={{0,25},{1,24},{8,1},{9,0},{16,9},{17,8},{24,17},{25,16},{2,27},{3,... | collective-permute-start | bytes 786440 | tf_op jit(solution)/shard_map/ppermute | solution.py:209
  197.6 37.9 %collective-permute-start.23 = (bf16[512,256]{1,0:T(8,128)(2,1)S(1)}, bf16[512,256]{1,0:T(8,128)(2,1)S(1)}, u32[]{:S(2)}, u32[]{:S(2)}) collective-permute-start(bf16[512,256]{1,0:T(8,128)(2,1)S(1)} %copy-done.17), channel_id=1, source_target_pairs={{0,17},{1,16},{8,25},{9,24},{16,1},{17,0},{24,9},{25,8},{2,19},{3,... | collective-permute-start | bytes 786440 | tf_op jit(solution)/shard_map/ppermute | solution.py:209
  212.9 28.9 %collective-permute-start.24 = (bf16[512,256]{1,0:T(8,128)(2,1)S(1)}, bf16[512,256]{1,0:T(8,128)(2,1)S(1)}, u32[]{:S(2)}, u32[]{:S(2)}) collective-permute-start(bf16[512,256]{1,0:T(8,128)(2,1)S(1)} %copy-done.15), channel_id=1, source_target_pairs={{0,9},{1,8},{8,17},{9,16},{16,25},{17,24},{24,1},{25,0},{2,11},{3,... | collective-permute-start | bytes 786440 | tf_op jit(solution)/shard_map/ppermute | solution.py:209
  231.5 23.6 %collective-permute-start.26 = (bf16[256,2304]{1,0:T(8,128)(2,1)S(1)}, bf16[256,2304]{1,0:T(8,128)(2,1)S(1)}, u32[]{:S(2)}, u32[]{:S(2)}) collective-permute-start(bf16[256,2304]{1,0:T(8,128)(2,1)S(1)} %pad_maximum_fusion), channel_id=1, source_target_pairs={{0,2},{2,4},{4,6},{6,0},{1,3},{3,5},{5,7},{7,1},{8,10},{10,12},{12... | collective-permute-start | bytes 3538952 | tf_op jit(solution)/shard_map/ppermute | solution.py:220
  231.5 23.6 %collective-permute-start.28 = (bf16[256,2304]{1,0:T(8,128)(2,1)S(1)}, bf16[256,2304]{1,0:T(8,128)(2,1)S(1)}, u32[]{:S(2)}, u32[]{:S(2)}) collective-permute-start(bf16[256,2304]{1,0:T(8,128)(2,1)S(1)} %pad_maximum_fusion.1), channel_id=1, source_target_pairs={{0,6},{2,0},{4,2},{6,4},{1,7},{3,1},{5,3},{7,5},{8,14},{10,8},{12,... | collective-permute-start | bytes 3538952 | tf_op jit(solution)/shard_map/ppermute | solution.py:221
  (26 other events, 339.6 us)
Sparse Core Ops, SparseCore 0:
  28.3 38.3 all-gather.1

commit v2 on v0

v2 whole, which is shorter than its diff:
```python
import jax
import jax.numpy as jnp
from jax import lax
from jax.experimental import pallas as pl
from jax.experimental.pallas import tpu as pltpu
from jax.sharding import Mesh, PartitionSpec as P

BLOCK = 128
BF = jnp.bfloat16
F32 = jnp.float32
VMEM_LIMIT = 56 * 1024 * 1024


def params():
    return pltpu.CompilerParams(vmem_limit_bytes=VMEM_LIMIT)


def cost(flops, moved):
    return pl.CostEstimate(flops=flops, bytes_accessed=moved, transcendentals=0)


def whole(shape):
    return pl.BlockSpec(shape, lambda *_: (0,) * len(shape))


SCALAR = pl.BlockSpec(memory_space=pltpu.SMEM)
ANY = pl.BlockSpec(memory_space=pl.ANY)


def ring(size, step):
    return [(i, (i + step) % size) for i in range(size)]


def prepare_kernel(scales, quantized, inputs, grad, top, bottom, split, passed):
    passed[...] = grad[...]
    for r, half in enumerate((top, bottom)):
        for c in range(scales.shape[1]):
            lanes = pl.ds(c * BLOCK, BLOCK)
            block = quantized[pl.ds(r * BLOCK, BLOCK), lanes].astype(F32)
            half[:, lanes] = (block * scales[r, c]).astype(BF)
    for zh in range(2):
        for zl in range(4):
            split[zl * 2 + zh] = inputs[:, zh * 256 : zh * 256 + 256]


def prepare(scales, quantized, inputs, grad):
    half = (BLOCK, quantized.shape[1])
    return pl.pallas_call(
        prepare_kernel,
        out_shape=[
            jax.ShapeDtypeStruct(half, BF),
            jax.ShapeDtypeStruct(half, BF),
            jax.ShapeDtypeStruct((8, 512, 256), BF),
            jax.ShapeDtypeStruct(grad.shape, BF),
        ],
        in_specs=[SCALAR, whole(quantized.shape), whole(inputs.shape), whole(grad.shape)],
        out_specs=[whole(half), whole(half), whole((8, 512, 256)), whole(grad.shape)],
        compiler_params=params(),
        cost_estimate=cost(quantized.size, 8 * quantized.size),
    )(scales, quantized, inputs, grad)


PRODUCT = cost(1024 * 1024, 1024 * 1024)


def stacked(refs):
    return jnp.concatenate([ref[...] for ref in refs], axis=0)


def halves(top, bottom, top_up, up, down, bottom_down):
    first, second = pl.ds(0, BLOCK), pl.ds(BLOCK, BLOCK)
    return (
        top, bottom, top_up, up.at[second],
        up.at[first], down.at[second], down.at[first], bottom_down,
    )


def forward_kernel(place, _, panel, *refs):
    weights, (own, other, left) = halves(*refs[:6]), refs[6:]
    x, y, k, zh = place[0], place[1], place[2], place[3]

    @pl.when(pl.program_id(0) == 0)
    def _():
        for at in range(8):
            m = lax.rem(x - at // 2 + 4, 4)
            s = lax.rem(at % 2 + zh, 2)
            lanes = pl.ds(pl.multiple_of(m * 256, 256), 256)
            for b in range(8):
                e = lax.rem(y - b // 2 + 4, 4)
                kk = lax.rem(k + b % 2, 2)
                rows = pl.ds(pl.multiple_of(kk * 512 + e * 128 + s * 64, 64), 64)
                left[rows, lanes] = panel[at, b * 64 : b * 64 + 64, :]

    total = jnp.dot(left[...], stacked(weights), preferred_element_type=F32)
    own[...] = total[:512].astype(BF)
    other[...] = total[512:].astype(BF)


def forward(place, after, panel, weights):
    width = weights[0].shape[1]
    tile = width // 3
    return pl.pallas_call(
        forward_kernel,
        grid=(width // tile,),
        out_shape=[jax.ShapeDtypeStruct((512, width), BF)] * 2,
        in_specs=[SCALAR, ANY, whole(panel.shape)]
        + [pl.BlockSpec((w.shape[0], tile), lambda n: (0, n)) for w in weights],
        out_specs=[pl.BlockSpec((512, tile), lambda n: (0, n))] * 2,
        scratch_shapes=[pltpu.VMEM((1024, 1024), BF)],
        compiler_params=params(),
        cost_estimate=PRODUCT,
    )(place, after, panel, *weights)


def weight_grad_kernel(place, _, panel, near, mine, theirs, *refs):
    outs, left, right = refs[:5], refs[5], refs[6]
    x, y, k, zh = place[0], place[1], place[2], place[3]

    @pl.when(pl.program_id(0) == 0)
    def _():
        for at in range(8):
            m = lax.rem(x - at // 2 + 4, 4)
            s = lax.rem(at % 2 + zh, 2)
            rows = pl.ds(pl.multiple_of(m * 256, 256), 256)
            lanes = pl.ds(pl.multiple_of(s * 512, 512), 512)
            left[rows, lanes] = panel[at].T

    right[:512, :] = near[...]
    for e in range(4):
        for kk, source in enumerate((mine, theirs)):
            block = lax.rem(y - e + 4, 4) * 2 + lax.rem(k + kk, 2)
            rows = pl.ds(pl.multiple_of(512 + block * 64, 64), 64)
            right[rows, :] = source[e * 64 : e * 64 + 64, :]
    total = jnp.dot(left[...], right[...], preferred_element_type=F32)
    at = 0
    for out in outs:
        out[...] = total[at : at + out.shape[0]].astype(BF)
        at += out.shape[0]


def weight_grad(place, after, panel, near, mine, theirs):
    width = near.shape[1]
    tile = width // 3
    sizes = (256, 256, 128, 128, 256)
    return pl.pallas_call(
        weight_grad_kernel,
        grid=(width // tile,),
        out_shape=[jax.ShapeDtypeStruct((rows, width), BF) for rows in sizes],
        in_specs=[SCALAR, ANY, whole(panel.shape)]
        + [pl.BlockSpec((rows, tile), lambda n: (0, n)) for rows in (512, 256, 256)],
        out_specs=[pl.BlockSpec((rows, tile), lambda n: (0, n)) for rows in sizes],
        scratch_shapes=[pltpu.VMEM((1024, 1024), BF), pltpu.VMEM((1024, tile), BF)],
        compiler_params=params(),
        cost_estimate=PRODUCT,
    )(place, after, panel, near, mine, theirs)


def backward_kernel(place, _, near, mine, theirs, *refs):
    weights, out = halves(*refs[:6]), refs[6]
    x, y, k, zh = place[0], place[1], place[2], place[3]
    step = pl.program_id(0)
    rows = pl.ds(pl.multiple_of(step * 256, 256), 256)
    far = stacked((mine, theirs))
    for m in range(4):
        at = lax.rem(x - m + 4, 4) * 2
        right = stacked(weights[2 * m : 2 * m + 2])
        total = lax.dot_general(
            near[...], right, (((1,), (1,)), ((), ())), preferred_element_type=F32
        )
        out[at + zh, rows, :] = total.astype(BF)
        total = lax.dot_general(
            far, right, (((1,), (1,)), ((), ())), preferred_element_type=F32
        ).astype(BF)
        for i in range(4):
            block = lax.rem(y - 2 * step - i % 2 + 4, 4) * 2 + lax.rem(k + i // 2, 2)
            target = pl.ds(pl.multiple_of(block * 64, 64), 64)
            out[at + 1 - zh, target, :] = total[i * 64 : i * 64 + 64]


def backward(place, after, near, mine, theirs, weights):
    width = near.shape[1]
    return pl.pallas_call(
        backward_kernel,
        grid=(2,),
        out_shape=jax.ShapeDtypeStruct((8, 512, 256), BF),
        in_specs=[SCALAR, ANY]
        + [pl.BlockSpec((rows, width), lambda n: (n, 0)) for rows in (256, 128, 128)]
        + [whole(w.shape) for w in weights],
        out_specs=whole((8, 512, 256)),
        compiler_params=params(),
        cost_estimate=PRODUCT,
    )(place, after, near, mine, theirs, *weights)


def summed(*refs):
    total = refs[0].astype(F32)
    for ref in refs[1:]:
        total = total + ref.astype(F32)
    return total.astype(BF)


def local(kernel, outs, after, *args):
    after = after if isinstance(after, tuple) else (after,)
    moved = sum(2 * a.size for a in args) + sum(2 * a * b for a, b in outs)
    return pl.pallas_call(
        lambda *refs: kernel(*refs[len(after) :]),
        out_shape=[jax.ShapeDtypeStruct(shape, BF) for shape in outs],
        in_specs=[ANY] * len(after) + [whole(a.shape) for a in args],
        out_specs=[whole(shape) for shape in outs],
        compiler_params=params(),
        cost_estimate=cost(moved, moved),
    )(*after, *args)


def relay_kernel(grad, top, bottom, top_up, bottom_down, passed, up, down):
    passed[...] = grad[...]
    up[:BLOCK], up[BLOCK:] = top_up[...], bottom[...]
    down[:BLOCK], down[BLOCK:] = top[...], bottom_down[...]


def collect_kernel(here, up, across, down, out):
    at = 0
    for part in (here, up, across, down):
        out[pl.ds(at, part.shape[0]), :] = part[...]
        at += part.shape[0]


def pair_kernel(mine, theirs, *parts):
    at = 0
    for part in parts:
        rows = pl.ds(at, part.shape[0])
        part[...] = summed(mine[rows, :], theirs[rows, :])
        at += part.shape[0]


def onward_kernel(up, down, from_below, from_above, up_out, down_out):
    half = from_below.shape[0]
    up_out[:half] = summed(up[:half], from_below[...])
    up_out[half:] = up[half:]
    down_out[:half] = down[:half]
    down_out[half:] = summed(down[half:], from_above[...])


def finish_kernel(own, from_below, from_above, *outs):
    at = 0
    for out in outs:
        rows = pl.ds(at, out.shape[0])
        out[...] = summed(own[rows, :], from_below[rows, :], from_above[rows, :])
        at += out.shape[0]


def shift(array, axis, step):
    return lax.ppermute(array, axis, ring(lax.axis_size(axis), step))


def per_device(inputs, qweight, scales, grad_out):
    x, y, k, zh = (lax.axis_index(name) for name in ("x", "y", "k", "zh"))
    place = jnp.stack([x, y, k, zh]).astype(jnp.int32)
    F = qweight.shape[1]

    near = lax.all_gather(grad_out[0], ("y", "k"), axis=0, tiled=True)

    top, bottom, split, passed = prepare(scales, qweight, inputs[0], grad_out[0])
    panel = lax.all_to_all(split, ("zl", "zh"), 0, 0, tiled=True)

    top_up, bottom_down = shift(top, "x", 1), shift(bottom, "x", -1)
    far, up, down = local(
        relay_kernel,
        [passed.shape, (256, F), (256, F)],
        (),
        shift(passed, "zh", 1), top, bottom, top_up, bottom_down,
    )
    up, down = shift(up, "x", 1), shift(down, "x", -1)
    weights = (top, bottom, top_up, up, down, bottom_down)
    others = [shift(far, "y", e) for e in (1, 2, 3)]
    (mine,) = local(collect_kernel, [(256, F)], (), far, *others)
    theirs = shift(mine, "k", 1)

    sums = backward(place, mine, near, mine, theirs, weights)
    own, other = forward(place, sums, panel, weights)
    other = shift(other, "k", 1)
    terms = weight_grad(place, own, panel, near, mine, theirs)

    shapes = [(128, F), (128, F), (64, F), (64, F), (128, F)]
    here, down, top, bottom, up = local(pair_kernel, shapes, terms[0], own, other)
    top, bottom = shift(top, "y", 1), shift(bottom, "y", -1)
    up, down = local(onward_kernel, [(128, F)] * 2, here, up, down, top, bottom)
    up, down = shift(up, "y", 1), shift(down, "y", -1)
    mine, far = local(finish_kernel, [(64, F)] * 2, here, here, up, down)
    projected = summed(mine, shift(far, "zh", 1))

    sums = lax.all_to_all(sums, ("zl", "zh"), 0, 0, tiled=True)
    grad_inputs = jnp.concatenate(
        [summed(*[sums[zl * 2 + h] for zl in range(4)]) for h in range(2)], axis=1
    )

    here, down, top, bottom, up = terms
    top, bottom = shift(top, "x", 1), shift(bottom, "x", -1)
    up, down = local(onward_kernel, [(256, F)] * 2, up, up, down, top, bottom)
    up, down = shift(up, "x", 1), shift(down, "x", -1)
    (grad_weight,) = local(finish_kernel, [(256, F)], here, here, up, down)

    return projected[None], grad_inputs[None], grad_weight


def solution(mesh):
    axes = Mesh(mesh.devices.reshape(4, 2, 4, 4, 2), ("y", "k", "zl", "x", "zh"))
    return jax.shard_map(
        per_device,
        mesh=axes,
        in_specs=(
            P(("x", "zh"), None, ("y", "k", "zl")),
            P(("y", "k", "x", "zh"), "zl"),
            P(("y", "k", "x", "zh"), "zl"),
            P(("x", "zh"), ("y", "k"), "zl"),
        ),
        out_specs=(
            P(("x", "zh"), ("y", "k"), "zl"),
            P(("x", "zh"), None, ("y", "k", "zl")),
            P(("y", "k", "x", "zh"), "zl"),
        ),
        check_vma=False,
    )
```

time: 597 us -> 230 us (0.39)
  waiting for transfers between devices: 539 us -> 105 us
  Pallas kernels: 0 us -> 53.8 us
  starting transfers between devices: 0.24 us -> 43.9 us
  matrix products: 30 us -> 0 us
    all_gather x3 -> x1, waiting for transfers between devices: 269 us -> 0.01 us  [per_device(): near = lax.all_gather(grad_out[0], ('y', 'k'), axis=0, tiled=True)]
    reduce_scatter x2 -> x0, waiting for transfers between devices: 229 us -> none  [the longest x1 203 us: per_device(): lax.psum_scatter(transposed_product(panel, grad_rows).astype(jnp.bfloat16...]
    ppermute x0 -> x19, waiting for transfers between devices: none -> 104 us  [shift(): return lax.ppermute(array, axis, ring(lax.axis_size(axis), step))]
    pallas_call x0 -> x11, Pallas kernels: none -> 53.8 us  [the longest x7 21.4 us: local(): pl.pallas_call(lambda *refs: kernel(*refs[len(after):]), out_shape=[jax.S...]
    unnamed x7 -> x1, waiting for transfers between devices: 40.7 us -> 0.68 us
    ppermute x0 -> x19, starting transfers between devices: none -> 31.4 us  [shift(): return lax.ppermute(array, axis, ring(lax.axis_size(axis), step))]
    dot_general x3 -> x0, matrix products: 30 us -> none  [the longest x1 10.7 us: against_rows(): lax.dot_general(left, right, (((1,), (1,)), ((), ())), preferred_element_...]
    all_to_all x0 -> x2, starting transfers between devices: none -> 12.5 us  [the longest x1 8.71 us: per_device(): panel = lax.all_to_all(split, ('zl', 'zh'), 0, 0, tiled=True)]
  transfers between devices with their start and end apart: 6 -> 22, of which waited for: 6 -> 9; matrix products, arithmetic and copies ran while one was open for 7% -> 1% of each run, Pallas kernels for 0% -> 19%
where the time goes in v2:
time: 230 us; the launch traced here: 229 us
  waiting for transfers between devices  105 us (46%)
  Pallas kernels  53.8 us (23%)
  starting transfers between devices  43.9 us (19%)
  between operations  14.1 us (6%)
  local copies, waits for them, and re-layouts  9.97 us (4%)
  other arithmetic  2.53 us (1%)
    ppermute x19, waiting for transfers between devices, shift(): return lax.ppermute(array, axis, ring(lax.axis_size(axis), step))  104 us
    ppermute x19, starting transfers between devices, shift(): return lax.ppermute(array, axis, ring(lax.axis_size(axis), step))  31.4 us
    pallas_call x7, Pallas kernels, local(): pl.pallas_call(lambda *refs: kernel(*refs[len(after):]), out_shape=[jax.S...  21.4 us
    unnamed x38, local copies, waits for them, and re-layouts  9.97 us
    pallas_call x1, Pallas kernels, backward(): pl.pallas_call(backward_kernel, grid=(2,), out_shape=jax.ShapeDtypeStruct...  9.86 us
    pallas_call x1, Pallas kernels, weight_grad(): pl.pallas_call(weight_grad_kernel, grid=(width // tile,), out_shape=[jax....  9.73 us
    pallas_call x1, Pallas kernels, forward(): pl.pallas_call(forward_kernel, grid=(width // tile,), out_shape=[jax.Shap...  9.34 us
    all_to_all x1, starting transfers between devices, per_device(): panel = lax.all_to_all(split, ('zl', 'zh'), 0, 0, tiled=True)  8.71 us
  transfers between devices with their start and end apart: 22, of which 9 were waited for; matrix products, arithmetic and copies ran while one was open for 1% of the time, Pallas kernels for 19%

profile of v2, /device:TPU:32, one launch (start us, length us, event | category | flops | bytes accessed | tf_op | source)
XLA Modules:
  0.0 229.4 jit_solution(801016621568241501)
XLA Ops:
  7.9 3.5 %shard_map.67 = (bf16[128,2304]{1,0:T(8,128)(2,1)}, bf16[128,2304]{1,0:T(8,128)(2,1)}, bf16[8,512,256]{2,1,0:T(8,128)(2,1)}, bf16[64,2304]{1,0:T(8,128)(2,1)}) custom-call(f32[2,18]{1,0:T(2,128)} %scales.1, bf16[256,2304]{1,0:T(8,128)(2,1)} %quantized.1, bf16[512,512]{1,0:T(8,128)(2,1)} %bitcast.18, bf16[64,2304]{1,0:T(8,128)(2,1)} %bitcast.17), custom_call_target="tpu_custom_call" | custom-call | flops 589824 | bytes 4718592 | tf_op jit(solution)/shard_map/pallas_call | solution.py:48
  11.4 8.7 %all-to-all-start = ((bf16[8,512,256]{2,1,0:T(8,128)(2,1)}), bf16[8,512,256]{2,1,0:T(8,128)(2,1)S(1)}, u32[]{:S(2)}, u32[]{:S(2)}) async-start(bf16[8,512,256]{2,1,0:T(8,128)(2,1)} %get-tuple-element.34), calls=%async_computation | async-start | bytes 4194304 | tf_op jit(solution)/shard_map/all_to_all | solution.py:264
  23.3 4.5 %collective-permute-start = (bf16[64,2304]{1,0:T(8,128)(2,1)}, bf16[64,2304]{1,0:T(8,128)(2,1)S(1)}, u32[]{:S(2)}, u32[]{:S(2)}) collective-permute-start(bf16[64,2304]{1,0:T(8,128)(2,1)} %get-tuple-element.28), channel_id=1, source_target_pairs={{0,1},{1,0},{2,3},{3,2},{4,5},{5,4},{6,7},{7,6},{8,9},{9,8},{10,11... | collective-permute-start | bytes 884744 | tf_op jit(solution)/shard_map/ppermute | solution.py:253
  27.8 54.7 %collective-permute-done.refs_0_ = bf16[64,2304]{1,0:T(8,128)(2,1)S(1)} collective-permute-done((bf16[64,2304]{1,0:T(8,128)(2,1)}, bf16[64,2304]{1,0:T(8,128)(2,1)S(1)}, u32[]{:S(2)}, u32[]{:S(2)}) %collective-permute-start) | collective-permute-done | bytes 294944 | tf_op jit(solution)/shard_map/ppermute | solution.py:253
  84.3 3.3 %shard_map.68 = (bf16[64,2304]{1,0:T(8,128)(2,1)}, bf16[256,2304]{1,0:T(8,128)(2,1)}, bf16[256,2304]{1,0:T(8,128)(2,1)}) custom-call(bf16[64,2304]{1,0:T(8,128)(2,1)} %copy-done.18, bf16[128,2304]{1,0:T(8,128)(2,1)} %get-tuple-element.29.refs_1_.refs_0_, bf16[128,2304]{1,0:T(8,128)(2,1)} %get-tuple-element.30.refs_2_.refs_1_, bf16[128,2304]{1,0:T(8,128)(2,1)} %copy-done.3, ...), custom_call_target="tpu_custom_call" | custom-call | flops 5308416 | bytes 5308416 | tf_op jit(solution)/shard_map/pallas_call | solution.py:205
  87.5 3.0 %collective-permute-start.5 = (bf16[64,2304]{1,0:T(8,128)(2,1)}, bf16[64,2304]{1,0:T(8,128)(2,1)S(1)}, u32[]{:S(2)}, u32[]{:S(2)}) collective-permute-start(bf16[64,2304]{1,0:T(8,128)(2,1)} %get-tuple-element.31.refs_0_), channel_id=1, source_target_pairs={{0,192},{64,0},{128,64},{192,128},{1,193},{65,1},{129,65},{193,129... | collective-permute-start | bytes 884744 | tf_op jit(solution)/shard_map/ppermute | solution.py:253
  95.4 7.9 %collective-permute-done.5.refs_3_ = bf16[64,2304]{1,0:T(8,128)(2,1)S(1)} collective-permute-done((bf16[64,2304]{1,0:T(8,128)(2,1)}, bf16[64,2304]{1,0:T(8,128)(2,1)S(1)}, u32[]{:S(2)}, u32[]{:S(2)}) %collective-permute-start.5) | collective-permute-done | bytes 294944 | tf_op jit(solution)/shard_map/ppermute | solution.py:253
  103.3 3.6 %collective-permute-done.3.refs_1_ = bf16[64,2304]{1,0:T(8,128)(2,1)S(1)} collective-permute-done((bf16[64,2304]{1,0:T(8,128)(2,1)}, bf16[64,2304]{1,0:T(8,128)(2,1)S(1)}, u32[]{:S(2)}, u32[]{:S(2)}) %collective-permute-start.3) | collective-permute-done | bytes 294944 | tf_op jit(solution)/shard_map/ppermute | solution.py:253
  110.6 9.7 %collective-permute-done.7.refs_3_ = bf16[256,2304]{1,0:T(8,128)(2,1)S(1)} collective-permute-done((bf16[256,2304]{1,0:T(8,128)(2,1)}, bf16[256,2304]{1,0:T(8,128)(2,1)S(1)}, u32[]{:S(2)}, u32[]{:S(2)}) %collective-permute-start.7) | collective-permute-done | bytes 1179680 | tf_op jit(solution)/shard_map/ppermute | solution.py:253
  121.3 9.9 %shard_map.70._ = bf16[8,512,256]{2,1,0:T(8,128)(2,1)} custom-call(s32[4]{0:T(128)} %pad_add_fusion.place, bf16[256,2304]{1,0:T(8,128)(2,1)} %shard_map.69._.mine, bf16[512,2304]{1,0:T(8,128)(2,1)} %bitcast.15, bf16[256,2304]{1,0:T(8,128)(2,1)} %shard_map.69._.mine, bf16[256,2304]{1,0:T(8,128)(2,1)} %collective-permute-done.6.theirs, ...), custom_call_target="tpu_custom_call" | custom-call | flops 1048576 | bytes 1048576 | tf_op jit(solution)/shard_map/pallas_call | solution.py:182
  132.5 9.3 %shard_map.71 = (bf16[512,2304]{1,0:T(8,128)(2,1)}, bf16[512,2304]{1,0:T(8,128)(2,1)}) custom-call(s32[4]{0:T(128)} %pad_add_fusion.place, bf16[8,512,256]{2,1,0:T(8,128)(2,1)} %shard_map.70._, bf16[8,512,256]{2,1,0:T(8,128)(2,1)} %copy-done, bf16[128,2304]{1,0:T(8,128)(2,1)} %get-tuple-element.29.refs_1_.refs_0_, ...), custom_call_target="tpu_custom_call" | custom-call | flops 1048576 | bytes 1048576 | tf_op jit(solution)/shard_map/pallas_call | solution.py:102
  141.9 3.7 %all-to-all-start.1 = ((bf16[8,512,256]{2,1,0:T(8,128)(2,1)}), bf16[8,512,256]{2,1,0:T(8,128)(2,1)S(1)}, u32[]{:S(2)}, u32[]{:S(2)}) async-start(bf16[8,512,256]{2,1,0:T(8,128)(2,1)} %shard_map.70._), calls=%async_computation.1 | async-start | bytes 4194304 | tf_op jit(solution)/shard_map/all_to_all | solution.py:292
  145.6 9.7 %shard_map.72 = (bf16[256,2304]{1,0:T(8,128)(2,1)}, bf16[256,2304]{1,0:T(8,128)(2,1)}, bf16[128,2304]{1,0:T(8,128)(2,1)}, bf16[128,2304]{1,0:T(8,128)(2,1)}, bf16[256,2304]{1,0:T(8,128)(2,1)}) custom-call(s32[4]{0:T(128)} %pad_add_fusion.place, bf16[512,2304]{1,0:T(8,128)(2,1)} %get-tuple-element.35._.refs_1_, bf16[8,512,256]{2,1,0:T(8,128)(2,1)} %copy-done, ...), custom_call_target="tpu_custom_call" | custom-call | flops 1048576 | bytes 1048576 | tf_op jit(solution)/shard_map/pallas_call | solution.py:145
  156.0 2.6 %collective-permute-start.16 = (bf16[128,2304]{1,0:T(8,128)(2,1)}, bf16[128,2304]{1,0:T(8,128)(2,1)S(1)}, u32[]{:S(2)}, u32[]{:S(2)}) collective-permute-start(bf16[128,2304]{1,0:T(8,128)(2,1)} %get-tuple-element.50), channel_id=1, source_target_pairs={{0,6},{2,0},{4,2},{6,4},{1,7},{3,1},{5,3},{7,5},{8,14},{10,8},{12,... | collective-permute-start | bytes 1769480 | tf_op jit(solution)/shard_map/ppermute | solution.py:253
  158.6 3.9 %shard_map.73 = (bf16[128,2304]{1,0:T(8,128)(2,1)}, bf16[128,2304]{1,0:T(8,128)(2,1)}, bf16[64,2304]{1,0:T(8,128)(2,1)}, bf16[64,2304]{1,0:T(8,128)(2,1)}, bf16[128,2304]{1,0:T(8,128)(2,1)}) custom-call(bf16[256,2304]{1,0:T(8,128)(2,1)} %get-tuple-element.36.refs_0_.refs_1_, bf16[512,2304]{1,0:T(8,128)(2,1)} %get-tuple-element.35._.refs_1_, ...), custom_call_target="tpu_custom_call" | custom-call | flops 7077888 | bytes 7077888 | tf_op jit(solution)/shard_map/pallas_call | solution.py:205
  165.7 6.7 %collective-permute-done.15.refs_3_ = bf16[128,2304]{1,0:T(8,128)(2,1)S(1)} collective-permute-done((bf16[128,2304]{1,0:T(8,128)(2,1)}, bf16[128,2304]{1,0:T(8,128)(2,1)S(1)}, u32[]{:S(2)}, u32[]{:S(2)}) %collective-permute-start.15) | collective-permute-done | bytes 589856 | tf_op jit(solution)/shard_map/ppermute | solution.py:253
  173.6 3.6 %shard_map.76 = (bf16[256,2304]{1,0:T(8,128)(2,1)}, bf16[256,2304]{1,0:T(8,128)(2,1)}) custom-call(bf16[256,2304]{1,0:T(8,128)(2,1)} %get-tuple-element.47.refs_0_.refs_1_, bf16[256,2304]{1,0:T(8,128)(2,1)} %get-tuple-element.47.refs_0_.refs_1_, bf16[256,2304]{1,0:T(8,128)(2,1)} %get-tuple-element.48.refs_2_, bf16[128,2304]{1,0:T(8,128)(2,1)} %copy-done.8, ...), custom_call_target="tpu_custom_call" | custom-call | flops 5898240 | bytes 5898240 | tf_op jit(solution)/shard_map/pallas_call | solution.py:205
  177.2 3.1 %collective-permute-start.18 = (bf16[256,2304]{1,0:T(8,128)(2,1)}, bf16[256,2304]{1,0:T(8,128)(2,1)S(1)}, u32[]{:S(2)}, u32[]{:S(2)}) collective-permute-start(bf16[256,2304]{1,0:T(8,128)(2,1)} %get-tuple-element.52), channel_id=1, source_target_pairs={{0,6},{2,0},{4,2},{6,4},{1,7},{3,1},{5,3},{7,5},{8,14},{10,8},{12,... | collective-permute-start | bytes 3538952 | tf_op jit(solution)/shard_map/ppermute | solution.py:253
  181.2 2.5 %shard_map.74 = (bf16[128,2304]{1,0:T(8,128)(2,1)}, bf16[128,2304]{1,0:T(8,128)(2,1)}) custom-call(bf16[128,2304]{1,0:T(8,128)(2,1)} %get-tuple-element.38.refs_0_.refs_1_, bf16[128,2304]{1,0:T(8,128)(2,1)} %get-tuple-element.39.refs_1_, bf16[128,2304]{1,0:T(8,128)(2,1)} %get-tuple-element.40.refs_2_, bf16[64,2304]{1,0:T(8,128)(2,1)} %copy-done.12, ...), custom_call_target="tpu_custom_call" | custom-call | flops 2949120 | bytes 2949120 | tf_op jit(solution)/shard_map/pallas_call | solution.py:205
  187.0 12.6 %collective-permute-done.12.refs_2_ = bf16[128,2304]{1,0:T(8,128)(2,1)S(1)} collective-permute-done((bf16[128,2304]{1,0:T(8,128)(2,1)}, bf16[128,2304]{1,0:T(8,128)(2,1)S(1)}, u32[]{:S(2)}, u32[]{:S(2)}) %collective-permute-start.12) | collective-permute-done | bytes 589856 | tf_op jit(solution)/shard_map/ppermute | solution.py:253
  201.1 2.3 %shard_map.75 = (bf16[64,2304]{1,0:T(8,128)(2,1)}, bf16[64,2304]{1,0:T(8,128)(2,1)}) custom-call(bf16[128,2304]{1,0:T(8,128)(2,1)} %get-tuple-element.38.refs_0_.refs_1_, bf16[128,2304]{1,0:T(8,128)(2,1)} %get-tuple-element.38.refs_0_.refs_1_, bf16[128,2304]{1,0:T(8,128)(2,1)} %copy-done.10, bf16[128,2304]{1,0:T(8,128)(2,1)} %copy-done.11), custom_call_target="tpu_custom_call" | custom-call | flops 2359296 | bytes 2359296 | tf_op jit(solution)/shard_map/pallas_call | solution.py:205
  203.5 2.9 %collective-permute-start.14 = (bf16[64,2304]{1,0:T(8,128)(2,1)}, bf16[64,2304]{1,0:T(8,128)(2,1)S(1)}, u32[]{:S(2)}, u32[]{:S(2)}) collective-permute-start(bf16[64,2304]{1,0:T(8,128)(2,1)} %get-tuple-element.46), channel_id=1, source_target_pairs={{0,1},{1,0},{2,3},{3,2},{4,5},{5,4},{6,7},{7,6},{8,9},{9,8},{10,11... | collective-permute-start | bytes 884744 | tf_op jit(solution)/shard_map/ppermute | solution.py:253
  208.6 3.4 %shard_map.77 = bf16[256,2304]{1,0:T(8,128)(2,1)} custom-call(bf16[256,2304]{1,0:T(8,128)(2,1)} %get-tuple-element.36.refs_0_.refs_1_, bf16[256,2304]{1,0:T(8,128)(2,1)} %get-tuple-element.36.refs_0_.refs_1_, bf16[256,2304]{1,0:T(8,128)(2,1)} %copy-done.6, bf16[256,2304]{1,0:T(8,128)(2,1)} %copy-done.7), custom_call_target="tpu_custom_call" | custom-call | flops 4718592 | bytes 4718592 | tf_op jit(solution)/shard_map/pallas_call | solution.py:205
  212.0 8.7 %collective-permute-done.14 = bf16[64,2304]{1,0:T(8,128)(2,1)S(1)} collective-permute-done((bf16[64,2304]{1,0:T(8,128)(2,1)}, bf16[64,2304]{1,0:T(8,128)(2,1)S(1)}, u32[]{:S(2)}, u32[]{:S(2)}) %collective-permute-start.14) | collective-permute-done | bytes 294944 | tf_op jit(solution)/shard_map/ppermute | solution.py:253
  (74 shorter events, 31.4 us)
Async XLA Ops:
  7.2 113.2 %all-gather.3.cloned.1.call-start = ((), (), s32[]{:S(2)}) async-start(), calls=%async_computation.2 | async-start | bytes 2654208 | tf_op jit(solution)/shard_map/all_gather | solution.py:261
  11.4 10.2 %copy-start.2 = (bf16[128,2304]{1,0:T(8,128)(2,1)S(1)}, bf16[128,2304]{1,0:T(8,128)(2,1)}, u32[]{:S(2)}) copy-start(bf16[128,2304]{1,0:T(8,128)(2,1)} %get-tuple-element.30.refs_2_.refs_1_) | copy-start | bytes 1769476
  11.4 119.8 %all-to-all-start = ((bf16[8,512,256]{2,1,0:T(8,128)(2,1)}), bf16[8,512,256]{2,1,0:T(8,128)(2,1)S(1)}, u32[]{:S(2)}, u32[]{:S(2)}) async-start(bf16[8,512,256]{2,1,0:T(8,128)(2,1)} %get-tuple-element.34), calls=%async_computation | async-start | bytes 4194304 | tf_op jit(solution)/shard_map/all_to_all | solution.py:264
  20.1 62.4 %collective-permute-start.1 = (bf16[128,2304]{1,0:T(8,128)(2,1)S(1)}, bf16[128,2304]{1,0:T(8,128)(2,1)S(1)}, u32[]{:S(2)}, u32[]{:S(2)}) collective-permute-start(bf16[128,2304]{1,0:T(8,128)(2,1)S(1)} %copy-done.1), channel_id=1, source_target_pairs={{0,2},{2,4},{4,6},{6,0},{1,3},{3,5},{5,7},{7,1},{8,10},{10,12},{12... | collective-permute-start | bytes 1769480 | tf_op jit(solution)/shard_map/ppermute | solution.py:253
  21.6 60.9 %collective-permute-start.2 = (bf16[128,2304]{1,0:T(8,128)(2,1)S(1)}, bf16[128,2304]{1,0:T(8,128)(2,1)S(1)}, u32[]{:S(2)}, u32[]{:S(2)}) collective-permute-start(bf16[128,2304]{1,0:T(8,128)(2,1)S(1)} %copy-done.2), channel_id=1, source_target_pairs={{0,6},{2,0},{4,2},{6,4},{1,7},{3,1},{5,3},{7,5},{8,14},{10,8},{12,... | collective-permute-start | bytes 1769480 | tf_op jit(solution)/shard_map/ppermute | solution.py:253
  23.3 59.2 %collective-permute-start = (bf16[64,2304]{1,0:T(8,128)(2,1)}, bf16[64,2304]{1,0:T(8,128)(2,1)S(1)}, u32[]{:S(2)}, u32[]{:S(2)}) collective-permute-start(bf16[64,2304]{1,0:T(8,128)(2,1)} %get-tuple-element.28), channel_id=1, source_target_pairs={{0,1},{1,0},{2,3},{3,2},{4,5},{5,4},{6,7},{7,6},{8,9},{9,8},{10,11... | collective-permute-start | bytes 884744 | tf_op jit(solution)/shard_map/ppermute | solution.py:253
  87.5 15.7 %collective-permute-start.5 = (bf16[64,2304]{1,0:T(8,128)(2,1)}, bf16[64,2304]{1,0:T(8,128)(2,1)S(1)}, u32[]{:S(2)}, u32[]{:S(2)}) collective-permute-start(bf16[64,2304]{1,0:T(8,128)(2,1)} %get-tuple-element.31.refs_0_), channel_id=1, source_target_pairs={{0,192},{64,0},{128,64},{192,128},{1,193},{65,1},{129,65},{193,129... | collective-permute-start | bytes 884744 | tf_op jit(solution)/shard_map/ppermute | solution.py:253
  90.6 12.7 %collective-permute-start.4 = (bf16[64,2304]{1,0:T(8,128)(2,1)}, bf16[64,2304]{1,0:T(8,128)(2,1)S(1)}, u32[]{:S(2)}, u32[]{:S(2)}) collective-permute-start(bf16[64,2304]{1,0:T(8,128)(2,1)} %get-tuple-element.31.refs_0_), channel_id=1, source_target_pairs={{0,128},{64,192},{128,0},{192,64},{1,129},{65,193},{129,1},{193,65... | collective-permute-start | bytes 884744 | tf_op jit(solution)/shard_map/ppermute | solution.py:253
  91.2 15.7 %collective-permute-start.3 = (bf16[64,2304]{1,0:T(8,128)(2,1)}, bf16[64,2304]{1,0:T(8,128)(2,1)S(1)}, u32[]{:S(2)}, u32[]{:S(2)}) collective-permute-start(bf16[64,2304]{1,0:T(8,128)(2,1)} %get-tuple-element.31.refs_0_), channel_id=1, source_target_pairs={{0,64},{64,128},{128,192},{192,0},{1,65},{65,129},{129,193},{193,1... | collective-permute-start | bytes 884744 | tf_op jit(solution)/shard_map/ppermute | solution.py:253
  92.2 28.1 %collective-permute-start.7 = (bf16[256,2304]{1,0:T(8,128)(2,1)}, bf16[256,2304]{1,0:T(8,128)(2,1)S(1)}, u32[]{:S(2)}, u32[]{:S(2)}) collective-permute-start(bf16[256,2304]{1,0:T(8,128)(2,1)} %get-tuple-element.32), channel_id=1, source_target_pairs={{0,2},{2,4},{4,6},{6,0},{1,3},{3,5},{5,7},{7,1},{8,10},{10,12},{12... | collective-permute-start | bytes 3538952 | tf_op jit(solution)/shard_map/ppermute | solution.py:253
  93.7 26.7 %collective-permute-start.8 = (bf16[256,2304]{1,0:T(8,128)(2,1)}, bf16[256,2304]{1,0:T(8,128)(2,1)}, u32[]{:S(2)}, u32[]{:S(2)}) collective-permute-start(bf16[256,2304]{1,0:T(8,128)(2,1)} %get-tuple-element.33), channel_id=1, source_target_pairs={{0,6},{2,0},{4,2},{6,4},{1,7},{3,1},{5,3},{7,5},{8,14},{10,8},{12,... | collective-permute-start | bytes 3538952 | tf_op jit(solution)/shard_map/ppermute | solution.py:253
  109.9 10.4 %collective-permute-start.6 = (bf16[256,2304]{1,0:T(8,128)(2,1)}, bf16[256,2304]{1,0:T(8,128)(2,1)}, u32[]{:S(2)}, u32[]{:S(2)}) collective-permute-start(bf16[256,2304]{1,0:T(8,128)(2,1)} %shard_map.69._.mine), channel_id=1, source_target_pairs={{0,32},{32,0},{1,33},{33,1},{2,34},{34,2},{3,35},{35,3},{4,36},{36... | collective-permute-start | bytes 3538952 | tf_op jit(solution)/shard_map/ppermute | solution.py:253
  141.8 16.7 %collective-permute-start.9 = (bf16[512,2304]{1,0:T(8,128)(2,1)}, bf16[512,2304]{1,0:T(8,128)(2,1)}, u32[]{:S(2)}, u32[]{:S(2)}) collective-permute-start(bf16[512,2304]{1,0:T(8,128)(2,1)} %get-tuple-element.37), channel_id=1, source_target_pairs={{0,32},{32,0},{1,33},{33,1},{2,34},{34,2},{3,35},{35,3},{4,36},{36... | collective-permute-start | bytes 7077896 | tf_op jit(solution)/shard_map/ppermute | solution.py:253
  141.9 79.6 %all-to-all-start.1 = ((bf16[8,512,256]{2,1,0:T(8,128)(2,1)}), bf16[8,512,256]{2,1,0:T(8,128)(2,1)S(1)}, u32[]{:S(2)}, u32[]{:S(2)}) async-start(bf16[8,512,256]{2,1,0:T(8,128)(2,1)} %shard_map.70._), calls=%async_computation.1 | async-start | bytes 4194304 | tf_op jit(solution)/shard_map/all_to_all | solution.py:292
  155.3 17.1 %collective-permute-start.15 = (bf16[128,2304]{1,0:T(8,128)(2,1)}, bf16[128,2304]{1,0:T(8,128)(2,1)S(1)}, u32[]{:S(2)}, u32[]{:S(2)}) collective-permute-start(bf16[128,2304]{1,0:T(8,128)(2,1)} %get-tuple-element.49), channel_id=1, source_target_pairs={{0,2},{2,4},{4,6},{6,0},{1,3},{3,5},{5,7},{7,1},{8,10},{10,12},{12... | collective-permute-start | bytes 1769480 | tf_op jit(solution)/shard_map/ppermute | solution.py:253
  156.0 16.5 %collective-permute-start.16 = (bf16[128,2304]{1,0:T(8,128)(2,1)}, bf16[128,2304]{1,0:T(8,128)(2,1)S(1)}, u32[]{:S(2)}, u32[]{:S(2)}) collective-permute-start(bf16[128,2304]{1,0:T(8,128)(2,1)} %get-tuple-element.50), channel_id=1, source_target_pairs={{0,6},{2,0},{4,2},{6,4},{1,7},{3,1},{5,3},{7,5},{8,14},{10,8},{12,... | collective-permute-start | bytes 1769480 | tf_op jit(solution)/shard_map/ppermute | solution.py:253
  162.5 17.9 %collective-permute-start.10 = (bf16[64,2304]{1,0:T(8,128)(2,1)}, bf16[64,2304]{1,0:T(8,128)(2,1)S(1)}, u32[]{:S(2)}, u32[]{:S(2)}) collective-permute-start(bf16[64,2304]{1,0:T(8,128)(2,1)} %get-tuple-element.41), channel_id=1, source_target_pairs={{0,64},{64,128},{128,192},{192,0},{1,65},{65,129},{129,193},{193,1... | collective-permute-start | bytes 884744 | tf_op jit(solution)/shard_map/ppermute | solution.py:253
  164.4 16.0 %collective-permute-start.11 = (bf16[64,2304]{1,0:T(8,128)(2,1)}, bf16[64,2304]{1,0:T(8,128)(2,1)S(1)}, u32[]{:S(2)}, u32[]{:S(2)}) collective-permute-start(bf16[64,2304]{1,0:T(8,128)(2,1)} %get-tuple-element.42), channel_id=1, source_target_pairs={{0,192},{64,0},{128,64},{192,128},{1,193},{65,1},{129,65},{193,129... | collective-permute-start | bytes 884744 | tf_op jit(solution)/shard_map/ppermute | solution.py:253
  177.2 29.3 %collective-permute-start.17 = (bf16[256,2304]{1,0:T(8,128)(2,1)}, bf16[256,2304]{1,0:T(8,128)(2,1)S(1)}, u32[]{:S(2)}, u32[]{:S(2)}) collective-permute-start(bf16[256,2304]{1,0:T(8,128)(2,1)} %get-tuple-element.51), channel_id=1, source_target_pairs={{0,2},{2,4},{4,6},{6,0},{1,3},{3,5},{5,7},{7,1},{8,10},{10,12},{12... | collective-permute-start | bytes 3538952 | tf_op jit(solution)/shard_map/ppermute | solution.py:253
  177.2 29.2 %collective-permute-start.18 = (bf16[256,2304]{1,0:T(8,128)(2,1)}, bf16[256,2304]{1,0:T(8,128)(2,1)S(1)}, u32[]{:S(2)}, u32[]{:S(2)}) collective-permute-start(bf16[256,2304]{1,0:T(8,128)(2,1)} %get-tuple-element.52), channel_id=1, source_target_pairs={{0,6},{2,0},{4,2},{6,4},{1,7},{3,1},{5,3},{7,5},{8,14},{10,8},{12,... | collective-permute-start | bytes 3538952 | tf_op jit(solution)/shard_map/ppermute | solution.py:253
  183.7 15.8 %collective-permute-start.12 = (bf16[128,2304]{1,0:T(8,128)(2,1)}, bf16[128,2304]{1,0:T(8,128)(2,1)S(1)}, u32[]{:S(2)}, u32[]{:S(2)}) collective-permute-start(bf16[128,2304]{1,0:T(8,128)(2,1)} %get-tuple-element.43), channel_id=1, source_target_pairs={{0,64},{64,128},{128,192},{192,0},{1,65},{65,129},{129,193},{193,1... | collective-permute-start | bytes 1769480 | tf_op jit(solution)/shard_map/ppermute | solution.py:253
  185.6 14.3 %collective-permute-start.13 = (bf16[128,2304]{1,0:T(8,128)(2,1)}, bf16[128,2304]{1,0:T(8,128)(2,1)S(1)}, u32[]{:S(2)}, u32[]{:S(2)}) collective-permute-start(bf16[128,2304]{1,0:T(8,128)(2,1)} %get-tuple-element.44), channel_id=1, source_target_pairs={{0,192},{64,0},{128,64},{192,128},{1,193},{65,1},{129,65},{193,129... | collective-permute-start | bytes 1769480 | tf_op jit(solution)/shard_map/ppermute | solution.py:253
  203.5 17.2 %copy-start.17 = (bf16[64,2304]{1,0:T(8,128)(2,1)S(1)}, bf16[64,2304]{1,0:T(8,128)(2,1)}, u32[]{:S(2)}) copy-start(bf16[64,2304]{1,0:T(8,128)(2,1)} %get-tuple-element.45) | copy-start | bytes 884740
  203.5 17.2 %collective-permute-start.14 = (bf16[64,2304]{1,0:T(8,128)(2,1)}, bf16[64,2304]{1,0:T(8,128)(2,1)S(1)}, u32[]{:S(2)}, u32[]{:S(2)}) collective-permute-start(bf16[64,2304]{1,0:T(8,128)(2,1)} %get-tuple-element.46), channel_id=1, source_target_pairs={{0,1},{1,0},{2,3},{3,2},{4,5},{5,4},{6,7},{7,6},{8,9},{9,8},{10,11... | collective-permute-start | bytes 884744 | tf_op jit(solution)/shard_map/ppermute | solution.py:253
  (17 other events, 28.7 us)
Sparse Core Ops, SparseCore 0:
  9.8 30.7 all-gather.2

commit v3 on v2

v3 whole, which is shorter than its diff:
```python
import jax
import jax.numpy as jnp
from jax import lax
from jax.experimental import pallas as pl
from jax.experimental.pallas import tpu as pltpu
from jax.sharding import Mesh, PartitionSpec as P

BLOCK = 128
BF = jnp.bfloat16
F32 = jnp.float32
VMEM_LIMIT = 56 * 1024 * 1024


def params():
    return pltpu.CompilerParams(vmem_limit_bytes=VMEM_LIMIT)


def cost(flops, moved):
    return pl.CostEstimate(flops=flops, bytes_accessed=moved, transcendentals=0)


def whole(shape):
    return pl.BlockSpec(shape, lambda *_: (0,) * len(shape))


SCALAR = pl.BlockSpec(memory_space=pltpu.SMEM)
ANY = pl.BlockSpec(memory_space=pl.ANY)


def ring(size, step):
    return [(i, (i + step) % size) for i in range(size)]


def dequantize_kernel(scales, quantized, top, bottom):
    for r, half in enumerate((top, bottom)):
        for c in range(scales.shape[1]):
            lanes = pl.ds(c * BLOCK, BLOCK)
            block = quantized[pl.ds(r * BLOCK, BLOCK), lanes].astype(F32)
            half[:, lanes] = (block * scales[r, c]).astype(BF)


def dequantize(scales, quantized):
    half = (BLOCK, quantized.shape[1])
    return pl.pallas_call(
        dequantize_kernel,
        out_shape=[jax.ShapeDtypeStruct(half, BF)] * 2,
        in_specs=[SCALAR, whole(quantized.shape)],
        out_specs=[whole(half)] * 2,
        compiler_params=params(),
        cost_estimate=cost(1, 1),
    )(scales, quantized)


def split_kernel(inputs, split):
    for at in range(8):
        split[at] = inputs[:, at % 2 * 256 : at % 2 * 256 + 256]


def split_units(inputs):
    shape = (8, 512, 256)
    return pl.pallas_call(
        split_kernel,
        out_shape=jax.ShapeDtypeStruct(shape, BF),
        in_specs=[whole(inputs.shape)],
        out_specs=whole(shape),
        compiler_params=params(),
        cost_estimate=cost(1, 1),
    )(inputs)


PRODUCT = cost(1, 1)


def stacked(refs):
    return jnp.concatenate([ref[...] for ref in refs], axis=0)


def halves(top, bottom, top_up, up, down, bottom_down):
    first, second = pl.ds(0, BLOCK), pl.ds(BLOCK, BLOCK)
    return (
        top, bottom, top_up, up.at[second],
        up.at[first], down.at[second], down.at[first], bottom_down,
    )


def forward_kernel(place, _, panel, *refs):
    weights, (own, other, left) = halves(*refs[:6]), refs[6:]
    x, k, zh = place[0], place[2], place[3]

    @pl.when(pl.program_id(0) == 0)
    def _():
        for at in range(8):
            m = lax.rem(x - at // 2 + 4, 4)
            s = lax.rem(at % 2 + zh, 2)
            lanes = pl.ds(pl.multiple_of(m * 256, 256), 256)
            for b in range(8):
                kk = lax.rem(k + b % 2, 2)
                row = kk * 512 + b // 2 * 128 + s * 64
                rows = pl.ds(pl.multiple_of(row, 64), 64)
                left[rows, lanes] = panel[at, b * 64 : b * 64 + 64, :]

    total = jnp.dot(left[...], stacked(weights), preferred_element_type=F32)
    own[...] = total[:512].astype(BF)
    other[...] = total[512:].astype(BF)


def forward(place, after, panel, weights):
    width = weights[0].shape[1]
    tile = width // 3
    return pl.pallas_call(
        forward_kernel,
        grid=(width // tile,),
        out_shape=[jax.ShapeDtypeStruct((512, width), BF)] * 2,
        in_specs=[SCALAR, ANY, whole(panel.shape)]
        + [pl.BlockSpec((w.shape[0], tile), lambda n: (0, n)) for w in weights],
        out_specs=[pl.BlockSpec((512, tile), lambda n: (0, n))] * 2,
        scratch_shapes=[pltpu.VMEM((1024, 1024), BF)],
        compiler_params=params(),
        cost_estimate=PRODUCT,
    )(place, after, panel, *weights)


def weight_grad_kernel(place, _, panel, near, *refs):
    far, outs, (left, right) = refs[:4], refs[4:9], refs[9:]
    x, y, k, zh = place[0], place[1], place[2], place[3]

    @pl.when(pl.program_id(0) == 0)
    def _():
        for at in range(8):
            m = lax.rem(x - at // 2 + 4, 4)
            s = lax.rem(at % 2 + zh, 2)
            rows = pl.ds(pl.multiple_of(m * 256, 256), 256)
            lanes = pl.ds(pl.multiple_of(s * 512, 512), 512)
            left[rows, lanes] = panel[at].T

    right[:512, :] = near[...]
    for e in range(4):
        for kk in range(2):
            block = lax.rem(y - e + 4, 4) * 2 + lax.rem(k + kk, 2)
            rows = pl.ds(pl.multiple_of(512 + block * 64, 64), 64)
            right[rows, :] = far[e][kk * 64 : kk * 64 + 64, :]
    total = jnp.dot(left[...], right[...], preferred_element_type=F32)
    at = 0
    for out in outs:
        out[...] = total[at : at + out.shape[0]].astype(BF)
        at += out.shape[0]


def weight_grad(place, after, panel, near, far):
    width = near.shape[1]
    tile = width // 3
    sizes = (256, 256, 128, 128, 256)
    return pl.pallas_call(
        weight_grad_kernel,
        grid=(width // tile,),
        out_shape=[jax.ShapeDtypeStruct((rows, width), BF) for rows in sizes],
        in_specs=[SCALAR, ANY, whole(panel.shape)]
        + [pl.BlockSpec((rows, tile), lambda n: (0, n)) for rows in (512, 128, 128, 128, 128)],
        out_specs=[pl.BlockSpec((rows, tile), lambda n: (0, n)) for rows in sizes],
        scratch_shapes=[pltpu.VMEM((1024, 1024), BF), pltpu.VMEM((1024, tile), BF)],
        compiler_params=params(),
        cost_estimate=PRODUCT,
    )(place, after, panel, near, *far)


def backward_kernel(place, near, *refs):
    far, weights, out = refs[:4], halves(*refs[4:10]), refs[10]
    x, y, k, zh = place[0], place[1], place[2], place[3]
    step = pl.program_id(0)
    rows = pl.ds(pl.multiple_of(step * 256, 256), 256)
    far = stacked(far)
    for m in range(4):
        at = lax.rem(x - m + 4, 4) * 2
        right = stacked(weights[2 * m : 2 * m + 2])
        total = lax.dot_general(
            near[...], right, (((1,), (1,)), ((), ())), preferred_element_type=F32
        )
        out[at + zh, rows, :] = total.astype(BF)
        total = lax.dot_general(
            far, right, (((1,), (1,)), ((), ())), preferred_element_type=F32
        ).astype(BF)
        for i in range(4):
            block = lax.rem(y - i + 4, 4) * 2 + lax.rem(k + step, 2)
            target = pl.ds(pl.multiple_of(block * 64, 64), 64)
            out[at + 1 - zh, target, :] = total[i * 64 : i * 64 + 64]


def backward(place, near, far, weights):
    width = near.shape[1]
    return pl.pallas_call(
        backward_kernel,
        grid=(2,),
        out_shape=jax.ShapeDtypeStruct((8, 512, 256), BF),
        in_specs=[SCALAR]
        + [pl.BlockSpec((rows, width), lambda n: (n, 0)) for rows in (256, 64, 64, 64, 64)]
        + [whole(w.shape) for w in weights],
        out_specs=whole((8, 512, 256)),
        compiler_params=params(),
        cost_estimate=PRODUCT,
    )(place, near, *far, *weights)


def summed(*refs):
    total = refs[0].astype(F32)
    for ref in refs[1:]:
        total = total + ref.astype(F32)
    return total.astype(BF)


def local(kernel, outs, after, *args):
    after = after if isinstance(after, tuple) else (after,)
    return pl.pallas_call(
        lambda *refs: kernel(*refs[len(after) :]),
        out_shape=[jax.ShapeDtypeStruct(shape, BF) for shape in outs],
        in_specs=[ANY] * len(after) + [whole(a.shape) for a in args],
        out_specs=[whole(shape) for shape in outs],
        compiler_params=params(),
        cost_estimate=cost(1, 1),
    )(*after, *args)


def follow(array, after):
    return pl.pallas_call(
        lambda *_: None,
        out_shape=jax.ShapeDtypeStruct(array.shape, array.dtype),
        in_specs=[ANY] * (1 + len(after)),
        out_specs=ANY,
        input_output_aliases={0: 0},
        cost_estimate=cost(1, 1),
    )(array, *after)


def relay_kernel(top, bottom, top_up, bottom_down, up, down):
    up[:BLOCK], up[BLOCK:] = top_up[...], bottom[...]
    down[:BLOCK], down[BLOCK:] = top[...], bottom_down[...]


def collect_kernel(mine, theirs, out):
    out[:64], out[64:] = mine[...], theirs[...]


def sum_kernel(*refs):
    refs[-1][...] = summed(*[ref[...] for ref in refs[:-1]])


def onward_kernel(up, down, from_below, from_above, up_out, down_out):
    half = from_below.shape[0]
    up_out[:half] = summed(up[:half], from_below[...])
    up_out[half:] = up[half:]
    down_out[:half] = down[:half]
    down_out[half:] = summed(down[half:], from_above[...])


def shift(array, axis, step):
    return lax.ppermute(array, axis, ring(lax.axis_size(axis), step))


def per_device(inputs, qweight, scales, grad_out):
    x, y, k, zh = (lax.axis_index(name) for name in ("x", "y", "k", "zh"))
    place = jnp.stack([x, y, k, zh]).astype(jnp.int32)
    F = qweight.shape[1]

    near = lax.all_gather(grad_out[0], ("y", "k"), axis=0, tiled=True)

    far = shift(grad_out[0], "zh", 1)
    top, bottom = dequantize(scales, qweight)
    top_up, bottom_down = shift(top, "x", 1), shift(bottom, "x", -1)
    split = follow(split_units(inputs[0]), (far, top_up, bottom_down))
    panel = lax.all_to_all(split, ("zl", "zh"), 0, 0, tiled=True)
    up, down = local(
        relay_kernel, [(256, F)] * 2, (), top, bottom, top_up, bottom_down
    )
    (far,) = local(collect_kernel, [(128, F)], up, far, shift(far, "k", 1))
    far = [far] + [shift(far, "y", e) for e in (1, 2, 3)]
    up, down = shift(up, "x", 1), shift(down, "x", -1)
    weights = (top, bottom, top_up, up, down, bottom_down)

    sums = backward(place, near, far, weights)
    own, other = forward(place, sums, panel, weights)
    other = shift(other, "k", 1)
    terms = weight_grad(place, own, panel, near, far)

    (both,) = local(sum_kernel, [(512, F)], terms[0], own, other)
    both = lax.psum_scatter(both, "y", scatter_dimension=0, tiled=True)
    projected = summed(both[:64], shift(both[64:], "zh", 1))

    sums = lax.all_to_all(sums, ("zl", "zh"), 0, 0, tiled=True)
    grad_inputs = jnp.concatenate(
        [summed(*[sums[zl * 2 + h] for zl in range(4)]) for h in range(2)], axis=1
    )

    here, down, top, bottom, up = terms
    top, bottom = shift(top, "x", 1), shift(bottom, "x", -1)
    up, down = local(onward_kernel, [(256, F)] * 2, (), up, down, top, bottom)
    up, down = shift(up, "x", 1), shift(down, "x", -1)
    (grad_weight,) = local(sum_kernel, [(256, F)], grad_inputs, here, up, down)

    return projected[None], grad_inputs[None], grad_weight


def solution(mesh):
    axes = Mesh(mesh.devices.reshape(4, 2, 4, 4, 2), ("y", "k", "zl", "x", "zh"))
    return jax.shard_map(
        per_device,
        mesh=axes,
        in_specs=(
            P(("x", "zh"), None, ("y", "k", "zl")),
            P(("y", "k", "x", "zh"), "zl"),
            P(("y", "k", "x", "zh"), "zl"),
            P(("x", "zh"), ("y", "k"), "zl"),
        ),
        out_specs=(
            P(("x", "zh"), ("y", "k"), "zl"),
            P(("x", "zh"), None, ("y", "k", "zl")),
            P(("y", "k", "x", "zh"), "zl"),
        ),
        check_vma=False,
    )
```

time: 230 us -> 201 us (0.87)
  waiting for transfers between devices: 105 us -> 79 us
  Pallas kernels: 53.8 us -> 50.6 us
    ppermute x19 -> x15, waiting for transfers between devices: 104 us -> 52.3 us  [shift(): return lax.ppermute(array, axis, ring(lax.axis_size(axis), step))]
    all_to_all x1, waiting for transfers between devices: 0.01 us -> 25.1 us  [per_device(): sums = lax.all_to_all(sums, ('zl', 'zh'), 0, 0, tiled=True)]
    pallas_call x7 -> x5, Pallas kernels: 21.4 us -> 16.5 us  [local(): pl.pallas_call(lambda *refs: kernel(*refs[len(after):]), out_shape=[jax.S...]
    ppermute x19 -> x15, starting transfers between devices: 31.4 us -> 27.7 us  [shift(): return lax.ppermute(array, axis, ring(lax.axis_size(axis), step))]
    all_to_all x1, starting transfers between devices: 3.75 us -> 7.35 us  [per_device(): sums = lax.all_to_all(sums, ('zl', 'zh'), 0, 0, tiled=True)]
    unnamed x38 -> x30, local copies, waits for them, and re-layouts: 9.97 us -> 8.23 us
    pallas_call x1 -> x3, Pallas kernels: 3.46 us -> 4.99 us  [the longest x1 2.55 us: split_units(): pl.pallas_call(split_kernel, out_shape=jax.ShapeDtypeStruct(shape, BF), i...]
  transfers between devices with their start and end apart: 22 -> 19, of which waited for: 9 -> 7; matrix products, arithmetic and copies ran while one was open for 1% -> 2% of each run, Pallas kernels for 19% -> 17%
where the time goes in v3:
time: 201 us; the launch traced here: 200 us
  waiting for transfers between devices  79 us (39%)
  Pallas kernels  50.6 us (25%)
  starting transfers between devices  42.5 us (21%)
  between operations  14.1 us (7%)
  local copies, waits for them, and re-layouts  9.92 us (5%)
  other arithmetic  3.68 us (2%)
    ppermute x15, waiting for transfers between devices, shift(): return lax.ppermute(array, axis, ring(lax.axis_size(axis), step))  52.3 us
    ppermute x15, starting transfers between devices, shift(): return lax.ppermute(array, axis, ring(lax.axis_size(axis), step))  27.7 us
    all_to_all x1, waiting for transfers between devices, per_device(): sums = lax.all_to_all(sums, ('zl', 'zh'), 0, 0, tiled=True)  25.1 us
    pallas_call x5, Pallas kernels, local(): pl.pallas_call(lambda *refs: kernel(*refs[len(after):]), out_shape=[jax.S...  16.5 us
    pallas_call x1, Pallas kernels, backward(): pl.pallas_call(backward_kernel, grid=(2,), out_shape=jax.ShapeDtypeStruct...  9.98 us
    pallas_call x1, Pallas kernels, weight_grad(): pl.pallas_call(weight_grad_kernel, grid=(width // tile,), out_shape=[jax....  9.8 us
    pallas_call x1, Pallas kernels, forward(): pl.pallas_call(forward_kernel, grid=(width // tile,), out_shape=[jax.Shap...  9.35 us
    unnamed x30, local copies, waits for them, and re-layouts  8.23 us
  transfers between devices with their start and end apart: 19, of which 7 were waited for; matrix products, arithmetic and copies ran while one was open for 2% of the time, Pallas kernels for 17%

profile of v3, /device:TPU:32, one launch (start us, length us, event | category | flops | bytes accessed | tf_op | source)
XLA Modules:
  0.0 199.8 jit_solution(9217049835604157221)
XLA Ops:
  7.2 2.4 %shard_map.67 = (bf16[128,2304]{1,0:T(8,128)(2,1)}, bf16[128,2304]{1,0:T(8,128)(2,1)}) custom-call(f32[2,18]{1,0:T(2,128)} %scales.1, bf16[256,2304]{1,0:T(8,128)(2,1)} %quantized.1), custom_call_target="tpu_custom_call" | custom-call | flops 1 | bytes 1 | tf_op jit(solution)/shard_map/pallas_call | solution.py:44
  11.2 1.7 collective-permute-start.1
  12.9 6.4 %collective-permute-start.2 = (bf16[64,2304]{1,0:T(8,128)(2,1)S(1)}, bf16[64,2304]{1,0:T(8,128)(2,1)S(1)}, u32[]{:S(2)}, u32[]{:S(2)}) collective-permute-start(bf16[64,2304]{1,0:T(8,128)(2,1)S(1)} %bitcast.18), channel_id=1, source_target_pairs={{0,1},{1,0},{2,3},{3,2},{4,5},{5,4},{6,7},{7,6},{8,9},{9,8},{10,11... | collective-permute-start | bytes 884744 | tf_op jit(solution)/shard_map/ppermute | solution.py:255
  19.3 2.5 %shard_map.71.__0_ = bf16[8,512,256]{2,1,0:T(8,128)(2,1)} custom-call(bf16[512,512]{1,0:T(8,128)(2,1)} %bitcast.17), custom_call_target="tpu_custom_call" | custom-call | flops 1 | bytes 1 | tf_op jit(solution)/shard_map/pallas_call | solution.py:61
  21.9 10.3 %collective-permute-done.2.refs_1_.__1_ = bf16[64,2304]{1,0:T(8,128)(2,1)S(1)} collective-permute-done((bf16[64,2304]{1,0:T(8,128)(2,1)S(1)}, bf16[64,2304]{1,0:T(8,128)(2,1)S(1)}, u32[]{:S(2)}, u32[]{:S(2)}) %collective-permute-start.2) | collective-permute-done | bytes 294944 | tf_op jit(solution)/shard_map/ppermute | solution.py:255
  33.9 7.4 %all-to-all-start = ((bf16[8,512,256]{2,1,0:T(8,128)(2,1)}), bf16[8,512,256]{2,1,0:T(8,128)(2,1)S(1)}, u32[]{:S(2)}, u32[]{:S(2)}) async-start(bf16[8,512,256]{2,1,0:T(8,128)(2,1)} %shard_map.72), calls=%async_computation | async-start | bytes 4194304 | tf_op jit(solution)/shard_map/all_to_all | solution.py:269
  41.3 3.2 %shard_map.68 = (bf16[256,2304]{1,0:T(8,128)(2,1)}, bf16[256,2304]{1,0:T(8,128)(2,1)}) custom-call(bf16[128,2304]{1,0:T(8,128)(2,1)} %get-tuple-element.16.refs_0_.refs_4_, bf16[128,2304]{1,0:T(8,128)(2,1)} %get-tuple-element.17.refs_1_.refs_5_, bf16[128,2304]{1,0:T(8,128)(2,1)} %copy-done.1, bf16[128,2304]{1,0:T(8,128)(2,1)} %copy-done.2), custom_call_target="tpu_custom_call" | custom-call | flops 1 | bytes 1 | tf_op jit(solution)/shard_map/pallas_call | solution.py:212
  48.8 1.9 shard_map.69.refs_0_
  50.7 3.0 %collective-permute-start.6 = (bf16[128,2304]{1,0:T(8,128)(2,1)}, bf16[128,2304]{1,0:T(8,128)(2,1)}, u32[]{:S(2)}, u32[]{:S(2)}) collective-permute-start(bf16[128,2304]{1,0:T(8,128)(2,1)} %shard_map.69.refs_0_), channel_id=1, source_target_pairs={{0,192},{64,0},{128,64},{192,128},{1,193},{65,1},{129,65},{193,129... | collective-permute-start | bytes 1769480 | tf_op jit(solution)/shard_map/ppermute | solution.py:255
  56.0 23.6 %collective-permute-done.6.refs_3_ = bf16[128,2304]{1,0:T(8,128)(2,1)} collective-permute-done((bf16[128,2304]{1,0:T(8,128)(2,1)}, bf16[128,2304]{1,0:T(8,128)(2,1)}, u32[]{:S(2)}, u32[]{:S(2)}) %collective-permute-start.6) | collective-permute-done | bytes 589856 | tf_op jit(solution)/shard_map/ppermute | solution.py:255
  79.6 3.7 %collective-permute-done.4.refs_1_ = bf16[128,2304]{1,0:T(8,128)(2,1)} collective-permute-done((bf16[128,2304]{1,0:T(8,128)(2,1)}, bf16[128,2304]{1,0:T(8,128)(2,1)}, u32[]{:S(2)}, u32[]{:S(2)}) %collective-permute-start.4) | collective-permute-done | bytes 589856 | tf_op jit(solution)/shard_map/ppermute | solution.py:255
  84.3 10.0 %shard_map.70._ = bf16[8,512,256]{2,1,0:T(8,128)(2,1)} custom-call(s32[4]{0:T(128)} %pad_add_fusion.place, bf16[512,2304]{1,0:T(8,128)(2,1)} %bitcast.15, bf16[128,2304]{1,0:T(8,128)(2,1)} %shard_map.69.refs_0_, bf16[128,2304]{1,0:T(8,128)(2,1)} %collective-permute-done.4.refs_1_, bf16[128,2304]{1,0:T(8,128)(2,1)} %collective-permute-done.5.refs_2_, ...), custom_call_target="tpu_custom_call" | custom-call | flops 1 | bytes 1 | tf_op jit(solution)/shard_map/pallas_call | solution.py:190
  95.6 9.3 %shard_map.73 = (bf16[512,2304]{1,0:T(8,128)(2,1)}, bf16[512,2304]{1,0:T(8,128)(2,1)}) custom-call(s32[4]{0:T(128)} %pad_add_fusion.place, bf16[8,512,256]{2,1,0:T(8,128)(2,1)} %shard_map.70._, bf16[8,512,256]{2,1,0:T(8,128)(2,1)} %copy-done, bf16[128,2304]{1,0:T(8,128)(2,1)} %get-tuple-element.16.refs_0_.refs_4_, ...), custom_call_target="tpu_custom_call" | custom-call | flops 1 | bytes 1 | tf_op jit(solution)/shard_map/pallas_call | solution.py:110
  105.1 9.8 %shard_map.74 = (bf16[256,2304]{1,0:T(8,128)(2,1)}, bf16[256,2304]{1,0:T(8,128)(2,1)}, bf16[128,2304]{1,0:T(8,128)(2,1)}, bf16[128,2304]{1,0:T(8,128)(2,1)}, bf16[256,2304]{1,0:T(8,128)(2,1)}) custom-call(s32[4]{0:T(128)} %pad_add_fusion.place, bf16[512,2304]{1,0:T(8,128)(2,1)} %get-tuple-element.20._.refs_1_, bf16[8,512,256]{2,1,0:T(8,128)(2,1)} %copy-done, ...), custom_call_target="tpu_custom_call" | custom-call | flops 1 | bytes 1 | tf_op jit(solution)/shard_map/pallas_call | solution.py:153
  116.3 4.3 %shard_map.75 = bf16[512,2304]{1,0:T(8,128)(2,1)} custom-call(bf16[256,2304]{1,0:T(8,128)(2,1)} %get-tuple-element.21.refs_0_.refs_1_, bf16[512,2304]{1,0:T(8,128)(2,1)} %get-tuple-element.20._.refs_1_, bf16[512,2304]{1,0:T(8,128)(2,1)} %copy-done.4), custom_call_target="tpu_custom_call" | custom-call | flops 1 | bytes 1 | tf_op jit(solution)/shard_map/pallas_call | solution.py:212
  120.7 7.3 %all-to-all-start.1 = ((bf16[8,512,256]{2,1,0:T(8,128)(2,1)}), bf16[8,512,256]{2,1,0:T(8,128)(2,1)S(1)}, u32[]{:S(2)}, u32[]{:S(2)}) async-start(bf16[8,512,256]{2,1,0:T(8,128)(2,1)} %shard_map.70._), calls=%async_computation.2 | async-start | bytes 4194304 | tf_op jit(solution)/shard_map/all_to_all | solution.py:287
  128.4 2.9 %collective-permute-start.12 = (bf16[128,2304]{1,0:T(8,128)(2,1)S(1)}, bf16[128,2304]{1,0:T(8,128)(2,1)S(1)}, u32[]{:S(2)}, u32[]{:S(2)}) collective-permute-start(bf16[128,2304]{1,0:T(8,128)(2,1)S(1)} %copy-done.13), channel_id=1, source_target_pairs={{0,6},{2,0},{4,2},{6,4},{1,7},{3,1},{5,3},{7,5},{8,14},{10,8},{12,... | collective-permute-start | bytes 1769480 | tf_op jit(solution)/shard_map/ppermute | solution.py:255
  131.3 13.1 %collective-permute-done.11.refs_2_ = bf16[128,2304]{1,0:T(8,128)(2,1)S(1)} collective-permute-done((bf16[128,2304]{1,0:T(8,128)(2,1)S(1)}, bf16[128,2304]{1,0:T(8,128)(2,1)S(1)}, u32[]{:S(2)}, u32[]{:S(2)}) %collective-permute-start.11) | collective-permute-done | bytes 589856 | tf_op jit(solution)/shard_map/ppermute | solution.py:255
  145.4 3.6 %shard_map.76 = (bf16[256,2304]{1,0:T(8,128)(2,1)}, bf16[256,2304]{1,0:T(8,128)(2,1)}) custom-call(bf16[256,2304]{1,0:T(8,128)(2,1)} %get-tuple-element.23.refs_0_, bf16[256,2304]{1,0:T(8,128)(2,1)} %get-tuple-element.24.refs_1_, bf16[128,2304]{1,0:T(8,128)(2,1)} %copy-done.8, bf16[128,2304]{1,0:T(8,128)(2,1)} %copy-done.9), custom_call_target="tpu_custom_call" | custom-call | flops 1 | bytes 1 | tf_op jit(solution)/shard_map/pallas_call | solution.py:212
  149.8 2.5 %collective-permute-start.14 = (bf16[256,2304]{1,0:T(8,128)(2,1)}, bf16[256,2304]{1,0:T(8,128)(2,1)}, u32[]{:S(2)}, u32[]{:S(2)}) collective-permute-start(bf16[256,2304]{1,0:T(8,128)(2,1)} %get-tuple-element.28), channel_id=1, source_target_pairs={{0,6},{2,0},{4,2},{6,4},{1,7},{3,1},{5,3},{7,5},{8,14},{10,8},{12,... | collective-permute-start | bytes 3538952 | tf_op jit(solution)/shard_map/ppermute | solution.py:255
  155.5 4.8 %collective-permute-start.10 = (bf16[64,2304]{1,0:T(8,128)(2,1)}, bf16[64,2304]{1,0:T(8,128)(2,1)}, u32[]{:S(2)}, u32[]{:S(2)}) collective-permute-start(bf16[64,2304]{1,0:T(8,128)(2,1)} %slice.41), channel_id=1, source_target_pairs={{0,1},{1,0},{2,3},{3,2},{4,5},{5,4},{6,7},{7,6},{8,9},{9,8},{10,11... | collective-permute-start | bytes 884744 | tf_op jit(solution)/shard_map/ppermute | solution.py:255
  160.3 25.1 %all-to-all-done.1 = bf16[8,512,256]{2,1,0:T(8,128)(2,1)S(1)} async-done(((bf16[8,512,256]{2,1,0:T(8,128)(2,1)}), bf16[8,512,256]{2,1,0:T(8,128)(2,1)S(1)}, u32[]{:S(2)}, u32[]{:S(2)}) %all-to-all-start.1) | async-done | bytes 2097184 | tf_op jit(solution)/shard_map/all_to_all | solution.py:287
  187.8 3.5 %shard_map.77 = bf16[256,2304]{1,0:T(8,128)(2,1)} custom-call(bf16[512,512]{1,0:T(8,128)(2,1)} %get-tuple-element.31.refs_0_, bf16[256,2304]{1,0:T(8,128)(2,1)} %get-tuple-element.21.refs_0_.refs_1_, bf16[256,2304]{1,0:T(8,128)(2,1)} %copy-done.7, bf16[256,2304]{1,0:T(8,128)(2,1)} %collective-permute-done.14.refs_3_), custom_call_target="tpu_custom_call" | custom-call | flops 1 | bytes 1 | tf_op jit(solution)/shard_map/pallas_call | solution.py:212
  191.2 1.7 fusion
  (62 shorter events, 21.4 us)
Async XLA Ops:
  7.2 5.8 %copy-start.12 = (bf16[1,64,2304]{2,1,0:T(8,128)(2,1)S(1)}, bf16[1,64,2304]{2,1,0:T(8,128)(2,1)}, u32[]{:S(2)}) copy-start(bf16[1,64,2304]{2,1,0:T(8,128)(2,1)} %param.7) | copy-start | bytes 884740
  7.2 76.1 %all-gather.3.cloned.1.call-start = ((), (), s32[]{:S(2)}) async-start(), calls=%async_computation.4 | async-start | bytes 2654208 | tf_op jit(solution)/shard_map/all_gather | solution.py:263
  9.7 22.5 %collective-permute-start = (bf16[128,2304]{1,0:T(8,128)(2,1)}, bf16[128,2304]{1,0:T(8,128)(2,1)S(1)}, u32[]{:S(2)}, u32[]{:S(2)}) collective-permute-start(bf16[128,2304]{1,0:T(8,128)(2,1)} %get-tuple-element.16.refs_0_.refs_4_), channel_id=1, source_target_pairs={{0,2},{2,4},{4,6},{6,0},{1,3},{3,5},{5,7},{7,1},{8,10},{10,12},{12... | collective-permute-start | bytes 1769480 | tf_op jit(solution)/shard_map/ppermute | solution.py:255
  11.2 21.0 %collective-permute-start.1 = (bf16[128,2304]{1,0:T(8,128)(2,1)}, bf16[128,2304]{1,0:T(8,128)(2,1)S(1)}, u32[]{:S(2)}, u32[]{:S(2)}) collective-permute-start(bf16[128,2304]{1,0:T(8,128)(2,1)} %get-tuple-element.17.refs_1_.refs_5_), channel_id=1, source_target_pairs={{0,6},{2,0},{4,2},{6,4},{1,7},{3,1},{5,3},{7,5},{8,14},{10,8},{12,... | collective-permute-start | bytes 1769480 | tf_op jit(solution)/shard_map/ppermute | solution.py:255
  12.9 19.2 %collective-permute-start.2 = (bf16[64,2304]{1,0:T(8,128)(2,1)S(1)}, bf16[64,2304]{1,0:T(8,128)(2,1)S(1)}, u32[]{:S(2)}, u32[]{:S(2)}) collective-permute-start(bf16[64,2304]{1,0:T(8,128)(2,1)S(1)} %bitcast.18), channel_id=1, source_target_pairs={{0,1},{1,0},{2,3},{3,2},{4,5},{5,4},{6,7},{7,6},{8,9},{9,8},{10,11... | collective-permute-start | bytes 884744 | tf_op jit(solution)/shard_map/ppermute | solution.py:255
  33.9 60.4 %all-to-all-start = ((bf16[8,512,256]{2,1,0:T(8,128)(2,1)}), bf16[8,512,256]{2,1,0:T(8,128)(2,1)S(1)}, u32[]{:S(2)}, u32[]{:S(2)}) async-start(bf16[8,512,256]{2,1,0:T(8,128)(2,1)} %shard_map.72), calls=%async_computation | async-start | bytes 4194304 | tf_op jit(solution)/shard_map/all_to_all | solution.py:269
  41.3 112.5 %reduce-scatter.2.cloned.1.call-start = ((), (), s32[]{:S(2)}) async-start(), calls=%async_computation.3 | async-start | bytes 2949120 | tf_op jit(solution)/shard_map/reduce_scatter | solution.py:284
  41.3 5.2 %copy-start.6 = (bf16[64,2304]{1,0:T(8,128)(2,1)S(1)}, bf16[64,2304]{1,0:T(8,128)(2,1)}, u32[]{:S(2)}) copy-start(bf16[64,2304]{1,0:T(8,128)(2,1)} %copy-done.5) | copy-start | bytes 884740
  44.5 38.8 %collective-permute-start.8 = (bf16[256,2304]{1,0:T(8,128)(2,1)}, bf16[256,2304]{1,0:T(8,128)(2,1)S(1)}, u32[]{:S(2)}, u32[]{:S(2)}) collective-permute-start(bf16[256,2304]{1,0:T(8,128)(2,1)} %get-tuple-element.19), channel_id=1, source_target_pairs={{0,6},{2,0},{4,2},{6,4},{1,7},{3,1},{5,3},{7,5},{8,14},{10,8},{12,... | collective-permute-start | bytes 3538952 | tf_op jit(solution)/shard_map/ppermute | solution.py:255
  46.1 37.2 %collective-permute-start.7 = (bf16[256,2304]{1,0:T(8,128)(2,1)}, bf16[256,2304]{1,0:T(8,128)(2,1)}, u32[]{:S(2)}, u32[]{:S(2)}) collective-permute-start(bf16[256,2304]{1,0:T(8,128)(2,1)} %get-tuple-element.18.refs_0_), channel_id=1, source_target_pairs={{0,2},{2,4},{4,6},{6,0},{1,3},{3,5},{5,7},{7,1},{8,10},{10,12},{12... | collective-permute-start | bytes 3538952 | tf_op jit(solution)/shard_map/ppermute | solution.py:255
  46.5 1.6 collective-permute-start.3
  50.7 28.8 %collective-permute-start.6 = (bf16[128,2304]{1,0:T(8,128)(2,1)}, bf16[128,2304]{1,0:T(8,128)(2,1)}, u32[]{:S(2)}, u32[]{:S(2)}) collective-permute-start(bf16[128,2304]{1,0:T(8,128)(2,1)} %shard_map.69.refs_0_), channel_id=1, source_target_pairs={{0,192},{64,0},{128,64},{192,128},{1,193},{65,1},{129,65},{193,129... | collective-permute-start | bytes 1769480 | tf_op jit(solution)/shard_map/ppermute | solution.py:255
  53.7 25.8 %collective-permute-start.5 = (bf16[128,2304]{1,0:T(8,128)(2,1)}, bf16[128,2304]{1,0:T(8,128)(2,1)}, u32[]{:S(2)}, u32[]{:S(2)}) collective-permute-start(bf16[128,2304]{1,0:T(8,128)(2,1)} %shard_map.69.refs_0_), channel_id=1, source_target_pairs={{0,128},{64,192},{128,0},{192,64},{1,129},{65,193},{129,1},{193,65... | collective-permute-start | bytes 1769480 | tf_op jit(solution)/shard_map/ppermute | solution.py:255
  54.4 28.9 %collective-permute-start.4 = (bf16[128,2304]{1,0:T(8,128)(2,1)}, bf16[128,2304]{1,0:T(8,128)(2,1)}, u32[]{:S(2)}, u32[]{:S(2)}) collective-permute-start(bf16[128,2304]{1,0:T(8,128)(2,1)} %shard_map.69.refs_0_), channel_id=1, source_target_pairs={{0,64},{64,128},{128,192},{192,0},{1,65},{65,129},{129,193},{193,1... | collective-permute-start | bytes 1769480 | tf_op jit(solution)/shard_map/ppermute | solution.py:255
  104.9 10.0 %collective-permute-start.9 = (bf16[512,2304]{1,0:T(8,128)(2,1)}, bf16[512,2304]{1,0:T(8,128)(2,1)S(1)}, u32[]{:S(2)}, u32[]{:S(2)}) collective-permute-start(bf16[512,2304]{1,0:T(8,128)(2,1)} %get-tuple-element.22), channel_id=1, source_target_pairs={{0,32},{32,0},{1,33},{33,1},{2,34},{34,2},{3,35},{35,3},{4,36},{36... | collective-permute-start | bytes 7077896 | tf_op jit(solution)/shard_map/ppermute | solution.py:255
  120.7 7.4 %copy-start.14 = (bf16[128,2304]{1,0:T(8,128)(2,1)S(1)}, bf16[128,2304]{1,0:T(8,128)(2,1)}, u32[]{:S(2)}) copy-start(bf16[128,2304]{1,0:T(8,128)(2,1)} %get-tuple-element.25) | copy-start | bytes 1769476
  120.7 7.7 %copy-start.13 = (bf16[128,2304]{1,0:T(8,128)(2,1)S(1)}, bf16[128,2304]{1,0:T(8,128)(2,1)}, u32[]{:S(2)}) copy-start(bf16[128,2304]{1,0:T(8,128)(2,1)} %get-tuple-element.26) | copy-start | bytes 1769476
  120.7 64.7 %all-to-all-start.1 = ((bf16[8,512,256]{2,1,0:T(8,128)(2,1)}), bf16[8,512,256]{2,1,0:T(8,128)(2,1)S(1)}, u32[]{:S(2)}, u32[]{:S(2)}) async-start(bf16[8,512,256]{2,1,0:T(8,128)(2,1)} %shard_map.70._), calls=%async_computation.2 | async-start | bytes 4194304 | tf_op jit(solution)/shard_map/all_to_all | solution.py:287
  128.1 16.4 %collective-permute-start.11 = (bf16[128,2304]{1,0:T(8,128)(2,1)S(1)}, bf16[128,2304]{1,0:T(8,128)(2,1)S(1)}, u32[]{:S(2)}, u32[]{:S(2)}) collective-permute-start(bf16[128,2304]{1,0:T(8,128)(2,1)S(1)} %copy-done.14), channel_id=1, source_target_pairs={{0,2},{2,4},{4,6},{6,0},{1,3},{3,5},{5,7},{7,1},{8,10},{10,12},{12... | collective-permute-start | bytes 1769480 | tf_op jit(solution)/shard_map/ppermute | solution.py:255
  128.4 16.1 %collective-permute-start.12 = (bf16[128,2304]{1,0:T(8,128)(2,1)S(1)}, bf16[128,2304]{1,0:T(8,128)(2,1)S(1)}, u32[]{:S(2)}, u32[]{:S(2)}) collective-permute-start(bf16[128,2304]{1,0:T(8,128)(2,1)S(1)} %copy-done.13), channel_id=1, source_target_pairs={{0,6},{2,0},{4,2},{6,4},{1,7},{3,1},{5,3},{7,5},{8,14},{10,8},{12,... | collective-permute-start | bytes 1769480 | tf_op jit(solution)/shard_map/ppermute | solution.py:255
  149.1 37.6 %collective-permute-start.13 = (bf16[256,2304]{1,0:T(8,128)(2,1)}, bf16[256,2304]{1,0:T(8,128)(2,1)S(1)}, u32[]{:S(2)}, u32[]{:S(2)}) collective-permute-start(bf16[256,2304]{1,0:T(8,128)(2,1)} %get-tuple-element.27), channel_id=1, source_target_pairs={{0,2},{2,4},{4,6},{6,0},{1,3},{3,5},{5,7},{7,1},{8,10},{10,12},{12... | collective-permute-start | bytes 3538952 | tf_op jit(solution)/shard_map/ppermute | solution.py:255
  149.8 36.9 %collective-permute-start.14 = (bf16[256,2304]{1,0:T(8,128)(2,1)}, bf16[256,2304]{1,0:T(8,128)(2,1)}, u32[]{:S(2)}, u32[]{:S(2)}) collective-permute-start(bf16[256,2304]{1,0:T(8,128)(2,1)} %get-tuple-element.28), channel_id=1, source_target_pairs={{0,6},{2,0},{4,2},{6,4},{1,7},{3,1},{5,3},{7,5},{8,14},{10,8},{12,... | collective-permute-start | bytes 3538952 | tf_op jit(solution)/shard_map/ppermute | solution.py:255
  155.5 35.7 %collective-permute-start.10 = (bf16[64,2304]{1,0:T(8,128)(2,1)}, bf16[64,2304]{1,0:T(8,128)(2,1)}, u32[]{:S(2)}, u32[]{:S(2)}) collective-permute-start(bf16[64,2304]{1,0:T(8,128)(2,1)} %slice.41), channel_id=1, source_target_pairs={{0,1},{1,0},{2,3},{3,2},{4,5},{5,4},{6,7},{7,6},{8,9},{9,8},{10,11... | collective-permute-start | bytes 884744 | tf_op jit(solution)/shard_map/ppermute | solution.py:255
  187.8 3.5 %copy-start.10 = (bf16[128,2304]{1,0:T(8,128)(2,1)S(1)}, bf16[128,2304]{1,0:T(8,128)(2,1)}, u32[]{:S(2)}) copy-start(bf16[128,2304]{1,0:T(8,128)(2,1)} %reduce-scatter.2.cloned.1.call-done) | copy-start | bytes 1769476
  (10 other events, 9.8 us)
Sparse Core Ops, SparseCore 0:
  13.0 29.5 all-gather.2
  120.8 32.9 reduce-scatter.1

commit v4 on v3

v4 whole, which is shorter than its diff:
```python
import jax
import jax.numpy as jnp
from jax import lax
from jax.experimental import pallas as pl
from jax.experimental.pallas import tpu as pltpu
from jax.sharding import Mesh, PartitionSpec as P

BLOCK = 128
BF = jnp.bfloat16
F32 = jnp.float32
VMEM_LIMIT = 56 * 1024 * 1024


def params():
    return pltpu.CompilerParams(vmem_limit_bytes=VMEM_LIMIT)


def cost(flops, moved):
    return pl.CostEstimate(flops=flops, bytes_accessed=moved, transcendentals=0)


def whole(shape):
    return pl.BlockSpec(shape, lambda *_: (0,) * len(shape))


SCALAR = pl.BlockSpec(memory_space=pltpu.SMEM)
ANY = pl.BlockSpec(memory_space=pl.ANY)


def ring(size, step):
    return [(i, (i + step) % size) for i in range(size)]


def dequantize_kernel(scales, quantized, top, bottom):
    for r, half in enumerate((top, bottom)):
        for c in range(scales.shape[1]):
            lanes = pl.ds(c * BLOCK, BLOCK)
            block = quantized[pl.ds(r * BLOCK, BLOCK), lanes].astype(F32)
            half[:, lanes] = (block * scales[r, c]).astype(BF)


def dequantize(scales, quantized):
    half = (BLOCK, quantized.shape[1])
    return pl.pallas_call(
        dequantize_kernel,
        out_shape=[jax.ShapeDtypeStruct(half, BF)] * 2,
        in_specs=[SCALAR, whole(quantized.shape)],
        out_specs=[whole(half)] * 2,
        compiler_params=params(),
        cost_estimate=cost(1, 1),
    )(scales, quantized)


def split_kernel(inputs, split):
    for at in range(8):
        split[at] = inputs[:, at % 2 * 256 : at % 2 * 256 + 256]


def split_units(inputs):
    shape = (8, 512, 256)
    return pl.pallas_call(
        split_kernel,
        out_shape=jax.ShapeDtypeStruct(shape, BF),
        in_specs=[whole(inputs.shape)],
        out_specs=whole(shape),
        compiler_params=params(),
        cost_estimate=cost(1, 1),
    )(inputs)


PRODUCT = cost(1, 1)


def stacked(refs):
    return jnp.concatenate([ref[...] for ref in refs], axis=0)


def halves(top, bottom, top_up, up, down, bottom_down):
    first, second = pl.ds(0, BLOCK), pl.ds(BLOCK, BLOCK)
    return (
        top, bottom, top_up, up.at[second],
        up.at[first], down.at[second], down.at[first], bottom_down,
    )


def forward_kernel(place, _, panel, *refs):
    weights, (out, left) = halves(*refs[:6]), refs[6:]
    x, zh = place[0], place[1]

    @pl.when(pl.program_id(0) == 0)
    def _():
        for at in range(8):
            m = lax.rem(x - at // 2 + 4, 4)
            s = lax.rem(at % 2 + zh, 2)
            lanes = pl.ds(pl.multiple_of(m * 256, 256), 256)
            for b in range(8):
                rows = pl.ds(pl.multiple_of(b * 128 + s * 64, 64), 64)
                left[rows, lanes] = panel[at, b * 64 : b * 64 + 64, :]

    total = jnp.dot(left[...], stacked(weights), preferred_element_type=F32)
    out[...] = total.astype(BF)


def forward(place, after, panel, weights):
    width = weights[0].shape[1]
    tile = width // 3
    return pl.pallas_call(
        forward_kernel,
        grid=(width // tile,),
        out_shape=jax.ShapeDtypeStruct((1024, width), BF),
        in_specs=[SCALAR, ANY, whole(panel.shape)]
        + [pl.BlockSpec((w.shape[0], tile), lambda n: (0, n)) for w in weights],
        out_specs=pl.BlockSpec((1024, tile), lambda n: (0, n)),
        scratch_shapes=[pltpu.VMEM((1024, 1024), BF)],
        compiler_params=params(),
        cost_estimate=PRODUCT,
    )(place, after, panel, *weights)


def weight_grad_kernel(place, _, panel, grad, *refs):
    outs, left = refs[:5], refs[5]

    @pl.when(pl.program_id(0) == 0)
    def _():
        for at in range(8):
            m = lax.rem(place[0] - at // 2 + 4, 4)
            s = lax.rem(at % 2 + place[1], 2)
            rows = pl.ds(pl.multiple_of(m * 256, 256), 256)
            lanes = pl.ds(pl.multiple_of(s * 512, 512), 512)
            left[rows, lanes] = panel[at].T

    total = jnp.dot(left[...], grad[...], preferred_element_type=F32)
    at = 0
    for out in outs:
        out[...] = total[at : at + out.shape[0]].astype(BF)
        at += out.shape[0]


def weight_grad(place, after, panel, grad):
    width = grad.shape[1]
    tile = width // 3
    sizes = (256, 256, 128, 128, 256)
    return pl.pallas_call(
        weight_grad_kernel,
        grid=(width // tile,),
        out_shape=[jax.ShapeDtypeStruct((rows, width), BF) for rows in sizes],
        in_specs=[
            SCALAR,
            ANY,
            whole(panel.shape),
            pl.BlockSpec((1024, tile), lambda n: (0, n)),
        ],
        out_specs=[pl.BlockSpec((rows, tile), lambda n: (0, n)) for rows in sizes],
        scratch_shapes=[pltpu.VMEM((1024, 1024), BF)],
        compiler_params=params(),
        cost_estimate=PRODUCT,
    )(place, after, panel, grad)


def backward_kernel(place, *refs):
    grads, weights, out = refs[:2], halves(*refs[2:8]), refs[8]
    rows = pl.ds(pl.multiple_of(pl.program_id(0) * 256, 256), 256)
    for m in range(4):
        at = lax.rem(place[0] - m + 4, 4) * 2
        right = stacked(weights[2 * m : 2 * m + 2])
        for s, grad in enumerate(grads):
            total = lax.dot_general(
                grad[...], right, (((1,), (1,)), ((), ())), preferred_element_type=F32
            )
            out[at + lax.rem(s + place[1], 2), rows, :] = total.astype(BF)


def backward(place, grad, weights):
    width = grad.shape[1]
    return pl.pallas_call(
        backward_kernel,
        grid=(2,),
        out_shape=jax.ShapeDtypeStruct((8, 512, 256), BF),
        in_specs=[
            SCALAR,
            pl.BlockSpec((256, width), lambda n: (n, 0)),
            pl.BlockSpec((256, width), lambda n: (n + 2, 0)),
        ]
        + [whole(w.shape) for w in weights],
        out_specs=whole((8, 512, 256)),
        compiler_params=params(),
        cost_estimate=PRODUCT,
    )(place, grad, grad, *weights)


def summed(*refs):
    total = refs[0].astype(F32)
    for ref in refs[1:]:
        total = total + ref.astype(F32)
    return total.astype(BF)


def local(kernel, outs, after, *args):
    after = after if isinstance(after, tuple) else (after,)
    return pl.pallas_call(
        lambda *refs: kernel(*refs[len(after) :]),
        out_shape=[jax.ShapeDtypeStruct(shape, BF) for shape in outs],
        in_specs=[ANY] * len(after) + [whole(a.shape) for a in args],
        out_specs=[whole(shape) for shape in outs],
        compiler_params=params(),
        cost_estimate=cost(1, 1),
    )(*after, *args)


def follow(array, after):
    return pl.pallas_call(
        lambda *_: None,
        out_shape=jax.ShapeDtypeStruct(array.shape, array.dtype),
        in_specs=[ANY] * (1 + len(after)),
        out_specs=ANY,
        input_output_aliases={0: 0},
        cost_estimate=cost(1, 1),
    )(array, *after)


def relay_kernel(top, bottom, top_up, bottom_down, mine, theirs, up, down, both):
    up[:BLOCK], up[BLOCK:] = top_up[...], bottom[...]
    down[:BLOCK], down[BLOCK:] = top[...], bottom_down[...]
    both[0], both[1] = mine[...], theirs[...]


def sum_kernel(*refs):
    refs[-1][...] = summed(*[ref[...] for ref in refs[:-1]])


def gather_kernel(sums, out):
    for h in range(2):
        lanes = pl.ds(h * 256, 256)
        out[:, lanes] = summed(*[sums[zl * 2 + h] for zl in range(4)])


def onward_kernel(up, down, from_below, from_above, up_out, down_out):
    half = from_below.shape[0]
    up_out[:half] = summed(up[:half], from_below[...])
    up_out[half:] = up[half:]
    down_out[:half] = down[:half]
    down_out[half:] = summed(down[half:], from_above[...])


def shift(array, axis, step):
    return lax.ppermute(array, axis, ring(lax.axis_size(axis), step))


def per_device(inputs, qweight, scales, grad_out):
    x, zh = lax.axis_index("x"), lax.axis_index("zh")
    place = jnp.stack([x, zh]).astype(jnp.int32)
    F = qweight.shape[1]

    top, bottom = dequantize(scales, qweight)
    top_up, bottom_down = shift(top, "x", 1), shift(bottom, "x", -1)
    up, down, both = local(
        relay_kernel,
        [(256, F), (256, F), (2, 64, F)],
        (),
        *(top, bottom, top_up, bottom_down),
        *(grad_out[0], shift(grad_out[0], "zh", 1)),
    )
    grad = lax.all_gather(both, ("y", "k"), axis=1, tiled=True).reshape(1024, F)

    split = follow(split_units(inputs[0]), (up,))
    panel = lax.all_to_all(split, ("zl", "zh"), 0, 0, tiled=True)

    up, down = shift(up, "x", 1), shift(down, "x", -1)
    weights = (top, bottom, top_up, up, down, bottom_down)

    sums = backward(place, grad, weights)
    product = forward(place, sums, panel, weights)
    terms = weight_grad(place, product, panel, grad)

    product = lax.psum_scatter(product, ("y", "k"), scatter_dimension=0, tiled=True)
    projected = summed(product[:64], shift(product[64:], "zh", 1))

    sums = lax.all_to_all(sums, ("zl", "zh"), 0, 0, tiled=True)
    (grad_inputs,) = local(gather_kernel, [(512, 512)], (), sums)

    here, down, top, bottom, up = terms
    top, bottom = shift(top, "x", 1), shift(bottom, "x", -1)
    up, down = local(onward_kernel, [(256, F)] * 2, (), up, down, top, bottom)
    up, down = shift(up, "x", 1), shift(down, "x", -1)
    (grad_weight,) = local(sum_kernel, [(256, F)], (), here, up, down)

    return projected[None], grad_inputs[None], grad_weight


def solution(mesh):
    axes = Mesh(mesh.devices.reshape(4, 2, 4, 4, 2), ("y", "k", "zl", "x", "zh"))
    return jax.shard_map(
        per_device,
        mesh=axes,
        in_specs=(
            P(("x", "zh"), None, ("y", "k", "zl")),
            P(("y", "k", "x", "zh"), "zl"),
            P(("y", "k", "x", "zh"), "zl"),
            P(("x", "zh"), ("y", "k"), "zl"),
        ),
        out_specs=(
            P(("x", "zh"), ("y", "k"), "zl"),
            P(("x", "zh"), None, ("y", "k", "zl")),
            P(("y", "k", "x", "zh"), "zl"),
        ),
        check_vma=False,
    )
```

time: 201 us -> 186 us (0.925)
  starting transfers between devices: 42.5 us -> 35.8 us
  Pallas kernels: 50.6 us -> 46.6 us
    all_to_all x1, waiting for transfers between devices: 25.1 us -> 0.01 us  [per_device(): sums = lax.all_to_all(sums, ('zl', 'zh'), 0, 0, tiled=True)]
    ppermute x15 -> x10, waiting for transfers between devices: 52.3 us -> 65.9 us  [shift(): return lax.ppermute(array, axis, ring(lax.axis_size(axis), step))]
    all_to_all x1, waiting for transfers between devices: 0.01 us -> 9.9 us  [per_device(): panel = lax.all_to_all(split, ('zl', 'zh'), 0, 0, tiled=True)]
    all_to_all x1, starting transfers between devices: 7.35 us -> 3.98 us  [per_device(): sums = lax.all_to_all(sums, ('zl', 'zh'), 0, 0, tiled=True)]
    pallas_call x5 -> x4, Pallas kernels: 16.5 us -> 13.2 us  [local(): pl.pallas_call(lambda *refs: kernel(*refs[len(after):]), out_shape=[jax.S...]
    ppermute x15 -> x10, starting transfers between devices: 27.7 us -> 24.4 us  [shift(): return lax.ppermute(array, axis, ring(lax.axis_size(axis), step))]
    unnamed x30 -> x22, local copies, waits for them, and re-layouts: 8.23 us -> 7.58 us
  transfers between devices with their start and end apart: 19 -> 14, of which waited for: 7 -> 6; matrix products, arithmetic and copies ran while one was open for 2% -> 1% of each run, Pallas kernels for 17% -> 17%
where the time goes in v4:
time: 186 us; the launch traced here: 185 us
  waiting for transfers between devices  77.3 us (42%)
  Pallas kernels  46.6 us (25%)
  starting transfers between devices  35.8 us (19%)
  between operations  14.1 us (8%)
  local copies, waits for them, and re-layouts  9.28 us (5%)
  other arithmetic  2.39 us (1%)
    ppermute x10, waiting for transfers between devices, shift(): return lax.ppermute(array, axis, ring(lax.axis_size(axis), step))  65.9 us
    ppermute x10, starting transfers between devices, shift(): return lax.ppermute(array, axis, ring(lax.axis_size(axis), step))  24.4 us
    pallas_call x4, Pallas kernels, local(): pl.pallas_call(lambda *refs: kernel(*refs[len(after):]), out_shape=[jax.S...  13.2 us
    all_to_all x1, waiting for transfers between devices, per_device(): panel = lax.all_to_all(split, ('zl', 'zh'), 0, 0, tiled=True)  9.9 us
    pallas_call x1, Pallas kernels, backward(): pl.pallas_call(backward_kernel, grid=(2,), out_shape=jax.ShapeDtypeStruct...  9.66 us
    pallas_call x1, Pallas kernels, forward(): pl.pallas_call(forward_kernel, grid=(width // tile,), out_shape=jax.Shape...  9.5 us
    pallas_call x1, Pallas kernels, weight_grad(): pl.pallas_call(weight_grad_kernel, grid=(width // tile,), out_shape=[jax....  9.27 us
    unnamed x22, local copies, waits for them, and re-layouts  7.58 us
  transfers between devices with their start and end apart: 14, of which 6 were waited for; matrix products, arithmetic and copies ran while one was open for 1% of the time, Pallas kernels for 17%

profile of v4, /device:TPU:32, one launch (start us, length us, event | category | flops | bytes accessed | tf_op | source)
XLA Modules:
  0.0 185.4 jit_solution(17580656348315789914)
XLA Ops:
  7.2 2.5 %shard_map.67 = (bf16[128,2304]{1,0:T(8,128)(2,1)}, bf16[128,2304]{1,0:T(8,128)(2,1)}) custom-call(f32[2,18]{1,0:T(2,128)} %scales.1, bf16[256,2304]{1,0:T(8,128)(2,1)} %quantized.1), custom_call_target="tpu_custom_call" | custom-call | flops 1 | bytes 1 | tf_op jit(solution)/shard_map/pallas_call | solution.py:44
  11.2 1.7 collective-permute-start.1
  12.9 6.3 %collective-permute-start.2 = (bf16[64,2304]{1,0:T(8,128)(2,1)S(1)}, bf16[64,2304]{1,0:T(8,128)(2,1)S(1)}, u32[]{:S(2)}, u32[]{:S(2)}) collective-permute-start(bf16[64,2304]{1,0:T(8,128)(2,1)S(1)} %bitcast.14), channel_id=1, source_target_pairs={{0,1},{1,0},{2,3},{3,2},{4,5},{5,4},{6,7},{7,6},{8,9},{9,8},{10,11... | collective-permute-start | bytes 884744 | tf_op jit(solution)/shard_map/ppermute | solution.py:246
  19.2 12.8 %collective-permute-done.2.refs_5_ = bf16[64,2304]{1,0:T(8,128)(2,1)S(1)} collective-permute-done((bf16[64,2304]{1,0:T(8,128)(2,1)S(1)}, bf16[64,2304]{1,0:T(8,128)(2,1)S(1)}, u32[]{:S(2)}, u32[]{:S(2)}) %collective-permute-start.2) | collective-permute-done | bytes 294944 | tf_op jit(solution)/shard_map/ppermute | solution.py:246
  33.8 3.4 %shard_map.68 = (bf16[256,2304]{1,0:T(8,128)(2,1)}, bf16[256,2304]{1,0:T(8,128)(2,1)}, bf16[2,64,2304]{2,1,0:T(8,128)(2,1)}) custom-call(bf16[128,2304]{1,0:T(8,128)(2,1)} %get-tuple-element.15.refs_0_.refs_2_, bf16[128,2304]{1,0:T(8,128)(2,1)} %get-tuple-element.16.refs_1_.refs_3_, bf16[128,2304]{1,0:T(8,128)(2,1)} %copy-done.2, ...), custom_call_target="tpu_custom_call" | custom-call | flops 1 | bytes 1 | tf_op jit(solution)/shard_map/pallas_call | solution.py:200
  37.3 2.5 %shard_map.70.__0_ = bf16[8,512,256]{2,1,0:T(8,128)(2,1)} custom-call(bf16[512,512]{1,0:T(8,128)(2,1)} %bitcast.11), custom_call_target="tpu_custom_call" | custom-call | flops 1 | bytes 1 | tf_op jit(solution)/shard_map/pallas_call | solution.py:61
  39.8 7.4 %all-to-all-start = ((bf16[8,512,256]{2,1,0:T(8,128)(2,1)}), bf16[8,512,256]{2,1,0:T(8,128)(2,1)S(1)}, u32[]{:S(2)}, u32[]{:S(2)}) async-start(bf16[8,512,256]{2,1,0:T(8,128)(2,1)} %shard_map.71), calls=%async_computation | async-start | bytes 4194304 | tf_op jit(solution)/shard_map/all_to_all | solution.py:266
  47.5 3.0 %collective-permute-start.4 = (bf16[256,2304]{1,0:T(8,128)(2,1)}, bf16[256,2304]{1,0:T(8,128)(2,1)}, u32[]{:S(2)}, u32[]{:S(2)}) collective-permute-start(bf16[256,2304]{1,0:T(8,128)(2,1)} %get-tuple-element.19), channel_id=1, source_target_pairs={{0,6},{2,0},{4,2},{6,4},{1,7},{3,1},{5,3},{7,5},{8,14},{10,8},{12,... | collective-permute-start | bytes 3538952 | tf_op jit(solution)/shard_map/ppermute | solution.py:246
  51.1 23.4 %collective-permute-done.3.refs_5_.refs_3_ = bf16[256,2304]{1,0:T(8,128)(2,1)S(1)} collective-permute-done((bf16[256,2304]{1,0:T(8,128)(2,1)}, bf16[256,2304]{1,0:T(8,128)(2,1)S(1)}, u32[]{:S(2)}, u32[]{:S(2)}) %collective-permute-start.3) | collective-permute-done | bytes 1179680 | tf_op jit(solution)/shard_map/ppermute | solution.py:246
  75.5 9.7 %shard_map.69._ = bf16[8,512,256]{2,1,0:T(8,128)(2,1)} custom-call(s32[2]{0:T(128)} %pad_add_fusion.place, bf16[1024,2304]{1,0:T(8,128)(2,1)} %bitcast.8, bf16[1024,2304]{1,0:T(8,128)(2,1)} %bitcast.9, bf16[128,2304]{1,0:T(8,128)(2,1)} %get-tuple-element.15.refs_0_.refs_2_, bf16[128,2304]{1,0:T(8,128)(2,1)} %get-tuple-element.16.refs_1_.refs_3_, ...), custom_call_target="tpu_custom_call" | custom-call | flops 1 | bytes 1 | tf_op jit(solution)/shard_map/pallas_call | solution.py:175
  85.2 9.9 %all-to-all-done.panel = bf16[8,512,256]{2,1,0:T(8,128)(2,1)S(1)} async-done(((bf16[8,512,256]{2,1,0:T(8,128)(2,1)}), bf16[8,512,256]{2,1,0:T(8,128)(2,1)S(1)}, u32[]{:S(2)}, u32[]{:S(2)}) %all-to-all-start) | async-done | bytes 2097184 | tf_op jit(solution)/shard_map/all_to_all | solution.py:266
  96.5 9.5 %shard_map.72._ = bf16[1024,2304]{1,0:T(8,128)(2,1)} custom-call(s32[2]{0:T(128)} %pad_add_fusion.place, bf16[8,512,256]{2,1,0:T(8,128)(2,1)} %shard_map.69._, bf16[8,512,256]{2,1,0:T(8,128)(2,1)} %copy-done, bf16[128,2304]{1,0:T(8,128)(2,1)} %get-tuple-element.15.refs_0_.refs_2_, bf16[128,2304]{1,0:T(8,128)(2,1)} %get-tuple-element.16.refs_1_.refs_3_, ...), custom_call_target="tpu_custom_call" | custom-call | flops 1 | bytes 1 | tf_op jit(solution)/shard_map/pallas_call | solution.py:107
  106.0 4.0 %all-to-all-start.1 = ((bf16[8,512,256]{2,1,0:T(8,128)(2,1)}), bf16[8,512,256]{2,1,0:T(8,128)(2,1)S(1)}, u32[]{:S(2)}, u32[]{:S(2)}) async-start(bf16[8,512,256]{2,1,0:T(8,128)(2,1)} %shard_map.69._), calls=%async_computation.2 | async-start | bytes 4194304 | tf_op jit(solution)/shard_map/all_to_all | solution.py:278
  110.0 9.3 %shard_map.74 = (bf16[256,2304]{1,0:T(8,128)(2,1)}, bf16[256,2304]{1,0:T(8,128)(2,1)}, bf16[128,2304]{1,0:T(8,128)(2,1)}, bf16[128,2304]{1,0:T(8,128)(2,1)}, bf16[256,2304]{1,0:T(8,128)(2,1)}) custom-call(s32[2]{0:T(128)} %pad_add_fusion.place, bf16[1024,2304]{1,0:T(8,128)(2,1)} %shard_map.72._, bf16[8,512,256]{2,1,0:T(8,128)(2,1)} %copy-done, ...), custom_call_target="tpu_custom_call" | custom-call | flops 1 | bytes 1 | tf_op jit(solution)/shard_map/pallas_call | solution.py:143
  119.7 2.8 %collective-permute-start.7 = (bf16[128,2304]{1,0:T(8,128)(2,1)}, bf16[128,2304]{1,0:T(8,128)(2,1)S(1)}, u32[]{:S(2)}, u32[]{:S(2)}) collective-permute-start(bf16[128,2304]{1,0:T(8,128)(2,1)} %get-tuple-element.24), channel_id=1, source_target_pairs={{0,6},{2,0},{4,2},{6,4},{1,7},{3,1},{5,3},{7,5},{8,14},{10,8},{12,... | collective-permute-start | bytes 1769480 | tf_op jit(solution)/shard_map/ppermute | solution.py:246
  122.5 13.0 %collective-permute-done.6.refs_2_ = bf16[128,2304]{1,0:T(8,128)(2,1)S(1)} collective-permute-done((bf16[128,2304]{1,0:T(8,128)(2,1)}, bf16[128,2304]{1,0:T(8,128)(2,1)S(1)}, u32[]{:S(2)}, u32[]{:S(2)}) %collective-permute-start.6) | collective-permute-done | bytes 589856 | tf_op jit(solution)/shard_map/ppermute | solution.py:246
  136.5 3.7 %shard_map.75 = (bf16[256,2304]{1,0:T(8,128)(2,1)}, bf16[256,2304]{1,0:T(8,128)(2,1)}) custom-call(bf16[256,2304]{1,0:T(8,128)(2,1)} %get-tuple-element.21.refs_0_, bf16[256,2304]{1,0:T(8,128)(2,1)} %get-tuple-element.22.refs_1_, bf16[128,2304]{1,0:T(8,128)(2,1)} %copy-done.6, bf16[128,2304]{1,0:T(8,128)(2,1)} %copy-done.7), custom_call_target="tpu_custom_call" | custom-call | flops 1 | bytes 1 | tf_op jit(solution)/shard_map/pallas_call | solution.py:200
  140.4 3.0 %collective-permute-start.9 = (bf16[256,2304]{1,0:T(8,128)(2,1)}, bf16[256,2304]{1,0:T(8,128)(2,1)}, u32[]{:S(2)}, u32[]{:S(2)}) collective-permute-start(bf16[256,2304]{1,0:T(8,128)(2,1)} %get-tuple-element.26), channel_id=1, source_target_pairs={{0,6},{2,0},{4,2},{6,4},{1,7},{3,1},{5,3},{7,5},{8,14},{10,8},{12,... | collective-permute-start | bytes 3538952 | tf_op jit(solution)/shard_map/ppermute | solution.py:246
  144.8 1.7 slice.9
  146.5 5.2 %collective-permute-start.5 = (bf16[64,2304]{1,0:T(8,128)(2,1)}, bf16[64,2304]{1,0:T(8,128)(2,1)}, u32[]{:S(2)}, u32[]{:S(2)}) collective-permute-start(bf16[64,2304]{1,0:T(8,128)(2,1)} %slice.9), channel_id=1, source_target_pairs={{0,1},{1,0},{2,3},{3,2},{4,5},{5,4},{6,7},{7,6},{8,9},{9,8},{10,11... | collective-permute-start | bytes 884744 | tf_op jit(solution)/shard_map/ppermute | solution.py:246
  151.7 16.6 %collective-permute-done.8.refs_1_ = bf16[256,2304]{1,0:T(8,128)(2,1)S(1)} collective-permute-done((bf16[256,2304]{1,0:T(8,128)(2,1)}, bf16[256,2304]{1,0:T(8,128)(2,1)S(1)}, u32[]{:S(2)}, u32[]{:S(2)}) %collective-permute-start.8) | collective-permute-done | bytes 1179680 | tf_op jit(solution)/shard_map/ppermute | solution.py:246
  169.4 3.4 %shard_map.76 = bf16[256,2304]{1,0:T(8,128)(2,1)} custom-call(bf16[256,2304]{1,0:T(8,128)(2,1)} %get-tuple-element.20.refs_0_, bf16[256,2304]{1,0:T(8,128)(2,1)} %copy-done.5, bf16[256,2304]{1,0:T(8,128)(2,1)} %collective-permute-done.9.refs_2_), custom_call_target="tpu_custom_call" | custom-call | flops 1 | bytes 1 | tf_op jit(solution)/shard_map/pallas_call | solution.py:200
  174.2 2.6 %shard_map.73 = bf16[512,512]{1,0:T(8,128)(2,1)} custom-call(bf16[8,512,256]{2,1,0:T(8,128)(2,1)} %copy-done.1), custom_call_target="tpu_custom_call" | custom-call | flops 1 | bytes 1 | tf_op jit(solution)/shard_map/pallas_call | solution.py:200
  176.9 1.7 fusion
  (41 shorter events, 12.1 us)
Async XLA Ops:
  7.2 5.8 %copy-start.9 = (bf16[1,64,2304]{2,1,0:T(8,128)(2,1)S(1)}, bf16[1,64,2304]{2,1,0:T(8,128)(2,1)}, u32[]{:S(2)}) copy-start(bf16[1,64,2304]{2,1,0:T(8,128)(2,1)} %param.7) | copy-start | bytes 884740
  7.2 67.4 %all-gather.2.cloned.1.call-start = ((), (), s32[]{:S(2)}) async-start(), calls=%async_computation.3 | async-start | bytes 5308416 | tf_op jit(solution)/shard_map/all_gather | solution.py:263
  9.7 22.4 %collective-permute-start = (bf16[128,2304]{1,0:T(8,128)(2,1)}, bf16[128,2304]{1,0:T(8,128)(2,1)S(1)}, u32[]{:S(2)}, u32[]{:S(2)}) collective-permute-start(bf16[128,2304]{1,0:T(8,128)(2,1)} %get-tuple-element.15.refs_0_.refs_2_), channel_id=1, source_target_pairs={{0,2},{2,4},{4,6},{6,0},{1,3},{3,5},{5,7},{7,1},{8,10},{10,12},{12... | collective-permute-start | bytes 1769480 | tf_op jit(solution)/shard_map/ppermute | solution.py:246
  11.2 20.9 %collective-permute-start.1 = (bf16[128,2304]{1,0:T(8,128)(2,1)}, bf16[128,2304]{1,0:T(8,128)(2,1)S(1)}, u32[]{:S(2)}, u32[]{:S(2)}) collective-permute-start(bf16[128,2304]{1,0:T(8,128)(2,1)} %get-tuple-element.16.refs_1_.refs_3_), channel_id=1, source_target_pairs={{0,6},{2,0},{4,2},{6,4},{1,7},{3,1},{5,3},{7,5},{8,14},{10,8},{12,... | collective-permute-start | bytes 1769480 | tf_op jit(solution)/shard_map/ppermute | solution.py:246
  12.9 19.1 %collective-permute-start.2 = (bf16[64,2304]{1,0:T(8,128)(2,1)S(1)}, bf16[64,2304]{1,0:T(8,128)(2,1)S(1)}, u32[]{:S(2)}, u32[]{:S(2)}) collective-permute-start(bf16[64,2304]{1,0:T(8,128)(2,1)S(1)} %bitcast.14), channel_id=1, source_target_pairs={{0,1},{1,0},{2,3},{3,2},{4,5},{5,4},{6,7},{7,6},{8,9},{9,8},{10,11... | collective-permute-start | bytes 884744 | tf_op jit(solution)/shard_map/ppermute | solution.py:246
  32.1 0.9 copy-start.2
  33.0 0.8 copy-start.3
  39.8 55.3 %all-to-all-start = ((bf16[8,512,256]{2,1,0:T(8,128)(2,1)}), bf16[8,512,256]{2,1,0:T(8,128)(2,1)S(1)}, u32[]{:S(2)}, u32[]{:S(2)}) async-start(bf16[8,512,256]{2,1,0:T(8,128)(2,1)} %shard_map.71), calls=%async_computation | async-start | bytes 4194304 | tf_op jit(solution)/shard_map/all_to_all | solution.py:266
  47.2 97.6 %reduce-scatter.2.cloned.1.call-start = ((), (), s32[]{:S(2)}) async-start(), calls=%async_computation.4 | async-start | bytes 5308416 | tf_op jit(solution)/shard_map/reduce_scatter | solution.py:275
  47.2 27.3 %collective-permute-start.3 = (bf16[256,2304]{1,0:T(8,128)(2,1)}, bf16[256,2304]{1,0:T(8,128)(2,1)S(1)}, u32[]{:S(2)}, u32[]{:S(2)}) collective-permute-start(bf16[256,2304]{1,0:T(8,128)(2,1)} %get-tuple-element.18.__1_), channel_id=1, source_target_pairs={{0,2},{2,4},{4,6},{6,0},{1,3},{3,5},{5,7},{7,1},{8,10},{10,12},{12... | collective-permute-start | bytes 3538952 | tf_op jit(solution)/shard_map/ppermute | solution.py:246
  47.5 27.0 %collective-permute-start.4 = (bf16[256,2304]{1,0:T(8,128)(2,1)}, bf16[256,2304]{1,0:T(8,128)(2,1)}, u32[]{:S(2)}, u32[]{:S(2)}) collective-permute-start(bf16[256,2304]{1,0:T(8,128)(2,1)} %get-tuple-element.19), channel_id=1, source_target_pairs={{0,6},{2,0},{4,2},{6,4},{1,7},{3,1},{5,3},{7,5},{8,14},{10,8},{12,... | collective-permute-start | bytes 3538952 | tf_op jit(solution)/shard_map/ppermute | solution.py:246
  74.5 1.0 copy-start.4
  95.1 1.4 copy-start
  106.0 66.9 %all-to-all-start.1 = ((bf16[8,512,256]{2,1,0:T(8,128)(2,1)}), bf16[8,512,256]{2,1,0:T(8,128)(2,1)S(1)}, u32[]{:S(2)}, u32[]{:S(2)}) async-start(bf16[8,512,256]{2,1,0:T(8,128)(2,1)} %shard_map.69._), calls=%async_computation.2 | async-start | bytes 4194304 | tf_op jit(solution)/shard_map/all_to_all | solution.py:278
  119.2 16.3 %collective-permute-start.6 = (bf16[128,2304]{1,0:T(8,128)(2,1)}, bf16[128,2304]{1,0:T(8,128)(2,1)S(1)}, u32[]{:S(2)}, u32[]{:S(2)}) collective-permute-start(bf16[128,2304]{1,0:T(8,128)(2,1)} %get-tuple-element.23), channel_id=1, source_target_pairs={{0,2},{2,4},{4,6},{6,0},{1,3},{3,5},{5,7},{7,1},{8,10},{10,12},{12... | collective-permute-start | bytes 1769480 | tf_op jit(solution)/shard_map/ppermute | solution.py:246
  119.7 15.9 %collective-permute-start.7 = (bf16[128,2304]{1,0:T(8,128)(2,1)}, bf16[128,2304]{1,0:T(8,128)(2,1)S(1)}, u32[]{:S(2)}, u32[]{:S(2)}) collective-permute-start(bf16[128,2304]{1,0:T(8,128)(2,1)} %get-tuple-element.24), channel_id=1, source_target_pairs={{0,6},{2,0},{4,2},{6,4},{1,7},{3,1},{5,3},{7,5},{8,14},{10,8},{12,... | collective-permute-start | bytes 1769480 | tf_op jit(solution)/shard_map/ppermute | solution.py:246
  135.5 0.9 copy-start.6
  135.5 1.0 copy-start.7
  140.2 28.1 %collective-permute-start.8 = (bf16[256,2304]{1,0:T(8,128)(2,1)}, bf16[256,2304]{1,0:T(8,128)(2,1)S(1)}, u32[]{:S(2)}, u32[]{:S(2)}) collective-permute-start(bf16[256,2304]{1,0:T(8,128)(2,1)} %get-tuple-element.25), channel_id=1, source_target_pairs={{0,2},{2,4},{4,6},{6,0},{1,3},{3,5},{5,7},{7,1},{8,10},{10,12},{12... | collective-permute-start | bytes 3538952 | tf_op jit(solution)/shard_map/ppermute | solution.py:246
  140.4 27.9 %collective-permute-start.9 = (bf16[256,2304]{1,0:T(8,128)(2,1)}, bf16[256,2304]{1,0:T(8,128)(2,1)}, u32[]{:S(2)}, u32[]{:S(2)}) collective-permute-start(bf16[256,2304]{1,0:T(8,128)(2,1)} %get-tuple-element.26), channel_id=1, source_target_pairs={{0,6},{2,0},{4,2},{6,4},{1,7},{3,1},{5,3},{7,5},{8,14},{10,8},{12,... | collective-permute-start | bytes 3538952 | tf_op jit(solution)/shard_map/ppermute | solution.py:246
  146.5 30.3 %collective-permute-start.5 = (bf16[64,2304]{1,0:T(8,128)(2,1)}, bf16[64,2304]{1,0:T(8,128)(2,1)}, u32[]{:S(2)}, u32[]{:S(2)}) collective-permute-start(bf16[64,2304]{1,0:T(8,128)(2,1)} %slice.9), channel_id=1, source_target_pairs={{0,1},{1,0},{2,3},{3,2},{4,5},{5,4},{6,7},{7,6},{8,9},{9,8},{10,11... | collective-permute-start | bytes 884744 | tf_op jit(solution)/shard_map/ppermute | solution.py:246
  168.3 1.1 copy-start.5
  172.9 4.0 %copy-start.8 = (bf16[128,2304]{1,0:T(8,128)(2,1)S(1)}, bf16[128,2304]{1,0:T(8,128)(2,1)}, u32[]{:S(2)}) copy-start(bf16[128,2304]{1,0:T(8,128)(2,1)} %reduce-scatter.2.cloned.1.call-done) | copy-start | bytes 1769476
  172.9 1.4 copy-start.1
  (1 other events, 0.7 us)
Sparse Core Ops, SparseCore 0:
  37.4 37.1 all-gather.1
  106.1 38.6 reduce-scatter.1

commit v5 on v4

--- a/solution.py
+++ b/solution.py
@@ -8,7 +8,7 @@
 BLOCK = 128
 BF = jnp.bfloat16
 F32 = jnp.float32
-VMEM_LIMIT = 56 * 1024 * 1024
+VMEM_LIMIT = 62 * 1024 * 1024
 
 
 def params():
@@ -117,7 +117,7 @@
     )(place, after, panel, *weights)
 
 
-def weight_grad_kernel(place, _, panel, grad, *refs):
+def weight_grad_kernel(place, _, panel, near, far, *refs):
     outs, left = refs[:5], refs[5]
 
     @pl.when(pl.program_id(0) == 0)
@@ -129,15 +129,15 @@
             lanes = pl.ds(pl.multiple_of(s * 512, 512), 512)
             left[rows, lanes] = panel[at].T
 
-    total = jnp.dot(left[...], grad[...], preferred_element_type=F32)
+    total = jnp.dot(left[...], stacked((near, far)), preferred_element_type=F32)
     at = 0
     for out in outs:
         out[...] = total[at : at + out.shape[0]].astype(BF)
         at += out.shape[0]
 
 
-def weight_grad(place, after, panel, grad):
-    width = grad.shape[1]
+def weight_grad(place, after, panel, near, far):
+    width = near.shape[1]
     tile = width // 3
     sizes = (256, 256, 128, 128, 256)
     return pl.pallas_call(
@@ -148,13 +148,14 @@
             SCALAR,
             ANY,
             whole(panel.shape),
-            pl.BlockSpec((1024, tile), lambda n: (0, n)),
+            pl.BlockSpec((512, tile), lambda n: (0, n)),
+            pl.BlockSpec((512, tile), lambda n: (0, n)),
         ],
         out_specs=[pl.BlockSpec((rows, tile), lambda n: (0, n)) for rows in sizes],
         scratch_shapes=[pltpu.VMEM((1024, 1024), BF)],
         compiler_params=params(),
         cost_estimate=PRODUCT,
-    )(place, after, panel, grad)
+    )(place, after, panel, near, far)
 
 
 def backward_kernel(place, *refs):
@@ -170,8 +171,8 @@
             out[at + lax.rem(s + place[1], 2), rows, :] = total.astype(BF)
 
 
-def backward(place, grad, weights):
-    width = grad.shape[1]
+def backward(place, near, far, weights):
+    width = near.shape[1]
     return pl.pallas_call(
         backward_kernel,
         grid=(2,),
@@ -179,13 +180,13 @@
         in_specs=[
             SCALAR,
             pl.BlockSpec((256, width), lambda n: (n, 0)),
-            pl.BlockSpec((256, width), lambda n: (n + 2, 0)),
+            pl.BlockSpec((256, width), lambda n: (n, 0)),
         ]
         + [whole(w.shape) for w in weights],
         out_specs=whole((8, 512, 256)),
         compiler_params=params(),
         cost_estimate=PRODUCT,
-    )(place, grad, grad, *weights)
+    )(place, near, far, *weights)
 
 
 def summed(*refs):
@@ -207,25 +208,18 @@
     )(*after, *args)
 
 
-def follow(array, after):
-    return pl.pallas_call(
-        lambda *_: None,
-        out_shape=jax.ShapeDtypeStruct(array.shape, array.dtype),
-        in_specs=[ANY] * (1 + len(after)),
-        out_specs=ANY,
-        input_output_aliases={0: 0},
-        cost_estimate=cost(1, 1),
-    )(array, *after)
-
-
-def relay_kernel(top, bottom, top_up, bottom_down, mine, theirs, up, down, both):
+def relay_kernel(top, bottom, top_up, bottom_down, far, up, down, passed):
     up[:BLOCK], up[BLOCK:] = top_up[...], bottom[...]
     down[:BLOCK], down[BLOCK:] = top[...], bottom_down[...]
-    both[0], both[1] = mine[...], theirs[...]
+    passed[...] = far[...]
 
 
 def sum_kernel(*refs):
     refs[-1][...] = summed(*[ref[...] for ref in refs[:-1]])
+
+
+def end_kernel(mine, theirs, out):
+    out[...] = summed(mine[:64], theirs[...])
 
 
 def gather_kernel(sums, out):
@@ -251,29 +245,31 @@
     place = jnp.stack([x, zh]).astype(jnp.int32)
     F = qweight.shape[1]
 
+    near = lax.all_gather(grad_out[0], ("y", "k"), axis=0, tiled=True)
+    split = split_units(inputs[0])
+    panel = lax.all_to_all(split, ("zl", "zh"), 0, 0, tiled=True)
+
     top, bottom = dequantize(scales, qweight)
     top_up, bottom_down = shift(top, "x", 1), shift(bottom, "x", -1)
-    up, down, both = local(
+    far = shift(grad_out[0], "zh", 1)
+    up, down, far = local(
         relay_kernel,
-        [(256, F), (256, F), (2, 64, F)],
-        (),
-        *(top, bottom, top_up, bottom_down),
-        *(grad_out[0], shift(grad_out[0], "zh", 1)),
+        [(256, F), (256, F), (64, F)],
+        split,
+        *(top, bottom, top_up, bottom_down, far),
     )
-    grad = lax.all_gather(both, ("y", "k"), axis=1, tiled=True).reshape(1024, F)
-
-    split = follow(split_units(inputs[0]), (up,))
-    panel = lax.all_to_all(split, ("zl", "zh"), 0, 0, tiled=True)
-
+    far = lax.all_gather(far, ("y", "k"), axis=0, tiled=True)
     up, down = shift(up, "x", 1), shift(down, "x", -1)
     weights = (top, bottom, top_up, up, down, bottom_down)
 
-    sums = backward(place, grad, weights)
+    sums = backward(place, near, far, weights)
     product = forward(place, sums, panel, weights)
-    terms = weight_grad(place, product, panel, grad)
+    terms = weight_grad(place, product, panel, near, far)
 
     product = lax.psum_scatter(product, ("y", "k"), scatter_dimension=0, tiled=True)
-    projected = summed(product[:64], shift(product[64:], "zh", 1))
+    (projected,) = local(
+        end_kernel, [(64, F)], (), product, shift(product[64:], "zh", 1)
+    )
 
     sums = lax.all_to_all(sums, ("zl", "zh"), 0, 0, tiled=True)
     (grad_inputs,) = local(gather_kernel, [(512, 512)], (), sums)
@@ -282,7 +278,7 @@
     top, bottom = shift(top, "x", 1), shift(bottom, "x", -1)
     up, down = local(onward_kernel, [(256, F)] * 2, (), up, down, top, bottom)
     up, down = shift(up, "x", 1), shift(down, "x", -1)
-    (grad_weight,) = local(sum_kernel, [(256, F)], (), here, up, down)
+    (grad_weight,) = local(sum_kernel, [(256, F)], (grad_inputs, projected), here, up, down)
 
     return projected[None], grad_inputs[None], grad_weight
 

time: 186 us -> 184 us (0.989)
  local copies, waits for them, and re-layouts: 9.28 us -> 6.46 us
    ppermute x10, waiting for transfers between devices: 65.9 us -> 52.9 us  [shift(): return lax.ppermute(array, axis, ring(lax.axis_size(axis), step))]
    all_to_all x1, waiting for transfers between devices: 0.01 us -> 11.7 us  [per_device(): sums = lax.all_to_all(sums, ('zl', 'zh'), 0, 0, tiled=True)]
    unnamed x22 -> x20, local copies, waits for them, and re-layouts: 7.58 us -> 5.48 us
    pallas_call x4 -> x5, Pallas kernels: 13.2 us -> 14.9 us  [local(): pl.pallas_call(lambda *refs: kernel(*refs[len(after):]), out_shape=[jax.S...]
  transfers between devices with their start and end apart: 14 -> 15, of which waited for: 6 -> 7; matrix products, arithmetic and copies ran while one was open for 1% -> 1% of each run, Pallas kernels for 17% -> 19%
where the time goes in v5:
time: 184 us; the launch traced here: 182 us
  waiting for transfers between devices  76.3 us (41%)
  Pallas kernels  48.3 us (26%)
  starting transfers between devices  36.3 us (20%)
  between operations  13.8 us (8%)
  local copies, waits for them, and re-layouts  6.46 us (4%)
    ppermute x10, waiting for transfers between devices, shift(): return lax.ppermute(array, axis, ring(lax.axis_size(axis), step))  52.9 us
    ppermute x10, starting transfers between devices, shift(): return lax.ppermute(array, axis, ring(lax.axis_size(axis), step))  24.4 us
    pallas_call x5, Pallas kernels, local(): pl.pallas_call(lambda *refs: kernel(*refs[len(after):]), out_shape=[jax.S...  14.9 us
    all_to_all x1, waiting for transfers between devices, per_device(): sums = lax.all_to_all(sums, ('zl', 'zh'), 0, 0, tiled=True)  11.7 us
    all_to_all x1, waiting for transfers between devices, per_device(): panel = lax.all_to_all(split, ('zl', 'zh'), 0, 0, tiled=True)  10 us
    pallas_call x1, Pallas kernels, backward(): pl.pallas_call(backward_kernel, grid=(2,), out_shape=jax.ShapeDtypeStruct...  9.65 us
    pallas_call x1, Pallas kernels, forward(): pl.pallas_call(forward_kernel, grid=(width // tile,), out_shape=jax.Shape...  9.45 us
    pallas_call x1, Pallas kernels, weight_grad(): pl.pallas_call(weight_grad_kernel, grid=(width // tile,), out_shape=[jax....  9.28 us
  transfers between devices with their start and end apart: 15, of which 7 were waited for; matrix products, arithmetic and copies ran while one was open for 1% of the time, Pallas kernels for 19%

profile of v5, /device:TPU:32, one launch (start us, length us, event | category | flops | bytes accessed | tf_op | source)
XLA Modules:
  0.0 181.8 jit_solution(9225660092462913929)
XLA Ops:
  8.0 2.4 %shard_map.68 = (bf16[128,2304]{1,0:T(8,128)(2,1)}, bf16[128,2304]{1,0:T(8,128)(2,1)}) custom-call(f32[2,18]{1,0:T(2,128)} %scales.1, bf16[256,2304]{1,0:T(8,128)(2,1)} %quantized.1), custom_call_target="tpu_custom_call" | custom-call | flops 1 | bytes 1 | tf_op jit(solution)/shard_map/pallas_call | solution.py:44
  11.9 1.7 collective-permute-start.1
  13.6 6.3 %collective-permute-start.2 = (bf16[64,2304]{1,0:T(8,128)(2,1)S(1)}, bf16[64,2304]{1,0:T(8,128)(2,1)S(1)}, u32[]{:S(2)}, u32[]{:S(2)}) collective-permute-start(bf16[64,2304]{1,0:T(8,128)(2,1)S(1)} %bitcast.12), channel_id=1, source_target_pairs={{0,1},{1,0},{2,3},{3,2},{4,5},{5,4},{6,7},{7,6},{8,9},{9,8},{10,11... | collective-permute-start | bytes 884744 | tf_op jit(solution)/shard_map/ppermute | solution.py:240
  19.9 2.5 %shard_map.67.refs_0_ = bf16[8,512,256]{2,1,0:T(8,128)(2,1)} custom-call(bf16[512,512]{1,0:T(8,128)(2,1)} %bitcast.11), custom_call_target="tpu_custom_call" | custom-call | flops 1 | bytes 1 | tf_op jit(solution)/shard_map/pallas_call | solution.py:61
  22.5 10.3 %collective-permute-done.2.refs_5_ = bf16[64,2304]{1,0:T(8,128)(2,1)S(1)} collective-permute-done((bf16[64,2304]{1,0:T(8,128)(2,1)S(1)}, bf16[64,2304]{1,0:T(8,128)(2,1)S(1)}, u32[]{:S(2)}, u32[]{:S(2)}) %collective-permute-start.2) | collective-permute-done | bytes 294944 | tf_op jit(solution)/shard_map/ppermute | solution.py:240
  34.5 3.3 %shard_map.69 = (bf16[256,2304]{1,0:T(8,128)(2,1)}, bf16[256,2304]{1,0:T(8,128)(2,1)}, bf16[64,2304]{1,0:T(8,128)(2,1)}) custom-call(bf16[8,512,256]{2,1,0:T(8,128)(2,1)} %shard_map.67.refs_0_, bf16[128,2304]{1,0:T(8,128)(2,1)} %get-tuple-element.15.refs_1_.refs_2_.refs_0_, bf16[128,2304]{1,0:T(8,128)(2,1)} %get-tuple-element.16.refs_2_.refs_3_.refs_1_, ...), custom_call_target="tpu_custom_call" | custom-call | flops 1 | bytes 1 | tf_op jit(solution)/shard_map/pallas_call | solution.py:201
  37.8 7.5 %all-to-all-start = ((bf16[8,512,256]{2,1,0:T(8,128)(2,1)}), bf16[8,512,256]{2,1,0:T(8,128)(2,1)}, u32[]{:S(2)}, u32[]{:S(2)}) async-start(bf16[8,512,256]{2,1,0:T(8,128)(2,1)} %shard_map.67.refs_0_), calls=%async_computation | async-start | bytes 4194304 | tf_op jit(solution)/shard_map/all_to_all | solution.py:250
  45.7 2.9 %collective-permute-start.4 = (bf16[256,2304]{1,0:T(8,128)(2,1)S(1)}, bf16[256,2304]{1,0:T(8,128)(2,1)}, u32[]{:S(2)}, u32[]{:S(2)}) collective-permute-start(bf16[256,2304]{1,0:T(8,128)(2,1)S(1)} %copy-done.9), channel_id=1, source_target_pairs={{0,6},{2,0},{4,2},{6,4},{1,7},{3,1},{5,3},{7,5},{8,14},{10,8},{12,... | collective-permute-start | bytes 3538952 | tf_op jit(solution)/shard_map/ppermute | solution.py:240
  49.2 23.4 %collective-permute-done.3.refs_5_.refs_3_ = bf16[256,2304]{1,0:T(8,128)(2,1)S(1)} collective-permute-done((bf16[256,2304]{1,0:T(8,128)(2,1)}, bf16[256,2304]{1,0:T(8,128)(2,1)S(1)}, u32[]{:S(2)}, u32[]{:S(2)}) %collective-permute-start.3) | collective-permute-done | bytes 1179680 | tf_op jit(solution)/shard_map/ppermute | solution.py:240
  73.7 9.7 %shard_map.70._ = bf16[8,512,256]{2,1,0:T(8,128)(2,1)} custom-call(s32[2]{0:T(128)} %pad_add_fusion.place, bf16[512,2304]{1,0:T(8,128)(2,1)} %bitcast.7, bf16[512,2304]{1,0:T(8,128)(2,1)} %all-gather.4.cloned.1.call-done.refs_1_.far, bf16[128,2304]{1,0:T(8,128)(2,1)} %get-tuple-element.15.refs_1_.refs_2_.refs_0_, ...), custom_call_target="tpu_custom_call" | custom-call | flops 1 | bytes 1 | tf_op jit(solution)/shard_map/pallas_call | solution.py:176
  83.3 10.0 %all-to-all-done.panel = bf16[8,512,256]{2,1,0:T(8,128)(2,1)} async-done(((bf16[8,512,256]{2,1,0:T(8,128)(2,1)}), bf16[8,512,256]{2,1,0:T(8,128)(2,1)}, u32[]{:S(2)}, u32[]{:S(2)}) %all-to-all-start) | async-done | bytes 2097184 | tf_op jit(solution)/shard_map/all_to_all | solution.py:250
  93.3 9.5 %shard_map.71._ = bf16[1024,2304]{1,0:T(8,128)(2,1)} custom-call(s32[2]{0:T(128)} %pad_add_fusion.place, bf16[8,512,256]{2,1,0:T(8,128)(2,1)} %shard_map.70._, bf16[8,512,256]{2,1,0:T(8,128)(2,1)} %all-to-all-done.panel, bf16[128,2304]{1,0:T(8,128)(2,1)} %get-tuple-element.15.refs_1_.refs_2_.refs_0_, ...), custom_call_target="tpu_custom_call" | custom-call | flops 1 | bytes 1 | tf_op jit(solution)/shard_map/pallas_call | solution.py:107
  102.8 4.3 %all-to-all-start.1 = ((bf16[8,512,256]{2,1,0:T(8,128)(2,1)}), bf16[8,512,256]{2,1,0:T(8,128)(2,1)}, u32[]{:S(2)}, u32[]{:S(2)}) async-start(bf16[8,512,256]{2,1,0:T(8,128)(2,1)} %shard_map.70._), calls=%async_computation.2 | async-start | bytes 4194304 | tf_op jit(solution)/shard_map/all_to_all | solution.py:274
  107.1 9.3 %shard_map.74 = (bf16[256,2304]{1,0:T(8,128)(2,1)}, bf16[256,2304]{1,0:T(8,128)(2,1)}, bf16[128,2304]{1,0:T(8,128)(2,1)}, bf16[128,2304]{1,0:T(8,128)(2,1)}, bf16[256,2304]{1,0:T(8,128)(2,1)}) custom-call(s32[2]{0:T(128)} %pad_add_fusion.place, bf16[1024,2304]{1,0:T(8,128)(2,1)} %shard_map.71._, bf16[8,512,256]{2,1,0:T(8,128)(2,1)} %all-to-all-done.panel, ...), custom_call_target="tpu_custom_call" | custom-call | flops 1 | bytes 1 | tf_op jit(solution)/shard_map/pallas_call | solution.py:143
  116.8 2.9 %collective-permute-start.7 = (bf16[128,2304]{1,0:T(8,128)(2,1)}, bf16[128,2304]{1,0:T(8,128)(2,1)S(1)}, u32[]{:S(2)}, u32[]{:S(2)}) collective-permute-start(bf16[128,2304]{1,0:T(8,128)(2,1)} %get-tuple-element.24), channel_id=1, source_target_pairs={{0,6},{2,0},{4,2},{6,4},{1,7},{3,1},{5,3},{7,5},{8,14},{10,8},{12,... | collective-permute-start | bytes 1769480 | tf_op jit(solution)/shard_map/ppermute | solution.py:240
  119.7 13.4 %collective-permute-done.6.refs_2_ = bf16[128,2304]{1,0:T(8,128)(2,1)S(1)} collective-permute-done((bf16[128,2304]{1,0:T(8,128)(2,1)}, bf16[128,2304]{1,0:T(8,128)(2,1)S(1)}, u32[]{:S(2)}, u32[]{:S(2)}) %collective-permute-start.6) | collective-permute-done | bytes 589856 | tf_op jit(solution)/shard_map/ppermute | solution.py:240
  134.1 3.7 %shard_map.75 = (bf16[256,2304]{1,0:T(8,128)(2,1)}, bf16[256,2304]{1,0:T(8,128)(2,1)}) custom-call(bf16[256,2304]{1,0:T(8,128)(2,1)} %get-tuple-element.21.refs_0_, bf16[256,2304]{1,0:T(8,128)(2,1)} %get-tuple-element.22.refs_1_, bf16[128,2304]{1,0:T(8,128)(2,1)} %copy-done.4, bf16[128,2304]{1,0:T(8,128)(2,1)} %copy-done.5), custom_call_target="tpu_custom_call" | custom-call | flops 1 | bytes 1 | tf_op jit(solution)/shard_map/pallas_call | solution.py:201
  137.9 3.1 %collective-permute-start.9 = (bf16[256,2304]{1,0:T(8,128)(2,1)}, bf16[256,2304]{1,0:T(8,128)(2,1)}, u32[]{:S(2)}, u32[]{:S(2)}) collective-permute-start(bf16[256,2304]{1,0:T(8,128)(2,1)} %get-tuple-element.26), channel_id=1, source_target_pairs={{0,6},{2,0},{4,2},{6,4},{1,7},{3,1},{5,3},{7,5},{8,14},{10,8},{12,... | collective-permute-start | bytes 3538952 | tf_op jit(solution)/shard_map/ppermute | solution.py:240
  142.9 5.1 %collective-permute-start.5 = (bf16[64,2304]{1,0:T(8,128)(2,1)S(1)}, bf16[64,2304]{1,0:T(8,128)(2,1)S(1)}, u32[]{:S(2)}, u32[]{:S(2)}) collective-permute-start(bf16[64,2304]{1,0:T(8,128)(2,1)S(1)} %slice.4), channel_id=1, source_target_pairs={{0,1},{1,0},{2,3},{3,2},{4,5},{5,4},{6,7},{7,6},{8,9},{9,8},{10,11... | collective-permute-start | bytes 884744 | tf_op jit(solution)/shard_map/ppermute | solution.py:240
  148.0 11.7 %all-to-all-done.1.refs_0_ = bf16[8,512,256]{2,1,0:T(8,128)(2,1)} async-done(((bf16[8,512,256]{2,1,0:T(8,128)(2,1)}), bf16[8,512,256]{2,1,0:T(8,128)(2,1)}, u32[]{:S(2)}, u32[]{:S(2)}) %all-to-all-start.1) | async-done | bytes 2097184 | tf_op jit(solution)/shard_map/all_to_all | solution.py:274
  159.8 2.6 %shard_map.73.refs_0_ = bf16[512,512]{1,0:T(8,128)(2,1)} custom-call(bf16[8,512,256]{2,1,0:T(8,128)(2,1)} %all-to-all-done.1.refs_0_), custom_call_target="tpu_custom_call" | custom-call | flops 1 | bytes 1 | tf_op jit(solution)/shard_map/pallas_call | solution.py:201
  162.4 5.8 %collective-permute-done.5.refs_1_ = bf16[64,2304]{1,0:T(8,128)(2,1)S(1)} collective-permute-done((bf16[64,2304]{1,0:T(8,128)(2,1)S(1)}, bf16[64,2304]{1,0:T(8,128)(2,1)S(1)}, u32[]{:S(2)}, u32[]{:S(2)}) %collective-permute-start.5) | collective-permute-done | bytes 294944 | tf_op jit(solution)/shard_map/ppermute | solution.py:240
  168.9 1.9 %shard_map.72.refs_1_ = bf16[64,2304]{1,0:T(8,128)(2,1)} custom-call(bf16[128,2304]{1,0:T(8,128)(2,1)} %reduce-scatter.2.cloned.1.call-done.refs_0_, bf16[64,2304]{1,0:T(8,128)(2,1)} %copy-done.8), custom_call_target="tpu_custom_call" | custom-call | flops 1 | bytes 1 | tf_op jit(solution)/shard_map/pallas_call | solution.py:201
  171.9 3.4 %shard_map.76 = bf16[256,2304]{1,0:T(8,128)(2,1)} custom-call(bf16[512,512]{1,0:T(8,128)(2,1)} %shard_map.73.refs_0_, bf16[64,2304]{1,0:T(8,128)(2,1)} %shard_map.72.refs_1_, bf16[256,2304]{1,0:T(8,128)(2,1)} %get-tuple-element.20.refs_2_, bf16[256,2304]{1,0:T(8,128)(2,1)} %copy-done.3, bf16[256,2304]{1,0:T(8,128)(2,1)} %collective-permute-done.9.refs_4_), custom_call_target="tpu_custom_call" | custom-call | flops 1 | bytes 1 | tf_op jit(solution)/shard_map/pallas_call | solution.py:201
  (41 shorter events, 11.1 us)
Async XLA Ops:
  7.2 6.5 %copy-start.7 = (bf16[1,64,2304]{2,1,0:T(8,128)(2,1)S(1)}, bf16[1,64,2304]{2,1,0:T(8,128)(2,1)}, u32[]{:S(2)}) copy-start(bf16[1,64,2304]{2,1,0:T(8,128)(2,1)} %param.7) | copy-start | bytes 884740
  7.2 65.5 %all-gather.6.cloned.1.call-start = ((), (), s32[]{:S(2)}) async-start(), calls=%async_computation.5 | async-start | bytes 2654208 | tf_op jit(solution)/shard_map/all_gather | solution.py:248
  7.9 64.8 %all-gather.4.cloned.1.call-start = ((), (), s32[]{:S(2)}) async-start(), calls=%async_computation.3 | async-start | bytes 2654208 | tf_op jit(solution)/shard_map/all_gather | solution.py:261
  10.4 22.4 %collective-permute-start = (bf16[128,2304]{1,0:T(8,128)(2,1)}, bf16[128,2304]{1,0:T(8,128)(2,1)S(1)}, u32[]{:S(2)}, u32[]{:S(2)}) collective-permute-start(bf16[128,2304]{1,0:T(8,128)(2,1)} %get-tuple-element.15.refs_1_.refs_2_.refs_0_), channel_id=1, source_target_pairs={{0,2},{2,4},{4,6},{6,0},{1,3},{3,5},{5,7},{7,1},{8,10},{10,12},{12... | collective-permute-start | bytes 1769480 | tf_op jit(solution)/shard_map/ppermute | solution.py:240
  11.9 20.9 %collective-permute-start.1 = (bf16[128,2304]{1,0:T(8,128)(2,1)}, bf16[128,2304]{1,0:T(8,128)(2,1)S(1)}, u32[]{:S(2)}, u32[]{:S(2)}) collective-permute-start(bf16[128,2304]{1,0:T(8,128)(2,1)} %get-tuple-element.16.refs_2_.refs_3_.refs_1_), channel_id=1, source_target_pairs={{0,6},{2,0},{4,2},{6,4},{1,7},{3,1},{5,3},{7,5},{8,14},{10,8},{12,... | collective-permute-start | bytes 1769480 | tf_op jit(solution)/shard_map/ppermute | solution.py:240
  13.6 19.1 %collective-permute-start.2 = (bf16[64,2304]{1,0:T(8,128)(2,1)S(1)}, bf16[64,2304]{1,0:T(8,128)(2,1)S(1)}, u32[]{:S(2)}, u32[]{:S(2)}) collective-permute-start(bf16[64,2304]{1,0:T(8,128)(2,1)S(1)} %bitcast.12), channel_id=1, source_target_pairs={{0,1},{1,0},{2,3},{3,2},{4,5},{5,4},{6,7},{7,6},{8,9},{9,8},{10,11... | collective-permute-start | bytes 884744 | tf_op jit(solution)/shard_map/ppermute | solution.py:240
  32.8 0.9 copy-start
  33.7 0.8 copy-start.1
  37.8 7.9 %copy-start.9 = (bf16[256,2304]{1,0:T(8,128)(2,1)S(1)}, bf16[256,2304]{1,0:T(8,128)(2,1)}, u32[]{:S(2)}) copy-start(bf16[256,2304]{1,0:T(8,128)(2,1)} %get-tuple-element.19) | copy-start | bytes 3538948
  37.8 55.5 %all-to-all-start = ((bf16[8,512,256]{2,1,0:T(8,128)(2,1)}), bf16[8,512,256]{2,1,0:T(8,128)(2,1)}, u32[]{:S(2)}, u32[]{:S(2)}) async-start(bf16[8,512,256]{2,1,0:T(8,128)(2,1)} %shard_map.67.refs_0_), calls=%async_computation | async-start | bytes 4194304 | tf_op jit(solution)/shard_map/all_to_all | solution.py:250
  45.4 96.5 %reduce-scatter.2.cloned.1.call-start = ((), (), s32[]{:S(2)}) async-start(), calls=%async_computation.4 | async-start | bytes 5308416 | tf_op jit(solution)/shard_map/reduce_scatter | solution.py:269
  45.4 27.3 %collective-permute-start.3 = (bf16[256,2304]{1,0:T(8,128)(2,1)}, bf16[256,2304]{1,0:T(8,128)(2,1)S(1)}, u32[]{:S(2)}, u32[]{:S(2)}) collective-permute-start(bf16[256,2304]{1,0:T(8,128)(2,1)} %get-tuple-element.18), channel_id=1, source_target_pairs={{0,2},{2,4},{4,6},{6,0},{1,3},{3,5},{5,7},{7,1},{8,10},{10,12},{12... | collective-permute-start | bytes 3538952 | tf_op jit(solution)/shard_map/ppermute | solution.py:240
  45.7 27.0 %collective-permute-start.4 = (bf16[256,2304]{1,0:T(8,128)(2,1)S(1)}, bf16[256,2304]{1,0:T(8,128)(2,1)}, u32[]{:S(2)}, u32[]{:S(2)}) collective-permute-start(bf16[256,2304]{1,0:T(8,128)(2,1)S(1)} %copy-done.9), channel_id=1, source_target_pairs={{0,6},{2,0},{4,2},{6,4},{1,7},{3,1},{5,3},{7,5},{8,14},{10,8},{12,... | collective-permute-start | bytes 3538952 | tf_op jit(solution)/shard_map/ppermute | solution.py:240
  72.7 1.0 copy-start.2
  102.8 57.0 %all-to-all-start.1 = ((bf16[8,512,256]{2,1,0:T(8,128)(2,1)}), bf16[8,512,256]{2,1,0:T(8,128)(2,1)}, u32[]{:S(2)}, u32[]{:S(2)}) async-start(bf16[8,512,256]{2,1,0:T(8,128)(2,1)} %shard_map.70._), calls=%async_computation.2 | async-start | bytes 4194304 | tf_op jit(solution)/shard_map/all_to_all | solution.py:274
  116.4 16.6 %collective-permute-start.6 = (bf16[128,2304]{1,0:T(8,128)(2,1)}, bf16[128,2304]{1,0:T(8,128)(2,1)S(1)}, u32[]{:S(2)}, u32[]{:S(2)}) collective-permute-start(bf16[128,2304]{1,0:T(8,128)(2,1)} %get-tuple-element.23), channel_id=1, source_target_pairs={{0,2},{2,4},{4,6},{6,0},{1,3},{3,5},{5,7},{7,1},{8,10},{10,12},{12... | collective-permute-start | bytes 1769480 | tf_op jit(solution)/shard_map/ppermute | solution.py:240
  116.8 16.3 %collective-permute-start.7 = (bf16[128,2304]{1,0:T(8,128)(2,1)}, bf16[128,2304]{1,0:T(8,128)(2,1)S(1)}, u32[]{:S(2)}, u32[]{:S(2)}) collective-permute-start(bf16[128,2304]{1,0:T(8,128)(2,1)} %get-tuple-element.24), channel_id=1, source_target_pairs={{0,6},{2,0},{4,2},{6,4},{1,7},{3,1},{5,3},{7,5},{8,14},{10,8},{12,... | collective-permute-start | bytes 1769480 | tf_op jit(solution)/shard_map/ppermute | solution.py:240
  133.0 0.9 copy-start.4
  133.0 1.0 copy-start.5
  137.8 33.1 %collective-permute-start.8 = (bf16[256,2304]{1,0:T(8,128)(2,1)}, bf16[256,2304]{1,0:T(8,128)(2,1)S(1)}, u32[]{:S(2)}, u32[]{:S(2)}) collective-permute-start(bf16[256,2304]{1,0:T(8,128)(2,1)} %get-tuple-element.25), channel_id=1, source_target_pairs={{0,2},{2,4},{4,6},{6,0},{1,3},{3,5},{5,7},{7,1},{8,10},{10,12},{12... | collective-permute-start | bytes 3538952 | tf_op jit(solution)/shard_map/ppermute | solution.py:240
  137.9 32.9 %collective-permute-start.9 = (bf16[256,2304]{1,0:T(8,128)(2,1)}, bf16[256,2304]{1,0:T(8,128)(2,1)}, u32[]{:S(2)}, u32[]{:S(2)}) collective-permute-start(bf16[256,2304]{1,0:T(8,128)(2,1)} %get-tuple-element.26), channel_id=1, source_target_pairs={{0,6},{2,0},{4,2},{6,4},{1,7},{3,1},{5,3},{7,5},{8,14},{10,8},{12,... | collective-permute-start | bytes 3538952 | tf_op jit(solution)/shard_map/ppermute | solution.py:240
  142.9 25.3 %collective-permute-start.5 = (bf16[64,2304]{1,0:T(8,128)(2,1)S(1)}, bf16[64,2304]{1,0:T(8,128)(2,1)S(1)}, u32[]{:S(2)}, u32[]{:S(2)}) collective-permute-start(bf16[64,2304]{1,0:T(8,128)(2,1)S(1)} %slice.4), channel_id=1, source_target_pairs={{0,1},{1,0},{2,3},{3,2},{4,5},{5,4},{6,7},{7,6},{8,9},{9,8},{10,11... | collective-permute-start | bytes 884744 | tf_op jit(solution)/shard_map/ppermute | solution.py:240
  168.2 0.7 copy-start.8
  170.8 1.0 copy-start.3
  (1 other events, 0.7 us)
Sparse Core Ops, SparseCore 0:
  9.8 30.7 all-gather.5
  43.1 28.7 all-gather.3
  102.9 38.9 reduce-scatter.1

commit v6 on v4

--- a/solution.py
+++ b/solution.py
@@ -8,7 +8,7 @@
 BLOCK = 128
 BF = jnp.bfloat16
 F32 = jnp.float32
-VMEM_LIMIT = 56 * 1024 * 1024
+VMEM_LIMIT = 62 * 1024 * 1024
 
 
 def params():
@@ -31,21 +31,25 @@
     return [(i, (i + step) % size) for i in range(size)]
 
 
-def dequantize_kernel(scales, quantized, top, bottom):
+def dequantize_kernel(scales, quantized, top, bottom, *quarters):
     for r, half in enumerate((top, bottom)):
         for c in range(scales.shape[1]):
             lanes = pl.ds(c * BLOCK, BLOCK)
             block = quantized[pl.ds(r * BLOCK, BLOCK), lanes].astype(F32)
-            half[:, lanes] = (block * scales[r, c]).astype(BF)
+            block = (block * scales[r, c]).astype(BF)
+            half[:, lanes] = block
+            quarters[2 * r][:, lanes] = block[:64]
+            quarters[2 * r + 1][:, lanes] = block[64:]
 
 
 def dequantize(scales, quantized):
-    half = (BLOCK, quantized.shape[1])
+    width = quantized.shape[1]
+    shapes = [(BLOCK, width)] * 2 + [(64, width)] * 4
     return pl.pallas_call(
         dequantize_kernel,
-        out_shape=[jax.ShapeDtypeStruct(half, BF)] * 2,
+        out_shape=[jax.ShapeDtypeStruct(shape, BF) for shape in shapes],
         in_specs=[SCALAR, whole(quantized.shape)],
-        out_specs=[whole(half)] * 2,
+        out_specs=[whole(shape) for shape in shapes],
         compiler_params=params(),
         cost_estimate=cost(1, 1),
     )(scales, quantized)
@@ -124,10 +128,8 @@
     def _():
         for at in range(8):
             m = lax.rem(place[0] - at // 2 + 4, 4)
-            s = lax.rem(at % 2 + place[1], 2)
             rows = pl.ds(pl.multiple_of(m * 256, 256), 256)
-            lanes = pl.ds(pl.multiple_of(s * 512, 512), 512)
-            left[rows, lanes] = panel[at].T
+            left[rows, pl.ds(at % 2 * 512, 512)] = panel[at].T
 
     total = jnp.dot(left[...], grad[...], preferred_element_type=F32)
     at = 0
@@ -163,11 +165,11 @@
     for m in range(4):
         at = lax.rem(place[0] - m + 4, 4) * 2
         right = stacked(weights[2 * m : 2 * m + 2])
-        for s, grad in enumerate(grads):
+        for h, grad in enumerate(grads):
             total = lax.dot_general(
                 grad[...], right, (((1,), (1,)), ((), ())), preferred_element_type=F32
             )
-            out[at + lax.rem(s + place[1], 2), rows, :] = total.astype(BF)
+            out[at + h, rows, :] = total.astype(BF)
 
 
 def backward(place, grad, weights):
@@ -207,25 +209,29 @@
     )(*after, *args)
 
 
-def follow(array, after):
-    return pl.pallas_call(
-        lambda *_: None,
-        out_shape=jax.ShapeDtypeStruct(array.shape, array.dtype),
-        in_specs=[ANY] * (1 + len(after)),
-        out_specs=ANY,
-        input_output_aliases={0: 0},
-        cost_estimate=cost(1, 1),
-    )(array, *after)
-
-
-def relay_kernel(top, bottom, top_up, bottom_down, mine, theirs, up, down, both):
-    up[:BLOCK], up[BLOCK:] = top_up[...], bottom[...]
-    down[:BLOCK], down[BLOCK:] = top[...], bottom_down[...]
-    both[0], both[1] = mine[...], theirs[...]
+def twice_kernel(source, out):
+    out[0], out[1] = source[...], source[...]
+
+
+def pass_kernel(source, out):
+    out[...] = source[...]
+
+
+def relay_kernel(top, bottom, *refs):
+    (top_up, bottom_down), (up, down, first, last) = (refs[:2], refs[2:4]), refs[4:]
+    for i in range(2):
+        rows = pl.ds(i * 64, 64)
+        up[rows, :] = first[rows, :] = top_up[i][...]
+        down[pl.ds(BLOCK + i * 64, 64), :] = last[rows, :] = bottom_down[i][...]
+    up[BLOCK:], down[:BLOCK] = bottom[...], top[...]
 
 
 def sum_kernel(*refs):
     refs[-1][...] = summed(*[ref[...] for ref in refs[:-1]])
+
+
+def end_kernel(mine, theirs, out):
+    out[...] = summed(mine[:64], theirs[...])
 
 
 def gather_kernel(sums, out):
@@ -251,20 +257,18 @@
     place = jnp.stack([x, zh]).astype(jnp.int32)
     F = qweight.shape[1]
 
-    top, bottom = dequantize(scales, qweight)
-    top_up, bottom_down = shift(top, "x", 1), shift(bottom, "x", -1)
-    up, down, both = local(
-        relay_kernel,
-        [(256, F), (256, F), (2, 64, F)],
-        (),
-        *(top, bottom, top_up, bottom_down),
-        *(grad_out[0], shift(grad_out[0], "zh", 1)),
-    )
-    grad = lax.all_gather(both, ("y", "k"), axis=1, tiled=True).reshape(1024, F)
-
-    split = follow(split_units(inputs[0]), (up,))
+    (grad,) = local(twice_kernel, [(2, 64, F)], (), grad_out[0])
+    grad = lax.all_to_all(grad, "zh", 0, 0, tiled=True)
+    top, bottom, *quarters = dequantize(scales, qweight)
+    came = [shift(quarter, "x", 1) for quarter in quarters[:2]]
+    came += [shift(quarter, "x", -1) for quarter in quarters[2:]]
+    split = split_units(inputs[0])
+    (grad,) = local(pass_kernel, [(2, 64, F)], (split, *came), grad)
+    grad = lax.all_gather(grad, ("y", "k"), axis=1, tiled=True).reshape(1024, F)
     panel = lax.all_to_all(split, ("zl", "zh"), 0, 0, tiled=True)
 
+    shapes = [(256, F), (256, F), (BLOCK, F), (BLOCK, F)]
+    up, down, top_up, bottom_down = local(relay_kernel, shapes, (), top, bottom, *came)
     up, down = shift(up, "x", 1), shift(down, "x", -1)
     weights = (top, bottom, top_up, up, down, bottom_down)
 
@@ -273,7 +277,9 @@
     terms = weight_grad(place, product, panel, grad)
 
     product = lax.psum_scatter(product, ("y", "k"), scatter_dimension=0, tiled=True)
-    projected = summed(product[:64], shift(product[64:], "zh", 1))
+    (projected,) = local(
+        end_kernel, [(64, F)], (), product, shift(product[64:], "zh", 1)
+    )
 
     sums = lax.all_to_all(sums, ("zl", "zh"), 0, 0, tiled=True)
     (grad_inputs,) = local(gather_kernel, [(512, 512)], (), sums)
@@ -282,7 +288,7 @@
     top, bottom = shift(top, "x", 1), shift(bottom, "x", -1)
     up, down = local(onward_kernel, [(256, F)] * 2, (), up, down, top, bottom)
     up, down = shift(up, "x", 1), shift(down, "x", -1)
-    (grad_weight,) = local(sum_kernel, [(256, F)], (), here, up, down)
+    (grad_weight,) = local(sum_kernel, [(256, F)], (grad_inputs, projected), here, up, down)
 
     return projected[None], grad_inputs[None], grad_weight
 

time: 186 us -> 187 us (level)
  Pallas kernels: 46.6 us -> 52.7 us
  waiting for transfers between devices: 77.3 us -> 72.3 us
  starting transfers between devices: 35.8 us -> 40 us
  local copies, waits for them, and re-layouts: 9.28 us -> 5.27 us
    ppermute x10 -> x11, waiting for transfers between devices: 65.9 us -> 54.2 us  [shift(): return lax.ppermute(array, axis, ring(lax.axis_size(axis), step))]
    all_to_all x1, waiting for transfers between devices: 0.01 us -> 8.5 us  [per_device(): sums = lax.all_to_all(sums, ('zl', 'zh'), 0, 0, tiled=True)]
    all_to_all x0 -> x1, starting transfers between devices: none -> 7.56 us  [per_device(): grad = lax.all_to_all(grad, 'zh', 0, 0, tiled=True)]
    pallas_call x4 -> x7, Pallas kernels: 13.2 us -> 18.9 us  [local(): pl.pallas_call(lambda *refs: kernel(*refs[len(after):]), out_shape=[jax.S...]
    ppermute x10 -> x11, starting transfers between devices: 24.4 us -> 20.1 us  [shift(): return lax.ppermute(array, axis, ring(lax.axis_size(axis), step))]
    all_to_all x1, waiting for transfers between devices: 9.9 us -> 6.58 us  [per_device(): panel = lax.all_to_all(split, ('zl', 'zh'), 0, 0, tiled=True)]
    unnamed x22 -> x20, local copies, waits for them, and re-layouts: 7.58 us -> 4.29 us
  transfers between devices with their start and end apart: 14 -> 16, of which waited for: 6 -> 10; matrix products, arithmetic and copies ran while one was open for 1% -> 1% of each run, Pallas kernels for 17% -> 19%
where the time goes in v6:
time: 187 us; the launch traced here: 185 us
  waiting for transfers between devices  72.3 us (39%)
  Pallas kernels  52.7 us (28%)
  starting transfers between devices  40 us (21%)
  between operations  14.1 us (8%)
  local copies, waits for them, and re-layouts  5.27 us (3%)
    ppermute x11, waiting for transfers between devices, shift(): return lax.ppermute(array, axis, ring(lax.axis_size(axis), step))  54.2 us
    ppermute x11, starting transfers between devices, shift(): return lax.ppermute(array, axis, ring(lax.axis_size(axis), step))  20.1 us
    pallas_call x7, Pallas kernels, local(): pl.pallas_call(lambda *refs: kernel(*refs[len(after):]), out_shape=[jax.S...  18.9 us
    pallas_call x1, Pallas kernels, backward(): pl.pallas_call(backward_kernel, grid=(2,), out_shape=jax.ShapeDtypeStruct...  9.62 us
    pallas_call x1, Pallas kernels, forward(): pl.pallas_call(forward_kernel, grid=(width // tile,), out_shape=jax.Shape...  9.49 us
    pallas_call x1, Pallas kernels, weight_grad(): pl.pallas_call(weight_grad_kernel, grid=(width // tile,), out_shape=[jax....  9.35 us
    all_to_all x1, waiting for transfers between devices, per_device(): sums = lax.all_to_all(sums, ('zl', 'zh'), 0, 0, tiled=True)  8.5 us
    all_to_all x1, starting transfers between devices, per_device(): panel = lax.all_to_all(split, ('zl', 'zh'), 0, 0, tiled=True)  7.94 us
  transfers between devices with their start and end apart: 16, of which 10 were waited for; matrix products, arithmetic and copies ran while one was open for 1% of the time, Pallas kernels for 19%

profile of v6, /device:TPU:32, one launch (start us, length us, event | category | flops | bytes accessed | tf_op | source)
XLA Modules:
  0.0 184.8 jit_solution(6435772784370019146)
XLA Ops:
  9.0 7.6 %all-to-all-start = ((bf16[2,64,2304]{2,1,0:T(8,128)(2,1)}), bf16[2,64,2304]{2,1,0:T(8,128)(2,1)S(1)}, u32[]{:S(2)}, u32[]{:S(2)}) async-start(bf16[2,64,2304]{2,1,0:T(8,128)(2,1)} %shard_map.69), calls=%async_computation | async-start | bytes 1179648 | tf_op jit(solution)/shard_map/all_to_all | solution.py:261
  16.5 2.8 %shard_map.68 = (bf16[128,2304]{1,0:T(8,128)(2,1)}, bf16[128,2304]{1,0:T(8,128)(2,1)}, bf16[64,2304]{1,0:T(8,128)(2,1)}, bf16[64,2304]{1,0:T(8,128)(2,1)}, bf16[...) custom-call(f32[2,18]{1,0:T(2,128)} %scales.1, bf16[256,2304]{1,0:T(8,128)(2,1)} %quantized.1), custom_call_target="tpu_custom_call" | custom-call | flops 1 | bytes 1 | tf_op jit(solution)/shard_map/pallas_call | solution.py:48
  24.6 2.5 %shard_map.67.refs_0_ = bf16[8,512,256]{2,1,0:T(8,128)(2,1)} custom-call(bf16[512,512]{1,0:T(8,128)(2,1)} %bitcast.12), custom_call_target="tpu_custom_call" | custom-call | flops 1 | bytes 1 | tf_op jit(solution)/shard_map/pallas_call | solution.py:65
  27.2 3.5 %collective-permute-done.refs_1_.refs_2_ = bf16[64,2304]{1,0:T(8,128)(2,1)S(1)} collective-permute-done((bf16[64,2304]{1,0:T(8,128)(2,1)}, bf16[64,2304]{1,0:T(8,128)(2,1)S(1)}, u32[]{:S(2)}, u32[]{:S(2)}) %collective-permute-start) | collective-permute-done | bytes 294944 | tf_op jit(solution)/shard_map/ppermute | solution.py:252
  30.7 4.9 %collective-permute-done.1.refs_2_.refs_3_ = bf16[64,2304]{1,0:T(8,128)(2,1)S(1)} collective-permute-done((bf16[64,2304]{1,0:T(8,128)(2,1)}, bf16[64,2304]{1,0:T(8,128)(2,1)S(1)}, u32[]{:S(2)}, u32[]{:S(2)}) %collective-permute-start.1) | collective-permute-done | bytes 294944 | tf_op jit(solution)/shard_map/ppermute | solution.py:252
  40.3 7.9 %all-to-all-start.1 = ((bf16[8,512,256]{2,1,0:T(8,128)(2,1)}), bf16[8,512,256]{2,1,0:T(8,128)(2,1)}, u32[]{:S(2)}, u32[]{:S(2)}) async-start(bf16[8,512,256]{2,1,0:T(8,128)(2,1)} %shard_map.67.refs_0_), calls=%async_computation.1 | async-start | bytes 4194304 | tf_op jit(solution)/shard_map/all_to_all | solution.py:268
  48.2 3.5 %shard_map.71 = (bf16[256,2304]{1,0:T(8,128)(2,1)}, bf16[256,2304]{1,0:T(8,128)(2,1)}, bf16[128,2304]{1,0:T(8,128)(2,1)}, bf16[128,2304]{1,0:T(8,128)(2,1)}) custom-call(bf16[128,2304]{1,0:T(8,128)(2,1)} %get-tuple-element.24.refs_0_.refs_2_, bf16[128,2304]{1,0:T(8,128)(2,1)} %get-tuple-element.25.refs_1_.refs_3_, bf16[64,2304]{1,0:T(8,128)(2,1)} %copy-done.2, ...), custom_call_target="tpu_custom_call" | custom-call | flops 1 | bytes 1 | tf_op jit(solution)/shard_map/pallas_call | solution.py:202
  52.9 2.0 %collective-permute-start.5 = (bf16[256,2304]{1,0:T(8,128)(2,1)}, bf16[256,2304]{1,0:T(8,128)(2,1)}, u32[]{:S(2)}, u32[]{:S(2)}) collective-permute-start(bf16[256,2304]{1,0:T(8,128)(2,1)} %get-tuple-element.28), channel_id=1, source_target_pairs={{0,6},{2,0},{4,2},{6,4},{1,7},{3,1},{5,3},{7,5},{8,14},{10,8},{12,... | collective-permute-start | bytes 3538952 | tf_op jit(solution)/shard_map/ppermute | solution.py:252
  55.5 22.7 %collective-permute-done.4.refs_5_.refs_3_ = bf16[256,2304]{1,0:T(8,128)(2,1)S(1)} collective-permute-done((bf16[256,2304]{1,0:T(8,128)(2,1)}, bf16[256,2304]{1,0:T(8,128)(2,1)S(1)}, u32[]{:S(2)}, u32[]{:S(2)}) %collective-permute-start.4) | collective-permute-done | bytes 1179680 | tf_op jit(solution)/shard_map/ppermute | solution.py:252
  79.2 9.6 %shard_map.72._ = bf16[8,512,256]{2,1,0:T(8,128)(2,1)} custom-call(s32[2]{0:T(128)} %pad_add_fusion.place, bf16[1024,2304]{1,0:T(8,128)(2,1)} %bitcast.7, bf16[1024,2304]{1,0:T(8,128)(2,1)} %bitcast.8, bf16[128,2304]{1,0:T(8,128)(2,1)} %get-tuple-element.24.refs_0_.refs_2_, bf16[128,2304]{1,0:T(8,128)(2,1)} %get-tuple-element.25.refs_1_.refs_3_, ...), custom_call_target="tpu_custom_call" | custom-call | flops 1 | bytes 1 | tf_op jit(solution)/shard_map/pallas_call | solution.py:177
  88.8 6.6 %all-to-all-done.1.panel = bf16[8,512,256]{2,1,0:T(8,128)(2,1)} async-done(((bf16[8,512,256]{2,1,0:T(8,128)(2,1)}), bf16[8,512,256]{2,1,0:T(8,128)(2,1)}, u32[]{:S(2)}, u32[]{:S(2)}) %all-to-all-start.1) | async-done | bytes 2097184 | tf_op jit(solution)/shard_map/all_to_all | solution.py:268
  95.4 9.5 %shard_map.73._ = bf16[1024,2304]{1,0:T(8,128)(2,1)} custom-call(s32[2]{0:T(128)} %pad_add_fusion.place, bf16[8,512,256]{2,1,0:T(8,128)(2,1)} %shard_map.72._, bf16[8,512,256]{2,1,0:T(8,128)(2,1)} %all-to-all-done.1.panel, bf16[128,2304]{1,0:T(8,128)(2,1)} %get-tuple-element.24.refs_0_.refs_2_, bf16[128,2304]{1,0:T(8,128)(2,1)} %get-tuple-element.25.refs_1_.refs_3_, ...), custom_call_target="tpu_custom_call" | custom-call | flops 1 | bytes 1 | tf_op jit(solution)/shard_map/pallas_call | solution.py:111
  104.9 4.3 %all-to-all-start.2 = ((bf16[8,512,256]{2,1,0:T(8,128)(2,1)}), bf16[8,512,256]{2,1,0:T(8,128)(2,1)}, u32[]{:S(2)}, u32[]{:S(2)}) async-start(bf16[8,512,256]{2,1,0:T(8,128)(2,1)} %shard_map.72._), calls=%async_computation.3 | async-start | bytes 4194304 | tf_op jit(solution)/shard_map/all_to_all | solution.py:284
  109.3 9.3 %shard_map.76 = (bf16[256,2304]{1,0:T(8,128)(2,1)}, bf16[256,2304]{1,0:T(8,128)(2,1)}, bf16[128,2304]{1,0:T(8,128)(2,1)}, bf16[128,2304]{1,0:T(8,128)(2,1)}, bf16[256,2304]{1,0:T(8,128)(2,1)}) custom-call(s32[2]{0:T(128)} %pad_add_fusion.place, bf16[1024,2304]{1,0:T(8,128)(2,1)} %shard_map.73._, bf16[8,512,256]{2,1,0:T(8,128)(2,1)} %all-to-all-done.1.panel, ...), custom_call_target="tpu_custom_call" | custom-call | flops 1 | bytes 1 | tf_op jit(solution)/shard_map/pallas_call | solution.py:145
  119.8 2.0 %collective-permute-start.8 = (bf16[128,2304]{1,0:T(8,128)(2,1)}, bf16[128,2304]{1,0:T(8,128)(2,1)S(1)}, u32[]{:S(2)}, u32[]{:S(2)}) collective-permute-start(bf16[128,2304]{1,0:T(8,128)(2,1)} %get-tuple-element.34), channel_id=1, source_target_pairs={{0,6},{2,0},{4,2},{6,4},{1,7},{3,1},{5,3},{7,5},{8,14},{10,8},{12,... | collective-permute-start | bytes 1769480 | tf_op jit(solution)/shard_map/ppermute | solution.py:252
  121.8 13.4 %collective-permute-done.7.refs_2_ = bf16[128,2304]{1,0:T(8,128)(2,1)S(1)} collective-permute-done((bf16[128,2304]{1,0:T(8,128)(2,1)}, bf16[128,2304]{1,0:T(8,128)(2,1)S(1)}, u32[]{:S(2)}, u32[]{:S(2)}) %collective-permute-start.7) | collective-permute-done | bytes 589856 | tf_op jit(solution)/shard_map/ppermute | solution.py:252
  136.3 3.7 %shard_map.77 = (bf16[256,2304]{1,0:T(8,128)(2,1)}, bf16[256,2304]{1,0:T(8,128)(2,1)}) custom-call(bf16[256,2304]{1,0:T(8,128)(2,1)} %get-tuple-element.31.refs_0_, bf16[256,2304]{1,0:T(8,128)(2,1)} %get-tuple-element.32.refs_1_, bf16[128,2304]{1,0:T(8,128)(2,1)} %copy-done.7, bf16[128,2304]{1,0:T(8,128)(2,1)} %copy-done.8), custom_call_target="tpu_custom_call" | custom-call | flops 1 | bytes 1 | tf_op jit(solution)/shard_map/pallas_call | solution.py:202
  140.8 2.4 %collective-permute-start.10 = (bf16[256,2304]{1,0:T(8,128)(2,1)}, bf16[256,2304]{1,0:T(8,128)(2,1)}, u32[]{:S(2)}, u32[]{:S(2)}) collective-permute-start(bf16[256,2304]{1,0:T(8,128)(2,1)} %get-tuple-element.36), channel_id=1, source_target_pairs={{0,6},{2,0},{4,2},{6,4},{1,7},{3,1},{5,3},{7,5},{8,14},{10,8},{12,... | collective-permute-start | bytes 3538952 | tf_op jit(solution)/shard_map/ppermute | solution.py:252
  143.2 2.0 %reduce-scatter.2.cloned.1.call-done.refs_0_ = bf16[128,2304]{1,0:T(8,128)(2,1)} async-done(((bf16[1024,2304]{1,0:T(8,128)(2,1)}), bf16[128,2304]{1,0:T(8,128)(2,1)}) %reduce-scatter.2.cloned.1.call-update) | async-done | bytes 589840 | tf_op jit(solution)/shard_map/reduce_scatter | solution.py:279
  146.2 5.2 %collective-permute-start.6 = (bf16[64,2304]{1,0:T(8,128)(2,1)S(1)}, bf16[64,2304]{1,0:T(8,128)(2,1)S(1)}, u32[]{:S(2)}, u32[]{:S(2)}) collective-permute-start(bf16[64,2304]{1,0:T(8,128)(2,1)S(1)} %slice.4), channel_id=1, source_target_pairs={{0,1},{1,0},{2,3},{3,2},{4,5},{5,4},{6,7},{7,6},{8,9},{9,8},{10,11... | collective-permute-start | bytes 884744 | tf_op jit(solution)/shard_map/ppermute | solution.py:252
  151.3 8.5 %all-to-all-done.2.refs_0_ = bf16[8,512,256]{2,1,0:T(8,128)(2,1)} async-done(((bf16[8,512,256]{2,1,0:T(8,128)(2,1)}), bf16[8,512,256]{2,1,0:T(8,128)(2,1)}, u32[]{:S(2)}, u32[]{:S(2)}) %all-to-all-start.2) | async-done | bytes 2097184 | tf_op jit(solution)/shard_map/all_to_all | solution.py:284
  159.8 2.6 %shard_map.75.refs_0_ = bf16[512,512]{1,0:T(8,128)(2,1)} custom-call(bf16[8,512,256]{2,1,0:T(8,128)(2,1)} %all-to-all-done.2.refs_0_), custom_call_target="tpu_custom_call" | custom-call | flops 1 | bytes 1 | tf_op jit(solution)/shard_map/pallas_call | solution.py:202
  162.5 8.4 %collective-permute-done.6.refs_1_ = bf16[64,2304]{1,0:T(8,128)(2,1)S(1)} collective-permute-done((bf16[64,2304]{1,0:T(8,128)(2,1)S(1)}, bf16[64,2304]{1,0:T(8,128)(2,1)S(1)}, u32[]{:S(2)}, u32[]{:S(2)}) %collective-permute-start.6) | collective-permute-done | bytes 294944 | tf_op jit(solution)/shard_map/ppermute | solution.py:252
  174.6 3.4 %shard_map.78 = bf16[256,2304]{1,0:T(8,128)(2,1)} custom-call(bf16[512,512]{1,0:T(8,128)(2,1)} %shard_map.75.refs_0_, bf16[64,2304]{1,0:T(8,128)(2,1)} %shard_map.74.refs_1_, bf16[256,2304]{1,0:T(8,128)(2,1)} %get-tuple-element.30.refs_2_, bf16[256,2304]{1,0:T(8,128)(2,1)} %copy-done.6, bf16[256,2304]{1,0:T(8,128)(2,1)} %collective-permute-done.10.refs_4_), custom_call_target="tpu_custom_call" | custom-call | flops 1 | bytes 1 | tf_op jit(solution)/shard_map/pallas_call | solution.py:202
  (44 shorter events, 22.4 us)
Async XLA Ops:
  9.0 27.8 %all-to-all-start = ((bf16[2,64,2304]{2,1,0:T(8,128)(2,1)}), bf16[2,64,2304]{2,1,0:T(8,128)(2,1)S(1)}, u32[]{:S(2)}, u32[]{:S(2)}) async-start(bf16[2,64,2304]{2,1,0:T(8,128)(2,1)} %shard_map.69), calls=%async_computation | async-start | bytes 1179648 | tf_op jit(solution)/shard_map/all_to_all | solution.py:261
  16.5 62.7 %all-gather.2.cloned.1.call-start = ((), (), s32[]{:S(2)}) async-start(), calls=%async_computation.4 | async-start | bytes 5308416 | tf_op jit(solution)/shard_map/all_gather | solution.py:267
  19.3 11.4 %collective-permute-start = (bf16[64,2304]{1,0:T(8,128)(2,1)}, bf16[64,2304]{1,0:T(8,128)(2,1)S(1)}, u32[]{:S(2)}, u32[]{:S(2)}) collective-permute-start(bf16[64,2304]{1,0:T(8,128)(2,1)} %get-tuple-element.20), channel_id=1, source_target_pairs={{0,2},{2,4},{4,6},{6,0},{1,3},{3,5},{5,7},{7,1},{8,10},{10,12},{12... | collective-permute-start | bytes 884744 | tf_op jit(solution)/shard_map/ppermute | solution.py:252
  20.8 14.7 %collective-permute-start.1 = (bf16[64,2304]{1,0:T(8,128)(2,1)}, bf16[64,2304]{1,0:T(8,128)(2,1)S(1)}, u32[]{:S(2)}, u32[]{:S(2)}) collective-permute-start(bf16[64,2304]{1,0:T(8,128)(2,1)} %get-tuple-element.21), channel_id=1, source_target_pairs={{0,2},{2,4},{4,6},{6,0},{1,3},{3,5},{5,7},{7,1},{8,10},{10,12},{12... | collective-permute-start | bytes 884744 | tf_op jit(solution)/shard_map/ppermute | solution.py:252
  22.3 13.2 %collective-permute-start.2 = (bf16[64,2304]{1,0:T(8,128)(2,1)}, bf16[64,2304]{1,0:T(8,128)(2,1)S(1)}, u32[]{:S(2)}, u32[]{:S(2)}) collective-permute-start(bf16[64,2304]{1,0:T(8,128)(2,1)} %get-tuple-element.22), channel_id=1, source_target_pairs={{0,6},{2,0},{4,2},{6,4},{1,7},{3,1},{5,3},{7,5},{8,14},{10,8},{12,... | collective-permute-start | bytes 884744 | tf_op jit(solution)/shard_map/ppermute | solution.py:252
  24.1 12.7 %collective-permute-start.3 = (bf16[64,2304]{1,0:T(8,128)(2,1)}, bf16[64,2304]{1,0:T(8,128)(2,1)S(1)}, u32[]{:S(2)}, u32[]{:S(2)}) collective-permute-start(bf16[64,2304]{1,0:T(8,128)(2,1)} %get-tuple-element.23), channel_id=1, source_target_pairs={{0,6},{2,0},{4,2},{6,4},{1,7},{3,1},{5,3},{7,5},{8,14},{10,8},{12,... | collective-permute-start | bytes 884744 | tf_op jit(solution)/shard_map/ppermute | solution.py:252
  30.7 6.1 %copy-start.2 = (bf16[64,2304]{1,0:T(8,128)(2,1)}, bf16[64,2304]{1,0:T(8,128)(2,1)S(1)}, u32[]{:S(2)}) copy-start(bf16[64,2304]{1,0:T(8,128)(2,1)S(1)} %collective-permute-done.refs_1_.refs_2_) | copy-start | bytes 884740
  35.6 1.2 copy-start.3
  35.6 1.2 copy-start.4
  37.5 0.8 copy-start.1
  40.3 55.1 %all-to-all-start.1 = ((bf16[8,512,256]{2,1,0:T(8,128)(2,1)}), bf16[8,512,256]{2,1,0:T(8,128)(2,1)}, u32[]{:S(2)}, u32[]{:S(2)}) async-start(bf16[8,512,256]{2,1,0:T(8,128)(2,1)} %shard_map.67.refs_0_), calls=%async_computation.1 | async-start | bytes 4194304 | tf_op jit(solution)/shard_map/all_to_all | solution.py:268
  48.2 97.0 %reduce-scatter.2.cloned.1.call-start = ((), (), s32[]{:S(2)}) async-start(), calls=%async_computation.5 | async-start | bytes 5308416 | tf_op jit(solution)/shard_map/reduce_scatter | solution.py:279
  51.7 26.5 %collective-permute-start.4 = (bf16[256,2304]{1,0:T(8,128)(2,1)}, bf16[256,2304]{1,0:T(8,128)(2,1)S(1)}, u32[]{:S(2)}, u32[]{:S(2)}) collective-permute-start(bf16[256,2304]{1,0:T(8,128)(2,1)} %get-tuple-element.27), channel_id=1, source_target_pairs={{0,2},{2,4},{4,6},{6,0},{1,3},{3,5},{5,7},{7,1},{8,10},{10,12},{12... | collective-permute-start | bytes 3538952 | tf_op jit(solution)/shard_map/ppermute | solution.py:252
  52.9 25.3 %collective-permute-start.5 = (bf16[256,2304]{1,0:T(8,128)(2,1)}, bf16[256,2304]{1,0:T(8,128)(2,1)}, u32[]{:S(2)}, u32[]{:S(2)}) collective-permute-start(bf16[256,2304]{1,0:T(8,128)(2,1)} %get-tuple-element.28), channel_id=1, source_target_pairs={{0,6},{2,0},{4,2},{6,4},{1,7},{3,1},{5,3},{7,5},{8,14},{10,8},{12,... | collective-permute-start | bytes 3538952 | tf_op jit(solution)/shard_map/ppermute | solution.py:252
  78.2 1.0 copy-start
  104.9 54.9 %all-to-all-start.2 = ((bf16[8,512,256]{2,1,0:T(8,128)(2,1)}), bf16[8,512,256]{2,1,0:T(8,128)(2,1)}, u32[]{:S(2)}, u32[]{:S(2)}) async-start(bf16[8,512,256]{2,1,0:T(8,128)(2,1)} %shard_map.72._), calls=%async_computation.3 | async-start | bytes 4194304 | tf_op jit(solution)/shard_map/all_to_all | solution.py:284
  118.6 16.6 %collective-permute-start.7 = (bf16[128,2304]{1,0:T(8,128)(2,1)}, bf16[128,2304]{1,0:T(8,128)(2,1)S(1)}, u32[]{:S(2)}, u32[]{:S(2)}) collective-permute-start(bf16[128,2304]{1,0:T(8,128)(2,1)} %get-tuple-element.33), channel_id=1, source_target_pairs={{0,2},{2,4},{4,6},{6,0},{1,3},{3,5},{5,7},{7,1},{8,10},{10,12},{12... | collective-permute-start | bytes 1769480 | tf_op jit(solution)/shard_map/ppermute | solution.py:252
  119.8 15.4 %collective-permute-start.8 = (bf16[128,2304]{1,0:T(8,128)(2,1)}, bf16[128,2304]{1,0:T(8,128)(2,1)S(1)}, u32[]{:S(2)}, u32[]{:S(2)}) collective-permute-start(bf16[128,2304]{1,0:T(8,128)(2,1)} %get-tuple-element.34), channel_id=1, source_target_pairs={{0,6},{2,0},{4,2},{6,4},{1,7},{3,1},{5,3},{7,5},{8,14},{10,8},{12,... | collective-permute-start | bytes 1769480 | tf_op jit(solution)/shard_map/ppermute | solution.py:252
  135.2 0.9 copy-start.7
  135.2 1.0 copy-start.8
  140.0 33.6 %collective-permute-start.9 = (bf16[256,2304]{1,0:T(8,128)(2,1)}, bf16[256,2304]{1,0:T(8,128)(2,1)S(1)}, u32[]{:S(2)}, u32[]{:S(2)}) collective-permute-start(bf16[256,2304]{1,0:T(8,128)(2,1)} %get-tuple-element.35), channel_id=1, source_target_pairs={{0,2},{2,4},{4,6},{6,0},{1,3},{3,5},{5,7},{7,1},{8,10},{10,12},{12... | collective-permute-start | bytes 3538952 | tf_op jit(solution)/shard_map/ppermute | solution.py:252
  140.8 32.7 %collective-permute-start.10 = (bf16[256,2304]{1,0:T(8,128)(2,1)}, bf16[256,2304]{1,0:T(8,128)(2,1)}, u32[]{:S(2)}, u32[]{:S(2)}) collective-permute-start(bf16[256,2304]{1,0:T(8,128)(2,1)} %get-tuple-element.36), channel_id=1, source_target_pairs={{0,6},{2,0},{4,2},{6,4},{1,7},{3,1},{5,3},{7,5},{8,14},{10,8},{12,... | collective-permute-start | bytes 3538952 | tf_op jit(solution)/shard_map/ppermute | solution.py:252
  146.2 24.7 %collective-permute-start.6 = (bf16[64,2304]{1,0:T(8,128)(2,1)S(1)}, bf16[64,2304]{1,0:T(8,128)(2,1)S(1)}, u32[]{:S(2)}, u32[]{:S(2)}) collective-permute-start(bf16[64,2304]{1,0:T(8,128)(2,1)S(1)} %slice.4), channel_id=1, source_target_pairs={{0,1},{1,0},{2,3},{3,2},{4,5},{5,4},{6,7},{7,6},{8,9},{9,8},{10,11... | collective-permute-start | bytes 884744 | tf_op jit(solution)/shard_map/ppermute | solution.py:252
  173.6 1.0 copy-start.6
  (2 other events, 1.4 us)
Sparse Core Ops, SparseCore 0:
  40.4 38.7 all-gather.1
  105.0 40.0 reduce-scatter.1

commit v7 on v5

--- a/solution.py
+++ b/solution.py
@@ -1,3 +1,5 @@
+import functools
+
 import jax
 import jax.numpy as jnp
 from jax import lax
@@ -51,18 +53,20 @@
     )(scales, quantized)
 
 
-def split_kernel(inputs, split):
-    for at in range(8):
-        split[at] = inputs[:, at % 2 * 256 : at % 2 * 256 + 256]
+def split_kernel(inputs, *halves):
+    for i, half in enumerate(halves):
+        for at in range(8):
+            lanes = slice(at % 2 * 256, at % 2 * 256 + 256)
+            half[at] = inputs[i * 256 : i * 256 + 256, lanes]
 
 
 def split_units(inputs):
-    shape = (8, 512, 256)
+    shape = (8, 256, 256)
     return pl.pallas_call(
         split_kernel,
-        out_shape=jax.ShapeDtypeStruct(shape, BF),
+        out_shape=[jax.ShapeDtypeStruct(shape, BF)] * 2,
         in_specs=[whole(inputs.shape)],
-        out_specs=whole(shape),
+        out_specs=[whole(shape)] * 2,
         compiler_params=params(),
         cost_estimate=cost(1, 1),
     )(inputs)
@@ -83,8 +87,8 @@
     )
 
 
-def forward_kernel(place, _, panel, *refs):
-    weights, (out, left) = halves(*refs[:6]), refs[6:]
+def forward_kernel(place, *refs):
+    panels, weights, (out, left) = refs[:2], halves(*refs[2:8]), refs[8:]
     x, zh = place[0], place[1]
 
     @pl.when(pl.program_id(0) == 0)
@@ -95,39 +99,42 @@
             lanes = pl.ds(pl.multiple_of(m * 256, 256), 256)
             for b in range(8):
                 rows = pl.ds(pl.multiple_of(b * 128 + s * 64, 64), 64)
-                left[rows, lanes] = panel[at, b * 64 : b * 64 + 64, :]
+                tokens = slice(b % 4 * 64, b % 4 * 64 + 64)
+                left[rows, lanes] = panels[b // 4][at, tokens, :]
 
     total = jnp.dot(left[...], stacked(weights), preferred_element_type=F32)
     out[...] = total.astype(BF)
 
 
-def forward(place, after, panel, weights):
+def forward(place, panels, weights):
     width = weights[0].shape[1]
     tile = width // 3
     return pl.pallas_call(
         forward_kernel,
         grid=(width // tile,),
         out_shape=jax.ShapeDtypeStruct((1024, width), BF),
-        in_specs=[SCALAR, ANY, whole(panel.shape)]
+        in_specs=[SCALAR]
+        + [whole(panel.shape) for panel in panels]
         + [pl.BlockSpec((w.shape[0], tile), lambda n: (0, n)) for w in weights],
         out_specs=pl.BlockSpec((1024, tile), lambda n: (0, n)),
         scratch_shapes=[pltpu.VMEM((1024, 1024), BF)],
         compiler_params=params(),
         cost_estimate=PRODUCT,
-    )(place, after, panel, *weights)
-
-
-def weight_grad_kernel(place, _, panel, near, far, *refs):
-    outs, left = refs[:5], refs[5]
+    )(place, *panels, *weights)
+
+
+def weight_grad_kernel(offsets, place, _, pa, pb, near, far, *refs):
+    outs, left = refs[:-1], refs[-1]
 
     @pl.when(pl.program_id(0) == 0)
     def _():
-        for at in range(8):
-            m = lax.rem(place[0] - at // 2 + 4, 4)
-            s = lax.rem(at % 2 + place[1], 2)
-            rows = pl.ds(pl.multiple_of(m * 256, 256), 256)
-            lanes = pl.ds(pl.multiple_of(s * 512, 512), 512)
-            left[rows, lanes] = panel[at].T
+        for i, offset in enumerate(offsets):
+            zl = lax.rem(place[0] - offset + 4, 4)
+            for h in range(2):
+                s = lax.rem(h + place[1], 2)
+                for j, panel in enumerate((pa, pb)):
+                    lanes = pl.ds(pl.multiple_of(s * 512 + j * 256, 256), 256)
+                    left[i * 256 : i * 256 + 256, lanes] = panel[zl * 2 + h].T
 
     total = jnp.dot(left[...], stacked((near, far)), preferred_element_type=F32)
     at = 0
@@ -136,29 +143,25 @@
         at += out.shape[0]
 
 
-def weight_grad(place, after, panel, near, far):
+def weight_grad(offsets, sizes, place, after, panels, near, far):
     width = near.shape[1]
     tile = width // 3
-    sizes = (256, 256, 128, 128, 256)
-    return pl.pallas_call(
-        weight_grad_kernel,
+    rows = 256 * len(offsets)
+    return pl.pallas_call(
+        functools.partial(weight_grad_kernel, offsets),
         grid=(width // tile,),
-        out_shape=[jax.ShapeDtypeStruct((rows, width), BF) for rows in sizes],
-        in_specs=[
-            SCALAR,
-            ANY,
-            whole(panel.shape),
-            pl.BlockSpec((512, tile), lambda n: (0, n)),
-            pl.BlockSpec((512, tile), lambda n: (0, n)),
-        ],
-        out_specs=[pl.BlockSpec((rows, tile), lambda n: (0, n)) for rows in sizes],
-        scratch_shapes=[pltpu.VMEM((1024, 1024), BF)],
+        out_shape=[jax.ShapeDtypeStruct((size, width), BF) for size in sizes],
+        in_specs=[SCALAR, ANY]
+        + [whole(panel.shape) for panel in panels]
+        + [pl.BlockSpec((512, tile), lambda n: (0, n))] * 2,
+        out_specs=[pl.BlockSpec((size, tile), lambda n: (0, n)) for size in sizes],
+        scratch_shapes=[pltpu.VMEM((rows, 1024), BF)],
         compiler_params=params(),
         cost_estimate=PRODUCT,
-    )(place, after, panel, near, far)
-
-
-def backward_kernel(place, *refs):
+    )(place, after, *panels, near, far)
+
+
+def backward_kernel(place, _, *refs):
     grads, weights, out = refs[:2], halves(*refs[2:8]), refs[8]
     rows = pl.ds(pl.multiple_of(pl.program_id(0) * 256, 256), 256)
     for m in range(4):
@@ -171,7 +174,7 @@
             out[at + lax.rem(s + place[1], 2), rows, :] = total.astype(BF)
 
 
-def backward(place, near, far, weights):
+def backward(place, after, near, far, weights):
     width = near.shape[1]
     return pl.pallas_call(
         backward_kernel,
@@ -179,6 +182,7 @@
         out_shape=jax.ShapeDtypeStruct((8, 512, 256), BF),
         in_specs=[
             SCALAR,
+            ANY,
             pl.BlockSpec((256, width), lambda n: (n, 0)),
             pl.BlockSpec((256, width), lambda n: (n, 0)),
         ]
@@ -186,7 +190,7 @@
         out_specs=whole((8, 512, 256)),
         compiler_params=params(),
         cost_estimate=PRODUCT,
-    )(place, near, far, *weights)
+    )(place, after, near, far, *weights)
 
 
 def summed(*refs):
@@ -198,20 +202,37 @@
 
 def local(kernel, outs, after, *args):
     after = after if isinstance(after, tuple) else (after,)
+    steps = 3 if len(outs[0]) == 2 and outs[0][1] % 384 == 0 else 1
+
+    def block(shape):
+        tile = (*shape[:-1], shape[-1] // steps)
+        return pl.BlockSpec(tile, lambda n: (0,) * (len(shape) - 1) + (n,))
+
     return pl.pallas_call(
         lambda *refs: kernel(*refs[len(after) :]),
+        grid=(steps,),
         out_shape=[jax.ShapeDtypeStruct(shape, BF) for shape in outs],
-        in_specs=[ANY] * len(after) + [whole(a.shape) for a in args],
-        out_specs=[whole(shape) for shape in outs],
+        in_specs=[ANY] * len(after) + [block(a.shape) for a in args],
+        out_specs=[block(shape) for shape in outs],
         compiler_params=params(),
         cost_estimate=cost(1, 1),
     )(*after, *args)
 
 
-def relay_kernel(top, bottom, top_up, bottom_down, far, up, down, passed):
+def follow(array, after):
+    return pl.pallas_call(
+        lambda *_: None,
+        out_shape=jax.ShapeDtypeStruct(array.shape, array.dtype),
+        in_specs=[ANY] * (1 + len(after)),
+        out_specs=ANY,
+        input_output_aliases={0: 0},
+        cost_estimate=cost(1, 1),
+    )(array, *after)
+
+
+def relay_kernel(top, bottom, top_up, bottom_down, up, down):
     up[:BLOCK], up[BLOCK:] = top_up[...], bottom[...]
     down[:BLOCK], down[BLOCK:] = top[...], bottom_down[...]
-    passed[...] = far[...]
 
 
 def sum_kernel(*refs):
@@ -246,25 +267,26 @@
     F = qweight.shape[1]
 
     near = lax.all_gather(grad_out[0], ("y", "k"), axis=0, tiled=True)
-    split = split_units(inputs[0])
-    panel = lax.all_to_all(split, ("zl", "zh"), 0, 0, tiled=True)
+    first, second = split_units(inputs[0])
+    first = lax.all_to_all(first, ("zl", "zh"), 0, 0, tiled=True)
 
     top, bottom = dequantize(scales, qweight)
     top_up, bottom_down = shift(top, "x", 1), shift(bottom, "x", -1)
-    far = shift(grad_out[0], "zh", 1)
-    up, down, far = local(
-        relay_kernel,
-        [(256, F), (256, F), (64, F)],
-        split,
-        *(top, bottom, top_up, bottom_down, far),
+    up, down = local(
+        relay_kernel, [(256, F)] * 2, (), top, bottom, top_up, bottom_down
     )
+    far = follow(shift(grad_out[0], "zh", 1), (first, up))
     far = lax.all_gather(far, ("y", "k"), axis=0, tiled=True)
+    second = follow(second, (first, up))
+    second = lax.all_to_all(second, ("zl", "zh"), 0, 0, tiled=True)
+    panels = first, second
     up, down = shift(up, "x", 1), shift(down, "x", -1)
     weights = (top, bottom, top_up, up, down, bottom_down)
 
-    sums = backward(place, near, far, weights)
-    product = forward(place, sums, panel, weights)
-    terms = weight_grad(place, product, panel, near, far)
+    product = forward(place, panels, weights)
+    sums = backward(place, product, near, far, weights)
+    top, bottom = weight_grad((2,), (128, 128), place, sums, panels, near, far)
+    here, down, up = weight_grad((0, 1, 3), (256,) * 3, place, top, panels, near, far)
 
     product = lax.psum_scatter(product, ("y", "k"), scatter_dimension=0, tiled=True)
     (projected,) = local(
@@ -274,7 +296,6 @@
     sums = lax.all_to_all(sums, ("zl", "zh"), 0, 0, tiled=True)
     (grad_inputs,) = local(gather_kernel, [(512, 512)], (), sums)
 
-    here, down, top, bottom, up = terms
     top, bottom = shift(top, "x", 1), shift(bottom, "x", -1)
     up, down = local(onward_kernel, [(256, F)] * 2, (), up, down, top, bottom)
     up, down = shift(up, "x", 1), shift(down, "x", -1)

time: 184 us -> 196 us (1.065)
  Pallas kernels: 48.3 us -> 55.2 us
  starting transfers between devices: 36.3 us -> 40.3 us
    all_to_all x1 -> x2, waiting for transfers between devices: 10 us -> 0.01 us  [the longest x1 0.01 us: per_device(): first = lax.all_to_all(first, ('zl', 'zh'), 0, 0, tiled=True)]
    pallas_call x7 -> x10, Pallas kernels: 26.8 us -> 33.7 us  [the longest x5 17.4 us: local(): pl.pallas_call(lambda *refs: kernel(*refs[len(after):]), grid=(steps,), o...]
    all_to_all x1, waiting for transfers between devices: 11.7 us -> 18.5 us  [per_device(): sums = lax.all_to_all(sums, ('zl', 'zh'), 0, 0, tiled=True)]
    ppermute x10, waiting for transfers between devices: 52.9 us -> 58.9 us  [shift(): return lax.ppermute(array, axis, ring(lax.axis_size(axis), step))]
    all_to_all x1 -> x2, starting transfers between devices: 7.55 us -> 13.5 us  [the longest x1 8.57 us: per_device(): first = lax.all_to_all(first, ('zl', 'zh'), 0, 0, tiled=True)]
    ppermute x10, starting transfers between devices: 24.4 us -> 20.3 us  [shift(): return lax.ppermute(array, axis, ring(lax.axis_size(axis), step))]
    all_to_all x1, starting transfers between devices: 4.32 us -> 6.41 us  [per_device(): sums = lax.all_to_all(sums, ('zl', 'zh'), 0, 0, tiled=True)]
    unnamed x20 -> x18, local copies, waits for them, and re-layouts: 5.48 us -> 6.48 us
  transfers between devices with their start and end apart: 15 -> 16, of which waited for: 7 -> 9; matrix products, arithmetic and copies ran while one was open for 1% -> 1% of each run, Pallas kernels for 19% -> 26%
where the time goes in v7:
time: 196 us
  waiting for transfers between devices  78.2 us (40%)
  Pallas kernels  55.2 us (28%)
  starting transfers between devices  40.3 us (21%)
  between operations  13.8 us (7%)
  local copies, waits for them, and re-layouts  7.46 us (4%)
    ppermute x10, waiting for transfers between devices, shift(): return lax.ppermute(array, axis, ring(lax.axis_size(axis), step))  58.9 us
    ppermute x10, starting transfers between devices, shift(): return lax.ppermute(array, axis, ring(lax.axis_size(axis), step))  20.3 us
    all_to_all x1, waiting for transfers between devices, per_device(): sums = lax.all_to_all(sums, ('zl', 'zh'), 0, 0, tiled=True)  18.5 us
    pallas_call x5, Pallas kernels, local(): pl.pallas_call(lambda *refs: kernel(*refs[len(after):]), grid=(steps,), o...  17.4 us
    pallas_call x2, Pallas kernels, weight_grad(): pl.pallas_call(functools.partial(weight_grad_kernel, offsets), grid=(widt...  13.9 us
    pallas_call x1, Pallas kernels, backward(): pl.pallas_call(backward_kernel, grid=(2,), out_shape=jax.ShapeDtypeStruct...  9.73 us
    pallas_call x1, Pallas kernels, forward(): pl.pallas_call(forward_kernel, grid=(width // tile,), out_shape=jax.Shape...  9.35 us
    all_to_all x1, starting transfers between devices, per_device(): first = lax.all_to_all(first, ('zl', 'zh'), 0, 0, tiled=True)  8.57 us
  transfers between devices with their start and end apart: 16, of which 9 were waited for; matrix products, arithmetic and copies ran while one was open for 1% of the time, Pallas kernels for 26%

profile of v7, /device:TPU:32, one launch (start us, length us, event | category | flops | bytes accessed | tf_op | source)
XLA Modules:
  0.0 195.6 jit_solution(3984741424034078198)
XLA Ops:
  7.9 2.5 %shard_map.67 = (bf16[8,256,256]{2,1,0:T(8,128)(2,1)}, bf16[8,256,256]{2,1,0:T(8,128)(2,1)}) custom-call(bf16[512,512]{1,0:T(8,128)(2,1)} %bitcast.12), custom_call_target="tpu_custom_call" | custom-call | flops 1 | bytes 1 | tf_op jit(solution)/shard_map/pallas_call | solution.py:65
  10.3 8.6 %all-to-all-start = ((bf16[8,256,256]{2,1,0:T(8,128)(2,1)}), bf16[8,256,256]{2,1,0:T(8,128)(2,1)S(1)}, u32[]{:S(2)}, u32[]{:S(2)}) async-start(bf16[8,256,256]{2,1,0:T(8,128)(2,1)} %get-tuple-element.16), calls=%async_computation | async-start | bytes 2097152 | tf_op jit(solution)/shard_map/all_to_all | solution.py:271
  18.9 2.4 %shard_map.68 = (bf16[128,2304]{1,0:T(8,128)(2,1)}, bf16[128,2304]{1,0:T(8,128)(2,1)}) custom-call(f32[2,18]{1,0:T(2,128)} %scales.1, bf16[256,2304]{1,0:T(8,128)(2,1)} %quantized.1), custom_call_target="tpu_custom_call" | custom-call | flops 1 | bytes 1 | tf_op jit(solution)/shard_map/pallas_call | solution.py:46
  24.6 4.5 %collective-permute-start.5 = (bf16[64,2304]{1,0:T(8,128)(2,1)}, bf16[64,2304]{1,0:T(8,128)(2,1)S(1)}, u32[]{:S(2)}, u32[]{:S(2)}) collective-permute-start(bf16[64,2304]{1,0:T(8,128)(2,1)} %bitcast.13), channel_id=1, source_target_pairs={{0,1},{1,0},{2,3},{3,2},{4,5},{5,4},{6,7},{7,6},{8,9},{9,8},{10,11... | collective-permute-start | bytes 884744 | tf_op jit(solution)/shard_map/ppermute | solution.py:261
  29.0 8.2 %collective-permute-done.refs_2_.refs_4_ = bf16[128,2304]{1,0:T(8,128)(2,1)S(1)} collective-permute-done((bf16[128,2304]{1,0:T(8,128)(2,1)}, bf16[128,2304]{1,0:T(8,128)(2,1)S(1)}, u32[]{:S(2)}, u32[]{:S(2)}) %collective-permute-start) | collective-permute-done | bytes 589856 | tf_op jit(solution)/shard_map/ppermute | solution.py:261
  38.1 4.0 %shard_map.69 = (bf16[256,2304]{1,0:T(8,128)(2,1)}, bf16[256,2304]{1,0:T(8,128)(2,1)}) custom-call(bf16[128,2304]{1,0:T(8,128)(2,1)} %get-tuple-element.18.refs_0_.refs_2_, bf16[128,2304]{1,0:T(8,128)(2,1)} %get-tuple-element.19.refs_1_.refs_3_, bf16[128,2304]{1,0:T(8,128)(2,1)} %copy-done.2, bf16[128,2304]{1,0:T(8,128)(2,1)} %collective-permute-done.1.refs_3_.refs_7_), custom_call_target="tpu_custom_call" | custom-call | flops 1 | bytes 1 | tf_op jit(solution)/shard_map/pallas_call | solution.py:211
  42.1 16.8 %collective-permute-done.5.__0_ = bf16[64,2304]{1,0:T(8,128)(2,1)S(1)} collective-permute-done((bf16[64,2304]{1,0:T(8,128)(2,1)}, bf16[64,2304]{1,0:T(8,128)(2,1)S(1)}, u32[]{:S(2)}, u32[]{:S(2)}) %collective-permute-start.5) | collective-permute-done | bytes 294944 | tf_op jit(solution)/shard_map/ppermute | solution.py:261
  60.0 5.0 %all-to-all-start.1 = ((bf16[8,256,256]{2,1,0:T(8,128)(2,1)}), bf16[8,256,256]{2,1,0:T(8,128)(2,1)S(1)}, u32[]{:S(2)}, u32[]{:S(2)}) async-start(bf16[8,256,256]{2,1,0:T(8,128)(2,1)} %shard_map.70), calls=%async_computation.1 | async-start | bytes 2097152 | tf_op jit(solution)/shard_map/all_to_all | solution.py:281
  65.0 2.8 %collective-permute-start.3 = (bf16[256,2304]{1,0:T(8,128)(2,1)}, bf16[256,2304]{1,0:T(8,128)(2,1)S(1)}, u32[]{:S(2)}, u32[]{:S(2)}) collective-permute-start(bf16[256,2304]{1,0:T(8,128)(2,1)} %get-tuple-element.21), channel_id=1, source_target_pairs={{0,6},{2,0},{4,2},{6,4},{1,7},{3,1},{5,3},{7,5},{8,14},{10,8},{12,... | collective-permute-start | bytes 3538952 | tf_op jit(solution)/shard_map/ppermute | solution.py:261
  68.4 23.4 %collective-permute-done.3.refs_6_ = bf16[256,2304]{1,0:T(8,128)(2,1)S(1)} collective-permute-done((bf16[256,2304]{1,0:T(8,128)(2,1)}, bf16[256,2304]{1,0:T(8,128)(2,1)S(1)}, u32[]{:S(2)}, u32[]{:S(2)}) %collective-permute-start.3) | collective-permute-done | bytes 1179680 | tf_op jit(solution)/shard_map/ppermute | solution.py:261
  96.2 9.3 %shard_map.71._ = bf16[1024,2304]{1,0:T(8,128)(2,1)} custom-call(s32[2]{0:T(128)} %pad_add_fusion.place, bf16[8,256,256]{2,1,0:T(8,128)(2,1)} %copy-done, bf16[8,256,256]{2,1,0:T(8,128)(2,1)} %copy-done.1, bf16[128,2304]{1,0:T(8,128)(2,1)} %get-tuple-element.18.refs_0_.refs_2_, bf16[128,2304]{1,0:T(8,128)(2,1)} %get-tuple-element.19.refs_1_.refs_3_, ...), custom_call_target="tpu_custom_call" | custom-call | flops 1 | bytes 1 | tf_op jit(solution)/shard_map/pallas_call | solution.py:112
  105.6 9.7 %shard_map.74._ = bf16[8,512,256]{2,1,0:T(8,128)(2,1)} custom-call(s32[2]{0:T(128)} %pad_add_fusion.place, bf16[1024,2304]{1,0:T(8,128)(2,1)} %shard_map.71._, bf16[512,2304]{1,0:T(8,128)(2,1)} %bitcast.7, bf16[512,2304]{1,0:T(8,128)(2,1)} %all-gather.4.cloned.1.call-done.refs_1_.far, bf16[128,2304]{1,0:T(8,128)(2,1)} %get-tuple-element.18.refs_0_.refs_2_, ...), custom_call_target="tpu_custom_call" | custom-call | flops 1 | bytes 1 | tf_op jit(solution)/shard_map/pallas_call | solution.py:179
  115.3 6.4 %all-to-all-start.2 = ((bf16[8,512,256]{2,1,0:T(8,128)(2,1)}), bf16[8,512,256]{2,1,0:T(8,128)(2,1)}, u32[]{:S(2)}, u32[]{:S(2)}) async-start(bf16[8,512,256]{2,1,0:T(8,128)(2,1)} %shard_map.74._), calls=%async_computation.3 | async-start | bytes 4194304 | tf_op jit(solution)/shard_map/all_to_all | solution.py:296
  121.7 5.9 %shard_map.76 = (bf16[128,2304]{1,0:T(8,128)(2,1)}, bf16[128,2304]{1,0:T(8,128)(2,1)}) custom-call(s32[2]{0:T(128)} %pad_add_fusion.place, bf16[8,512,256]{2,1,0:T(8,128)(2,1)} %shard_map.74._, bf16[8,256,256]{2,1,0:T(8,128)(2,1)} %copy-done, bf16[8,256,256]{2,1,0:T(8,128)(2,1)} %copy-done.1, bf16[512,2304]{1,0:T(8,128)(2,1)} %bitcast.8, ...), custom_call_target="tpu_custom_call" | custom-call | flops 1 | bytes 1 | tf_op jit(solution)/shard_map/pallas_call | solution.py:150
  129.6 8.0 %shard_map.77 = (bf16[256,2304]{1,0:T(8,128)(2,1)}, bf16[256,2304]{1,0:T(8,128)(2,1)}, bf16[256,2304]{1,0:T(8,128)(2,1)}) custom-call(s32[2]{0:T(128)} %pad_add_fusion.place, bf16[128,2304]{1,0:T(8,128)(2,1)} %get-tuple-element.22._, bf16[8,256,256]{2,1,0:T(8,128)(2,1)} %copy-done, bf16[8,256,256]{2,1,0:T(8,128)(2,1)} %copy-done.1, ...), custom_call_target="tpu_custom_call" | custom-call | flops 1 | bytes 1 | tf_op jit(solution)/shard_map/pallas_call | solution.py:150
  138.7 2.4 %collective-permute-done.6.refs_2_ = bf16[128,2304]{1,0:T(8,128)(2,1)S(1)} collective-permute-done((bf16[128,2304]{1,0:T(8,128)(2,1)}, bf16[128,2304]{1,0:T(8,128)(2,1)S(1)}, u32[]{:S(2)}, u32[]{:S(2)}) %collective-permute-start.6) | collective-permute-done | bytes 589856 | tf_op jit(solution)/shard_map/ppermute | solution.py:261
  142.0 4.2 %shard_map.78 = (bf16[256,2304]{1,0:T(8,128)(2,1)}, bf16[256,2304]{1,0:T(8,128)(2,1)}) custom-call(bf16[256,2304]{1,0:T(8,128)(2,1)} %get-tuple-element.24.refs_0_, bf16[256,2304]{1,0:T(8,128)(2,1)} %get-tuple-element.25.refs_1_, bf16[128,2304]{1,0:T(8,128)(2,1)} %copy-done.7, bf16[128,2304]{1,0:T(8,128)(2,1)} %copy-done.6), custom_call_target="tpu_custom_call" | custom-call | flops 1 | bytes 1 | tf_op jit(solution)/shard_map/pallas_call | solution.py:211
  146.2 3.2 %collective-permute-start.9 = (bf16[256,2304]{1,0:T(8,128)(2,1)}, bf16[256,2304]{1,0:T(8,128)(2,1)}, u32[]{:S(2)}, u32[]{:S(2)}) collective-permute-start(bf16[256,2304]{1,0:T(8,128)(2,1)} %get-tuple-element.28), channel_id=1, source_target_pairs={{0,6},{2,0},{4,2},{6,4},{1,7},{3,1},{5,3},{7,5},{8,14},{10,8},{12,... | collective-permute-start | bytes 3538952 | tf_op jit(solution)/shard_map/ppermute | solution.py:261
  150.4 4.6 %collective-permute-start.4 = (bf16[64,2304]{1,0:T(8,128)(2,1)S(1)}, bf16[64,2304]{1,0:T(8,128)(2,1)S(1)}, u32[]{:S(2)}, u32[]{:S(2)}) collective-permute-start(bf16[64,2304]{1,0:T(8,128)(2,1)S(1)} %slice.4), channel_id=1, source_target_pairs={{0,1},{1,0},{2,3},{3,2},{4,5},{5,4},{6,7},{7,6},{8,9},{9,8},{10,11... | collective-permute-start | bytes 884744 | tf_op jit(solution)/shard_map/ppermute | solution.py:261
  155.0 18.5 %all-to-all-done.2.refs_0_ = bf16[8,512,256]{2,1,0:T(8,128)(2,1)} async-done(((bf16[8,512,256]{2,1,0:T(8,128)(2,1)}), bf16[8,512,256]{2,1,0:T(8,128)(2,1)}, u32[]{:S(2)}, u32[]{:S(2)}) %all-to-all-start.2) | async-done | bytes 2097184 | tf_op jit(solution)/shard_map/all_to_all | solution.py:296
  173.5 2.6 %shard_map.75.refs_0_ = bf16[512,512]{1,0:T(8,128)(2,1)} custom-call(bf16[8,512,256]{2,1,0:T(8,128)(2,1)} %all-to-all-done.2.refs_0_), custom_call_target="tpu_custom_call" | custom-call | flops 1 | bytes 1 | tf_op jit(solution)/shard_map/pallas_call | solution.py:211
  176.1 4.5 %collective-permute-done.4.refs_1_ = bf16[64,2304]{1,0:T(8,128)(2,1)S(1)} collective-permute-done((bf16[64,2304]{1,0:T(8,128)(2,1)S(1)}, bf16[64,2304]{1,0:T(8,128)(2,1)S(1)}, u32[]{:S(2)}, u32[]{:S(2)}) %collective-permute-start.4) | collective-permute-done | bytes 294944 | tf_op jit(solution)/shard_map/ppermute | solution.py:261
  181.4 2.8 %shard_map.72.refs_1_ = bf16[64,2304]{1,0:T(8,128)(2,1)} custom-call(bf16[128,2304]{1,0:T(8,128)(2,1)} %reduce-scatter.2.cloned.1.call-done.refs_0_, bf16[64,2304]{1,0:T(8,128)(2,1)} %copy-done.8), custom_call_target="tpu_custom_call" | custom-call | flops 1 | bytes 1 | tf_op jit(solution)/shard_map/pallas_call | solution.py:211
  185.2 3.9 %shard_map.79 = bf16[256,2304]{1,0:T(8,128)(2,1)} custom-call(bf16[512,512]{1,0:T(8,128)(2,1)} %shard_map.75.refs_0_, bf16[64,2304]{1,0:T(8,128)(2,1)} %shard_map.72.refs_1_, bf16[256,2304]{1,0:T(8,128)(2,1)} %get-tuple-element.23.refs_2_, bf16[256,2304]{1,0:T(8,128)(2,1)} %copy-done.5, bf16[256,2304]{1,0:T(8,128)(2,1)} %collective-permute-done.9.refs_4_), custom_call_target="tpu_custom_call" | custom-call | flops 1 | bytes 1 | tf_op jit(solution)/shard_map/pallas_call | solution.py:211
  (44 shorter events, 17.8 us)
Async XLA Ops:
  7.2 98.4 %all-gather.6.cloned.1.call-start = ((), (), s32[]{:S(2)}) async-start(), calls=%async_computation.6 | async-start | bytes 2654208 | tf_op jit(solution)/shard_map/all_gather | solution.py:269
  10.3 48.5 %all-to-all-start = ((bf16[8,256,256]{2,1,0:T(8,128)(2,1)}), bf16[8,256,256]{2,1,0:T(8,128)(2,1)S(1)}, u32[]{:S(2)}, u32[]{:S(2)}) async-start(bf16[8,256,256]{2,1,0:T(8,128)(2,1)} %get-tuple-element.16), calls=%async_computation | async-start | bytes 2097152 | tf_op jit(solution)/shard_map/all_to_all | solution.py:271
  18.9 86.7 %all-gather.4.cloned.1.call-start = ((), (), s32[]{:S(2)}) async-start(), calls=%async_computation.5 | async-start | bytes 2654208 | tf_op jit(solution)/shard_map/all_gather | solution.py:279
  21.3 15.9 %collective-permute-start = (bf16[128,2304]{1,0:T(8,128)(2,1)}, bf16[128,2304]{1,0:T(8,128)(2,1)S(1)}, u32[]{:S(2)}, u32[]{:S(2)}) collective-permute-start(bf16[128,2304]{1,0:T(8,128)(2,1)} %get-tuple-element.18.refs_0_.refs_2_), channel_id=1, source_target_pairs={{0,2},{2,4},{4,6},{6,0},{1,3},{3,5},{5,7},{7,1},{8,10},{10,12},{12... | collective-permute-start | bytes 1769480 | tf_op jit(solution)/shard_map/ppermute | solution.py:261
  22.8 14.5 %collective-permute-start.1 = (bf16[128,2304]{1,0:T(8,128)(2,1)}, bf16[128,2304]{1,0:T(8,128)(2,1)}, u32[]{:S(2)}, u32[]{:S(2)}) collective-permute-start(bf16[128,2304]{1,0:T(8,128)(2,1)} %get-tuple-element.19.refs_1_.refs_3_), channel_id=1, source_target_pairs={{0,6},{2,0},{4,2},{6,4},{1,7},{3,1},{5,3},{7,5},{8,14},{10,8},{12,... | collective-permute-start | bytes 1769480 | tf_op jit(solution)/shard_map/ppermute | solution.py:261
  24.6 34.3 %collective-permute-start.5 = (bf16[64,2304]{1,0:T(8,128)(2,1)}, bf16[64,2304]{1,0:T(8,128)(2,1)S(1)}, u32[]{:S(2)}, u32[]{:S(2)}) collective-permute-start(bf16[64,2304]{1,0:T(8,128)(2,1)} %bitcast.13), channel_id=1, source_target_pairs={{0,1},{1,0},{2,3},{3,2},{4,5},{5,4},{6,7},{7,6},{8,9},{9,8},{10,11... | collective-permute-start | bytes 884744 | tf_op jit(solution)/shard_map/ppermute | solution.py:261
  37.3 0.8 copy-start.2
  58.8 0.7 copy-start.4
  58.8 1.1 copy-start
  60.0 35.2 %all-to-all-start.1 = ((bf16[8,256,256]{2,1,0:T(8,128)(2,1)}), bf16[8,256,256]{2,1,0:T(8,128)(2,1)S(1)}, u32[]{:S(2)}, u32[]{:S(2)}) async-start(bf16[8,256,256]{2,1,0:T(8,128)(2,1)} %shard_map.70), calls=%async_computation.1 | async-start | bytes 2097152 | tf_op jit(solution)/shard_map/all_to_all | solution.py:281
  65.0 84.5 %reduce-scatter.2.cloned.1.call-start = ((), (), s32[]{:S(2)}) async-start(), calls=%async_computation.4 | async-start | bytes 5308416 | tf_op jit(solution)/shard_map/reduce_scatter | solution.py:291
  65.0 26.8 %collective-permute-start.3 = (bf16[256,2304]{1,0:T(8,128)(2,1)}, bf16[256,2304]{1,0:T(8,128)(2,1)S(1)}, u32[]{:S(2)}, u32[]{:S(2)}) collective-permute-start(bf16[256,2304]{1,0:T(8,128)(2,1)} %get-tuple-element.21), channel_id=1, source_target_pairs={{0,6},{2,0},{4,2},{6,4},{1,7},{3,1},{5,3},{7,5},{8,14},{10,8},{12,... | collective-permute-start | bytes 3538952 | tf_op jit(solution)/shard_map/ppermute | solution.py:261
  67.7 27.4 %collective-permute-start.2 = (bf16[256,2304]{1,0:T(8,128)(2,1)}, bf16[256,2304]{1,0:T(8,128)(2,1)}, u32[]{:S(2)}, u32[]{:S(2)}) collective-permute-start(bf16[256,2304]{1,0:T(8,128)(2,1)} %get-tuple-element.20.__2_), channel_id=1, source_target_pairs={{0,2},{2,4},{4,6},{6,0},{1,3},{3,5},{5,7},{7,1},{8,10},{10,12},{12... | collective-permute-start | bytes 3538952 | tf_op jit(solution)/shard_map/ppermute | solution.py:261
  91.8 1.0 copy-start.3
  95.2 1.0 copy-start.1
  115.3 58.2 %all-to-all-start.2 = ((bf16[8,512,256]{2,1,0:T(8,128)(2,1)}), bf16[8,512,256]{2,1,0:T(8,128)(2,1)}, u32[]{:S(2)}, u32[]{:S(2)}) async-start(bf16[8,512,256]{2,1,0:T(8,128)(2,1)} %shard_map.74._), calls=%async_computation.3 | async-start | bytes 4194304 | tf_op jit(solution)/shard_map/all_to_all | solution.py:296
  127.6 11.2 %collective-permute-start.7 = (bf16[128,2304]{1,0:T(8,128)(2,1)}, bf16[128,2304]{1,0:T(8,128)(2,1)S(1)}, u32[]{:S(2)}, u32[]{:S(2)}) collective-permute-start(bf16[128,2304]{1,0:T(8,128)(2,1)} %get-tuple-element.26), channel_id=1, source_target_pairs={{0,6},{2,0},{4,2},{6,4},{1,7},{3,1},{5,3},{7,5},{8,14},{10,8},{12,... | collective-permute-start | bytes 1769480 | tf_op jit(solution)/shard_map/ppermute | solution.py:261
  128.8 12.4 %collective-permute-start.6 = (bf16[128,2304]{1,0:T(8,128)(2,1)}, bf16[128,2304]{1,0:T(8,128)(2,1)S(1)}, u32[]{:S(2)}, u32[]{:S(2)}) collective-permute-start(bf16[128,2304]{1,0:T(8,128)(2,1)} %get-tuple-element.22._), channel_id=1, source_target_pairs={{0,2},{2,4},{4,6},{6,0},{1,3},{3,5},{5,7},{7,1},{8,10},{10,12},{12... | collective-permute-start | bytes 1769480 | tf_op jit(solution)/shard_map/ppermute | solution.py:261
  138.7 2.4 %copy-start.6 = (bf16[128,2304]{1,0:T(8,128)(2,1)}, bf16[128,2304]{1,0:T(8,128)(2,1)S(1)}, u32[]{:S(2)}) copy-start(bf16[128,2304]{1,0:T(8,128)(2,1)S(1)} %collective-permute-done.7.refs_3_) | copy-start | bytes 1769476
  141.2 0.9 copy-start.7
  146.2 38.0 %collective-permute-start.8 = (bf16[256,2304]{1,0:T(8,128)(2,1)}, bf16[256,2304]{1,0:T(8,128)(2,1)S(1)}, u32[]{:S(2)}, u32[]{:S(2)}) collective-permute-start(bf16[256,2304]{1,0:T(8,128)(2,1)} %get-tuple-element.27), channel_id=1, source_target_pairs={{0,2},{2,4},{4,6},{6,0},{1,3},{3,5},{5,7},{7,1},{8,10},{10,12},{12... | collective-permute-start | bytes 3538952 | tf_op jit(solution)/shard_map/ppermute | solution.py:261
  146.2 38.0 %collective-permute-start.9 = (bf16[256,2304]{1,0:T(8,128)(2,1)}, bf16[256,2304]{1,0:T(8,128)(2,1)}, u32[]{:S(2)}, u32[]{:S(2)}) collective-permute-start(bf16[256,2304]{1,0:T(8,128)(2,1)} %get-tuple-element.28), channel_id=1, source_target_pairs={{0,6},{2,0},{4,2},{6,4},{1,7},{3,1},{5,3},{7,5},{8,14},{10,8},{12,... | collective-permute-start | bytes 3538952 | tf_op jit(solution)/shard_map/ppermute | solution.py:261
  150.4 30.2 %collective-permute-start.4 = (bf16[64,2304]{1,0:T(8,128)(2,1)S(1)}, bf16[64,2304]{1,0:T(8,128)(2,1)S(1)}, u32[]{:S(2)}, u32[]{:S(2)}) collective-permute-start(bf16[64,2304]{1,0:T(8,128)(2,1)S(1)} %slice.4), channel_id=1, source_target_pairs={{0,1},{1,0},{2,3},{3,2},{4,5},{5,4},{6,7},{7,6},{8,9},{9,8},{10,11... | collective-permute-start | bytes 884744 | tf_op jit(solution)/shard_map/ppermute | solution.py:261
  184.1 1.0 copy-start.5
  (1 other events, 0.7 us)
Sparse Core Ops, SparseCore 0:
  9.8 30.7 all-gather.5
  60.1 25.5 all-gather.3
  105.7 40.8 reduce-scatter.1

commit v8 on v5

--- a/solution.py
+++ b/solution.py
@@ -1,3 +1,5 @@
+import functools
+
 import jax
 import jax.numpy as jnp
 from jax import lax
@@ -117,17 +119,16 @@
     )(place, after, panel, *weights)
 
 
-def weight_grad_kernel(place, _, panel, near, far, *refs):
-    outs, left = refs[:5], refs[5]
+def weight_grad_kernel(count, place, _, *refs):
+    panels, (near, far) = refs[: 2 * count], refs[2 * count : 2 * count + 2]
+    outs, left = refs[2 * count + 2 : -1], refs[-1]
 
     @pl.when(pl.program_id(0) == 0)
     def _():
-        for at in range(8):
-            m = lax.rem(place[0] - at // 2 + 4, 4)
-            s = lax.rem(at % 2 + place[1], 2)
-            rows = pl.ds(pl.multiple_of(m * 256, 256), 256)
+        for i, panel in enumerate(panels):
+            s = lax.rem(i % 2 + place[1], 2)
             lanes = pl.ds(pl.multiple_of(s * 512, 512), 512)
-            left[rows, lanes] = panel[at].T
+            left[i // 2 * 256 : i // 2 * 256 + 256, lanes] = panel[0].T
 
     total = jnp.dot(left[...], stacked((near, far)), preferred_element_type=F32)
     at = 0
@@ -136,26 +137,30 @@
         at += out.shape[0]
 
 
-def weight_grad(place, after, panel, near, far):
+def weight_grad(offsets, sizes, place, after, panel, near, far):
     width = near.shape[1]
     tile = width // 3
-    sizes = (256, 256, 128, 128, 256)
-    return pl.pallas_call(
-        weight_grad_kernel,
-        grid=(width // tile,),
-        out_shape=[jax.ShapeDtypeStruct((rows, width), BF) for rows in sizes],
-        in_specs=[
-            SCALAR,
-            ANY,
-            whole(panel.shape),
-            pl.BlockSpec((512, tile), lambda n: (0, n)),
-            pl.BlockSpec((512, tile), lambda n: (0, n)),
-        ],
-        out_specs=[pl.BlockSpec((rows, tile), lambda n: (0, n)) for rows in sizes],
-        scratch_shapes=[pltpu.VMEM((1024, 1024), BF)],
+
+    def block(m, h):
+        return lambda n, place: (lax.rem(place[0] - m + 4, 4) * 2 + h, 0, 0)
+
+    blocks = [
+        pl.BlockSpec((1, 512, 256), block(m, h)) for m in offsets for h in range(2)
+    ]
+    columns = lambda n, place: (0, n)
+    return pl.pallas_call(
+        functools.partial(weight_grad_kernel, len(offsets)),
+        grid_spec=pltpu.PrefetchScalarGridSpec(
+            num_scalar_prefetch=1,
+            grid=(width // tile,),
+            in_specs=[ANY, *blocks] + [pl.BlockSpec((512, tile), columns)] * 2,
+            out_specs=[pl.BlockSpec((size, tile), columns) for size in sizes],
+            scratch_shapes=[pltpu.VMEM((256 * len(offsets), 1024), BF)],
+        ),
+        out_shape=[jax.ShapeDtypeStruct((size, width), BF) for size in sizes],
         compiler_params=params(),
         cost_estimate=PRODUCT,
-    )(place, after, panel, near, far)
+    )(place, after, *[panel] * len(blocks), near, far)
 
 
 def backward_kernel(place, *refs):
@@ -208,10 +213,13 @@
     )(*after, *args)
 
 
-def relay_kernel(top, bottom, top_up, bottom_down, far, up, down, passed):
+def pass_kernel(source, out):
+    out[...] = source[...]
+
+
+def relay_kernel(top, bottom, top_up, bottom_down, up, down):
     up[:BLOCK], up[BLOCK:] = top_up[...], bottom[...]
     down[:BLOCK], down[BLOCK:] = top[...], bottom_down[...]
-    passed[...] = far[...]
 
 
 def sum_kernel(*refs):
@@ -252,33 +260,31 @@
     top, bottom = dequantize(scales, qweight)
     top_up, bottom_down = shift(top, "x", 1), shift(bottom, "x", -1)
     far = shift(grad_out[0], "zh", 1)
-    up, down, far = local(
-        relay_kernel,
-        [(256, F), (256, F), (64, F)],
-        split,
-        *(top, bottom, top_up, bottom_down, far),
+    (far,) = local(pass_kernel, [(64, F)], (split, top_up, bottom_down), far)
+    far = lax.all_gather(far, ("y", "k"), axis=0, tiled=True)
+    up, down = local(
+        relay_kernel, [(256, F)] * 2, (), top, bottom, top_up, bottom_down
     )
-    far = lax.all_gather(far, ("y", "k"), axis=0, tiled=True)
     up, down = shift(up, "x", 1), shift(down, "x", -1)
     weights = (top, bottom, top_up, up, down, bottom_down)
 
     sums = backward(place, near, far, weights)
     product = forward(place, sums, panel, weights)
-    terms = weight_grad(place, product, panel, near, far)
-
-    product = lax.psum_scatter(product, ("y", "k"), scatter_dimension=0, tiled=True)
-    (projected,) = local(
-        end_kernel, [(64, F)], (), product, shift(product[64:], "zh", 1)
-    )
+    top, bottom = weight_grad((2,), (128, 128), place, product, panel, near, far)
+    here, down, up = weight_grad((0, 1, 3), (256,) * 3, place, top, panel, near, far)
 
     sums = lax.all_to_all(sums, ("zl", "zh"), 0, 0, tiled=True)
     (grad_inputs,) = local(gather_kernel, [(512, 512)], (), sums)
 
-    here, down, top, bottom, up = terms
     top, bottom = shift(top, "x", 1), shift(bottom, "x", -1)
     up, down = local(onward_kernel, [(256, F)] * 2, (), up, down, top, bottom)
     up, down = shift(up, "x", 1), shift(down, "x", -1)
-    (grad_weight,) = local(sum_kernel, [(256, F)], (grad_inputs, projected), here, up, down)
+    grad_weight = summed(here, up, down)
+
+    product = lax.psum_scatter(product, ("y", "k"), scatter_dimension=0, tiled=True)
+    other = shift(product[64:], "zh", 1)
+    after = grad_inputs, grad_weight
+    (projected,) = local(end_kernel, [(64, F)], after, product, other)
 
     return projected[None], grad_inputs[None], grad_weight
 

time: 184 us -> 178 us (0.967)
  waiting for transfers between devices: 76.3 us -> 67.2 us
  Pallas kernels: 48.3 us -> 51.9 us
  other arithmetic: 0.59 us -> 3.29 us
    all_to_all x1, waiting for transfers between devices: 11.7 us -> 0.01 us  [per_device(): sums = lax.all_to_all(sums, ('zl', 'zh'), 0, 0, tiled=True)]
    pallas_call x1 -> x2, Pallas kernels: 9.28 us -> 14.8 us  [weight_grad(): pl.pallas_call(functools.partial(weight_grad_kernel, len(offsets)), grid_...]
    ppermute x10, waiting for transfers between devices: 52.9 us -> 56.2 us  [shift(): return lax.ppermute(array, axis, ring(lax.axis_size(axis), step))]
    all_to_all x1, waiting for transfers between devices: 10 us -> 6.92 us  [per_device(): panel = lax.all_to_all(split, ('zl', 'zh'), 0, 0, tiled=True)]
    convert_element_type x0 -> x1, other arithmetic: none -> 2.7 us  [summed(): return total.astype(BF)]
    reduce_scatter x1, waiting for transfers between devices: 0.92 us -> 3.31 us  [per_device(): lax.psum_scatter(product, ('y', 'k'), scatter_dimension=0, tiled=True)]
    pallas_call x5, Pallas kernels: 14.9 us -> 13.1 us  [local(): pl.pallas_call(lambda *refs: kernel(*refs[len(after):]), out_shape=[jax.S...]
    unnamed x20 -> x18, local copies, waits for them, and re-layouts: 5.48 us -> 4.25 us
  transfers between devices with their start and end apart: 15 -> 15, of which waited for: 7 -> 7; matrix products, arithmetic and copies ran while one was open for 1% -> 2% of each run, Pallas kernels for 19% -> 23%
where the time goes in v8:
time: 178 us; the launch traced here: 176 us
  waiting for transfers between devices  67.2 us (38%)
  Pallas kernels  51.9 us (29%)
  starting transfers between devices  34.9 us (20%)
  between operations  13.8 us (8%)
  local copies, waits for them, and re-layouts  5.23 us (3%)
  other arithmetic  3.29 us (2%)
    ppermute x10, waiting for transfers between devices, shift(): return lax.ppermute(array, axis, ring(lax.axis_size(axis), step))  56.2 us
    ppermute x10, starting transfers between devices, shift(): return lax.ppermute(array, axis, ring(lax.axis_size(axis), step))  23.1 us
    pallas_call x2, Pallas kernels, weight_grad(): pl.pallas_call(functools.partial(weight_grad_kernel, len(offsets)), grid_...  14.8 us
    pallas_call x5, Pallas kernels, local(): pl.pallas_call(lambda *refs: kernel(*refs[len(after):]), out_shape=[jax.S...  13.1 us
    pallas_call x1, Pallas kernels, backward(): pl.pallas_call(backward_kernel, grid=(2,), out_shape=jax.ShapeDtypeStruct...  9.65 us
    pallas_call x1, Pallas kernels, forward(): pl.pallas_call(forward_kernel, grid=(width // tile,), out_shape=jax.Shape...  9.45 us
    all_to_all x1, starting transfers between devices, per_device(): panel = lax.all_to_all(split, ('zl', 'zh'), 0, 0, tiled=True)  7.41 us
    all_to_all x1, waiting for transfers between devices, per_device(): panel = lax.all_to_all(split, ('zl', 'zh'), 0, 0, tiled=True)  6.92 us
  transfers between devices with their start and end apart: 15, of which 7 were waited for; matrix products, arithmetic and copies ran while one was open for 2% of the time, Pallas kernels for 23%

profile of v8, /device:TPU:32, one launch (start us, length us, event | category | flops | bytes accessed | tf_op | source)
XLA Modules:
  0.0 176.4 jit_solution(12331597571516974810)
XLA Ops:
  8.0 2.4 %shard_map.68 = (bf16[128,2304]{1,0:T(8,128)(2,1)}, bf16[128,2304]{1,0:T(8,128)(2,1)}) custom-call(f32[2,18]{1,0:T(2,128)} %scales.1, bf16[256,2304]{1,0:T(8,128)(2,1)} %quantized.1), custom_call_target="tpu_custom_call" | custom-call | flops 1 | bytes 1 | tf_op jit(solution)/shard_map/pallas_call | solution.py:46
  13.6 6.3 %collective-permute-start.2 = (bf16[64,2304]{1,0:T(8,128)(2,1)S(1)}, bf16[64,2304]{1,0:T(8,128)(2,1)S(1)}, u32[]{:S(2)}, u32[]{:S(2)}) collective-permute-start(bf16[64,2304]{1,0:T(8,128)(2,1)S(1)} %bitcast.12), channel_id=1, source_target_pairs={{0,1},{1,0},{2,3},{3,2},{4,5},{5,4},{6,7},{7,6},{8,9},{9,8},{10,11... | collective-permute-start | bytes 884744 | tf_op jit(solution)/shard_map/ppermute | solution.py:248
  19.9 2.6 %shard_map.67.refs_0_ = bf16[8,512,256]{2,1,0:T(8,128)(2,1)} custom-call(bf16[512,512]{1,0:T(8,128)(2,1)} %bitcast.11), custom_call_target="tpu_custom_call" | custom-call | flops 1 | bytes 1 | tf_op jit(solution)/shard_map/pallas_call | solution.py:63
  22.5 10.3 %collective-permute-done.2.refs_3_ = bf16[64,2304]{1,0:T(8,128)(2,1)S(1)} collective-permute-done((bf16[64,2304]{1,0:T(8,128)(2,1)S(1)}, bf16[64,2304]{1,0:T(8,128)(2,1)S(1)}, u32[]{:S(2)}, u32[]{:S(2)}) %collective-permute-start.2) | collective-permute-done | bytes 294944 | tf_op jit(solution)/shard_map/ppermute | solution.py:248
  36.2 7.4 %all-to-all-start.1 = ((bf16[8,512,256]{2,1,0:T(8,128)(2,1)}), bf16[8,512,256]{2,1,0:T(8,128)(2,1)}, u32[]{:S(2)}, u32[]{:S(2)}) async-start(bf16[8,512,256]{2,1,0:T(8,128)(2,1)} %shard_map.67.refs_0_), calls=%async_computation.1 | async-start | bytes 4194304 | tf_op jit(solution)/shard_map/all_to_all | solution.py:258
  43.6 3.1 %shard_map.70 = (bf16[256,2304]{1,0:T(8,128)(2,1)}, bf16[256,2304]{1,0:T(8,128)(2,1)}) custom-call(bf16[128,2304]{1,0:T(8,128)(2,1)} %get-tuple-element.14.refs_0_.refs_2_, bf16[128,2304]{1,0:T(8,128)(2,1)} %get-tuple-element.15.refs_1_.refs_3_, bf16[128,2304]{1,0:T(8,128)(2,1)} %copy-done, bf16[128,2304]{1,0:T(8,128)(2,1)} %copy-done.1), custom_call_target="tpu_custom_call" | custom-call | flops 1 | bytes 1 | tf_op jit(solution)/shard_map/pallas_call | solution.py:206
  47.0 2.9 %collective-permute-start.4 = (bf16[256,2304]{1,0:T(8,128)(2,1)}, bf16[256,2304]{1,0:T(8,128)(2,1)}, u32[]{:S(2)}, u32[]{:S(2)}) collective-permute-start(bf16[256,2304]{1,0:T(8,128)(2,1)} %get-tuple-element.17), channel_id=1, source_target_pairs={{0,6},{2,0},{4,2},{6,4},{1,7},{3,1},{5,3},{7,5},{8,14},{10,8},{12,... | collective-permute-start | bytes 3538952 | tf_op jit(solution)/shard_map/ppermute | solution.py:248
  50.6 23.4 %collective-permute-done.3.refs_5_.refs_3_ = bf16[256,2304]{1,0:T(8,128)(2,1)S(1)} collective-permute-done((bf16[256,2304]{1,0:T(8,128)(2,1)}, bf16[256,2304]{1,0:T(8,128)(2,1)S(1)}, u32[]{:S(2)}, u32[]{:S(2)}) %collective-permute-start.3) | collective-permute-done | bytes 1179680 | tf_op jit(solution)/shard_map/ppermute | solution.py:248
  75.0 9.7 %shard_map.71._ = bf16[8,512,256]{2,1,0:T(8,128)(2,1)} custom-call(s32[2]{0:T(128)} %pad_add_fusion.place, bf16[512,2304]{1,0:T(8,128)(2,1)} %bitcast.7, bf16[512,2304]{1,0:T(8,128)(2,1)} %all-gather.4.cloned.1.call-done.refs_1_.refs_3_.refs_7_, bf16[128,2304]{1,0:T(8,128)(2,1)} %get-tuple-element.14.refs_0_.refs_2_, ...), custom_call_target="tpu_custom_call" | custom-call | flops 1 | bytes 1 | tf_op jit(solution)/shard_map/pallas_call | solution.py:181
  84.7 6.9 %all-to-all-done.1.panel.refs_0_.refs_1_.refs_2_.refs_3_.refs_4_.refs_5_ = bf16[8,512,256]{2,1,0:T(8,128)(2,1)} async-done(((bf16[8,512,256]{2,1,0:T(8,128)(2,1)}), bf16[8,512,256]{2,1,0:T(8,128)(2,1)}, u32[]{:S(2)}, u32[]{:S(2)}) %all-to-all-start.1) | async-done | bytes 2097184 | tf_op jit(solution)/shard_map/all_to_all | solution.py:258
  91.6 9.5 %shard_map.73._ = bf16[1024,2304]{1,0:T(8,128)(2,1)} custom-call(s32[2]{0:T(128)} %pad_add_fusion.place, bf16[8,512,256]{2,1,0:T(8,128)(2,1)} %shard_map.71._, bf16[8,512,256]{2,1,0:T(8,128)(2,1)} %all-to-all-done.1.panel.refs_0_.refs_1_.refs_2_.refs_3_.refs_4_.refs_5_, bf16[128,2304]{1,0:T(8,128)(2,1)} %get-tuple-element.14.refs_0_.refs_2_, ...), custom_call_target="tpu_custom_call" | custom-call | flops 1 | bytes 1 | tf_op jit(solution)/shard_map/pallas_call | solution.py:109
  101.1 4.3 %all-to-all-start = ((bf16[8,512,256]{2,1,0:T(8,128)(2,1)}), bf16[8,512,256]{2,1,0:T(8,128)(2,1)}, u32[]{:S(2)}, u32[]{:S(2)}) async-start(bf16[8,512,256]{2,1,0:T(8,128)(2,1)} %shard_map.71._), calls=%async_computation | async-start | bytes 4194304 | tf_op jit(solution)/shard_map/all_to_all | solution.py:276
  105.4 6.2 %shard_map.74 = (bf16[128,2304]{1,0:T(8,128)(2,1)}, bf16[128,2304]{1,0:T(8,128)(2,1)}) custom-call(s32[2]{0:T(128)} %pad_add_fusion.place, bf16[1024,2304]{1,0:T(8,128)(2,1)} %shard_map.73._, bf16[8,512,256]{2,1,0:T(8,128)(2,1)} %all-to-all-done.1.panel.refs_0_.refs_1_.refs_2_.refs_3_.refs_4_.refs_5_, ...), custom_call_target="tpu_custom_call" | custom-call | flops 1 | bytes 1 | tf_op jit(solution)/shard_map/pallas_call | solution.py:151
  113.7 8.5 %shard_map.75 = (bf16[256,2304]{1,0:T(8,128)(2,1)}, bf16[256,2304]{1,0:T(8,128)(2,1)}, bf16[256,2304]{1,0:T(8,128)(2,1)}) custom-call(s32[2]{0:T(128)} %pad_add_fusion.place, bf16[128,2304]{1,0:T(8,128)(2,1)} %get-tuple-element.18._, bf16[8,512,256]{2,1,0:T(8,128)(2,1)} %all-to-all-done.1.panel.refs_0_.refs_1_.refs_2_.refs_3_.refs_4_.refs_5_, ...), custom_call_target="tpu_custom_call" | custom-call | flops 1 | bytes 1 | tf_op jit(solution)/shard_map/pallas_call | solution.py:151
  122.2 4.8 %collective-permute-done.6.refs_3_ = bf16[128,2304]{1,0:T(8,128)(2,1)S(1)} collective-permute-done((bf16[128,2304]{1,0:T(8,128)(2,1)}, bf16[128,2304]{1,0:T(8,128)(2,1)S(1)}, u32[]{:S(2)}, u32[]{:S(2)}) %collective-permute-start.6) | collective-permute-done | bytes 589856 | tf_op jit(solution)/shard_map/ppermute | solution.py:248
  127.0 2.1 %collective-permute-done.5.refs_2_ = bf16[128,2304]{1,0:T(8,128)(2,1)S(1)} collective-permute-done((bf16[128,2304]{1,0:T(8,128)(2,1)}, bf16[128,2304]{1,0:T(8,128)(2,1)S(1)}, u32[]{:S(2)}, u32[]{:S(2)}) %collective-permute-start.5) | collective-permute-done | bytes 589856 | tf_op jit(solution)/shard_map/ppermute | solution.py:248
  130.0 3.7 %shard_map.76 = (bf16[256,2304]{1,0:T(8,128)(2,1)}, bf16[256,2304]{1,0:T(8,128)(2,1)}) custom-call(bf16[256,2304]{1,0:T(8,128)(2,1)} %get-tuple-element.20.refs_0_, bf16[256,2304]{1,0:T(8,128)(2,1)} %get-tuple-element.21.refs_1_, bf16[128,2304]{1,0:T(8,128)(2,1)} %copy-done.5, bf16[128,2304]{1,0:T(8,128)(2,1)} %copy-done.4), custom_call_target="tpu_custom_call" | custom-call | flops 1 | bytes 1 | tf_op jit(solution)/shard_map/pallas_call | solution.py:206
  133.7 3.2 %collective-permute-start.8 = (bf16[256,2304]{1,0:T(8,128)(2,1)}, bf16[256,2304]{1,0:T(8,128)(2,1)}, u32[]{:S(2)}, u32[]{:S(2)}) collective-permute-start(bf16[256,2304]{1,0:T(8,128)(2,1)} %get-tuple-element.24), channel_id=1, source_target_pairs={{0,6},{2,0},{4,2},{6,4},{1,7},{3,1},{5,3},{7,5},{8,14},{10,8},{12,... | collective-permute-start | bytes 3538952 | tf_op jit(solution)/shard_map/ppermute | solution.py:248
  136.9 3.3 %reduce-scatter.2.cloned.1.call-done.refs_2_ = bf16[128,2304]{1,0:T(8,128)(2,1)} async-done(((bf16[1024,2304]{1,0:T(8,128)(2,1)}), bf16[128,2304]{1,0:T(8,128)(2,1)}) %reduce-scatter.2.cloned.1.call-update) | async-done | bytes 589840 | tf_op jit(solution)/shard_map/reduce_scatter | solution.py:284
  141.2 5.1 %collective-permute-start.9 = (bf16[64,2304]{1,0:T(8,128)(2,1)S(1)}, bf16[64,2304]{1,0:T(8,128)(2,1)S(1)}, u32[]{:S(2)}, u32[]{:S(2)}) collective-permute-start(bf16[64,2304]{1,0:T(8,128)(2,1)S(1)} %slice.4), channel_id=1, source_target_pairs={{0,1},{1,0},{2,3},{3,2},{4,5},{5,4},{6,7},{7,6},{8,9},{9,8},{10,11... | collective-permute-start | bytes 884744 | tf_op jit(solution)/shard_map/ppermute | solution.py:248
  146.3 15.5 %collective-permute-done.7 = bf16[256,2304]{1,0:T(8,128)(2,1)S(1)} collective-permute-done((bf16[256,2304]{1,0:T(8,128)(2,1)}, bf16[256,2304]{1,0:T(8,128)(2,1)S(1)}, u32[]{:S(2)}, u32[]{:S(2)}) %collective-permute-start.7) | collective-permute-done | bytes 1179680 | tf_op jit(solution)/shard_map/ppermute | solution.py:248
  161.8 2.7 %add_convert_fusion.refs_1_ = bf16[256,2304]{1,0:T(8,128)(2,1)} fusion(bf16[256,2304]{1,0:T(8,128)(2,1)} %collective-permute-done.8, bf16[256,2304]{1,0:T(8,128)(2,1)S(1)} %collective-permute-done.7, bf16[256,2304]{1,0:T(8,128)(2,1)S(1)} %copy-done.3), kind=kLoop, calls=%fused_computation | loop fusion | flops 3538944 | bytes 4718592 | tf_op jit(solution)/shard_map/convert_element_type | solution.py:201
  164.6 2.6 %shard_map.72.refs_0_ = bf16[512,512]{1,0:T(8,128)(2,1)} custom-call(bf16[8,512,256]{2,1,0:T(8,128)(2,1)} %all-to-all-done.refs_0_), custom_call_target="tpu_custom_call" | custom-call | flops 1 | bytes 1 | tf_op jit(solution)/shard_map/pallas_call | solution.py:206
  167.9 1.9 %shard_map.77 = bf16[64,2304]{1,0:T(8,128)(2,1)} custom-call(bf16[512,512]{1,0:T(8,128)(2,1)} %shard_map.72.refs_0_, bf16[256,2304]{1,0:T(8,128)(2,1)} %add_convert_fusion.refs_1_, bf16[128,2304]{1,0:T(8,128)(2,1)} %reduce-scatter.2.cloned.1.call-done.refs_2_, bf16[64,2304]{1,0:T(8,128)(2,1)} %copy-done.7), custom_call_target="tpu_custom_call" | custom-call | flops 1 | bytes 1 | tf_op jit(solution)/shard_map/pallas_call | solution.py:206
  (41 shorter events, 13.9 us)
Async XLA Ops:
  7.2 6.5 %copy-start.6 = (bf16[1,64,2304]{2,1,0:T(8,128)(2,1)S(1)}, bf16[1,64,2304]{2,1,0:T(8,128)(2,1)}, u32[]{:S(2)}) copy-start(bf16[1,64,2304]{2,1,0:T(8,128)(2,1)} %param.7) | copy-start | bytes 884740
  7.2 66.8 %all-gather.6.cloned.1.call-start = ((), (), s32[]{:S(2)}) async-start(), calls=%async_computation.5 | async-start | bytes 2654208 | tf_op jit(solution)/shard_map/all_gather | solution.py:256
  7.9 66.1 %all-gather.4.cloned.1.call-start = ((), (), s32[]{:S(2)}) async-start(), calls=%async_computation.3 | async-start | bytes 2654208 | tf_op jit(solution)/shard_map/all_gather | solution.py:264
  10.4 22.4 %collective-permute-start = (bf16[128,2304]{1,0:T(8,128)(2,1)}, bf16[128,2304]{1,0:T(8,128)(2,1)S(1)}, u32[]{:S(2)}, u32[]{:S(2)}) collective-permute-start(bf16[128,2304]{1,0:T(8,128)(2,1)} %get-tuple-element.14.refs_0_.refs_2_), channel_id=1, source_target_pairs={{0,2},{2,4},{4,6},{6,0},{1,3},{3,5},{5,7},{7,1},{8,10},{10,12},{12... | collective-permute-start | bytes 1769480 | tf_op jit(solution)/shard_map/ppermute | solution.py:248
  11.9 20.9 %collective-permute-start.1 = (bf16[128,2304]{1,0:T(8,128)(2,1)}, bf16[128,2304]{1,0:T(8,128)(2,1)S(1)}, u32[]{:S(2)}, u32[]{:S(2)}) collective-permute-start(bf16[128,2304]{1,0:T(8,128)(2,1)} %get-tuple-element.15.refs_1_.refs_3_), channel_id=1, source_target_pairs={{0,6},{2,0},{4,2},{6,4},{1,7},{3,1},{5,3},{7,5},{8,14},{10,8},{12,... | collective-permute-start | bytes 1769480 | tf_op jit(solution)/shard_map/ppermute | solution.py:248
  13.6 19.1 %collective-permute-start.2 = (bf16[64,2304]{1,0:T(8,128)(2,1)S(1)}, bf16[64,2304]{1,0:T(8,128)(2,1)S(1)}, u32[]{:S(2)}, u32[]{:S(2)}) collective-permute-start(bf16[64,2304]{1,0:T(8,128)(2,1)S(1)} %bitcast.12), channel_id=1, source_target_pairs={{0,1},{1,0},{2,3},{3,2},{4,5},{5,4},{6,7},{7,6},{8,9},{9,8},{10,11... | collective-permute-start | bytes 884744 | tf_op jit(solution)/shard_map/ppermute | solution.py:248
  32.8 0.7 copy-start.8
  32.8 0.9 copy-start
  33.7 0.8 copy-start.1
  36.2 55.4 %all-to-all-start.1 = ((bf16[8,512,256]{2,1,0:T(8,128)(2,1)}), bf16[8,512,256]{2,1,0:T(8,128)(2,1)}, u32[]{:S(2)}, u32[]{:S(2)}) async-start(bf16[8,512,256]{2,1,0:T(8,128)(2,1)} %shard_map.67.refs_0_), calls=%async_computation.1 | async-start | bytes 4194304 | tf_op jit(solution)/shard_map/all_to_all | solution.py:258
  43.6 96.6 %reduce-scatter.2.cloned.1.call-start = ((), (), s32[]{:S(2)}) async-start(), calls=%async_computation.4 | async-start | bytes 5308416 | tf_op jit(solution)/shard_map/reduce_scatter | solution.py:284
  46.7 27.3 %collective-permute-start.3 = (bf16[256,2304]{1,0:T(8,128)(2,1)}, bf16[256,2304]{1,0:T(8,128)(2,1)S(1)}, u32[]{:S(2)}, u32[]{:S(2)}) collective-permute-start(bf16[256,2304]{1,0:T(8,128)(2,1)} %get-tuple-element.16), channel_id=1, source_target_pairs={{0,2},{2,4},{4,6},{6,0},{1,3},{3,5},{5,7},{7,1},{8,10},{10,12},{12... | collective-permute-start | bytes 3538952 | tf_op jit(solution)/shard_map/ppermute | solution.py:248
  47.0 27.0 %collective-permute-start.4 = (bf16[256,2304]{1,0:T(8,128)(2,1)}, bf16[256,2304]{1,0:T(8,128)(2,1)}, u32[]{:S(2)}, u32[]{:S(2)}) collective-permute-start(bf16[256,2304]{1,0:T(8,128)(2,1)} %get-tuple-element.17), channel_id=1, source_target_pairs={{0,6},{2,0},{4,2},{6,4},{1,7},{3,1},{5,3},{7,5},{8,14},{10,8},{12,... | collective-permute-start | bytes 3538952 | tf_op jit(solution)/shard_map/ppermute | solution.py:248
  74.0 1.0 copy-start.2
  101.1 63.5 %all-to-all-start = ((bf16[8,512,256]{2,1,0:T(8,128)(2,1)}), bf16[8,512,256]{2,1,0:T(8,128)(2,1)}, u32[]{:S(2)}, u32[]{:S(2)}) async-start(bf16[8,512,256]{2,1,0:T(8,128)(2,1)} %shard_map.71._), calls=%async_computation | async-start | bytes 4194304 | tf_op jit(solution)/shard_map/all_to_all | solution.py:276
  111.6 15.3 %collective-permute-start.6 = (bf16[128,2304]{1,0:T(8,128)(2,1)}, bf16[128,2304]{1,0:T(8,128)(2,1)S(1)}, u32[]{:S(2)}, u32[]{:S(2)}) collective-permute-start(bf16[128,2304]{1,0:T(8,128)(2,1)} %get-tuple-element.22), channel_id=1, source_target_pairs={{0,6},{2,0},{4,2},{6,4},{1,7},{3,1},{5,3},{7,5},{8,14},{10,8},{12,... | collective-permute-start | bytes 1769480 | tf_op jit(solution)/shard_map/ppermute | solution.py:248
  112.8 16.3 %collective-permute-start.5 = (bf16[128,2304]{1,0:T(8,128)(2,1)}, bf16[128,2304]{1,0:T(8,128)(2,1)S(1)}, u32[]{:S(2)}, u32[]{:S(2)}) collective-permute-start(bf16[128,2304]{1,0:T(8,128)(2,1)} %get-tuple-element.18._), channel_id=1, source_target_pairs={{0,2},{2,4},{4,6},{6,0},{1,3},{3,5},{5,7},{7,1},{8,10},{10,12},{12... | collective-permute-start | bytes 1769480 | tf_op jit(solution)/shard_map/ppermute | solution.py:248
  127.0 3.0 %copy-start.4 = (bf16[128,2304]{1,0:T(8,128)(2,1)}, bf16[128,2304]{1,0:T(8,128)(2,1)S(1)}, u32[]{:S(2)}) copy-start(bf16[128,2304]{1,0:T(8,128)(2,1)S(1)} %collective-permute-done.6.refs_3_) | copy-start | bytes 1769476
  129.1 0.8 copy-start.5
  130.0 31.9 %copy-start.3 = (bf16[256,2304]{1,0:T(8,128)(2,1)S(1)}, bf16[256,2304]{1,0:T(8,128)(2,1)}, u32[]{:S(2)}) copy-start(bf16[256,2304]{1,0:T(8,128)(2,1)} %get-tuple-element.19) | copy-start | bytes 3538948
  133.7 28.1 %collective-permute-start.7 = (bf16[256,2304]{1,0:T(8,128)(2,1)}, bf16[256,2304]{1,0:T(8,128)(2,1)S(1)}, u32[]{:S(2)}, u32[]{:S(2)}) collective-permute-start(bf16[256,2304]{1,0:T(8,128)(2,1)} %get-tuple-element.23), channel_id=1, source_target_pairs={{0,2},{2,4},{4,6},{6,0},{1,3},{3,5},{5,7},{7,1},{8,10},{10,12},{12... | collective-permute-start | bytes 3538952 | tf_op jit(solution)/shard_map/ppermute | solution.py:248
  133.7 28.1 %collective-permute-start.8 = (bf16[256,2304]{1,0:T(8,128)(2,1)}, bf16[256,2304]{1,0:T(8,128)(2,1)}, u32[]{:S(2)}, u32[]{:S(2)}) collective-permute-start(bf16[256,2304]{1,0:T(8,128)(2,1)} %get-tuple-element.24), channel_id=1, source_target_pairs={{0,6},{2,0},{4,2},{6,4},{1,7},{3,1},{5,3},{7,5},{8,14},{10,8},{12,... | collective-permute-start | bytes 3538952 | tf_op jit(solution)/shard_map/ppermute | solution.py:248
  141.2 26.0 %collective-permute-start.9 = (bf16[64,2304]{1,0:T(8,128)(2,1)S(1)}, bf16[64,2304]{1,0:T(8,128)(2,1)S(1)}, u32[]{:S(2)}, u32[]{:S(2)}) collective-permute-start(bf16[64,2304]{1,0:T(8,128)(2,1)S(1)} %slice.4), channel_id=1, source_target_pairs={{0,1},{1,0},{2,3},{3,2},{4,5},{5,4},{6,7},{7,6},{8,9},{9,8},{10,11... | collective-permute-start | bytes 884744 | tf_op jit(solution)/shard_map/ppermute | solution.py:248
  167.2 0.7 copy-start.7
Sparse Core Ops, SparseCore 0:
  9.8 30.7 all-gather.5
  43.1 28.7 all-gather.3
  101.2 38.9 reduce-scatter.1

commit v9 on v8

--- a/solution.py
+++ b/solution.py
@@ -10,7 +10,7 @@
 BLOCK = 128
 BF = jnp.bfloat16
 F32 = jnp.float32
-VMEM_LIMIT = 62 * 1024 * 1024
+VMEM_LIMIT = 64 * 1024 * 1024 - 4096
 
 
 def params():
@@ -213,6 +213,17 @@
     )(*after, *args)
 
 
+def follow(array, after):
+    return pl.pallas_call(
+        lambda *_: None,
+        out_shape=jax.ShapeDtypeStruct(array.shape, array.dtype),
+        in_specs=[ANY] * (1 + len(after)),
+        out_specs=ANY,
+        input_output_aliases={0: 0},
+        cost_estimate=cost(1, 1),
+    )(array, *after)
+
+
 def pass_kernel(source, out):
     out[...] = source[...]
 
@@ -260,7 +271,7 @@
     top, bottom = dequantize(scales, qweight)
     top_up, bottom_down = shift(top, "x", 1), shift(bottom, "x", -1)
     far = shift(grad_out[0], "zh", 1)
-    (far,) = local(pass_kernel, [(64, F)], (split, top_up, bottom_down), far)
+    far = follow(far, (split, top_up, bottom_down))
     far = lax.all_gather(far, ("y", "k"), axis=0, tiled=True)
     up, down = local(
         relay_kernel, [(256, F)] * 2, (), top, bottom, top_up, bottom_down

time: 178 us -> 174 us (0.978)
  local copies, waits for them, and re-layouts: 5.23 us -> 1.69 us
  Pallas kernels: 51.9 us -> 50.1 us
    unnamed x18 -> x0, local copies, waits for them, and re-layouts: 4.25 us -> none
    pallas_call x5 -> x4, Pallas kernels: 13.1 us -> 11.4 us  [local(): pl.pallas_call(lambda *refs: kernel(*refs[len(after):]), out_shape=[jax.S...]
  transfers between devices with their start and end apart: 15 -> 15, of which waited for: 7 -> 9; matrix products, arithmetic and copies ran while one was open for 2% -> 3% of each run, Pallas kernels for 23% -> 23%
where the time goes in v9:
time: 174 us; the launch traced here: 172 us
  waiting for transfers between devices  68.5 us (39%)
  Pallas kernels  50.1 us (29%)
  starting transfers between devices  34.9 us (20%)
  between operations  13.8 us (8%)
  other arithmetic  3.28 us (2%)
    ppermute x10, waiting for transfers between devices, shift(): return lax.ppermute(array, axis, ring(lax.axis_size(axis), step))  55.9 us
    ppermute x10, starting transfers between devices, shift(): return lax.ppermute(array, axis, ring(lax.axis_size(axis), step))  23.1 us
    pallas_call x2, Pallas kernels, weight_grad(): pl.pallas_call(functools.partial(weight_grad_kernel, len(offsets)), grid_...  14.7 us
    pallas_call x4, Pallas kernels, local(): pl.pallas_call(lambda *refs: kernel(*refs[len(after):]), out_shape=[jax.S...  11.4 us
    pallas_call x1, Pallas kernels, backward(): pl.pallas_call(backward_kernel, grid=(2,), out_shape=jax.ShapeDtypeStruct...  9.65 us
    pallas_call x1, Pallas kernels, forward(): pl.pallas_call(forward_kernel, grid=(width // tile,), out_shape=jax.Shape...  9.46 us
    all_to_all x1, waiting for transfers between devices, per_device(): panel = lax.all_to_all(split, ('zl', 'zh'), 0, 0, tiled=True)  7.54 us
    all_to_all x1, starting transfers between devices, per_device(): panel = lax.all_to_all(split, ('zl', 'zh'), 0, 0, tiled=True)  7.42 us
  transfers between devices with their start and end apart: 15, of which 9 were waited for; matrix products, arithmetic and copies ran while one was open for 3% of the time, Pallas kernels for 23%

profile of v9, /device:TPU:32, one launch (start us, length us, event | category | flops | bytes accessed | tf_op | source)
XLA Modules:
  0.0 172.3 jit_solution(7310591096922061284)
XLA Ops:
  7.9 2.4 %shard_map.68 = (bf16[128,2304]{1,0:T(8,128)(2,1)}, bf16[128,2304]{1,0:T(8,128)(2,1)}) custom-call(f32[2,18]{1,0:T(2,128)} %scales.1, bf16[256,2304]{1,0:T(8,128)(2,1)} %quantized.1), custom_call_target="tpu_custom_call" | custom-call | flops 1 | bytes 1 | tf_op jit(solution)/shard_map/pallas_call | solution.py:46
  13.6 6.3 %collective-permute-start = (bf16[64,2304]{1,0:T(8,128)(2,1)}, bf16[64,2304]{1,0:T(8,128)(2,1)}, u32[]{:S(2)}, u32[]{:S(2)}) collective-permute-start(bf16[64,2304]{1,0:T(8,128)(2,1)} %bitcast.12), channel_id=1, source_target_pairs={{0,1},{1,0},{2,3},{3,2},{4,5},{5,4},{6,7},{7,6},{8,9},{9,8},{10,11... | collective-permute-start | bytes 884744 | tf_op jit(solution)/shard_map/ppermute | solution.py:259
  19.9 2.5 %shard_map.67.__1_ = bf16[8,512,256]{2,1,0:T(8,128)(2,1)} custom-call(bf16[512,512]{1,0:T(8,128)(2,1)} %bitcast.11), custom_call_target="tpu_custom_call" | custom-call | flops 1 | bytes 1 | tf_op jit(solution)/shard_map/pallas_call | solution.py:63
  22.4 10.7 %collective-permute-done.__0_ = bf16[64,2304]{1,0:T(8,128)(2,1)} collective-permute-done((bf16[64,2304]{1,0:T(8,128)(2,1)}, bf16[64,2304]{1,0:T(8,128)(2,1)}, u32[]{:S(2)}, u32[]{:S(2)}) %collective-permute-start) | collective-permute-done | bytes 294944 | tf_op jit(solution)/shard_map/ppermute | solution.py:259
  33.1 7.4 %all-to-all-start.1 = ((bf16[8,512,256]{2,1,0:T(8,128)(2,1)}), bf16[8,512,256]{2,1,0:T(8,128)(2,1)}, u32[]{:S(2)}, u32[]{:S(2)}) async-start(bf16[8,512,256]{2,1,0:T(8,128)(2,1)} %shard_map.67.__1_), calls=%async_computation.1 | async-start | bytes 4194304 | tf_op jit(solution)/shard_map/all_to_all | solution.py:269
  40.5 3.1 %shard_map.70 = (bf16[256,2304]{1,0:T(8,128)(2,1)}, bf16[256,2304]{1,0:T(8,128)(2,1)}) custom-call(bf16[128,2304]{1,0:T(8,128)(2,1)} %get-tuple-element.14.refs_0_.refs_2_, bf16[128,2304]{1,0:T(8,128)(2,1)} %get-tuple-element.15.refs_1_.refs_3_, bf16[128,2304]{1,0:T(8,128)(2,1)} %collective-permute-done.1.__2_.refs_2_.refs_4_, ...), custom_call_target="tpu_custom_call" | custom-call | flops 1 | bytes 1 | tf_op jit(solution)/shard_map/pallas_call | solution.py:206
  43.9 2.9 %collective-permute-start.4 = (bf16[256,2304]{1,0:T(8,128)(2,1)}, bf16[256,2304]{1,0:T(8,128)(2,1)}, u32[]{:S(2)}, u32[]{:S(2)}) collective-permute-start(bf16[256,2304]{1,0:T(8,128)(2,1)} %get-tuple-element.17), channel_id=1, source_target_pairs={{0,6},{2,0},{4,2},{6,4},{1,7},{3,1},{5,3},{7,5},{8,14},{10,8},{12,... | collective-permute-start | bytes 3538952 | tf_op jit(solution)/shard_map/ppermute | solution.py:259
  47.4 23.6 %collective-permute-done.3.refs_5_.refs_3_ = bf16[256,2304]{1,0:T(8,128)(2,1)} collective-permute-done((bf16[256,2304]{1,0:T(8,128)(2,1)}, bf16[256,2304]{1,0:T(8,128)(2,1)}, u32[]{:S(2)}, u32[]{:S(2)}) %collective-permute-start.3) | collective-permute-done | bytes 1179680 | tf_op jit(solution)/shard_map/ppermute | solution.py:259
  71.3 9.7 %shard_map.71._ = bf16[8,512,256]{2,1,0:T(8,128)(2,1)} custom-call(s32[2]{0:T(128)} %pad_add_fusion.place, bf16[512,2304]{1,0:T(8,128)(2,1)} %bitcast.7, bf16[512,2304]{1,0:T(8,128)(2,1)} %all-gather.4.cloned.1.call-done.refs_1_.refs_3_.refs_7_, bf16[128,2304]{1,0:T(8,128)(2,1)} %get-tuple-element.14.refs_0_.refs_2_, ...), custom_call_target="tpu_custom_call" | custom-call | flops 1 | bytes 1 | tf_op jit(solution)/shard_map/pallas_call | solution.py:181
  80.9 7.5 %all-to-all-done.1.panel.refs_0_.refs_1_.refs_2_.refs_3_.refs_4_.refs_5_ = bf16[8,512,256]{2,1,0:T(8,128)(2,1)} async-done(((bf16[8,512,256]{2,1,0:T(8,128)(2,1)}), bf16[8,512,256]{2,1,0:T(8,128)(2,1)}, u32[]{:S(2)}, u32[]{:S(2)}) %all-to-all-start.1) | async-done | bytes 2097184 | tf_op jit(solution)/shard_map/all_to_all | solution.py:269
  88.5 9.5 %shard_map.73._ = bf16[1024,2304]{1,0:T(8,128)(2,1)} custom-call(s32[2]{0:T(128)} %pad_add_fusion.place, bf16[8,512,256]{2,1,0:T(8,128)(2,1)} %shard_map.71._, bf16[8,512,256]{2,1,0:T(8,128)(2,1)} %all-to-all-done.1.panel.refs_0_.refs_1_.refs_2_.refs_3_.refs_4_.refs_5_, bf16[128,2304]{1,0:T(8,128)(2,1)} %get-tuple-element.14.refs_0_.refs_2_, ...), custom_call_target="tpu_custom_call" | custom-call | flops 1 | bytes 1 | tf_op jit(solution)/shard_map/pallas_call | solution.py:109
  97.9 4.3 %all-to-all-start = ((bf16[8,512,256]{2,1,0:T(8,128)(2,1)}), bf16[8,512,256]{2,1,0:T(8,128)(2,1)}, u32[]{:S(2)}, u32[]{:S(2)}) async-start(bf16[8,512,256]{2,1,0:T(8,128)(2,1)} %shard_map.71._), calls=%async_computation | async-start | bytes 4194304 | tf_op jit(solution)/shard_map/all_to_all | solution.py:287
  102.2 6.2 %shard_map.74 = (bf16[128,2304]{1,0:T(8,128)(2,1)}, bf16[128,2304]{1,0:T(8,128)(2,1)}) custom-call(s32[2]{0:T(128)} %pad_add_fusion.place, bf16[1024,2304]{1,0:T(8,128)(2,1)} %shard_map.73._, bf16[8,512,256]{2,1,0:T(8,128)(2,1)} %all-to-all-done.1.panel.refs_0_.refs_1_.refs_2_.refs_3_.refs_4_.refs_5_, ...), custom_call_target="tpu_custom_call" | custom-call | flops 1 | bytes 1 | tf_op jit(solution)/shard_map/pallas_call | solution.py:151
  110.5 8.5 %shard_map.75 = (bf16[256,2304]{1,0:T(8,128)(2,1)}, bf16[256,2304]{1,0:T(8,128)(2,1)}, bf16[256,2304]{1,0:T(8,128)(2,1)}) custom-call(s32[2]{0:T(128)} %pad_add_fusion.place, bf16[128,2304]{1,0:T(8,128)(2,1)} %get-tuple-element.18._, bf16[8,512,256]{2,1,0:T(8,128)(2,1)} %all-to-all-done.1.panel.refs_0_.refs_1_.refs_2_.refs_3_.refs_4_.refs_5_, ...), custom_call_target="tpu_custom_call" | custom-call | flops 1 | bytes 1 | tf_op jit(solution)/shard_map/pallas_call | solution.py:151
  119.0 4.9 %collective-permute-done.6.refs_3_ = bf16[128,2304]{1,0:T(8,128)(2,1)} collective-permute-done((bf16[128,2304]{1,0:T(8,128)(2,1)}, bf16[128,2304]{1,0:T(8,128)(2,1)}, u32[]{:S(2)}, u32[]{:S(2)}) %collective-permute-start.6) | collective-permute-done | bytes 589856 | tf_op jit(solution)/shard_map/ppermute | solution.py:259
  123.9 2.2 %collective-permute-done.5.refs_2_ = bf16[128,2304]{1,0:T(8,128)(2,1)} collective-permute-done((bf16[128,2304]{1,0:T(8,128)(2,1)}, bf16[128,2304]{1,0:T(8,128)(2,1)}, u32[]{:S(2)}, u32[]{:S(2)}) %collective-permute-start.5) | collective-permute-done | bytes 589856 | tf_op jit(solution)/shard_map/ppermute | solution.py:259
  126.1 3.7 %shard_map.76 = (bf16[256,2304]{1,0:T(8,128)(2,1)}, bf16[256,2304]{1,0:T(8,128)(2,1)}) custom-call(bf16[256,2304]{1,0:T(8,128)(2,1)} %get-tuple-element.20.refs_0_, bf16[256,2304]{1,0:T(8,128)(2,1)} %get-tuple-element.21.refs_1_, bf16[128,2304]{1,0:T(8,128)(2,1)} %collective-permute-done.5.refs_2_, bf16[128,2304]{1,0:T(8,128)(2,1)} %collective-permute-done.6.refs_3_), custom_call_target="tpu_custom_call" | custom-call | flops 1 | bytes 1 | tf_op jit(solution)/shard_map/pallas_call | solution.py:206
  129.8 3.2 %collective-permute-start.8 = (bf16[256,2304]{1,0:T(8,128)(2,1)}, bf16[256,2304]{1,0:T(8,128)(2,1)S(1)}, u32[]{:S(2)}, u32[]{:S(2)}) collective-permute-start(bf16[256,2304]{1,0:T(8,128)(2,1)} %get-tuple-element.24), channel_id=1, source_target_pairs={{0,6},{2,0},{4,2},{6,4},{1,7},{3,1},{5,3},{7,5},{8,14},{10,8},{12,... | collective-permute-start | bytes 3538952 | tf_op jit(solution)/shard_map/ppermute | solution.py:259
  133.0 4.1 %reduce-scatter.2.cloned.1.call-done.refs_2_ = bf16[128,2304]{1,0:T(8,128)(2,1)} async-done(((bf16[1024,2304]{1,0:T(8,128)(2,1)}), bf16[128,2304]{1,0:T(8,128)(2,1)}) %reduce-scatter.2.cloned.1.call-update) | async-done | bytes 589840 | tf_op jit(solution)/shard_map/reduce_scatter | solution.py:295
  138.8 5.1 %collective-permute-start.9 = (bf16[64,2304]{1,0:T(8,128)(2,1)}, bf16[64,2304]{1,0:T(8,128)(2,1)}, u32[]{:S(2)}, u32[]{:S(2)}) collective-permute-start(bf16[64,2304]{1,0:T(8,128)(2,1)} %slice.4), channel_id=1, source_target_pairs={{0,1},{1,0},{2,3},{3,2},{4,5},{5,4},{6,7},{7,6},{8,9},{9,8},{10,11... | collective-permute-start | bytes 884744 | tf_op jit(solution)/shard_map/ppermute | solution.py:259
  143.8 14.0 %collective-permute-done.7 = bf16[256,2304]{1,0:T(8,128)(2,1)S(1)} collective-permute-done((bf16[256,2304]{1,0:T(8,128)(2,1)}, bf16[256,2304]{1,0:T(8,128)(2,1)S(1)}, u32[]{:S(2)}, u32[]{:S(2)}) %collective-permute-start.7) | collective-permute-done | bytes 1179680 | tf_op jit(solution)/shard_map/ppermute | solution.py:259
  157.9 2.7 %add_convert_fusion.refs_1_ = bf16[256,2304]{1,0:T(8,128)(2,1)} fusion(bf16[256,2304]{1,0:T(8,128)(2,1)S(1)} %collective-permute-done.8, bf16[256,2304]{1,0:T(8,128)(2,1)S(1)} %collective-permute-done.7, bf16[256,2304]{1,0:T(8,128)(2,1)} %get-tuple-element.19), kind=kLoop, calls=%fused_computation | loop fusion | flops 3538944 | bytes 4718592 | tf_op jit(solution)/shard_map/convert_element_type | solution.py:201
  160.6 2.6 %shard_map.72.refs_0_ = bf16[512,512]{1,0:T(8,128)(2,1)} custom-call(bf16[8,512,256]{2,1,0:T(8,128)(2,1)} %all-to-all-done.refs_0_), custom_call_target="tpu_custom_call" | custom-call | flops 1 | bytes 1 | tf_op jit(solution)/shard_map/pallas_call | solution.py:206
  163.8 1.9 %shard_map.77 = bf16[64,2304]{1,0:T(8,128)(2,1)} custom-call(bf16[512,512]{1,0:T(8,128)(2,1)} %shard_map.72.refs_0_, bf16[256,2304]{1,0:T(8,128)(2,1)} %add_convert_fusion.refs_1_, bf16[128,2304]{1,0:T(8,128)(2,1)} %reduce-scatter.2.cloned.1.call-done.refs_2_, bf16[64,2304]{1,0:T(8,128)(2,1)} %collective-permute-done.9.refs_3_), custom_call_target="tpu_custom_call" | custom-call | flops 1 | bytes 1 | tf_op jit(solution)/shard_map/pallas_call | solution.py:206
  (23 shorter events, 9.5 us)
Async XLA Ops:
  7.2 63.8 %all-gather.6.cloned.1.call-start = ((), (), s32[]{:S(2)}) async-start(), calls=%async_computation.5 | async-start | bytes 2654208 | tf_op jit(solution)/shard_map/all_gather | solution.py:267
  7.9 63.4 %all-gather.4.cloned.1.call-start = ((), (), s32[]{:S(2)}) async-start(), calls=%async_computation.3 | async-start | bytes 2654208 | tf_op jit(solution)/shard_map/all_gather | solution.py:275
  10.4 22.7 %collective-permute-start.1 = (bf16[128,2304]{1,0:T(8,128)(2,1)}, bf16[128,2304]{1,0:T(8,128)(2,1)}, u32[]{:S(2)}, u32[]{:S(2)}) collective-permute-start(bf16[128,2304]{1,0:T(8,128)(2,1)} %get-tuple-element.14.refs_0_.refs_2_), channel_id=1, source_target_pairs={{0,2},{2,4},{4,6},{6,0},{1,3},{3,5},{5,7},{7,1},{8,10},{10,12},{12... | collective-permute-start | bytes 1769480 | tf_op jit(solution)/shard_map/ppermute | solution.py:259
  11.8 21.2 %collective-permute-start.2 = (bf16[128,2304]{1,0:T(8,128)(2,1)}, bf16[128,2304]{1,0:T(8,128)(2,1)}, u32[]{:S(2)}, u32[]{:S(2)}) collective-permute-start(bf16[128,2304]{1,0:T(8,128)(2,1)} %get-tuple-element.15.refs_1_.refs_3_), channel_id=1, source_target_pairs={{0,6},{2,0},{4,2},{6,4},{1,7},{3,1},{5,3},{7,5},{8,14},{10,8},{12,... | collective-permute-start | bytes 1769480 | tf_op jit(solution)/shard_map/ppermute | solution.py:259
  13.6 19.5 %collective-permute-start = (bf16[64,2304]{1,0:T(8,128)(2,1)}, bf16[64,2304]{1,0:T(8,128)(2,1)}, u32[]{:S(2)}, u32[]{:S(2)}) collective-permute-start(bf16[64,2304]{1,0:T(8,128)(2,1)} %bitcast.12), channel_id=1, source_target_pairs={{0,1},{1,0},{2,3},{3,2},{4,5},{5,4},{6,7},{7,6},{8,9},{9,8},{10,11... | collective-permute-start | bytes 884744 | tf_op jit(solution)/shard_map/ppermute | solution.py:259
  33.1 55.4 %all-to-all-start.1 = ((bf16[8,512,256]{2,1,0:T(8,128)(2,1)}), bf16[8,512,256]{2,1,0:T(8,128)(2,1)}, u32[]{:S(2)}, u32[]{:S(2)}) async-start(bf16[8,512,256]{2,1,0:T(8,128)(2,1)} %shard_map.67.__1_), calls=%async_computation.1 | async-start | bytes 4194304 | tf_op jit(solution)/shard_map/all_to_all | solution.py:269
  40.5 96.6 %reduce-scatter.2.cloned.1.call-start = ((), (), s32[]{:S(2)}) async-start(), calls=%async_computation.4 | async-start | bytes 5308416 | tf_op jit(solution)/shard_map/reduce_scatter | solution.py:295
  43.6 27.4 %collective-permute-start.3 = (bf16[256,2304]{1,0:T(8,128)(2,1)}, bf16[256,2304]{1,0:T(8,128)(2,1)}, u32[]{:S(2)}, u32[]{:S(2)}) collective-permute-start(bf16[256,2304]{1,0:T(8,128)(2,1)} %get-tuple-element.16), channel_id=1, source_target_pairs={{0,2},{2,4},{4,6},{6,0},{1,3},{3,5},{5,7},{7,1},{8,10},{10,12},{12... | collective-permute-start | bytes 3538952 | tf_op jit(solution)/shard_map/ppermute | solution.py:259
  43.9 27.1 %collective-permute-start.4 = (bf16[256,2304]{1,0:T(8,128)(2,1)}, bf16[256,2304]{1,0:T(8,128)(2,1)}, u32[]{:S(2)}, u32[]{:S(2)}) collective-permute-start(bf16[256,2304]{1,0:T(8,128)(2,1)} %get-tuple-element.17), channel_id=1, source_target_pairs={{0,6},{2,0},{4,2},{6,4},{1,7},{3,1},{5,3},{7,5},{8,14},{10,8},{12,... | collective-permute-start | bytes 3538952 | tf_op jit(solution)/shard_map/ppermute | solution.py:259
  97.9 62.6 %all-to-all-start = ((bf16[8,512,256]{2,1,0:T(8,128)(2,1)}), bf16[8,512,256]{2,1,0:T(8,128)(2,1)}, u32[]{:S(2)}, u32[]{:S(2)}) async-start(bf16[8,512,256]{2,1,0:T(8,128)(2,1)} %shard_map.71._), calls=%async_computation | async-start | bytes 4194304 | tf_op jit(solution)/shard_map/all_to_all | solution.py:287
  108.5 15.4 %collective-permute-start.6 = (bf16[128,2304]{1,0:T(8,128)(2,1)}, bf16[128,2304]{1,0:T(8,128)(2,1)}, u32[]{:S(2)}, u32[]{:S(2)}) collective-permute-start(bf16[128,2304]{1,0:T(8,128)(2,1)} %get-tuple-element.22), channel_id=1, source_target_pairs={{0,6},{2,0},{4,2},{6,4},{1,7},{3,1},{5,3},{7,5},{8,14},{10,8},{12,... | collective-permute-start | bytes 1769480 | tf_op jit(solution)/shard_map/ppermute | solution.py:259
  109.6 16.4 %collective-permute-start.5 = (bf16[128,2304]{1,0:T(8,128)(2,1)}, bf16[128,2304]{1,0:T(8,128)(2,1)}, u32[]{:S(2)}, u32[]{:S(2)}) collective-permute-start(bf16[128,2304]{1,0:T(8,128)(2,1)} %get-tuple-element.18._), channel_id=1, source_target_pairs={{0,2},{2,4},{4,6},{6,0},{1,3},{3,5},{5,7},{7,1},{8,10},{10,12},{12... | collective-permute-start | bytes 1769480 | tf_op jit(solution)/shard_map/ppermute | solution.py:259
  129.8 28.1 %collective-permute-start.7 = (bf16[256,2304]{1,0:T(8,128)(2,1)}, bf16[256,2304]{1,0:T(8,128)(2,1)S(1)}, u32[]{:S(2)}, u32[]{:S(2)}) collective-permute-start(bf16[256,2304]{1,0:T(8,128)(2,1)} %get-tuple-element.23), channel_id=1, source_target_pairs={{0,2},{2,4},{4,6},{6,0},{1,3},{3,5},{5,7},{7,1},{8,10},{10,12},{12... | collective-permute-start | bytes 3538952 | tf_op jit(solution)/shard_map/ppermute | solution.py:259
  129.8 28.1 %collective-permute-start.8 = (bf16[256,2304]{1,0:T(8,128)(2,1)}, bf16[256,2304]{1,0:T(8,128)(2,1)S(1)}, u32[]{:S(2)}, u32[]{:S(2)}) collective-permute-start(bf16[256,2304]{1,0:T(8,128)(2,1)} %get-tuple-element.24), channel_id=1, source_target_pairs={{0,6},{2,0},{4,2},{6,4},{1,7},{3,1},{5,3},{7,5},{8,14},{10,8},{12,... | collective-permute-start | bytes 3538952 | tf_op jit(solution)/shard_map/ppermute | solution.py:259
  138.8 25.1 %collective-permute-start.9 = (bf16[64,2304]{1,0:T(8,128)(2,1)}, bf16[64,2304]{1,0:T(8,128)(2,1)}, u32[]{:S(2)}, u32[]{:S(2)}) collective-permute-start(bf16[64,2304]{1,0:T(8,128)(2,1)} %slice.4), channel_id=1, source_target_pairs={{0,1},{1,0},{2,3},{3,2},{4,5},{5,4},{6,7},{7,6},{8,9},{9,8},{10,11... | collective-permute-start | bytes 884744 | tf_op jit(solution)/shard_map/ppermute | solution.py:259
Sparse Core Ops, SparseCore 0:
  9.8 30.7 all-gather.5
  42.5 28.7 all-gather.3
  98.1 38.9 reduce-scatter.1

commit v10 on v9

--- a/solution.py
+++ b/solution.py
@@ -159,7 +159,7 @@
         ),
         out_shape=[jax.ShapeDtypeStruct((size, width), BF) for size in sizes],
         compiler_params=params(),
-        cost_estimate=PRODUCT,
+        cost_estimate=cost(10**12 if len(offsets) > 1 else 1, 1),
     )(place, after, *[panel] * len(blocks), near, far)
 
 

time: 174 us -> 173 us (level)
    ppermute x10, waiting for transfers between devices: 55.9 us -> 48.5 us  [shift(): return lax.ppermute(array, axis, ring(lax.axis_size(axis), step))]
    reduce_scatter x1, waiting for transfers between devices: 4.08 us -> 11.2 us  [per_device(): lax.psum_scatter(product, ('y', 'k'), scatter_dimension=0, tiled=True)]
  transfers between devices with their start and end apart: 15 -> 15, of which waited for: 9 -> 8; matrix products, arithmetic and copies ran while one was open for 3% -> 3% of each run, Pallas kernels for 23% -> 28%
where the time goes in v10:
time: 173 us; the launch traced here: 172 us
  waiting for transfers between devices  68.2 us (39%)
  Pallas kernels  49.7 us (29%)
  starting transfers between devices  35 us (20%)
  between operations  13.8 us (8%)
  other arithmetic  3.28 us (2%)
    ppermute x10, waiting for transfers between devices, shift(): return lax.ppermute(array, axis, ring(lax.axis_size(axis), step))  48.5 us
    ppermute x10, starting transfers between devices, shift(): return lax.ppermute(array, axis, ring(lax.axis_size(axis), step))  23.2 us
    pallas_call x2, Pallas kernels, weight_grad(): pl.pallas_call(functools.partial(weight_grad_kernel, len(offsets)), grid_...  14.2 us
    pallas_call x4, Pallas kernels, local(): pl.pallas_call(lambda *refs: kernel(*refs[len(after):]), out_shape=[jax.S...  11.3 us
    reduce_scatter x1, waiting for transfers between devices, per_device(): lax.psum_scatter(product, ('y', 'k'), scatter_dimension=0, tiled=True)  11.2 us
    pallas_call x1, Pallas kernels, backward(): pl.pallas_call(backward_kernel, grid=(2,), out_shape=jax.ShapeDtypeStruct...  9.65 us
    pallas_call x1, Pallas kernels, forward(): pl.pallas_call(forward_kernel, grid=(width // tile,), out_shape=jax.Shape...  9.48 us
    all_to_all x1, waiting for transfers between devices, per_device(): panel = lax.all_to_all(split, ('zl', 'zh'), 0, 0, tiled=True)  7.57 us
  transfers between devices with their start and end apart: 15, of which 8 were waited for; matrix products, arithmetic and copies ran while one was open for 3% of the time, Pallas kernels for 28%

profile of v10, /device:TPU:32, one launch (start us, length us, event | category | flops | bytes accessed | tf_op | source)
XLA Modules:
  0.0 171.7 jit_solution(10075709084439698664)
XLA Ops:
  7.9 2.4 %shard_map.68 = (bf16[128,2304]{1,0:T(8,128)(2,1)}, bf16[128,2304]{1,0:T(8,128)(2,1)}) custom-call(f32[2,18]{1,0:T(2,128)} %scales.1, bf16[256,2304]{1,0:T(8,128)(2,1)} %quantized.1), custom_call_target="tpu_custom_call" | custom-call | flops 1 | bytes 1 | tf_op jit(solution)/shard_map/pallas_call | solution.py:46
  13.6 6.3 %collective-permute-start = (bf16[64,2304]{1,0:T(8,128)(2,1)}, bf16[64,2304]{1,0:T(8,128)(2,1)}, u32[]{:S(2)}, u32[]{:S(2)}) collective-permute-start(bf16[64,2304]{1,0:T(8,128)(2,1)} %bitcast.12), channel_id=1, source_target_pairs={{0,1},{1,0},{2,3},{3,2},{4,5},{5,4},{6,7},{7,6},{8,9},{9,8},{10,11... | collective-permute-start | bytes 884744 | tf_op jit(solution)/shard_map/ppermute | solution.py:259
  19.9 2.6 %shard_map.67.__1_ = bf16[8,512,256]{2,1,0:T(8,128)(2,1)} custom-call(bf16[512,512]{1,0:T(8,128)(2,1)} %bitcast.11), custom_call_target="tpu_custom_call" | custom-call | flops 1 | bytes 1 | tf_op jit(solution)/shard_map/pallas_call | solution.py:63
  22.5 10.5 %collective-permute-done.__0_ = bf16[64,2304]{1,0:T(8,128)(2,1)} collective-permute-done((bf16[64,2304]{1,0:T(8,128)(2,1)}, bf16[64,2304]{1,0:T(8,128)(2,1)}, u32[]{:S(2)}, u32[]{:S(2)}) %collective-permute-start) | collective-permute-done | bytes 294944 | tf_op jit(solution)/shard_map/ppermute | solution.py:259
  33.1 7.4 %all-to-all-start.1 = ((bf16[8,512,256]{2,1,0:T(8,128)(2,1)}), bf16[8,512,256]{2,1,0:T(8,128)(2,1)}, u32[]{:S(2)}, u32[]{:S(2)}) async-start(bf16[8,512,256]{2,1,0:T(8,128)(2,1)} %shard_map.67.__1_), calls=%async_computation.1 | async-start | bytes 4194304 | tf_op jit(solution)/shard_map/all_to_all | solution.py:269
  40.5 3.1 %shard_map.70 = (bf16[256,2304]{1,0:T(8,128)(2,1)}, bf16[256,2304]{1,0:T(8,128)(2,1)}) custom-call(bf16[128,2304]{1,0:T(8,128)(2,1)} %get-tuple-element.14.refs_0_.refs_2_, bf16[128,2304]{1,0:T(8,128)(2,1)} %get-tuple-element.15.refs_1_.refs_3_, bf16[128,2304]{1,0:T(8,128)(2,1)} %collective-permute-done.1.__2_.refs_2_.refs_4_, ...), custom_call_target="tpu_custom_call" | custom-call | flops 1 | bytes 1 | tf_op jit(solution)/shard_map/pallas_call | solution.py:206
  44.0 2.9 %collective-permute-start.4 = (bf16[256,2304]{1,0:T(8,128)(2,1)}, bf16[256,2304]{1,0:T(8,128)(2,1)}, u32[]{:S(2)}, u32[]{:S(2)}) collective-permute-start(bf16[256,2304]{1,0:T(8,128)(2,1)} %get-tuple-element.17), channel_id=1, source_target_pairs={{0,6},{2,0},{4,2},{6,4},{1,7},{3,1},{5,3},{7,5},{8,14},{10,8},{12,... | collective-permute-start | bytes 3538952 | tf_op jit(solution)/shard_map/ppermute | solution.py:259
  47.5 23.6 %collective-permute-done.3.refs_5_.refs_3_ = bf16[256,2304]{1,0:T(8,128)(2,1)} collective-permute-done((bf16[256,2304]{1,0:T(8,128)(2,1)}, bf16[256,2304]{1,0:T(8,128)(2,1)}, u32[]{:S(2)}, u32[]{:S(2)}) %collective-permute-start.3) | collective-permute-done | bytes 1179680 | tf_op jit(solution)/shard_map/ppermute | solution.py:259
  71.3 9.7 %shard_map.71._ = bf16[8,512,256]{2,1,0:T(8,128)(2,1)} custom-call(s32[2]{0:T(128)} %pad_add_fusion.place, bf16[512,2304]{1,0:T(8,128)(2,1)} %bitcast.7, bf16[512,2304]{1,0:T(8,128)(2,1)} %all-gather.4.cloned.1.call-done.refs_1_.refs_3_.refs_7_, bf16[128,2304]{1,0:T(8,128)(2,1)} %get-tuple-element.14.refs_0_.refs_2_, ...), custom_call_target="tpu_custom_call" | custom-call | flops 1 | bytes 1 | tf_op jit(solution)/shard_map/pallas_call | solution.py:181
  80.9 7.6 %all-to-all-done.1.panel.refs_0_.refs_1_.refs_2_.refs_3_.refs_4_.refs_5_ = bf16[8,512,256]{2,1,0:T(8,128)(2,1)} async-done(((bf16[8,512,256]{2,1,0:T(8,128)(2,1)}), bf16[8,512,256]{2,1,0:T(8,128)(2,1)}, u32[]{:S(2)}, u32[]{:S(2)}) %all-to-all-start.1) | async-done | bytes 2097184 | tf_op jit(solution)/shard_map/all_to_all | solution.py:269
  88.5 4.3 %all-to-all-start = ((bf16[8,512,256]{2,1,0:T(8,128)(2,1)}), bf16[8,512,256]{2,1,0:T(8,128)(2,1)}, u32[]{:S(2)}, u32[]{:S(2)}) async-start(bf16[8,512,256]{2,1,0:T(8,128)(2,1)} %shard_map.71._), calls=%async_computation | async-start | bytes 4194304 | tf_op jit(solution)/shard_map/all_to_all | solution.py:287
  92.8 9.5 %shard_map.73._ = bf16[1024,2304]{1,0:T(8,128)(2,1)} custom-call(s32[2]{0:T(128)} %pad_add_fusion.place, bf16[8,512,256]{2,1,0:T(8,128)(2,1)} %shard_map.71._, bf16[8,512,256]{2,1,0:T(8,128)(2,1)} %all-to-all-done.1.panel.refs_0_.refs_1_.refs_2_.refs_3_.refs_4_.refs_5_, bf16[128,2304]{1,0:T(8,128)(2,1)} %get-tuple-element.14.refs_0_.refs_2_, ...), custom_call_target="tpu_custom_call" | custom-call | flops 1 | bytes 1 | tf_op jit(solution)/shard_map/pallas_call | solution.py:109
  102.3 5.8 %shard_map.74 = (bf16[128,2304]{1,0:T(8,128)(2,1)}, bf16[128,2304]{1,0:T(8,128)(2,1)}) custom-call(s32[2]{0:T(128)} %pad_add_fusion.place, bf16[1024,2304]{1,0:T(8,128)(2,1)} %shard_map.73._, bf16[8,512,256]{2,1,0:T(8,128)(2,1)} %all-to-all-done.1.panel.refs_0_.refs_1_.refs_2_.refs_3_.refs_4_.refs_5_, ...), custom_call_target="tpu_custom_call" | custom-call | flops 1 | bytes 1 | tf_op jit(solution)/shard_map/pallas_call | solution.py:151
  110.2 8.4 %shard_map.75 = (bf16[256,2304]{1,0:T(8,128)(2,1)}, bf16[256,2304]{1,0:T(8,128)(2,1)}, bf16[256,2304]{1,0:T(8,128)(2,1)}) custom-call(s32[2]{0:T(128)} %pad_add_fusion.place, bf16[128,2304]{1,0:T(8,128)(2,1)} %get-tuple-element.18._, bf16[8,512,256]{2,1,0:T(8,128)(2,1)} %all-to-all-done.1.panel.refs_0_.refs_1_.refs_2_.refs_3_.refs_4_.refs_5_, ...), custom_call_target="tpu_custom_call" | custom-call | flops 999999995904 | bytes 1 | tf_op jit(solution)/shard_map/pallas_call | solution.py:151
  118.6 5.1 %collective-permute-done.6.refs_3_ = bf16[128,2304]{1,0:T(8,128)(2,1)} collective-permute-done((bf16[128,2304]{1,0:T(8,128)(2,1)}, bf16[128,2304]{1,0:T(8,128)(2,1)}, u32[]{:S(2)}, u32[]{:S(2)}) %collective-permute-start.6) | collective-permute-done | bytes 589856 | tf_op jit(solution)/shard_map/ppermute | solution.py:259
  123.7 2.5 %collective-permute-done.5.refs_2_ = bf16[128,2304]{1,0:T(8,128)(2,1)} collective-permute-done((bf16[128,2304]{1,0:T(8,128)(2,1)}, bf16[128,2304]{1,0:T(8,128)(2,1)}, u32[]{:S(2)}, u32[]{:S(2)}) %collective-permute-start.5) | collective-permute-done | bytes 589856 | tf_op jit(solution)/shard_map/ppermute | solution.py:259
  126.2 3.7 %shard_map.76 = (bf16[256,2304]{1,0:T(8,128)(2,1)}, bf16[256,2304]{1,0:T(8,128)(2,1)}) custom-call(bf16[256,2304]{1,0:T(8,128)(2,1)} %get-tuple-element.20.refs_0_, bf16[256,2304]{1,0:T(8,128)(2,1)} %get-tuple-element.21.refs_1_, bf16[128,2304]{1,0:T(8,128)(2,1)} %collective-permute-done.5.refs_2_, bf16[128,2304]{1,0:T(8,128)(2,1)} %collective-permute-done.6.refs_3_), custom_call_target="tpu_custom_call" | custom-call | flops 1 | bytes 1 | tf_op jit(solution)/shard_map/pallas_call | solution.py:206
  129.8 3.2 %collective-permute-start.8 = (bf16[256,2304]{1,0:T(8,128)(2,1)}, bf16[256,2304]{1,0:T(8,128)(2,1)S(1)}, u32[]{:S(2)}, u32[]{:S(2)}) collective-permute-start(bf16[256,2304]{1,0:T(8,128)(2,1)} %get-tuple-element.24), channel_id=1, source_target_pairs={{0,6},{2,0},{4,2},{6,4},{1,7},{3,1},{5,3},{7,5},{8,14},{10,8},{12,... | collective-permute-start | bytes 3538952 | tf_op jit(solution)/shard_map/ppermute | solution.py:259
  133.1 11.2 %reduce-scatter.2.cloned.1.call-done.refs_2_ = bf16[128,2304]{1,0:T(8,128)(2,1)} async-done(((bf16[1024,2304]{1,0:T(8,128)(2,1)}), bf16[128,2304]{1,0:T(8,128)(2,1)}) %reduce-scatter.2.cloned.1.call-update) | async-done | bytes 589840 | tf_op jit(solution)/shard_map/reduce_scatter | solution.py:295
  146.0 5.2 %collective-permute-start.9 = (bf16[64,2304]{1,0:T(8,128)(2,1)}, bf16[64,2304]{1,0:T(8,128)(2,1)}, u32[]{:S(2)}, u32[]{:S(2)}) collective-permute-start(bf16[64,2304]{1,0:T(8,128)(2,1)} %slice.4), channel_id=1, source_target_pairs={{0,1},{1,0},{2,3},{3,2},{4,5},{5,4},{6,7},{7,6},{8,9},{9,8},{10,11... | collective-permute-start | bytes 884744 | tf_op jit(solution)/shard_map/ppermute | solution.py:259
  151.1 6.8 %collective-permute-done.7 = bf16[256,2304]{1,0:T(8,128)(2,1)S(1)} collective-permute-done((bf16[256,2304]{1,0:T(8,128)(2,1)}, bf16[256,2304]{1,0:T(8,128)(2,1)S(1)}, u32[]{:S(2)}, u32[]{:S(2)}) %collective-permute-start.7) | collective-permute-done | bytes 1179680 | tf_op jit(solution)/shard_map/ppermute | solution.py:259
  157.9 2.7 %add_convert_fusion.refs_1_ = bf16[256,2304]{1,0:T(8,128)(2,1)} fusion(bf16[256,2304]{1,0:T(8,128)(2,1)S(1)} %collective-permute-done.8, bf16[256,2304]{1,0:T(8,128)(2,1)S(1)} %collective-permute-done.7, bf16[256,2304]{1,0:T(8,128)(2,1)} %get-tuple-element.19), kind=kLoop, calls=%fused_computation | loop fusion | flops 3538944 | bytes 4718592 | tf_op jit(solution)/shard_map/convert_element_type | solution.py:201
  160.6 2.6 %shard_map.72.refs_0_ = bf16[512,512]{1,0:T(8,128)(2,1)} custom-call(bf16[8,512,256]{2,1,0:T(8,128)(2,1)} %all-to-all-done.refs_0_), custom_call_target="tpu_custom_call" | custom-call | flops 1 | bytes 1 | tf_op jit(solution)/shard_map/pallas_call | solution.py:206
  163.3 1.9 %shard_map.77 = bf16[64,2304]{1,0:T(8,128)(2,1)} custom-call(bf16[512,512]{1,0:T(8,128)(2,1)} %shard_map.72.refs_0_, bf16[256,2304]{1,0:T(8,128)(2,1)} %add_convert_fusion.refs_1_, bf16[128,2304]{1,0:T(8,128)(2,1)} %reduce-scatter.2.cloned.1.call-done.refs_2_, bf16[64,2304]{1,0:T(8,128)(2,1)} %collective-permute-done.9.refs_3_), custom_call_target="tpu_custom_call" | custom-call | flops 1 | bytes 1 | tf_op jit(solution)/shard_map/pallas_call | solution.py:206
  (23 shorter events, 8.9 us)
Async XLA Ops:
  7.2 63.9 %all-gather.6.cloned.1.call-start = ((), (), s32[]{:S(2)}) async-start(), calls=%async_computation.5 | async-start | bytes 2654208 | tf_op jit(solution)/shard_map/all_gather | solution.py:267
  7.9 63.4 %all-gather.4.cloned.1.call-start = ((), (), s32[]{:S(2)}) async-start(), calls=%async_computation.3 | async-start | bytes 2654208 | tf_op jit(solution)/shard_map/all_gather | solution.py:275
  10.4 22.7 %collective-permute-start.1 = (bf16[128,2304]{1,0:T(8,128)(2,1)}, bf16[128,2304]{1,0:T(8,128)(2,1)}, u32[]{:S(2)}, u32[]{:S(2)}) collective-permute-start(bf16[128,2304]{1,0:T(8,128)(2,1)} %get-tuple-element.14.refs_0_.refs_2_), channel_id=1, source_target_pairs={{0,2},{2,4},{4,6},{6,0},{1,3},{3,5},{5,7},{7,1},{8,10},{10,12},{12... | collective-permute-start | bytes 1769480 | tf_op jit(solution)/shard_map/ppermute | solution.py:259
  11.9 21.2 %collective-permute-start.2 = (bf16[128,2304]{1,0:T(8,128)(2,1)}, bf16[128,2304]{1,0:T(8,128)(2,1)}, u32[]{:S(2)}, u32[]{:S(2)}) collective-permute-start(bf16[128,2304]{1,0:T(8,128)(2,1)} %get-tuple-element.15.refs_1_.refs_3_), channel_id=1, source_target_pairs={{0,6},{2,0},{4,2},{6,4},{1,7},{3,1},{5,3},{7,5},{8,14},{10,8},{12,... | collective-permute-start | bytes 1769480 | tf_op jit(solution)/shard_map/ppermute | solution.py:259
  13.6 19.5 %collective-permute-start = (bf16[64,2304]{1,0:T(8,128)(2,1)}, bf16[64,2304]{1,0:T(8,128)(2,1)}, u32[]{:S(2)}, u32[]{:S(2)}) collective-permute-start(bf16[64,2304]{1,0:T(8,128)(2,1)} %bitcast.12), channel_id=1, source_target_pairs={{0,1},{1,0},{2,3},{3,2},{4,5},{5,4},{6,7},{7,6},{8,9},{9,8},{10,11... | collective-permute-start | bytes 884744 | tf_op jit(solution)/shard_map/ppermute | solution.py:259
  33.1 55.4 %all-to-all-start.1 = ((bf16[8,512,256]{2,1,0:T(8,128)(2,1)}), bf16[8,512,256]{2,1,0:T(8,128)(2,1)}, u32[]{:S(2)}, u32[]{:S(2)}) async-start(bf16[8,512,256]{2,1,0:T(8,128)(2,1)} %shard_map.67.__1_), calls=%async_computation.1 | async-start | bytes 4194304 | tf_op jit(solution)/shard_map/all_to_all | solution.py:269
  43.6 27.4 %collective-permute-start.3 = (bf16[256,2304]{1,0:T(8,128)(2,1)}, bf16[256,2304]{1,0:T(8,128)(2,1)}, u32[]{:S(2)}, u32[]{:S(2)}) collective-permute-start(bf16[256,2304]{1,0:T(8,128)(2,1)} %get-tuple-element.16), channel_id=1, source_target_pairs={{0,2},{2,4},{4,6},{6,0},{1,3},{3,5},{5,7},{7,1},{8,10},{10,12},{12... | collective-permute-start | bytes 3538952 | tf_op jit(solution)/shard_map/ppermute | solution.py:259
  44.0 27.1 %collective-permute-start.4 = (bf16[256,2304]{1,0:T(8,128)(2,1)}, bf16[256,2304]{1,0:T(8,128)(2,1)}, u32[]{:S(2)}, u32[]{:S(2)}) collective-permute-start(bf16[256,2304]{1,0:T(8,128)(2,1)} %get-tuple-element.17), channel_id=1, source_target_pairs={{0,6},{2,0},{4,2},{6,4},{1,7},{3,1},{5,3},{7,5},{8,14},{10,8},{12,... | collective-permute-start | bytes 3538952 | tf_op jit(solution)/shard_map/ppermute | solution.py:259
  88.5 72.1 %all-to-all-start = ((bf16[8,512,256]{2,1,0:T(8,128)(2,1)}), bf16[8,512,256]{2,1,0:T(8,128)(2,1)}, u32[]{:S(2)}, u32[]{:S(2)}) async-start(bf16[8,512,256]{2,1,0:T(8,128)(2,1)} %shard_map.71._), calls=%async_computation | async-start | bytes 4194304 | tf_op jit(solution)/shard_map/all_to_all | solution.py:287
  92.8 51.5 %reduce-scatter.2.cloned.1.call-start = ((), (), s32[]{:S(2)}) async-start(), calls=%async_computation.4 | async-start | bytes 5308416 | tf_op jit(solution)/shard_map/reduce_scatter | solution.py:295
  108.2 15.5 %collective-permute-start.6 = (bf16[128,2304]{1,0:T(8,128)(2,1)}, bf16[128,2304]{1,0:T(8,128)(2,1)}, u32[]{:S(2)}, u32[]{:S(2)}) collective-permute-start(bf16[128,2304]{1,0:T(8,128)(2,1)} %get-tuple-element.22), channel_id=1, source_target_pairs={{0,6},{2,0},{4,2},{6,4},{1,7},{3,1},{5,3},{7,5},{8,14},{10,8},{12,... | collective-permute-start | bytes 1769480 | tf_op jit(solution)/shard_map/ppermute | solution.py:259
  109.7 16.4 %collective-permute-start.5 = (bf16[128,2304]{1,0:T(8,128)(2,1)}, bf16[128,2304]{1,0:T(8,128)(2,1)}, u32[]{:S(2)}, u32[]{:S(2)}) collective-permute-start(bf16[128,2304]{1,0:T(8,128)(2,1)} %get-tuple-element.18._), channel_id=1, source_target_pairs={{0,2},{2,4},{4,6},{6,0},{1,3},{3,5},{5,7},{7,1},{8,10},{10,12},{12... | collective-permute-start | bytes 1769480 | tf_op jit(solution)/shard_map/ppermute | solution.py:259
  129.8 28.1 %collective-permute-start.7 = (bf16[256,2304]{1,0:T(8,128)(2,1)}, bf16[256,2304]{1,0:T(8,128)(2,1)S(1)}, u32[]{:S(2)}, u32[]{:S(2)}) collective-permute-start(bf16[256,2304]{1,0:T(8,128)(2,1)} %get-tuple-element.23), channel_id=1, source_target_pairs={{0,2},{2,4},{4,6},{6,0},{1,3},{3,5},{5,7},{7,1},{8,10},{10,12},{12... | collective-permute-start | bytes 3538952 | tf_op jit(solution)/shard_map/ppermute | solution.py:259
  129.8 28.1 %collective-permute-start.8 = (bf16[256,2304]{1,0:T(8,128)(2,1)}, bf16[256,2304]{1,0:T(8,128)(2,1)S(1)}, u32[]{:S(2)}, u32[]{:S(2)}) collective-permute-start(bf16[256,2304]{1,0:T(8,128)(2,1)} %get-tuple-element.24), channel_id=1, source_target_pairs={{0,6},{2,0},{4,2},{6,4},{1,7},{3,1},{5,3},{7,5},{8,14},{10,8},{12,... | collective-permute-start | bytes 3538952 | tf_op jit(solution)/shard_map/ppermute | solution.py:259
  146.0 17.3 %collective-permute-start.9 = (bf16[64,2304]{1,0:T(8,128)(2,1)}, bf16[64,2304]{1,0:T(8,128)(2,1)}, u32[]{:S(2)}, u32[]{:S(2)}) collective-permute-start(bf16[64,2304]{1,0:T(8,128)(2,1)} %slice.4), channel_id=1, source_target_pairs={{0,1},{1,0},{2,3},{3,2},{4,5},{5,4},{6,7},{7,6},{8,9},{9,8},{10,11... | collective-permute-start | bytes 884744 | tf_op jit(solution)/shard_map/ppermute | solution.py:259
Sparse Core Ops, SparseCore 0:
  9.8 30.7 all-gather.5
  42.5 28.7 all-gather.3
  102.5 41.7 reduce-scatter.1

commit v11 on v10

--- a/solution.py
+++ b/solution.py
@@ -8,6 +8,7 @@
 from jax.sharding import Mesh, PartitionSpec as P
 
 BLOCK = 128
+COLLECT = 28 * 10**9
 BF = jnp.bfloat16
 F32 = jnp.float32
 VMEM_LIMIT = 64 * 1024 * 1024 - 4096
@@ -119,9 +120,14 @@
     )(place, after, panel, *weights)
 
 
+def far_tokens(place, e, kk):
+    block = lax.rem(place[2] - e + 4, 4) * 2 + lax.rem(place[3] + kk, 2)
+    return pl.multiple_of(block * 64, 64)
+
+
 def weight_grad_kernel(count, place, _, *refs):
-    panels, (near, far) = refs[: 2 * count], refs[2 * count : 2 * count + 2]
-    outs, left = refs[2 * count + 2 : -1], refs[-1]
+    panels, near, far = refs[: 2 * count], refs[2 * count], refs[2 * count + 1 :][:4]
+    outs, (left, right) = refs[2 * count + 5 : -2], refs[-2:]
 
     @pl.when(pl.program_id(0) == 0)
     def _():
@@ -130,7 +136,12 @@
             lanes = pl.ds(pl.multiple_of(s * 512, 512), 512)
             left[i // 2 * 256 : i // 2 * 256 + 256, lanes] = panel[0].T
 
-    total = jnp.dot(left[...], stacked((near, far)), preferred_element_type=F32)
+    right[:512, :] = near[...]
+    for e in range(4):
+        for kk in range(2):
+            rows = pl.ds(512 + far_tokens(place, e, kk), 64)
+            right[rows, :] = far[e][kk * 64 : kk * 64 + 64, :]
+    total = jnp.dot(left[...], right[...], preferred_element_type=F32)
     at = 0
     for out in outs:
         out[...] = total[at : at + out.shape[0]].astype(BF)
@@ -153,27 +164,38 @@
         grid_spec=pltpu.PrefetchScalarGridSpec(
             num_scalar_prefetch=1,
             grid=(width // tile,),
-            in_specs=[ANY, *blocks] + [pl.BlockSpec((512, tile), columns)] * 2,
+            in_specs=[ANY, *blocks]
+            + [pl.BlockSpec((rows, tile), columns) for rows in (512, *[128] * 4)],
             out_specs=[pl.BlockSpec((size, tile), columns) for size in sizes],
-            scratch_shapes=[pltpu.VMEM((256 * len(offsets), 1024), BF)],
+            scratch_shapes=[
+                pltpu.VMEM((256 * len(offsets), 1024), BF),
+                pltpu.VMEM((1024, tile), BF),
+            ],
         ),
         out_shape=[jax.ShapeDtypeStruct((size, width), BF) for size in sizes],
         compiler_params=params(),
         cost_estimate=cost(10**12 if len(offsets) > 1 else 1, 1),
-    )(place, after, *[panel] * len(blocks), near, far)
-
-
-def backward_kernel(place, *refs):
-    grads, weights, out = refs[:2], halves(*refs[2:8]), refs[8]
-    rows = pl.ds(pl.multiple_of(pl.program_id(0) * 256, 256), 256)
+    )(place, after, *[panel] * len(blocks), near, *far)
+
+
+def backward_kernel(place, near, *refs):
+    far, weights, out = refs[:4], halves(*refs[4:10]), refs[10]
+    step = pl.program_id(0)
+    rows = pl.ds(pl.multiple_of(step * 256, 256), 256)
+    far = stacked(far)
     for m in range(4):
         at = lax.rem(place[0] - m + 4, 4) * 2
         right = stacked(weights[2 * m : 2 * m + 2])
-        for s, grad in enumerate(grads):
-            total = lax.dot_general(
-                grad[...], right, (((1,), (1,)), ((), ())), preferred_element_type=F32
-            )
-            out[at + lax.rem(s + place[1], 2), rows, :] = total.astype(BF)
+        total = lax.dot_general(
+            near[...], right, (((1,), (1,)), ((), ())), preferred_element_type=F32
+        )
+        out[at + place[1], rows, :] = total.astype(BF)
+        total = lax.dot_general(
+            far, right, (((1,), (1,)), ((), ())), preferred_element_type=F32
+        ).astype(BF)
+        for e in range(4):
+            target = pl.ds(far_tokens(place, e, step), 64)
+            out[at + 1 - place[1], target, :] = total[e * 64 : e * 64 + 64]
 
 
 def backward(place, near, far, weights):
@@ -182,16 +204,13 @@
         backward_kernel,
         grid=(2,),
         out_shape=jax.ShapeDtypeStruct((8, 512, 256), BF),
-        in_specs=[
-            SCALAR,
-            pl.BlockSpec((256, width), lambda n: (n, 0)),
-            pl.BlockSpec((256, width), lambda n: (n, 0)),
-        ]
+        in_specs=[SCALAR]
+        + [pl.BlockSpec((rows, width), lambda n: (n, 0)) for rows in (256, *[64] * 4)]
         + [whole(w.shape) for w in weights],
         out_specs=whole((8, 512, 256)),
         compiler_params=params(),
         cost_estimate=PRODUCT,
-    )(place, near, far, *weights)
+    )(place, near, *far, *weights)
 
 
 def summed(*refs):
@@ -201,7 +220,7 @@
     return total.astype(BF)
 
 
-def local(kernel, outs, after, *args):
+def local(kernel, outs, after, *args, flops=1):
     after = after if isinstance(after, tuple) else (after,)
     return pl.pallas_call(
         lambda *refs: kernel(*refs[len(after) :]),
@@ -209,7 +228,7 @@
         in_specs=[ANY] * len(after) + [whole(a.shape) for a in args],
         out_specs=[whole(shape) for shape in outs],
         compiler_params=params(),
-        cost_estimate=cost(1, 1),
+        cost_estimate=cost(flops, 1),
     )(*after, *args)
 
 
@@ -224,8 +243,8 @@
     )(array, *after)
 
 
-def pass_kernel(source, out):
-    out[...] = source[...]
+def collect_kernel(mine, theirs, out):
+    out[:64], out[64:] = mine[...], theirs[...]
 
 
 def relay_kernel(top, bottom, top_up, bottom_down, up, down):
@@ -260,8 +279,8 @@
 
 
 def per_device(inputs, qweight, scales, grad_out):
-    x, zh = lax.axis_index("x"), lax.axis_index("zh")
-    place = jnp.stack([x, zh]).astype(jnp.int32)
+    names = ("x", "zh", "y", "k")
+    place = jnp.stack([lax.axis_index(name) for name in names]).astype(jnp.int32)
     F = qweight.shape[1]
 
     near = lax.all_gather(grad_out[0], ("y", "k"), axis=0, tiled=True)
@@ -271,8 +290,10 @@
     top, bottom = dequantize(scales, qweight)
     top_up, bottom_down = shift(top, "x", 1), shift(bottom, "x", -1)
     far = shift(grad_out[0], "zh", 1)
-    far = follow(far, (split, top_up, bottom_down))
-    far = lax.all_gather(far, ("y", "k"), axis=0, tiled=True)
+    (far,) = local(
+        collect_kernel, [(128, F)], (), far, shift(far, "k", 1), flops=COLLECT
+    )
+    far = [far] + [shift(far, "y", e) for e in (1, 2, 3)]
     up, down = local(
         relay_kernel, [(256, F)] * 2, (), top, bottom, top_up, bottom_down
     )

time: 173 us -> 175 us (1.012)
  waiting for transfers between devices: 68.2 us -> 60.5 us
  starting transfers between devices: 35 us -> 41.5 us
  Pallas kernels: 49.7 us -> 52.8 us
    all_to_all x1, waiting for transfers between devices: 7.57 us -> 0.01 us  [per_device(): panel = lax.all_to_all(split, ('zl', 'zh'), 0, 0, tiled=True)]
    all_to_all x1, starting transfers between devices: 4.31 us -> 8.75 us  [per_device(): sums = lax.all_to_all(sums, ('zl', 'zh'), 0, 0, tiled=True)]
    ppermute x10 -> x14, starting transfers between devices: 23.2 us -> 27.5 us  [shift(): return lax.ppermute(array, axis, ring(lax.axis_size(axis), step))]
    all_to_all x1, starting transfers between devices: 7.42 us -> 5.24 us  [per_device(): panel = lax.all_to_all(split, ('zl', 'zh'), 0, 0, tiled=True)]
    ppermute x10 -> x14, waiting for transfers between devices: 48.5 us -> 50.4 us  [shift(): return lax.ppermute(array, axis, ring(lax.axis_size(axis), step))]
    pallas_call x4 -> x5, Pallas kernels: 11.3 us -> 13.3 us  [local(): pl.pallas_call(lambda *refs: kernel(*refs[len(after):]), out_shape=[jax.S...]
    reduce_scatter x1, waiting for transfers between devices: 11.2 us -> 9.36 us  [per_device(): lax.psum_scatter(product, ('y', 'k'), scatter_dimension=0, tiled=True)]
  transfers between devices with their start and end apart: 15 -> 18, of which waited for: 8 -> 7; matrix products, arithmetic and copies ran while one was open for 3% -> 3% of each run, Pallas kernels for 28% -> 29%
where the time goes in v11:
time: 175 us; the launch traced here: 174 us
  waiting for transfers between devices  60.5 us (35%)
  Pallas kernels  52.8 us (30%)
  starting transfers between devices  41.5 us (24%)
  between operations  14.1 us (8%)
  other arithmetic  3.34 us (2%)
    ppermute x14, waiting for transfers between devices, shift(): return lax.ppermute(array, axis, ring(lax.axis_size(axis), step))  50.4 us
    ppermute x14, starting transfers between devices, shift(): return lax.ppermute(array, axis, ring(lax.axis_size(axis), step))  27.5 us
    pallas_call x2, Pallas kernels, weight_grad(): pl.pallas_call(functools.partial(weight_grad_kernel, len(offsets)), grid_...  15.2 us
    pallas_call x5, Pallas kernels, local(): pl.pallas_call(lambda *refs: kernel(*refs[len(after):]), out_shape=[jax.S...  13.3 us
    pallas_call x1, Pallas kernels, backward(): pl.pallas_call(backward_kernel, grid=(2,), out_shape=jax.ShapeDtypeStruct...  9.97 us
    pallas_call x1, Pallas kernels, forward(): pl.pallas_call(forward_kernel, grid=(width // tile,), out_shape=jax.Shape...  9.5 us
    reduce_scatter x1, waiting for transfers between devices, per_device(): lax.psum_scatter(product, ('y', 'k'), scatter_dimension=0, tiled=True)  9.36 us
    all_to_all x1, starting transfers between devices, per_device(): sums = lax.all_to_all(sums, ('zl', 'zh'), 0, 0, tiled=True)  8.75 us
  transfers between devices with their start and end apart: 18, of which 7 were waited for; matrix products, arithmetic and copies ran while one was open for 3% of the time, Pallas kernels for 29%

profile of v11, /device:TPU:32, one launch (start us, length us, event | category | flops | bytes accessed | tf_op | source)
XLA Modules:
  0.0 173.9 jit_solution(6230030860067674355)
XLA Ops:
  7.9 2.4 %shard_map.68 = (bf16[128,2304]{1,0:T(8,128)(2,1)}, bf16[128,2304]{1,0:T(8,128)(2,1)}) custom-call(f32[2,18]{1,0:T(2,128)} %scales.1, bf16[256,2304]{1,0:T(8,128)(2,1)} %quantized.1), custom_call_target="tpu_custom_call" | custom-call | flops 1 | bytes 1 | tf_op jit(solution)/shard_map/pallas_call | solution.py:47
  13.6 6.3 %collective-permute-start = (bf16[64,2304]{1,0:T(8,128)(2,1)}, bf16[64,2304]{1,0:T(8,128)(2,1)}, u32[]{:S(2)}, u32[]{:S(2)}) collective-permute-start(bf16[64,2304]{1,0:T(8,128)(2,1)} %bitcast.14), channel_id=1, source_target_pairs={{0,1},{1,0},{2,3},{3,2},{4,5},{5,4},{6,7},{7,6},{8,9},{9,8},{10,11... | collective-permute-start | bytes 884744 | tf_op jit(solution)/shard_map/ppermute | solution.py:278
  19.9 2.5 %shard_map.72 = bf16[8,512,256]{2,1,0:T(8,128)(2,1)} custom-call(bf16[512,512]{1,0:T(8,128)(2,1)} %bitcast.13), custom_call_target="tpu_custom_call" | custom-call | flops 1 | bytes 1 | tf_op jit(solution)/shard_map/pallas_call | solution.py:64
  22.3 5.2 %all-to-all-start.1 = ((bf16[8,512,256]{2,1,0:T(8,128)(2,1)}), bf16[8,512,256]{2,1,0:T(8,128)(2,1)}, u32[]{:S(2)}, u32[]{:S(2)}) async-start(bf16[8,512,256]{2,1,0:T(8,128)(2,1)} %shard_map.72), calls=%async_computation.1 | async-start | bytes 4194304 | tf_op jit(solution)/shard_map/all_to_all | solution.py:288
  27.6 9.5 %collective-permute-done.refs_0_ = bf16[64,2304]{1,0:T(8,128)(2,1)} collective-permute-done((bf16[64,2304]{1,0:T(8,128)(2,1)}, bf16[64,2304]{1,0:T(8,128)(2,1)}, u32[]{:S(2)}, u32[]{:S(2)}) %collective-permute-start) | collective-permute-done | bytes 294944 | tf_op jit(solution)/shard_map/ppermute | solution.py:278
  37.1 3.1 %shard_map.69 = (bf16[256,2304]{1,0:T(8,128)(2,1)}, bf16[256,2304]{1,0:T(8,128)(2,1)}) custom-call(bf16[128,2304]{1,0:T(8,128)(2,1)} %get-tuple-element.14.refs_0_.refs_4_, bf16[128,2304]{1,0:T(8,128)(2,1)} %get-tuple-element.15.refs_1_.refs_5_, bf16[128,2304]{1,0:T(8,128)(2,1)} %collective-permute-done.5.refs_2_.refs_6_, ...), custom_call_target="tpu_custom_call" | custom-call | flops 1 | bytes 1 | tf_op jit(solution)/shard_map/pallas_call | solution.py:225
  40.5 2.9 %collective-permute-start.8 = (bf16[256,2304]{1,0:T(8,128)(2,1)}, bf16[256,2304]{1,0:T(8,128)(2,1)}, u32[]{:S(2)}, u32[]{:S(2)}) collective-permute-start(bf16[256,2304]{1,0:T(8,128)(2,1)} %get-tuple-element.17), channel_id=1, source_target_pairs={{0,6},{2,0},{4,2},{6,4},{1,7},{3,1},{5,3},{7,5},{8,14},{10,8},{12,... | collective-permute-start | bytes 3538952 | tf_op jit(solution)/shard_map/ppermute | solution.py:278
  43.5 1.9 %shard_map.67.refs_0_.refs_3_.refs_7_ = bf16[128,2304]{1,0:T(8,128)(2,1)} custom-call(bf16[64,2304]{1,0:T(8,128)(2,1)} %collective-permute-done.refs_0_, bf16[64,2304]{1,0:T(8,128)(2,1)} %collective-permute-done.1.refs_1_), custom_call_target="tpu_custom_call" | custom-call | flops 28000000000 | bytes 1 | tf_op jit(solution)/shard_map/pallas_call | solution.py:225
  45.4 3.0 %collective-permute-start.4 = (bf16[128,2304]{1,0:T(8,128)(2,1)}, bf16[128,2304]{1,0:T(8,128)(2,1)}, u32[]{:S(2)}, u32[]{:S(2)}) collective-permute-start(bf16[128,2304]{1,0:T(8,128)(2,1)} %shard_map.67.refs_0_.refs_3_.refs_7_), channel_id=1, source_target_pairs={{0,192},{64,0},{128,64},{192,128},{1,193},{65,1},{129,65},{193,129... | collective-permute-start | bytes 1769480 | tf_op jit(solution)/shard_map/ppermute | solution.py:278
  50.7 23.4 %collective-permute-done.4.refs_3_.refs_6_.refs_10_ = bf16[128,2304]{1,0:T(8,128)(2,1)} collective-permute-done((bf16[128,2304]{1,0:T(8,128)(2,1)}, bf16[128,2304]{1,0:T(8,128)(2,1)}, u32[]{:S(2)}, u32[]{:S(2)}) %collective-permute-start.4) | collective-permute-done | bytes 589856 | tf_op jit(solution)/shard_map/ppermute | solution.py:278
  74.1 3.7 %collective-permute-done.2.refs_1_.refs_4_.refs_8_ = bf16[128,2304]{1,0:T(8,128)(2,1)} collective-permute-done((bf16[128,2304]{1,0:T(8,128)(2,1)}, bf16[128,2304]{1,0:T(8,128)(2,1)}, u32[]{:S(2)}, u32[]{:S(2)}) %collective-permute-start.2) | collective-permute-done | bytes 589856 | tf_op jit(solution)/shard_map/ppermute | solution.py:278
  77.8 10.0 %shard_map.70._ = bf16[8,512,256]{2,1,0:T(8,128)(2,1)} custom-call(s32[4]{0:T(128)} %pad_add_fusion.place, bf16[512,2304]{1,0:T(8,128)(2,1)} %bitcast.9, bf16[128,2304]{1,0:T(8,128)(2,1)} %shard_map.67.refs_0_.refs_3_.refs_7_, bf16[128,2304]{1,0:T(8,128)(2,1)} %collective-permute-done.2.refs_1_.refs_4_.refs_8_, ...), custom_call_target="tpu_custom_call" | custom-call | flops 1 | bytes 1 | tf_op jit(solution)/shard_map/pallas_call | solution.py:203
  87.8 8.8 %all-to-all-start = ((bf16[8,512,256]{2,1,0:T(8,128)(2,1)}), bf16[8,512,256]{2,1,0:T(8,128)(2,1)}, u32[]{:S(2)}, u32[]{:S(2)}) async-start(bf16[8,512,256]{2,1,0:T(8,128)(2,1)} %shard_map.70._), calls=%async_computation | async-start | bytes 4194304 | tf_op jit(solution)/shard_map/all_to_all | solution.py:308
  96.5 9.5 %shard_map.73._ = bf16[1024,2304]{1,0:T(8,128)(2,1)} custom-call(s32[4]{0:T(128)} %pad_add_fusion.place, bf16[8,512,256]{2,1,0:T(8,128)(2,1)} %shard_map.70._, bf16[8,512,256]{2,1,0:T(8,128)(2,1)} %all-to-all-done.1.panel.refs_0_.refs_1_.refs_2_.refs_3_.refs_4_.refs_5_, bf16[128,2304]{1,0:T(8,128)(2,1)} %get-tuple-element.14.refs_0_.refs_4_, ...), custom_call_target="tpu_custom_call" | custom-call | flops 1 | bytes 1 | tf_op jit(solution)/shard_map/pallas_call | solution.py:110
  106.0 6.3 %shard_map.74 = (bf16[128,2304]{1,0:T(8,128)(2,1)}, bf16[128,2304]{1,0:T(8,128)(2,1)}) custom-call(s32[4]{0:T(128)} %pad_add_fusion.place, bf16[1024,2304]{1,0:T(8,128)(2,1)} %shard_map.73._, bf16[8,512,256]{2,1,0:T(8,128)(2,1)} %all-to-all-done.1.panel.refs_0_.refs_1_.refs_2_.refs_3_.refs_4_.refs_5_, ...), custom_call_target="tpu_custom_call" | custom-call | flops 1 | bytes 1 | tf_op jit(solution)/shard_map/pallas_call | solution.py:162
  114.3 8.9 %shard_map.75 = (bf16[256,2304]{1,0:T(8,128)(2,1)}, bf16[256,2304]{1,0:T(8,128)(2,1)}, bf16[256,2304]{1,0:T(8,128)(2,1)}) custom-call(s32[4]{0:T(128)} %pad_add_fusion.place, bf16[128,2304]{1,0:T(8,128)(2,1)} %get-tuple-element.18._, bf16[8,512,256]{2,1,0:T(8,128)(2,1)} %all-to-all-done.1.panel.refs_0_.refs_1_.refs_2_.refs_3_.refs_4_.refs_5_, ...), custom_call_target="tpu_custom_call" | custom-call | flops 999999995904 | bytes 1 | tf_op jit(solution)/shard_map/pallas_call | solution.py:162
  123.2 4.1 %collective-permute-done.10.refs_3_ = bf16[128,2304]{1,0:T(8,128)(2,1)} collective-permute-done((bf16[128,2304]{1,0:T(8,128)(2,1)}, bf16[128,2304]{1,0:T(8,128)(2,1)}, u32[]{:S(2)}, u32[]{:S(2)}) %collective-permute-start.10) | collective-permute-done | bytes 589856 | tf_op jit(solution)/shard_map/ppermute | solution.py:278
  128.6 3.6 %shard_map.76 = (bf16[256,2304]{1,0:T(8,128)(2,1)}, bf16[256,2304]{1,0:T(8,128)(2,1)}) custom-call(bf16[256,2304]{1,0:T(8,128)(2,1)} %get-tuple-element.20.refs_0_, bf16[256,2304]{1,0:T(8,128)(2,1)} %get-tuple-element.21.refs_1_, bf16[128,2304]{1,0:T(8,128)(2,1)} %collective-permute-done.9.refs_2_, bf16[128,2304]{1,0:T(8,128)(2,1)} %collective-permute-done.10.refs_3_), custom_call_target="tpu_custom_call" | custom-call | flops 1 | bytes 1 | tf_op jit(solution)/shard_map/pallas_call | solution.py:225
  132.7 2.8 %collective-permute-start.12 = (bf16[256,2304]{1,0:T(8,128)(2,1)}, bf16[256,2304]{1,0:T(8,128)(2,1)S(1)}, u32[]{:S(2)}, u32[]{:S(2)}) collective-permute-start(bf16[256,2304]{1,0:T(8,128)(2,1)} %get-tuple-element.24), channel_id=1, source_target_pairs={{0,6},{2,0},{4,2},{6,4},{1,7},{3,1},{5,3},{7,5},{8,14},{10,8},{12,... | collective-permute-start | bytes 3538952 | tf_op jit(solution)/shard_map/ppermute | solution.py:278
  135.5 9.4 %reduce-scatter.2.cloned.1.call-done.refs_2_ = bf16[128,2304]{1,0:T(8,128)(2,1)} async-done(((bf16[1024,2304]{1,0:T(8,128)(2,1)}), bf16[128,2304]{1,0:T(8,128)(2,1)}) %reduce-scatter.2.cloned.1.call-update) | async-done | bytes 589840 | tf_op jit(solution)/shard_map/reduce_scatter | solution.py:316
  146.5 4.8 %collective-permute-start.13 = (bf16[64,2304]{1,0:T(8,128)(2,1)}, bf16[64,2304]{1,0:T(8,128)(2,1)}, u32[]{:S(2)}, u32[]{:S(2)}) collective-permute-start(bf16[64,2304]{1,0:T(8,128)(2,1)} %slice.4), channel_id=1, source_target_pairs={{0,1},{1,0},{2,3},{3,2},{4,5},{5,4},{6,7},{7,6},{8,9},{9,8},{10,11... | collective-permute-start | bytes 884744 | tf_op jit(solution)/shard_map/ppermute | solution.py:278
  151.4 8.4 %collective-permute-done.11 = bf16[256,2304]{1,0:T(8,128)(2,1)S(1)} collective-permute-done((bf16[256,2304]{1,0:T(8,128)(2,1)}, bf16[256,2304]{1,0:T(8,128)(2,1)S(1)}, u32[]{:S(2)}, u32[]{:S(2)}) %collective-permute-start.11) | collective-permute-done | bytes 1179680 | tf_op jit(solution)/shard_map/ppermute | solution.py:278
  159.8 2.7 %add_convert_fusion.refs_1_ = bf16[256,2304]{1,0:T(8,128)(2,1)} fusion(bf16[256,2304]{1,0:T(8,128)(2,1)S(1)} %collective-permute-done.12, bf16[256,2304]{1,0:T(8,128)(2,1)S(1)} %collective-permute-done.11, bf16[256,2304]{1,0:T(8,128)(2,1)} %get-tuple-element.19), kind=kLoop, calls=%fused_computation | loop fusion | flops 3538944 | bytes 4718592 | tf_op jit(solution)/shard_map/convert_element_type | solution.py:220
  162.5 2.6 %shard_map.71.refs_0_ = bf16[512,512]{1,0:T(8,128)(2,1)} custom-call(bf16[8,512,256]{2,1,0:T(8,128)(2,1)} %all-to-all-done.refs_0_), custom_call_target="tpu_custom_call" | custom-call | flops 1 | bytes 1 | tf_op jit(solution)/shard_map/pallas_call | solution.py:225
  (28 shorter events, 14.0 us)
Async XLA Ops:
  7.2 70.6 %all-gather.3.cloned.1.call-start = ((), (), s32[]{:S(2)}) async-start(), calls=%async_computation.4 | async-start | bytes 2654208 | tf_op jit(solution)/shard_map/all_gather | solution.py:286
  10.3 26.7 %collective-permute-start.5 = (bf16[128,2304]{1,0:T(8,128)(2,1)}, bf16[128,2304]{1,0:T(8,128)(2,1)}, u32[]{:S(2)}, u32[]{:S(2)}) collective-permute-start(bf16[128,2304]{1,0:T(8,128)(2,1)} %get-tuple-element.14.refs_0_.refs_4_), channel_id=1, source_target_pairs={{0,2},{2,4},{4,6},{6,0},{1,3},{3,5},{5,7},{7,1},{8,10},{10,12},{12... | collective-permute-start | bytes 1769480 | tf_op jit(solution)/shard_map/ppermute | solution.py:278
  11.8 25.3 %collective-permute-start.6 = (bf16[128,2304]{1,0:T(8,128)(2,1)}, bf16[128,2304]{1,0:T(8,128)(2,1)}, u32[]{:S(2)}, u32[]{:S(2)}) collective-permute-start(bf16[128,2304]{1,0:T(8,128)(2,1)} %get-tuple-element.15.refs_1_.refs_5_), channel_id=1, source_target_pairs={{0,6},{2,0},{4,2},{6,4},{1,7},{3,1},{5,3},{7,5},{8,14},{10,8},{12,... | collective-permute-start | bytes 1769480 | tf_op jit(solution)/shard_map/ppermute | solution.py:278
  13.6 23.5 %collective-permute-start = (bf16[64,2304]{1,0:T(8,128)(2,1)}, bf16[64,2304]{1,0:T(8,128)(2,1)}, u32[]{:S(2)}, u32[]{:S(2)}) collective-permute-start(bf16[64,2304]{1,0:T(8,128)(2,1)} %bitcast.14), channel_id=1, source_target_pairs={{0,1},{1,0},{2,3},{3,2},{4,5},{5,4},{6,7},{7,6},{8,9},{9,8},{10,11... | collective-permute-start | bytes 884744 | tf_op jit(solution)/shard_map/ppermute | solution.py:278
  22.3 65.4 %all-to-all-start.1 = ((bf16[8,512,256]{2,1,0:T(8,128)(2,1)}), bf16[8,512,256]{2,1,0:T(8,128)(2,1)}, u32[]{:S(2)}, u32[]{:S(2)}) async-start(bf16[8,512,256]{2,1,0:T(8,128)(2,1)} %shard_map.72), calls=%async_computation.1 | async-start | bytes 4194304 | tf_op jit(solution)/shard_map/all_to_all | solution.py:288
  37.1 6.4 %collective-permute-start.1 = (bf16[64,2304]{1,0:T(8,128)(2,1)}, bf16[64,2304]{1,0:T(8,128)(2,1)}, u32[]{:S(2)}, u32[]{:S(2)}) collective-permute-start(bf16[64,2304]{1,0:T(8,128)(2,1)} %collective-permute-done.refs_0_), channel_id=1, source_target_pairs={{0,32},{32,0},{1,33},{33,1},{2,34},{34,2},{3,35},{35,3},{4,36},{36... | collective-permute-start | bytes 884744 | tf_op jit(solution)/shard_map/ppermute | solution.py:278
  40.2 37.5 %collective-permute-start.7 = (bf16[256,2304]{1,0:T(8,128)(2,1)}, bf16[256,2304]{1,0:T(8,128)(2,1)}, u32[]{:S(2)}, u32[]{:S(2)}) collective-permute-start(bf16[256,2304]{1,0:T(8,128)(2,1)} %get-tuple-element.16), channel_id=1, source_target_pairs={{0,2},{2,4},{4,6},{6,0},{1,3},{3,5},{5,7},{7,1},{8,10},{10,12},{12... | collective-permute-start | bytes 3538952 | tf_op jit(solution)/shard_map/ppermute | solution.py:278
  40.5 37.2 %collective-permute-start.8 = (bf16[256,2304]{1,0:T(8,128)(2,1)}, bf16[256,2304]{1,0:T(8,128)(2,1)}, u32[]{:S(2)}, u32[]{:S(2)}) collective-permute-start(bf16[256,2304]{1,0:T(8,128)(2,1)} %get-tuple-element.17), channel_id=1, source_target_pairs={{0,6},{2,0},{4,2},{6,4},{1,7},{3,1},{5,3},{7,5},{8,14},{10,8},{12,... | collective-permute-start | bytes 3538952 | tf_op jit(solution)/shard_map/ppermute | solution.py:278
  45.4 28.7 %collective-permute-start.4 = (bf16[128,2304]{1,0:T(8,128)(2,1)}, bf16[128,2304]{1,0:T(8,128)(2,1)}, u32[]{:S(2)}, u32[]{:S(2)}) collective-permute-start(bf16[128,2304]{1,0:T(8,128)(2,1)} %shard_map.67.refs_0_.refs_3_.refs_7_), channel_id=1, source_target_pairs={{0,192},{64,0},{128,64},{192,128},{1,193},{65,1},{129,65},{193,129... | collective-permute-start | bytes 1769480 | tf_op jit(solution)/shard_map/ppermute | solution.py:278
  48.4 25.6 %collective-permute-start.3 = (bf16[128,2304]{1,0:T(8,128)(2,1)}, bf16[128,2304]{1,0:T(8,128)(2,1)}, u32[]{:S(2)}, u32[]{:S(2)}) collective-permute-start(bf16[128,2304]{1,0:T(8,128)(2,1)} %shard_map.67.refs_0_.refs_3_.refs_7_), channel_id=1, source_target_pairs={{0,128},{64,192},{128,0},{192,64},{1,129},{65,193},{129,1},{193,65... | collective-permute-start | bytes 1769480 | tf_op jit(solution)/shard_map/ppermute | solution.py:278
  49.1 28.7 %collective-permute-start.2 = (bf16[128,2304]{1,0:T(8,128)(2,1)}, bf16[128,2304]{1,0:T(8,128)(2,1)}, u32[]{:S(2)}, u32[]{:S(2)}) collective-permute-start(bf16[128,2304]{1,0:T(8,128)(2,1)} %shard_map.67.refs_0_.refs_3_.refs_7_), channel_id=1, source_target_pairs={{0,64},{64,128},{128,192},{192,0},{1,65},{65,129},{129,193},{193,1... | collective-permute-start | bytes 1769480 | tf_op jit(solution)/shard_map/ppermute | solution.py:278
  87.8 74.8 %all-to-all-start = ((bf16[8,512,256]{2,1,0:T(8,128)(2,1)}), bf16[8,512,256]{2,1,0:T(8,128)(2,1)}, u32[]{:S(2)}, u32[]{:S(2)}) async-start(bf16[8,512,256]{2,1,0:T(8,128)(2,1)} %shard_map.70._), calls=%async_computation | async-start | bytes 4194304 | tf_op jit(solution)/shard_map/all_to_all | solution.py:308
  96.5 48.3 %reduce-scatter.2.cloned.1.call-start = ((), (), s32[]{:S(2)}) async-start(), calls=%async_computation.3 | async-start | bytes 5308416 | tf_op jit(solution)/shard_map/reduce_scatter | solution.py:316
  112.3 15.0 %collective-permute-start.10 = (bf16[128,2304]{1,0:T(8,128)(2,1)}, bf16[128,2304]{1,0:T(8,128)(2,1)}, u32[]{:S(2)}, u32[]{:S(2)}) collective-permute-start(bf16[128,2304]{1,0:T(8,128)(2,1)} %get-tuple-element.22), channel_id=1, source_target_pairs={{0,6},{2,0},{4,2},{6,4},{1,7},{3,1},{5,3},{7,5},{8,14},{10,8},{12,... | collective-permute-start | bytes 1769480 | tf_op jit(solution)/shard_map/ppermute | solution.py:278
  112.6 16.0 %collective-permute-start.9 = (bf16[128,2304]{1,0:T(8,128)(2,1)}, bf16[128,2304]{1,0:T(8,128)(2,1)}, u32[]{:S(2)}, u32[]{:S(2)}) collective-permute-start(bf16[128,2304]{1,0:T(8,128)(2,1)} %get-tuple-element.18._), channel_id=1, source_target_pairs={{0,2},{2,4},{4,6},{6,0},{1,3},{3,5},{5,7},{7,1},{8,10},{10,12},{12... | collective-permute-start | bytes 1769480 | tf_op jit(solution)/shard_map/ppermute | solution.py:278
  132.2 27.6 %collective-permute-start.11 = (bf16[256,2304]{1,0:T(8,128)(2,1)}, bf16[256,2304]{1,0:T(8,128)(2,1)S(1)}, u32[]{:S(2)}, u32[]{:S(2)}) collective-permute-start(bf16[256,2304]{1,0:T(8,128)(2,1)} %get-tuple-element.23), channel_id=1, source_target_pairs={{0,2},{2,4},{4,6},{6,0},{1,3},{3,5},{5,7},{7,1},{8,10},{10,12},{12... | collective-permute-start | bytes 3538952 | tf_op jit(solution)/shard_map/ppermute | solution.py:278
  132.7 27.1 %collective-permute-start.12 = (bf16[256,2304]{1,0:T(8,128)(2,1)}, bf16[256,2304]{1,0:T(8,128)(2,1)S(1)}, u32[]{:S(2)}, u32[]{:S(2)}) collective-permute-start(bf16[256,2304]{1,0:T(8,128)(2,1)} %get-tuple-element.24), channel_id=1, source_target_pairs={{0,6},{2,0},{4,2},{6,4},{1,7},{3,1},{5,3},{7,5},{8,14},{10,8},{12,... | collective-permute-start | bytes 3538952 | tf_op jit(solution)/shard_map/ppermute | solution.py:278
  146.5 18.6 %collective-permute-start.13 = (bf16[64,2304]{1,0:T(8,128)(2,1)}, bf16[64,2304]{1,0:T(8,128)(2,1)}, u32[]{:S(2)}, u32[]{:S(2)}) collective-permute-start(bf16[64,2304]{1,0:T(8,128)(2,1)} %slice.4), channel_id=1, source_target_pairs={{0,1},{1,0},{2,3},{3,2},{4,5},{5,4},{6,7},{7,6},{8,9},{9,8},{10,11... | collective-permute-start | bytes 884744 | tf_op jit(solution)/shard_map/ppermute | solution.py:278
Sparse Core Ops, SparseCore 0:
  9.8 30.7 all-gather.2
  106.2 38.6 reduce-scatter.1

commit v12 on v11

--- a/solution.py
+++ b/solution.py
@@ -140,7 +140,8 @@
     for e in range(4):
         for kk in range(2):
             rows = pl.ds(512 + far_tokens(place, e, kk), 64)
-            right[rows, :] = far[e][kk * 64 : kk * 64 + 64, :]
+            source = far[e // 2 * 2 + kk]
+            right[rows, :] = source[e % 2 * 64 : e % 2 * 64 + 64, :]
     total = jnp.dot(left[...], right[...], preferred_element_type=F32)
     at = 0
     for out in outs:
@@ -193,9 +194,9 @@
         total = lax.dot_general(
             far, right, (((1,), (1,)), ((), ())), preferred_element_type=F32
         ).astype(BF)
-        for e in range(4):
-            target = pl.ds(far_tokens(place, e, step), 64)
-            out[at + 1 - place[1], target, :] = total[e * 64 : e * 64 + 64]
+        for i in range(4):
+            target = pl.ds(far_tokens(place, i // 2 * 2 + step, i % 2), 64)
+            out[at + 1 - place[1], target, :] = total[i * 64 : i * 64 + 64]
 
 
 def backward(place, near, far, weights):
@@ -243,8 +244,9 @@
     )(array, *after)
 
 
-def collect_kernel(mine, theirs, out):
-    out[:64], out[64:] = mine[...], theirs[...]
+def collect_kernel(*refs):
+    for e, ref in enumerate(refs[:4]):
+        refs[4 + e // 2][e % 2 * 64 : e % 2 * 64 + 64, :] = ref[...]
 
 
 def relay_kernel(top, bottom, top_up, bottom_down, up, down):
@@ -290,13 +292,12 @@
     top, bottom = dequantize(scales, qweight)
     top_up, bottom_down = shift(top, "x", 1), shift(bottom, "x", -1)
     far = shift(grad_out[0], "zh", 1)
-    (far,) = local(
-        collect_kernel, [(128, F)], (), far, shift(far, "k", 1), flops=COLLECT
-    )
     far = [far] + [shift(far, "y", e) for e in (1, 2, 3)]
     up, down = local(
         relay_kernel, [(256, F)] * 2, (), top, bottom, top_up, bottom_down
     )
+    mine = local(collect_kernel, [(128, F)] * 2, up, *far, flops=COLLECT)
+    far = [part for own in mine for part in (own, shift(own, "k", 1))]
     up, down = shift(up, "x", 1), shift(down, "x", -1)
     weights = (top, bottom, top_up, up, down, bottom_down)
 

time: 175 us -> 165 us (0.943)
  waiting for transfers between devices: 60.5 us -> 52.1 us
    ppermute x14 -> x15, waiting for transfers between devices: 50.4 us -> 39.1 us  [shift(): return lax.ppermute(array, axis, ring(lax.axis_size(axis), step))]
    reduce_scatter x1, waiting for transfers between devices: 9.36 us -> 12.3 us  [per_device(): lax.psum_scatter(product, ('y', 'k'), scatter_dimension=0, tiled=True)]
    ppermute x14 -> x15, starting transfers between devices: 27.5 us -> 27 us  [shift(): return lax.ppermute(array, axis, ring(lax.axis_size(axis), step))]
  transfers between devices with their start and end apart: 18 -> 19, of which waited for: 7 -> 12; matrix products, arithmetic and copies ran while one was open for 3% -> 3% of each run, Pallas kernels for 29% -> 31%
where the time goes in v12:
time: 165 us; the launch traced here: 164 us
  Pallas kernels  53.4 us (32%)
  waiting for transfers between devices  52.1 us (32%)
  starting transfers between devices  39.8 us (24%)
  between operations  14.1 us (9%)
  other arithmetic  3.26 us (2%)
  local copies, waits for them, and re-layouts  1.69 us (1%)
    ppermute x15, waiting for transfers between devices, shift(): return lax.ppermute(array, axis, ring(lax.axis_size(axis), step))  39.1 us
    ppermute x15, starting transfers between devices, shift(): return lax.ppermute(array, axis, ring(lax.axis_size(axis), step))  27 us
    pallas_call x2, Pallas kernels, weight_grad(): pl.pallas_call(functools.partial(weight_grad_kernel, len(offsets)), grid_...  15.5 us
    pallas_call x5, Pallas kernels, local(): pl.pallas_call(lambda *refs: kernel(*refs[len(after):]), out_shape=[jax.S...  13.6 us
    reduce_scatter x1, waiting for transfers between devices, per_device(): lax.psum_scatter(product, ('y', 'k'), scatter_dimension=0, tiled=True)  12.3 us
    pallas_call x1, Pallas kernels, backward(): pl.pallas_call(backward_kernel, grid=(2,), out_shape=jax.ShapeDtypeStruct...  9.86 us
    pallas_call x1, Pallas kernels, forward(): pl.pallas_call(forward_kernel, grid=(width // tile,), out_shape=jax.Shape...  9.53 us
    all_to_all x1, starting transfers between devices, per_device(): sums = lax.all_to_all(sums, ('zl', 'zh'), 0, 0, tiled=True)  7.51 us
  transfers between devices with their start and end apart: 19, of which 12 were waited for; matrix products, arithmetic and copies ran while one was open for 3% of the time, Pallas kernels for 31%

profile of v12, /device:TPU:32, one launch (start us, length us, event | category | flops | bytes accessed | tf_op | source)
XLA Modules:
  0.0 164.3 jit_solution(4515228127264391176)
XLA Ops:
  7.9 2.4 %shard_map.67 = (bf16[128,2304]{1,0:T(8,128)(2,1)}, bf16[128,2304]{1,0:T(8,128)(2,1)}) custom-call(f32[2,18]{1,0:T(2,128)} %scales.1, bf16[256,2304]{1,0:T(8,128)(2,1)} %quantized.1), custom_call_target="tpu_custom_call" | custom-call | flops 1 | bytes 1 | tf_op jit(solution)/shard_map/pallas_call | solution.py:47
  13.6 6.3 %collective-permute-start.2 = (bf16[64,2304]{1,0:T(8,128)(2,1)}, bf16[64,2304]{1,0:T(8,128)(2,1)}, u32[]{:S(2)}, u32[]{:S(2)}) collective-permute-start(bf16[64,2304]{1,0:T(8,128)(2,1)} %bitcast.14), channel_id=1, source_target_pairs={{0,1},{1,0},{2,3},{3,2},{4,5},{5,4},{6,7},{7,6},{8,9},{9,8},{10,11... | collective-permute-start | bytes 884744 | tf_op jit(solution)/shard_map/ppermute | solution.py:280
  19.9 2.5 %shard_map.72 = bf16[8,512,256]{2,1,0:T(8,128)(2,1)} custom-call(bf16[512,512]{1,0:T(8,128)(2,1)} %bitcast.13), custom_call_target="tpu_custom_call" | custom-call | flops 1 | bytes 1 | tf_op jit(solution)/shard_map/pallas_call | solution.py:64
  22.4 5.2 %all-to-all-start.1 = ((bf16[8,512,256]{2,1,0:T(8,128)(2,1)}), bf16[8,512,256]{2,1,0:T(8,128)(2,1)}, u32[]{:S(2)}, u32[]{:S(2)}) async-start(bf16[8,512,256]{2,1,0:T(8,128)(2,1)} %shard_map.72), calls=%async_computation.1 | async-start | bytes 4194304 | tf_op jit(solution)/shard_map/all_to_all | solution.py:290
  27.6 9.5 %collective-permute-done.2.refs_1_ = bf16[64,2304]{1,0:T(8,128)(2,1)} collective-permute-done((bf16[64,2304]{1,0:T(8,128)(2,1)}, bf16[64,2304]{1,0:T(8,128)(2,1)}, u32[]{:S(2)}, u32[]{:S(2)}) %collective-permute-start.2) | collective-permute-done | bytes 294944 | tf_op jit(solution)/shard_map/ppermute | solution.py:280
  37.0 3.0 %collective-permute-start.5 = (bf16[64,2304]{1,0:T(8,128)(2,1)}, bf16[64,2304]{1,0:T(8,128)(2,1)}, u32[]{:S(2)}, u32[]{:S(2)}) collective-permute-start(bf16[64,2304]{1,0:T(8,128)(2,1)} %collective-permute-done.2.refs_1_), channel_id=1, source_target_pairs={{0,192},{64,0},{128,64},{192,128},{1,193},{65,1},{129,65},{193,129... | collective-permute-start | bytes 884744 | tf_op jit(solution)/shard_map/ppermute | solution.py:280
  41.7 3.1 %shard_map.68 = (bf16[256,2304]{1,0:T(8,128)(2,1)}, bf16[256,2304]{1,0:T(8,128)(2,1)}) custom-call(bf16[128,2304]{1,0:T(8,128)(2,1)} %get-tuple-element.16.refs_0_.refs_4_, bf16[128,2304]{1,0:T(8,128)(2,1)} %get-tuple-element.17.refs_1_.refs_5_, bf16[128,2304]{1,0:T(8,128)(2,1)} %collective-permute-done.refs_2_.refs_6_, ...), custom_call_target="tpu_custom_call" | custom-call | flops 1 | bytes 1 | tf_op jit(solution)/shard_map/pallas_call | solution.py:226
  46.8 3.2 %collective-permute-done.5.refs_4_ = bf16[64,2304]{1,0:T(8,128)(2,1)} collective-permute-done((bf16[64,2304]{1,0:T(8,128)(2,1)}, bf16[64,2304]{1,0:T(8,128)(2,1)}, u32[]{:S(2)}, u32[]{:S(2)}) %collective-permute-start.5) | collective-permute-done | bytes 294944 | tf_op jit(solution)/shard_map/ppermute | solution.py:280
  51.8 2.3 %shard_map.69 = (bf16[128,2304]{1,0:T(8,128)(2,1)}, bf16[128,2304]{1,0:T(8,128)(2,1)}) custom-call(bf16[256,2304]{1,0:T(8,128)(2,1)} %get-tuple-element.18.refs_0_, bf16[64,2304]{1,0:T(8,128)(2,1)} %collective-permute-done.2.refs_1_, bf16[64,2304]{1,0:T(8,128)(2,1)} %collective-permute-done.3.refs_2_, bf16[64,2304]{1,0:T(8,128)(2,1)} %collective-permute-done.4.refs_3_, ...), custom_call_target="tpu_custom_call" | custom-call | flops 28000000000 | bytes 1 | tf_op jit(solution)/shard_map/pallas_call | solution.py:226
  57.2 9.4 %collective-permute-done.9.refs_8_.refs_4_ = bf16[256,2304]{1,0:T(8,128)(2,1)} collective-permute-done((bf16[256,2304]{1,0:T(8,128)(2,1)}, bf16[256,2304]{1,0:T(8,128)(2,1)}, u32[]{:S(2)}, u32[]{:S(2)}) %collective-permute-start.9) | collective-permute-done | bytes 1179680 | tf_op jit(solution)/shard_map/ppermute | solution.py:280
  66.7 2.5 %collective-permute-done.8.refs_7_.refs_3_ = bf16[256,2304]{1,0:T(8,128)(2,1)} collective-permute-done((bf16[256,2304]{1,0:T(8,128)(2,1)}, bf16[256,2304]{1,0:T(8,128)(2,1)}, u32[]{:S(2)}, u32[]{:S(2)}) %collective-permute-start.8) | collective-permute-done | bytes 1179680 | tf_op jit(solution)/shard_map/ppermute | solution.py:280
  69.2 9.9 %shard_map.70._ = bf16[8,512,256]{2,1,0:T(8,128)(2,1)} custom-call(s32[4]{0:T(128)} %pad_add_fusion.place, bf16[512,2304]{1,0:T(8,128)(2,1)} %bitcast.9, bf16[128,2304]{1,0:T(8,128)(2,1)} %get-tuple-element.19.refs_0_.refs_3_.refs_7_, bf16[128,2304]{1,0:T(8,128)(2,1)} %collective-permute-done.6.refs_1_.refs_4_.refs_8_, ...), custom_call_target="tpu_custom_call" | custom-call | flops 1 | bytes 1 | tf_op jit(solution)/shard_map/pallas_call | solution.py:204
  79.0 7.5 %all-to-all-start = ((bf16[8,512,256]{2,1,0:T(8,128)(2,1)}), bf16[8,512,256]{2,1,0:T(8,128)(2,1)}, u32[]{:S(2)}, u32[]{:S(2)}) async-start(bf16[8,512,256]{2,1,0:T(8,128)(2,1)} %shard_map.70._), calls=%async_computation | async-start | bytes 4194304 | tf_op jit(solution)/shard_map/all_to_all | solution.py:309
  86.5 9.5 %shard_map.73._ = bf16[1024,2304]{1,0:T(8,128)(2,1)} custom-call(s32[4]{0:T(128)} %pad_add_fusion.place, bf16[8,512,256]{2,1,0:T(8,128)(2,1)} %shard_map.70._, bf16[8,512,256]{2,1,0:T(8,128)(2,1)} %all-to-all-done.1.panel.refs_0_.refs_1_.refs_2_.refs_3_.refs_4_.refs_5_, bf16[128,2304]{1,0:T(8,128)(2,1)} %get-tuple-element.16.refs_0_.refs_4_, ...), custom_call_target="tpu_custom_call" | custom-call | flops 1 | bytes 1 | tf_op jit(solution)/shard_map/pallas_call | solution.py:110
  96.1 6.3 %shard_map.74 = (bf16[128,2304]{1,0:T(8,128)(2,1)}, bf16[128,2304]{1,0:T(8,128)(2,1)}) custom-call(s32[4]{0:T(128)} %pad_add_fusion.place, bf16[1024,2304]{1,0:T(8,128)(2,1)} %shard_map.73._, bf16[8,512,256]{2,1,0:T(8,128)(2,1)} %all-to-all-done.1.panel.refs_0_.refs_1_.refs_2_.refs_3_.refs_4_.refs_5_, ...), custom_call_target="tpu_custom_call" | custom-call | flops 1 | bytes 1 | tf_op jit(solution)/shard_map/pallas_call | solution.py:163
  104.4 9.2 %shard_map.75 = (bf16[256,2304]{1,0:T(8,128)(2,1)}, bf16[256,2304]{1,0:T(8,128)(2,1)}, bf16[256,2304]{1,0:T(8,128)(2,1)}) custom-call(s32[4]{0:T(128)} %pad_add_fusion.place, bf16[128,2304]{1,0:T(8,128)(2,1)} %get-tuple-element.22._, bf16[8,512,256]{2,1,0:T(8,128)(2,1)} %all-to-all-done.1.panel.refs_0_.refs_1_.refs_2_.refs_3_.refs_4_.refs_5_, ...), custom_call_target="tpu_custom_call" | custom-call | flops 999999995904 | bytes 1 | tf_op jit(solution)/shard_map/pallas_call | solution.py:163
  115.7 2.5 %collective-permute-done.10.refs_2_ = bf16[128,2304]{1,0:T(8,128)(2,1)} collective-permute-done((bf16[128,2304]{1,0:T(8,128)(2,1)}, bf16[128,2304]{1,0:T(8,128)(2,1)}, u32[]{:S(2)}, u32[]{:S(2)}) %collective-permute-start.10) | collective-permute-done | bytes 589856 | tf_op jit(solution)/shard_map/ppermute | solution.py:280
  118.1 3.6 %shard_map.76 = (bf16[256,2304]{1,0:T(8,128)(2,1)}, bf16[256,2304]{1,0:T(8,128)(2,1)}) custom-call(bf16[256,2304]{1,0:T(8,128)(2,1)} %get-tuple-element.24.refs_0_, bf16[256,2304]{1,0:T(8,128)(2,1)} %get-tuple-element.25.refs_1_, bf16[128,2304]{1,0:T(8,128)(2,1)} %collective-permute-done.10.refs_2_, bf16[128,2304]{1,0:T(8,128)(2,1)} %collective-permute-done.11.refs_3_), custom_call_target="tpu_custom_call" | custom-call | flops 1 | bytes 1 | tf_op jit(solution)/shard_map/pallas_call | solution.py:226
  121.8 3.2 %collective-permute-start.13 = (bf16[256,2304]{1,0:T(8,128)(2,1)}, bf16[256,2304]{1,0:T(8,128)(2,1)S(1)}, u32[]{:S(2)}, u32[]{:S(2)}) collective-permute-start(bf16[256,2304]{1,0:T(8,128)(2,1)} %get-tuple-element.28), channel_id=1, source_target_pairs={{0,6},{2,0},{4,2},{6,4},{1,7},{3,1},{5,3},{7,5},{8,14},{10,8},{12,... | collective-permute-start | bytes 3538952 | tf_op jit(solution)/shard_map/ppermute | solution.py:280
  125.0 12.3 %reduce-scatter.2.cloned.1.call-done.refs_2_ = bf16[128,2304]{1,0:T(8,128)(2,1)} async-done(((bf16[1024,2304]{1,0:T(8,128)(2,1)}), bf16[128,2304]{1,0:T(8,128)(2,1)}) %reduce-scatter.2.cloned.1.call-update) | async-done | bytes 589840 | tf_op jit(solution)/shard_map/reduce_scatter | solution.py:317
  139.0 5.1 %collective-permute-start.14 = (bf16[64,2304]{1,0:T(8,128)(2,1)}, bf16[64,2304]{1,0:T(8,128)(2,1)}, u32[]{:S(2)}, u32[]{:S(2)}) collective-permute-start(bf16[64,2304]{1,0:T(8,128)(2,1)} %slice.4), channel_id=1, source_target_pairs={{0,1},{1,0},{2,3},{3,2},{4,5},{5,4},{6,7},{7,6},{8,9},{9,8},{10,11... | collective-permute-start | bytes 884744 | tf_op jit(solution)/shard_map/ppermute | solution.py:280
  144.0 4.7 %collective-permute-done.12 = bf16[256,2304]{1,0:T(8,128)(2,1)S(1)} collective-permute-done((bf16[256,2304]{1,0:T(8,128)(2,1)}, bf16[256,2304]{1,0:T(8,128)(2,1)S(1)}, u32[]{:S(2)}, u32[]{:S(2)}) %collective-permute-start.12) | collective-permute-done | bytes 1179680 | tf_op jit(solution)/shard_map/ppermute | solution.py:280
  148.8 2.7 %add_convert_fusion.refs_1_ = bf16[256,2304]{1,0:T(8,128)(2,1)} fusion(bf16[256,2304]{1,0:T(8,128)(2,1)S(1)} %collective-permute-done.13, bf16[256,2304]{1,0:T(8,128)(2,1)S(1)} %collective-permute-done.12, bf16[256,2304]{1,0:T(8,128)(2,1)} %get-tuple-element.23), kind=kLoop, calls=%fused_computation | loop fusion | flops 3538944 | bytes 4718592 | tf_op jit(solution)/shard_map/convert_element_type | solution.py:221
  151.5 2.6 %shard_map.71.refs_0_ = bf16[512,512]{1,0:T(8,128)(2,1)} custom-call(bf16[8,512,256]{2,1,0:T(8,128)(2,1)} %all-to-all-done.refs_0_), custom_call_target="tpu_custom_call" | custom-call | flops 1 | bytes 1 | tf_op jit(solution)/shard_map/pallas_call | solution.py:226
  (30 shorter events, 21.7 us)
Async XLA Ops:
  7.2 62.0 %all-gather.3.cloned.1.call-start = ((), (), s32[]{:S(2)}) async-start(), calls=%async_computation.4 | async-start | bytes 2654208 | tf_op jit(solution)/shard_map/all_gather | solution.py:288
  10.3 31.3 %collective-permute-start = (bf16[128,2304]{1,0:T(8,128)(2,1)}, bf16[128,2304]{1,0:T(8,128)(2,1)}, u32[]{:S(2)}, u32[]{:S(2)}) collective-permute-start(bf16[128,2304]{1,0:T(8,128)(2,1)} %get-tuple-element.16.refs_0_.refs_4_), channel_id=1, source_target_pairs={{0,2},{2,4},{4,6},{6,0},{1,3},{3,5},{5,7},{7,1},{8,10},{10,12},{12... | collective-permute-start | bytes 1769480 | tf_op jit(solution)/shard_map/ppermute | solution.py:280
  11.8 29.9 %collective-permute-start.1 = (bf16[128,2304]{1,0:T(8,128)(2,1)}, bf16[128,2304]{1,0:T(8,128)(2,1)}, u32[]{:S(2)}, u32[]{:S(2)}) collective-permute-start(bf16[128,2304]{1,0:T(8,128)(2,1)} %get-tuple-element.17.refs_1_.refs_5_), channel_id=1, source_target_pairs={{0,6},{2,0},{4,2},{6,4},{1,7},{3,1},{5,3},{7,5},{8,14},{10,8},{12,... | collective-permute-start | bytes 1769480 | tf_op jit(solution)/shard_map/ppermute | solution.py:280
  13.6 23.5 %collective-permute-start.2 = (bf16[64,2304]{1,0:T(8,128)(2,1)}, bf16[64,2304]{1,0:T(8,128)(2,1)}, u32[]{:S(2)}, u32[]{:S(2)}) collective-permute-start(bf16[64,2304]{1,0:T(8,128)(2,1)} %bitcast.14), channel_id=1, source_target_pairs={{0,1},{1,0},{2,3},{3,2},{4,5},{5,4},{6,7},{7,6},{8,9},{9,8},{10,11... | collective-permute-start | bytes 884744 | tf_op jit(solution)/shard_map/ppermute | solution.py:280
  22.4 56.6 %all-to-all-start.1 = ((bf16[8,512,256]{2,1,0:T(8,128)(2,1)}), bf16[8,512,256]{2,1,0:T(8,128)(2,1)}, u32[]{:S(2)}, u32[]{:S(2)}) async-start(bf16[8,512,256]{2,1,0:T(8,128)(2,1)} %shard_map.72), calls=%async_computation.1 | async-start | bytes 4194304 | tf_op jit(solution)/shard_map/all_to_all | solution.py:290
  37.0 12.9 %collective-permute-start.5 = (bf16[64,2304]{1,0:T(8,128)(2,1)}, bf16[64,2304]{1,0:T(8,128)(2,1)}, u32[]{:S(2)}, u32[]{:S(2)}) collective-permute-start(bf16[64,2304]{1,0:T(8,128)(2,1)} %collective-permute-done.2.refs_1_), channel_id=1, source_target_pairs={{0,192},{64,0},{128,64},{192,128},{1,193},{65,1},{129,65},{193,129... | collective-permute-start | bytes 884744 | tf_op jit(solution)/shard_map/ppermute | solution.py:280
  40.1 9.9 %collective-permute-start.4 = (bf16[64,2304]{1,0:T(8,128)(2,1)}, bf16[64,2304]{1,0:T(8,128)(2,1)}, u32[]{:S(2)}, u32[]{:S(2)}) collective-permute-start(bf16[64,2304]{1,0:T(8,128)(2,1)} %collective-permute-done.2.refs_1_), channel_id=1, source_target_pairs={{0,128},{64,192},{128,0},{192,64},{1,129},{65,193},{129,1},{193,65... | collective-permute-start | bytes 884744 | tf_op jit(solution)/shard_map/ppermute | solution.py:280
  40.7 11.1 %collective-permute-start.3 = (bf16[64,2304]{1,0:T(8,128)(2,1)}, bf16[64,2304]{1,0:T(8,128)(2,1)}, u32[]{:S(2)}, u32[]{:S(2)}) collective-permute-start(bf16[64,2304]{1,0:T(8,128)(2,1)} %collective-permute-done.2.refs_1_), channel_id=1, source_target_pairs={{0,64},{64,128},{128,192},{192,0},{1,65},{65,129},{129,193},{193,1... | collective-permute-start | bytes 884744 | tf_op jit(solution)/shard_map/ppermute | solution.py:280
  44.8 21.9 %collective-permute-start.9 = (bf16[256,2304]{1,0:T(8,128)(2,1)}, bf16[256,2304]{1,0:T(8,128)(2,1)}, u32[]{:S(2)}, u32[]{:S(2)}) collective-permute-start(bf16[256,2304]{1,0:T(8,128)(2,1)} %get-tuple-element.21), channel_id=1, source_target_pairs={{0,6},{2,0},{4,2},{6,4},{1,7},{3,1},{5,3},{7,5},{8,14},{10,8},{12,... | collective-permute-start | bytes 3538952 | tf_op jit(solution)/shard_map/ppermute | solution.py:280
  46.3 22.8 %collective-permute-start.8 = (bf16[256,2304]{1,0:T(8,128)(2,1)}, bf16[256,2304]{1,0:T(8,128)(2,1)}, u32[]{:S(2)}, u32[]{:S(2)}) collective-permute-start(bf16[256,2304]{1,0:T(8,128)(2,1)} %get-tuple-element.18.refs_0_), channel_id=1, source_target_pairs={{0,2},{2,4},{4,6},{6,0},{1,3},{3,5},{5,7},{7,1},{8,10},{10,12},{12... | collective-permute-start | bytes 3538952 | tf_op jit(solution)/shard_map/ppermute | solution.py:280
  54.1 2.3 %collective-permute-start.6 = (bf16[128,2304]{1,0:T(8,128)(2,1)}, bf16[128,2304]{1,0:T(8,128)(2,1)}, u32[]{:S(2)}, u32[]{:S(2)}) collective-permute-start(bf16[128,2304]{1,0:T(8,128)(2,1)} %get-tuple-element.19.refs_0_.refs_3_.refs_7_), channel_id=1, source_target_pairs={{0,32},{32,0},{1,33},{33,1},{2,34},{34,2},{3,35},{35,3},{4,36},{36... | collective-permute-start | bytes 1769480 | tf_op jit(solution)/shard_map/ppermute | solution.py:280
  54.1 3.2 %collective-permute-start.7 = (bf16[128,2304]{1,0:T(8,128)(2,1)}, bf16[128,2304]{1,0:T(8,128)(2,1)}, u32[]{:S(2)}, u32[]{:S(2)}) collective-permute-start(bf16[128,2304]{1,0:T(8,128)(2,1)} %get-tuple-element.20.refs_2_.refs_5_.refs_9_), channel_id=1, source_target_pairs={{0,32},{32,0},{1,33},{33,1},{2,34},{34,2},{3,35},{35,3},{4,36},{36... | collective-permute-start | bytes 1769480 | tf_op jit(solution)/shard_map/ppermute | solution.py:280
  79.0 72.4 %all-to-all-start = ((bf16[8,512,256]{2,1,0:T(8,128)(2,1)}), bf16[8,512,256]{2,1,0:T(8,128)(2,1)}, u32[]{:S(2)}, u32[]{:S(2)}) async-start(bf16[8,512,256]{2,1,0:T(8,128)(2,1)} %shard_map.70._), calls=%async_computation | async-start | bytes 4194304 | tf_op jit(solution)/shard_map/all_to_all | solution.py:309
  86.5 50.7 %reduce-scatter.2.cloned.1.call-start = ((), (), s32[]{:S(2)}) async-start(), calls=%async_computation.3 | async-start | bytes 5308416 | tf_op jit(solution)/shard_map/reduce_scatter | solution.py:317
  102.4 13.3 %collective-permute-start.11 = (bf16[128,2304]{1,0:T(8,128)(2,1)}, bf16[128,2304]{1,0:T(8,128)(2,1)}, u32[]{:S(2)}, u32[]{:S(2)}) collective-permute-start(bf16[128,2304]{1,0:T(8,128)(2,1)} %get-tuple-element.26), channel_id=1, source_target_pairs={{0,6},{2,0},{4,2},{6,4},{1,7},{3,1},{5,3},{7,5},{8,14},{10,8},{12,... | collective-permute-start | bytes 1769480 | tf_op jit(solution)/shard_map/ppermute | solution.py:280
  102.8 15.4 %collective-permute-start.10 = (bf16[128,2304]{1,0:T(8,128)(2,1)}, bf16[128,2304]{1,0:T(8,128)(2,1)}, u32[]{:S(2)}, u32[]{:S(2)}) collective-permute-start(bf16[128,2304]{1,0:T(8,128)(2,1)} %get-tuple-element.22._), channel_id=1, source_target_pairs={{0,2},{2,4},{4,6},{6,0},{1,3},{3,5},{5,7},{7,1},{8,10},{10,12},{12... | collective-permute-start | bytes 1769480 | tf_op jit(solution)/shard_map/ppermute | solution.py:280
  121.8 27.0 %collective-permute-start.12 = (bf16[256,2304]{1,0:T(8,128)(2,1)}, bf16[256,2304]{1,0:T(8,128)(2,1)S(1)}, u32[]{:S(2)}, u32[]{:S(2)}) collective-permute-start(bf16[256,2304]{1,0:T(8,128)(2,1)} %get-tuple-element.27), channel_id=1, source_target_pairs={{0,2},{2,4},{4,6},{6,0},{1,3},{3,5},{5,7},{7,1},{8,10},{10,12},{12... | collective-permute-start | bytes 3538952 | tf_op jit(solution)/shard_map/ppermute | solution.py:280
  121.8 27.0 %collective-permute-start.13 = (bf16[256,2304]{1,0:T(8,128)(2,1)}, bf16[256,2304]{1,0:T(8,128)(2,1)S(1)}, u32[]{:S(2)}, u32[]{:S(2)}) collective-permute-start(bf16[256,2304]{1,0:T(8,128)(2,1)} %get-tuple-element.28), channel_id=1, source_target_pairs={{0,6},{2,0},{4,2},{6,4},{1,7},{3,1},{5,3},{7,5},{8,14},{10,8},{12,... | collective-permute-start | bytes 3538952 | tf_op jit(solution)/shard_map/ppermute | solution.py:280
  139.0 16.6 %collective-permute-start.14 = (bf16[64,2304]{1,0:T(8,128)(2,1)}, bf16[64,2304]{1,0:T(8,128)(2,1)}, u32[]{:S(2)}, u32[]{:S(2)}) collective-permute-start(bf16[64,2304]{1,0:T(8,128)(2,1)} %slice.4), channel_id=1, source_target_pairs={{0,1},{1,0},{2,3},{3,2},{4,5},{5,4},{6,7},{7,6},{8,9},{9,8},{10,11... | collective-permute-start | bytes 884744 | tf_op jit(solution)/shard_map/ppermute | solution.py:280
Sparse Core Ops, SparseCore 0:
  9.8 34.2 all-gather.2
  96.2 41.0 reduce-scatter.1

commit v13 on v12

--- a/solution.py
+++ b/solution.py
@@ -175,7 +175,7 @@
         ),
         out_shape=[jax.ShapeDtypeStruct((size, width), BF) for size in sizes],
         compiler_params=params(),
-        cost_estimate=cost(10**12 if len(offsets) > 1 else 1, 1),
+        cost_estimate=cost(1, 1),
     )(place, after, *[panel] * len(blocks), near, *far)
 
 

time: 165 us -> 168 us (1.018)
  the two profiles are of different devices: /device:TPU:32 before, /device:TPU:24 now
where the time goes in v13:
time: 168 us; the launch traced here: 167 us
  waiting for transfers between devices  56.2 us (33%)
  Pallas kernels  53.5 us (32%)
  starting transfers between devices  38.5 us (23%)
  between operations  14.1 us (8%)
  other arithmetic  3.26 us (2%)
  local copies, waits for them, and re-layouts  1.69 us (1%)
    ppermute x15, waiting for transfers between devices, shift(): return lax.ppermute(array, axis, ring(lax.axis_size(axis), step))  48.2 us
    ppermute x15, starting transfers between devices, shift(): return lax.ppermute(array, axis, ring(lax.axis_size(axis), step))  27.8 us
    pallas_call x2, Pallas kernels, weight_grad(): pl.pallas_call(functools.partial(weight_grad_kernel, len(offsets)), grid_...  15.6 us
    pallas_call x5, Pallas kernels, local(): pl.pallas_call(lambda *refs: kernel(*refs[len(after):]), out_shape=[jax.S...  13.6 us
    pallas_call x1, Pallas kernels, backward(): pl.pallas_call(backward_kernel, grid=(2,), out_shape=jax.ShapeDtypeStruct...  9.86 us
    pallas_call x1, Pallas kernels, forward(): pl.pallas_call(forward_kernel, grid=(width // tile,), out_shape=jax.Shape...  9.53 us
    all_to_all x1, starting transfers between devices, per_device(): sums = lax.all_to_all(sums, ('zl', 'zh'), 0, 0, tiled=True)  6.34 us
    all_to_all x1, waiting for transfers between devices, per_device(): panel = lax.all_to_all(split, ('zl', 'zh'), 0, 0, tiled=True)  5.52 us
  transfers between devices with their start and end apart: 19, of which 12 were waited for; matrix products, arithmetic and copies ran while one was open for 3% of the time, Pallas kernels for 25%

profile of v13, /device:TPU:24, one launch (start us, length us, event | category | flops | bytes accessed | tf_op | source)
XLA Modules:
  0.0 167.2 jit_solution(6503032728081445516)
XLA Ops:
  7.9 2.4 %shard_map.67 = (bf16[128,2304]{1,0:T(8,128)(2,1)}, bf16[128,2304]{1,0:T(8,128)(2,1)}) custom-call(f32[2,18]{1,0:T(2,128)} %scales.1, bf16[256,2304]{1,0:T(8,128)(2,1)} %quantized.1), custom_call_target="tpu_custom_call" | custom-call | flops 1 | bytes 1 | tf_op jit(solution)/shard_map/pallas_call | solution.py:47
  13.6 7.2 %collective-permute-start.2 = (bf16[64,2304]{1,0:T(8,128)(2,1)}, bf16[64,2304]{1,0:T(8,128)(2,1)}, u32[]{:S(2)}, u32[]{:S(2)}) collective-permute-start(bf16[64,2304]{1,0:T(8,128)(2,1)} %bitcast.14), channel_id=1, source_target_pairs={{0,1},{1,0},{2,3},{3,2},{4,5},{5,4},{6,7},{7,6},{8,9},{9,8},{10,11... | collective-permute-start | bytes 884744 | tf_op jit(solution)/shard_map/ppermute | solution.py:280
  20.7 2.5 %shard_map.72 = bf16[8,512,256]{2,1,0:T(8,128)(2,1)} custom-call(bf16[512,512]{1,0:T(8,128)(2,1)} %bitcast.13), custom_call_target="tpu_custom_call" | custom-call | flops 1 | bytes 1 | tf_op jit(solution)/shard_map/pallas_call | solution.py:64
  23.3 4.4 %all-to-all-start.1 = ((bf16[8,512,256]{2,1,0:T(8,128)(2,1)}), bf16[8,512,256]{2,1,0:T(8,128)(2,1)}, u32[]{:S(2)}, u32[]{:S(2)}) async-start(bf16[8,512,256]{2,1,0:T(8,128)(2,1)} %shard_map.72), calls=%async_computation.1 | async-start | bytes 4194304 | tf_op jit(solution)/shard_map/all_to_all | solution.py:290
  27.7 5.4 %collective-permute-done.2.refs_1_ = bf16[64,2304]{1,0:T(8,128)(2,1)} collective-permute-done((bf16[64,2304]{1,0:T(8,128)(2,1)}, bf16[64,2304]{1,0:T(8,128)(2,1)}, u32[]{:S(2)}, u32[]{:S(2)}) %collective-permute-start.2) | collective-permute-done | bytes 294944 | tf_op jit(solution)/shard_map/ppermute | solution.py:280
  37.0 3.1 %shard_map.68 = (bf16[256,2304]{1,0:T(8,128)(2,1)}, bf16[256,2304]{1,0:T(8,128)(2,1)}) custom-call(bf16[128,2304]{1,0:T(8,128)(2,1)} %get-tuple-element.16.refs_0_.refs_4_, bf16[128,2304]{1,0:T(8,128)(2,1)} %get-tuple-element.17.refs_1_.refs_5_, bf16[128,2304]{1,0:T(8,128)(2,1)} %collective-permute-done.refs_2_.refs_6_, ...), custom_call_target="tpu_custom_call" | custom-call | flops 1 | bytes 1 | tf_op jit(solution)/shard_map/pallas_call | solution.py:226
  42.1 7.7 %collective-permute-done.5.refs_4_ = bf16[64,2304]{1,0:T(8,128)(2,1)} collective-permute-done((bf16[64,2304]{1,0:T(8,128)(2,1)}, bf16[64,2304]{1,0:T(8,128)(2,1)}, u32[]{:S(2)}, u32[]{:S(2)}) %collective-permute-start.5) | collective-permute-done | bytes 294944 | tf_op jit(solution)/shard_map/ppermute | solution.py:280
  55.3 6.2 %collective-permute-done.9.refs_8_.refs_4_ = bf16[256,2304]{1,0:T(8,128)(2,1)} collective-permute-done((bf16[256,2304]{1,0:T(8,128)(2,1)}, bf16[256,2304]{1,0:T(8,128)(2,1)}, u32[]{:S(2)}, u32[]{:S(2)}) %collective-permute-start.9) | collective-permute-done | bytes 1179680 | tf_op jit(solution)/shard_map/ppermute | solution.py:280
  61.5 2.5 %collective-permute-done.8.refs_7_.refs_3_ = bf16[256,2304]{1,0:T(8,128)(2,1)} collective-permute-done((bf16[256,2304]{1,0:T(8,128)(2,1)}, bf16[256,2304]{1,0:T(8,128)(2,1)}, u32[]{:S(2)}, u32[]{:S(2)}) %collective-permute-start.8) | collective-permute-done | bytes 1179680 | tf_op jit(solution)/shard_map/ppermute | solution.py:280
  64.0 9.9 %shard_map.70._ = bf16[8,512,256]{2,1,0:T(8,128)(2,1)} custom-call(s32[4]{0:T(128)} %pad_add_fusion.place, bf16[512,2304]{1,0:T(8,128)(2,1)} %bitcast.9, bf16[128,2304]{1,0:T(8,128)(2,1)} %get-tuple-element.19.refs_0_.refs_3_.refs_7_, bf16[128,2304]{1,0:T(8,128)(2,1)} %collective-permute-done.6.refs_1_.refs_4_.refs_8_, ...), custom_call_target="tpu_custom_call" | custom-call | flops 1 | bytes 1 | tf_op jit(solution)/shard_map/pallas_call | solution.py:204
  73.9 5.5 %all-to-all-done.1.panel.refs_0_.refs_1_.refs_2_.refs_3_.refs_4_.refs_5_ = bf16[8,512,256]{2,1,0:T(8,128)(2,1)} async-done(((bf16[8,512,256]{2,1,0:T(8,128)(2,1)}), bf16[8,512,256]{2,1,0:T(8,128)(2,1)}, u32[]{:S(2)}, u32[]{:S(2)}) %all-to-all-start.1) | async-done | bytes 2097184 | tf_op jit(solution)/shard_map/all_to_all | solution.py:290
  79.4 9.5 %shard_map.73._ = bf16[1024,2304]{1,0:T(8,128)(2,1)} custom-call(s32[4]{0:T(128)} %pad_add_fusion.place, bf16[8,512,256]{2,1,0:T(8,128)(2,1)} %shard_map.70._, bf16[8,512,256]{2,1,0:T(8,128)(2,1)} %all-to-all-done.1.panel.refs_0_.refs_1_.refs_2_.refs_3_.refs_4_.refs_5_, bf16[128,2304]{1,0:T(8,128)(2,1)} %get-tuple-element.16.refs_0_.refs_4_, ...), custom_call_target="tpu_custom_call" | custom-call | flops 1 | bytes 1 | tf_op jit(solution)/shard_map/pallas_call | solution.py:110
  88.9 6.3 %all-to-all-start = ((bf16[8,512,256]{2,1,0:T(8,128)(2,1)}), bf16[8,512,256]{2,1,0:T(8,128)(2,1)}, u32[]{:S(2)}, u32[]{:S(2)}) async-start(bf16[8,512,256]{2,1,0:T(8,128)(2,1)} %shard_map.70._), calls=%async_computation | async-start | bytes 4194304 | tf_op jit(solution)/shard_map/all_to_all | solution.py:309
  95.3 6.6 %shard_map.74 = (bf16[128,2304]{1,0:T(8,128)(2,1)}, bf16[128,2304]{1,0:T(8,128)(2,1)}) custom-call(s32[4]{0:T(128)} %pad_add_fusion.place, bf16[1024,2304]{1,0:T(8,128)(2,1)} %shard_map.73._, bf16[8,512,256]{2,1,0:T(8,128)(2,1)} %all-to-all-done.1.panel.refs_0_.refs_1_.refs_2_.refs_3_.refs_4_.refs_5_, ...), custom_call_target="tpu_custom_call" | custom-call | flops 1 | bytes 1 | tf_op jit(solution)/shard_map/pallas_call | solution.py:163
  103.9 8.9 %shard_map.75 = (bf16[256,2304]{1,0:T(8,128)(2,1)}, bf16[256,2304]{1,0:T(8,128)(2,1)}, bf16[256,2304]{1,0:T(8,128)(2,1)}) custom-call(s32[4]{0:T(128)} %pad_add_fusion.place, bf16[128,2304]{1,0:T(8,128)(2,1)} %get-tuple-element.22._, bf16[8,512,256]{2,1,0:T(8,128)(2,1)} %all-to-all-done.1.panel.refs_0_.refs_1_.refs_2_.refs_3_.refs_4_.refs_5_, ...), custom_call_target="tpu_custom_call" | custom-call | flops 1 | bytes 1 | tf_op jit(solution)/shard_map/pallas_call | solution.py:163
  112.9 3.0 %collective-permute-done.11.refs_3_ = bf16[128,2304]{1,0:T(8,128)(2,1)} collective-permute-done((bf16[128,2304]{1,0:T(8,128)(2,1)}, bf16[128,2304]{1,0:T(8,128)(2,1)}, u32[]{:S(2)}, u32[]{:S(2)}) %collective-permute-start.11) | collective-permute-done | bytes 589856 | tf_op jit(solution)/shard_map/ppermute | solution.py:280
  115.8 2.5 %collective-permute-done.10.refs_2_ = bf16[128,2304]{1,0:T(8,128)(2,1)} collective-permute-done((bf16[128,2304]{1,0:T(8,128)(2,1)}, bf16[128,2304]{1,0:T(8,128)(2,1)}, u32[]{:S(2)}, u32[]{:S(2)}) %collective-permute-start.10) | collective-permute-done | bytes 589856 | tf_op jit(solution)/shard_map/ppermute | solution.py:280
  118.3 3.6 %shard_map.76 = (bf16[256,2304]{1,0:T(8,128)(2,1)}, bf16[256,2304]{1,0:T(8,128)(2,1)}) custom-call(bf16[256,2304]{1,0:T(8,128)(2,1)} %get-tuple-element.24.refs_0_, bf16[256,2304]{1,0:T(8,128)(2,1)} %get-tuple-element.25.refs_1_, bf16[128,2304]{1,0:T(8,128)(2,1)} %collective-permute-done.10.refs_2_, bf16[128,2304]{1,0:T(8,128)(2,1)} %collective-permute-done.11.refs_3_), custom_call_target="tpu_custom_call" | custom-call | flops 1 | bytes 1 | tf_op jit(solution)/shard_map/pallas_call | solution.py:226
  122.0 3.2 %collective-permute-start.13 = (bf16[256,2304]{1,0:T(8,128)(2,1)}, bf16[256,2304]{1,0:T(8,128)(2,1)S(1)}, u32[]{:S(2)}, u32[]{:S(2)}) collective-permute-start(bf16[256,2304]{1,0:T(8,128)(2,1)} %get-tuple-element.28), channel_id=1, source_target_pairs={{0,6},{2,0},{4,2},{6,4},{1,7},{3,1},{5,3},{7,5},{8,14},{10,8},{12,... | collective-permute-start | bytes 3538952 | tf_op jit(solution)/shard_map/ppermute | solution.py:280
  128.6 5.7 %collective-permute-start.14 = (bf16[64,2304]{1,0:T(8,128)(2,1)}, bf16[64,2304]{1,0:T(8,128)(2,1)}, u32[]{:S(2)}, u32[]{:S(2)}) collective-permute-start(bf16[64,2304]{1,0:T(8,128)(2,1)} %slice.4), channel_id=1, source_target_pairs={{0,1},{1,0},{2,3},{3,2},{4,5},{5,4},{6,7},{7,6},{8,9},{9,8},{10,11... | collective-permute-start | bytes 884744 | tf_op jit(solution)/shard_map/ppermute | solution.py:280
  134.3 14.9 %collective-permute-done.12 = bf16[256,2304]{1,0:T(8,128)(2,1)S(1)} collective-permute-done((bf16[256,2304]{1,0:T(8,128)(2,1)}, bf16[256,2304]{1,0:T(8,128)(2,1)S(1)}, u32[]{:S(2)}, u32[]{:S(2)}) %collective-permute-start.12) | collective-permute-done | bytes 1179680 | tf_op jit(solution)/shard_map/ppermute | solution.py:280
  149.2 2.7 %add_convert_fusion.refs_1_ = bf16[256,2304]{1,0:T(8,128)(2,1)} fusion(bf16[256,2304]{1,0:T(8,128)(2,1)S(1)} %collective-permute-done.13, bf16[256,2304]{1,0:T(8,128)(2,1)S(1)} %collective-permute-done.12, bf16[256,2304]{1,0:T(8,128)(2,1)} %get-tuple-element.23), kind=kLoop, calls=%fused_computation | loop fusion | flops 3538944 | bytes 4718592 | tf_op jit(solution)/shard_map/convert_element_type | solution.py:221
  151.9 2.6 %shard_map.71.refs_0_ = bf16[512,512]{1,0:T(8,128)(2,1)} custom-call(bf16[8,512,256]{2,1,0:T(8,128)(2,1)} %all-to-all-done.refs_0_), custom_call_target="tpu_custom_call" | custom-call | flops 1 | bytes 1 | tf_op jit(solution)/shard_map/pallas_call | solution.py:226
  154.6 3.9 %collective-permute-done.14.refs_3_ = bf16[64,2304]{1,0:T(8,128)(2,1)} collective-permute-done((bf16[64,2304]{1,0:T(8,128)(2,1)}, bf16[64,2304]{1,0:T(8,128)(2,1)}, u32[]{:S(2)}, u32[]{:S(2)}) %collective-permute-start.14) | collective-permute-done | bytes 294944 | tf_op jit(solution)/shard_map/ppermute | solution.py:280
  (30 shorter events, 22.8 us)
Async XLA Ops:
  7.2 56.8 %all-gather.3.cloned.1.call-start = ((), (), s32[]{:S(2)}) async-start(), calls=%async_computation.4 | async-start | bytes 2654208 | tf_op jit(solution)/shard_map/all_gather | solution.py:288
  10.3 26.6 %collective-permute-start = (bf16[128,2304]{1,0:T(8,128)(2,1)}, bf16[128,2304]{1,0:T(8,128)(2,1)}, u32[]{:S(2)}, u32[]{:S(2)}) collective-permute-start(bf16[128,2304]{1,0:T(8,128)(2,1)} %get-tuple-element.16.refs_0_.refs_4_), channel_id=1, source_target_pairs={{0,2},{2,4},{4,6},{6,0},{1,3},{3,5},{5,7},{7,1},{8,10},{10,12},{12... | collective-permute-start | bytes 1769480 | tf_op jit(solution)/shard_map/ppermute | solution.py:280
  11.8 25.1 %collective-permute-start.1 = (bf16[128,2304]{1,0:T(8,128)(2,1)}, bf16[128,2304]{1,0:T(8,128)(2,1)}, u32[]{:S(2)}, u32[]{:S(2)}) collective-permute-start(bf16[128,2304]{1,0:T(8,128)(2,1)} %get-tuple-element.17.refs_1_.refs_5_), channel_id=1, source_target_pairs={{0,6},{2,0},{4,2},{6,4},{1,7},{3,1},{5,3},{7,5},{8,14},{10,8},{12,... | collective-permute-start | bytes 1769480 | tf_op jit(solution)/shard_map/ppermute | solution.py:280
  13.6 19.5 %collective-permute-start.2 = (bf16[64,2304]{1,0:T(8,128)(2,1)}, bf16[64,2304]{1,0:T(8,128)(2,1)}, u32[]{:S(2)}, u32[]{:S(2)}) collective-permute-start(bf16[64,2304]{1,0:T(8,128)(2,1)} %bitcast.14), channel_id=1, source_target_pairs={{0,1},{1,0},{2,3},{3,2},{4,5},{5,4},{6,7},{7,6},{8,9},{9,8},{10,11... | collective-permute-start | bytes 884744 | tf_op jit(solution)/shard_map/ppermute | solution.py:280
  23.3 56.1 %all-to-all-start.1 = ((bf16[8,512,256]{2,1,0:T(8,128)(2,1)}), bf16[8,512,256]{2,1,0:T(8,128)(2,1)}, u32[]{:S(2)}, u32[]{:S(2)}) async-start(bf16[8,512,256]{2,1,0:T(8,128)(2,1)} %shard_map.72), calls=%async_computation.1 | async-start | bytes 4194304 | tf_op jit(solution)/shard_map/all_to_all | solution.py:290
  27.6 99.3 %reduce-scatter.2.cloned.1.call-start = ((), (), s32[]{:S(2)}) async-start(), calls=%async_computation.3 | async-start | bytes 5308416 | tf_op jit(solution)/shard_map/reduce_scatter | solution.py:317
  33.1 16.7 %collective-permute-start.5 = (bf16[64,2304]{1,0:T(8,128)(2,1)}, bf16[64,2304]{1,0:T(8,128)(2,1)}, u32[]{:S(2)}, u32[]{:S(2)}) collective-permute-start(bf16[64,2304]{1,0:T(8,128)(2,1)} %collective-permute-done.2.refs_1_), channel_id=1, source_target_pairs={{0,192},{64,0},{128,64},{192,128},{1,193},{65,1},{129,65},{193,129... | collective-permute-start | bytes 884744 | tf_op jit(solution)/shard_map/ppermute | solution.py:280
  33.8 16.0 %collective-permute-start.4 = (bf16[64,2304]{1,0:T(8,128)(2,1)}, bf16[64,2304]{1,0:T(8,128)(2,1)}, u32[]{:S(2)}, u32[]{:S(2)}) collective-permute-start(bf16[64,2304]{1,0:T(8,128)(2,1)} %collective-permute-done.2.refs_1_), channel_id=1, source_target_pairs={{0,128},{64,192},{128,0},{192,64},{1,129},{65,193},{129,1},{193,65... | collective-permute-start | bytes 884744 | tf_op jit(solution)/shard_map/ppermute | solution.py:280
  34.8 15.1 %collective-permute-start.3 = (bf16[64,2304]{1,0:T(8,128)(2,1)}, bf16[64,2304]{1,0:T(8,128)(2,1)}, u32[]{:S(2)}, u32[]{:S(2)}) collective-permute-start(bf16[64,2304]{1,0:T(8,128)(2,1)} %collective-permute-done.2.refs_1_), channel_id=1, source_target_pairs={{0,64},{64,128},{128,192},{192,0},{1,65},{65,129},{129,193},{193,1... | collective-permute-start | bytes 884744 | tf_op jit(solution)/shard_map/ppermute | solution.py:280
  40.1 21.4 %collective-permute-start.9 = (bf16[256,2304]{1,0:T(8,128)(2,1)}, bf16[256,2304]{1,0:T(8,128)(2,1)}, u32[]{:S(2)}, u32[]{:S(2)}) collective-permute-start(bf16[256,2304]{1,0:T(8,128)(2,1)} %get-tuple-element.21), channel_id=1, source_target_pairs={{0,6},{2,0},{4,2},{6,4},{1,7},{3,1},{5,3},{7,5},{8,14},{10,8},{12,... | collective-permute-start | bytes 3538952 | tf_op jit(solution)/shard_map/ppermute | solution.py:280
  41.7 22.3 %collective-permute-start.8 = (bf16[256,2304]{1,0:T(8,128)(2,1)}, bf16[256,2304]{1,0:T(8,128)(2,1)}, u32[]{:S(2)}, u32[]{:S(2)}) collective-permute-start(bf16[256,2304]{1,0:T(8,128)(2,1)} %get-tuple-element.18.refs_0_), channel_id=1, source_target_pairs={{0,2},{2,4},{4,6},{6,0},{1,3},{3,5},{5,7},{7,1},{8,10},{10,12},{12... | collective-permute-start | bytes 3538952 | tf_op jit(solution)/shard_map/ppermute | solution.py:280
  52.1 2.3 %collective-permute-start.6 = (bf16[128,2304]{1,0:T(8,128)(2,1)}, bf16[128,2304]{1,0:T(8,128)(2,1)}, u32[]{:S(2)}, u32[]{:S(2)}) collective-permute-start(bf16[128,2304]{1,0:T(8,128)(2,1)} %get-tuple-element.19.refs_0_.refs_3_.refs_7_), channel_id=1, source_target_pairs={{0,32},{32,0},{1,33},{33,1},{2,34},{34,2},{3,35},{35,3},{4,36},{36... | collective-permute-start | bytes 1769480 | tf_op jit(solution)/shard_map/ppermute | solution.py:280
  52.1 3.2 %collective-permute-start.7 = (bf16[128,2304]{1,0:T(8,128)(2,1)}, bf16[128,2304]{1,0:T(8,128)(2,1)}, u32[]{:S(2)}, u32[]{:S(2)}) collective-permute-start(bf16[128,2304]{1,0:T(8,128)(2,1)} %get-tuple-element.20.refs_2_.refs_5_.refs_9_), channel_id=1, source_target_pairs={{0,32},{32,0},{1,33},{33,1},{2,34},{34,2},{3,35},{35,3},{4,36},{36... | collective-permute-start | bytes 1769480 | tf_op jit(solution)/shard_map/ppermute | solution.py:280
  88.9 63.0 %all-to-all-start = ((bf16[8,512,256]{2,1,0:T(8,128)(2,1)}), bf16[8,512,256]{2,1,0:T(8,128)(2,1)}, u32[]{:S(2)}, u32[]{:S(2)}) async-start(bf16[8,512,256]{2,1,0:T(8,128)(2,1)} %shard_map.70._), calls=%async_computation | async-start | bytes 4194304 | tf_op jit(solution)/shard_map/all_to_all | solution.py:309
  101.9 13.9 %collective-permute-start.11 = (bf16[128,2304]{1,0:T(8,128)(2,1)}, bf16[128,2304]{1,0:T(8,128)(2,1)}, u32[]{:S(2)}, u32[]{:S(2)}) collective-permute-start(bf16[128,2304]{1,0:T(8,128)(2,1)} %get-tuple-element.26), channel_id=1, source_target_pairs={{0,6},{2,0},{4,2},{6,4},{1,7},{3,1},{5,3},{7,5},{8,14},{10,8},{12,... | collective-permute-start | bytes 1769480 | tf_op jit(solution)/shard_map/ppermute | solution.py:280
  102.7 15.7 %collective-permute-start.10 = (bf16[128,2304]{1,0:T(8,128)(2,1)}, bf16[128,2304]{1,0:T(8,128)(2,1)}, u32[]{:S(2)}, u32[]{:S(2)}) collective-permute-start(bf16[128,2304]{1,0:T(8,128)(2,1)} %get-tuple-element.22._), channel_id=1, source_target_pairs={{0,2},{2,4},{4,6},{6,0},{1,3},{3,5},{5,7},{7,1},{8,10},{10,12},{12... | collective-permute-start | bytes 1769480 | tf_op jit(solution)/shard_map/ppermute | solution.py:280
  122.0 27.3 %collective-permute-start.12 = (bf16[256,2304]{1,0:T(8,128)(2,1)}, bf16[256,2304]{1,0:T(8,128)(2,1)S(1)}, u32[]{:S(2)}, u32[]{:S(2)}) collective-permute-start(bf16[256,2304]{1,0:T(8,128)(2,1)} %get-tuple-element.27), channel_id=1, source_target_pairs={{0,2},{2,4},{4,6},{6,0},{1,3},{3,5},{5,7},{7,1},{8,10},{10,12},{12... | collective-permute-start | bytes 3538952 | tf_op jit(solution)/shard_map/ppermute | solution.py:280
  122.0 27.3 %collective-permute-start.13 = (bf16[256,2304]{1,0:T(8,128)(2,1)}, bf16[256,2304]{1,0:T(8,128)(2,1)S(1)}, u32[]{:S(2)}, u32[]{:S(2)}) collective-permute-start(bf16[256,2304]{1,0:T(8,128)(2,1)} %get-tuple-element.28), channel_id=1, source_target_pairs={{0,6},{2,0},{4,2},{6,4},{1,7},{3,1},{5,3},{7,5},{8,14},{10,8},{12,... | collective-permute-start | bytes 3538952 | tf_op jit(solution)/shard_map/ppermute | solution.py:280
  128.6 29.9 %collective-permute-start.14 = (bf16[64,2304]{1,0:T(8,128)(2,1)}, bf16[64,2304]{1,0:T(8,128)(2,1)}, u32[]{:S(2)}, u32[]{:S(2)}) collective-permute-start(bf16[64,2304]{1,0:T(8,128)(2,1)} %slice.4), channel_id=1, source_target_pairs={{0,1},{1,0},{2,3},{3,2},{4,5},{5,4},{6,7},{7,6},{8,9},{9,8},{10,11... | collective-permute-start | bytes 884744 | tf_op jit(solution)/shard_map/ppermute | solution.py:280
Sparse Core Ops, SparseCore 0:
  9.8 33.8 all-gather.2
  89.1 37.8 reduce-scatter.1

commit v14 on v12

--- a/solution.py
+++ b/solution.py
@@ -249,11 +249,6 @@
         refs[4 + e // 2][e % 2 * 64 : e % 2 * 64 + 64, :] = ref[...]
 
 
-def relay_kernel(top, bottom, top_up, bottom_down, up, down):
-    up[:BLOCK], up[BLOCK:] = top_up[...], bottom[...]
-    down[:BLOCK], down[BLOCK:] = top[...], bottom_down[...]
-
-
 def sum_kernel(*refs):
     refs[-1][...] = summed(*[ref[...] for ref in refs[:-1]])
 
@@ -293,10 +288,9 @@
     top_up, bottom_down = shift(top, "x", 1), shift(bottom, "x", -1)
     far = shift(grad_out[0], "zh", 1)
     far = [far] + [shift(far, "y", e) for e in (1, 2, 3)]
-    up, down = local(
-        relay_kernel, [(256, F)] * 2, (), top, bottom, top_up, bottom_down
-    )
-    mine = local(collect_kernel, [(128, F)] * 2, up, *far, flops=COLLECT)
+    up = jnp.concatenate([top_up, bottom])
+    down = jnp.concatenate([top, bottom_down])
+    mine = local(collect_kernel, [(128, F)] * 2, (up, down), *far, flops=COLLECT)
     far = [part for own in mine for part in (own, shift(own, "k", 1))]
     up, down = shift(up, "x", 1), shift(down, "x", -1)
     weights = (top, bottom, top_up, up, down, bottom_down)

time: 165 us -> 166 us (level)
  local copies, waits for them, and re-layouts: 1.69 us -> 7.25 us
  waiting for transfers between devices: 52.1 us -> 47.8 us
  Pallas kernels: 53.4 us -> 49.8 us
  starting transfers between devices: 39.8 us -> 42.8 us
    ppermute x15, waiting for transfers between devices: 39.1 us -> 34.2 us  [shift(): return lax.ppermute(array, axis, ring(lax.axis_size(axis), step))]
    pallas_call x5 -> x4, Pallas kernels: 13.6 us -> 10.4 us  [local(): pl.pallas_call(lambda *refs: kernel(*refs[len(after):]), out_shape=[jax.S...]
    ppermute x15, starting transfers between devices: 27 us -> 29.8 us  [shift(): return lax.ppermute(array, axis, ring(lax.axis_size(axis), step))]
    unnamed x0 -> x6, local copies, waits for them, and re-layouts: none -> 2.79 us
    concatenate x0 -> x2, local copies, waits for them, and re-layouts: none -> 2.77 us  [the longest x1 1.92 us: per_device(): down = jnp.concatenate([top, bottom_down])]
  transfers between devices with their start and end apart: 19 -> 19, of which waited for: 12 -> 9; matrix products, arithmetic and copies ran while one was open for 3% -> 6% of each run, Pallas kernels for 31% -> 28%
where the time goes in v14:
time: 166 us; the launch traced here: 165 us
  Pallas kernels  49.8 us (30%)
  waiting for transfers between devices  47.8 us (29%)
  starting transfers between devices  42.8 us (26%)
  between operations  14.1 us (8%)
  local copies, waits for them, and re-layouts  7.25 us (4%)
  other arithmetic  3.28 us (2%)
    ppermute x15, waiting for transfers between devices, shift(): return lax.ppermute(array, axis, ring(lax.axis_size(axis), step))  34.2 us
    ppermute x15, starting transfers between devices, shift(): return lax.ppermute(array, axis, ring(lax.axis_size(axis), step))  29.8 us
    pallas_call x2, Pallas kernels, weight_grad(): pl.pallas_call(functools.partial(weight_grad_kernel, len(offsets)), grid_...  15.1 us
    reduce_scatter x1, waiting for transfers between devices, per_device(): lax.psum_scatter(product, ('y', 'k'), scatter_dimension=0, tiled=True)  13.6 us
    pallas_call x4, Pallas kernels, local(): pl.pallas_call(lambda *refs: kernel(*refs[len(after):]), out_shape=[jax.S...  10.4 us
    pallas_call x1, Pallas kernels, backward(): pl.pallas_call(backward_kernel, grid=(2,), out_shape=jax.ShapeDtypeStruct...  9.85 us
    pallas_call x1, Pallas kernels, forward(): pl.pallas_call(forward_kernel, grid=(width // tile,), out_shape=jax.Shape...  9.48 us
    all_to_all x1, starting transfers between devices, per_device(): sums = lax.all_to_all(sums, ('zl', 'zh'), 0, 0, tiled=True)  7.53 us
  transfers between devices with their start and end apart: 19, of which 9 were waited for; matrix products, arithmetic and copies ran while one was open for 6% of the time, Pallas kernels for 28%

profile of v14, /device:TPU:32, one launch (start us, length us, event | category | flops | bytes accessed | tf_op | source)
XLA Modules:
  0.0 165.0 jit_solution(10391348510984884225)
XLA Ops:
  7.2 2.4 %shard_map.67 = (bf16[128,2304]{1,0:T(8,128)(2,1)}, bf16[128,2304]{1,0:T(8,128)(2,1)}) custom-call(f32[2,18]{1,0:T(2,128)} %scales.1, bf16[256,2304]{1,0:T(8,128)(2,1)} %quantized.1), custom_call_target="tpu_custom_call" | custom-call | flops 1 | bytes 1 | tf_op jit(solution)/shard_map/pallas_call | solution.py:47
  9.6 2.8 %collective-permute-start.1 = (bf16[128,2304]{1,0:T(8,128)(2,1)}, bf16[128,2304]{1,0:T(8,128)(2,1)}, u32[]{:S(2)}, u32[]{:S(2)}) collective-permute-start(bf16[128,2304]{1,0:T(8,128)(2,1)} %get-tuple-element.15.refs_5_.refs_1_), channel_id=1, source_target_pairs={{0,6},{2,0},{4,2},{6,4},{1,7},{3,1},{5,3},{7,5},{8,14},{10,8},{12,... | collective-permute-start | bytes 1769480 | tf_op jit(solution)/shard_map/ppermute | solution.py:275
  12.4 6.4 %collective-permute-start.2 = (bf16[64,2304]{1,0:T(8,128)(2,1)}, bf16[64,2304]{1,0:T(8,128)(2,1)}, u32[]{:S(2)}, u32[]{:S(2)}) collective-permute-start(bf16[64,2304]{1,0:T(8,128)(2,1)} %bitcast.14), channel_id=1, source_target_pairs={{0,1},{1,0},{2,3},{3,2},{4,5},{5,4},{6,7},{7,6},{8,9},{9,8},{10,11... | collective-permute-start | bytes 884744 | tf_op jit(solution)/shard_map/ppermute | solution.py:275
  18.8 2.5 %shard_map.71 = bf16[8,512,256]{2,1,0:T(8,128)(2,1)} custom-call(bf16[512,512]{1,0:T(8,128)(2,1)} %bitcast.13), custom_call_target="tpu_custom_call" | custom-call | flops 1 | bytes 1 | tf_op jit(solution)/shard_map/pallas_call | solution.py:64
  21.3 5.4 %all-to-all-start.1 = ((bf16[8,512,256]{2,1,0:T(8,128)(2,1)}), bf16[8,512,256]{2,1,0:T(8,128)(2,1)}, u32[]{:S(2)}, u32[]{:S(2)}) async-start(bf16[8,512,256]{2,1,0:T(8,128)(2,1)} %shard_map.71), calls=%async_computation.1 | async-start | bytes 4194304 | tf_op jit(solution)/shard_map/all_to_all | solution.py:285
  27.5 8.6 %collective-permute-done.2.refs_2_ = bf16[64,2304]{1,0:T(8,128)(2,1)} collective-permute-done((bf16[64,2304]{1,0:T(8,128)(2,1)}, bf16[64,2304]{1,0:T(8,128)(2,1)}, u32[]{:S(2)}, u32[]{:S(2)}) %collective-permute-start.2) | collective-permute-done | bytes 294944 | tf_op jit(solution)/shard_map/ppermute | solution.py:275
  37.7 2.9 %collective-permute-start.4 = (bf16[64,2304]{1,0:T(8,128)(2,1)}, bf16[64,2304]{1,0:T(8,128)(2,1)}, u32[]{:S(2)}, u32[]{:S(2)}) collective-permute-start(bf16[64,2304]{1,0:T(8,128)(2,1)} %collective-permute-done.2.refs_2_), channel_id=1, source_target_pairs={{0,128},{64,192},{128,0},{192,64},{1,129},{65,193},{129,1},{193,65... | collective-permute-start | bytes 884744 | tf_op jit(solution)/shard_map/ppermute | solution.py:275
  43.9 3.0 %collective-permute-start.9 = (bf16[256,2304]{1,0:T(8,128)(2,1)}, bf16[256,2304]{1,0:T(8,128)(2,1)}, u32[]{:S(2)}, u32[]{:S(2)}) collective-permute-start(bf16[256,2304]{1,0:T(8,128)(2,1)} %constant_dynamic-update-slice_fusion.2.refs_1_), channel_id=1, source_target_pairs={{0,6},{2,0},{4,2},{6,4},{1,7},{3,1},{5,3},{7,5},{8,14},{10,8},{12,... | collective-permute-start | bytes 3538952 | tf_op jit(solution)/shard_map/ppermute | solution.py:275
  49.7 4.2 %collective-permute-done.4.refs_4_ = bf16[64,2304]{1,0:T(8,128)(2,1)} collective-permute-done((bf16[64,2304]{1,0:T(8,128)(2,1)}, bf16[64,2304]{1,0:T(8,128)(2,1)}, u32[]{:S(2)}, u32[]{:S(2)}) %collective-permute-start.4) | collective-permute-done | bytes 294944 | tf_op jit(solution)/shard_map/ppermute | solution.py:275
  59.4 7.0 %collective-permute-done.9.refs_8_.refs_4_ = bf16[256,2304]{1,0:T(8,128)(2,1)} collective-permute-done((bf16[256,2304]{1,0:T(8,128)(2,1)}, bf16[256,2304]{1,0:T(8,128)(2,1)}, u32[]{:S(2)}, u32[]{:S(2)}) %collective-permute-start.9) | collective-permute-done | bytes 1179680 | tf_op jit(solution)/shard_map/ppermute | solution.py:275
  66.4 6.2 %collective-permute-done.8.refs_7_.refs_3_ = bf16[256,2304]{1,0:T(8,128)(2,1)} collective-permute-done((bf16[256,2304]{1,0:T(8,128)(2,1)}, bf16[256,2304]{1,0:T(8,128)(2,1)}, u32[]{:S(2)}, u32[]{:S(2)}) %collective-permute-start.8) | collective-permute-done | bytes 1179680 | tf_op jit(solution)/shard_map/ppermute | solution.py:275
  72.6 9.8 %shard_map.69._ = bf16[8,512,256]{2,1,0:T(8,128)(2,1)} custom-call(s32[4]{0:T(128)} %pad_add_fusion.place, bf16[512,2304]{1,0:T(8,128)(2,1)} %bitcast.9, bf16[128,2304]{1,0:T(8,128)(2,1)} %get-tuple-element.16.refs_0_.refs_3_.refs_7_, bf16[128,2304]{1,0:T(8,128)(2,1)} %collective-permute-done.6.refs_1_.refs_4_.refs_8_, ...), custom_call_target="tpu_custom_call" | custom-call | flops 1 | bytes 1 | tf_op jit(solution)/shard_map/pallas_call | solution.py:204
  82.4 7.5 %all-to-all-start = ((bf16[8,512,256]{2,1,0:T(8,128)(2,1)}), bf16[8,512,256]{2,1,0:T(8,128)(2,1)}, u32[]{:S(2)}, u32[]{:S(2)}) async-start(bf16[8,512,256]{2,1,0:T(8,128)(2,1)} %shard_map.69._), calls=%async_computation | async-start | bytes 4194304 | tf_op jit(solution)/shard_map/all_to_all | solution.py:303
  90.0 9.5 %shard_map.72._ = bf16[1024,2304]{1,0:T(8,128)(2,1)} custom-call(s32[4]{0:T(128)} %pad_add_fusion.place, bf16[8,512,256]{2,1,0:T(8,128)(2,1)} %shard_map.69._, bf16[8,512,256]{2,1,0:T(8,128)(2,1)} %all-to-all-done.1.panel.refs_0_.refs_1_.refs_2_.refs_3_.refs_4_.refs_5_, bf16[128,2304]{1,0:T(8,128)(2,1)} %get-tuple-element.14.refs_4_.refs_0_, ...), custom_call_target="tpu_custom_call" | custom-call | flops 1 | bytes 1 | tf_op jit(solution)/shard_map/pallas_call | solution.py:110
  99.5 6.3 %shard_map.73 = (bf16[128,2304]{1,0:T(8,128)(2,1)}, bf16[128,2304]{1,0:T(8,128)(2,1)}) custom-call(s32[4]{0:T(128)} %pad_add_fusion.place, bf16[1024,2304]{1,0:T(8,128)(2,1)} %shard_map.72._, bf16[8,512,256]{2,1,0:T(8,128)(2,1)} %all-to-all-done.1.panel.refs_0_.refs_1_.refs_2_.refs_3_.refs_4_.refs_5_, ...), custom_call_target="tpu_custom_call" | custom-call | flops 1 | bytes 1 | tf_op jit(solution)/shard_map/pallas_call | solution.py:163
  105.7 3.2 %collective-permute-start.11 = (bf16[128,2304]{1,0:T(8,128)(2,1)}, bf16[128,2304]{1,0:T(8,128)(2,1)}, u32[]{:S(2)}, u32[]{:S(2)}) collective-permute-start(bf16[128,2304]{1,0:T(8,128)(2,1)} %get-tuple-element.22), channel_id=1, source_target_pairs={{0,6},{2,0},{4,2},{6,4},{1,7},{3,1},{5,3},{7,5},{8,14},{10,8},{12,... | collective-permute-start | bytes 1769480 | tf_op jit(solution)/shard_map/ppermute | solution.py:275
  108.9 8.9 %shard_map.74 = (bf16[256,2304]{1,0:T(8,128)(2,1)}, bf16[256,2304]{1,0:T(8,128)(2,1)}, bf16[256,2304]{1,0:T(8,128)(2,1)}) custom-call(s32[4]{0:T(128)} %pad_add_fusion.place, bf16[128,2304]{1,0:T(8,128)(2,1)} %get-tuple-element.18._, bf16[8,512,256]{2,1,0:T(8,128)(2,1)} %all-to-all-done.1.panel.refs_0_.refs_1_.refs_2_.refs_3_.refs_4_.refs_5_, ...), custom_call_target="tpu_custom_call" | custom-call | flops 999999995904 | bytes 1 | tf_op jit(solution)/shard_map/pallas_call | solution.py:163
  117.9 3.6 %shard_map.75 = (bf16[256,2304]{1,0:T(8,128)(2,1)}, bf16[256,2304]{1,0:T(8,128)(2,1)}) custom-call(bf16[256,2304]{1,0:T(8,128)(2,1)} %get-tuple-element.20.refs_0_, bf16[256,2304]{1,0:T(8,128)(2,1)} %get-tuple-element.21.refs_1_, bf16[128,2304]{1,0:T(8,128)(2,1)} %collective-permute-done.10.refs_2_, bf16[128,2304]{1,0:T(8,128)(2,1)} %collective-permute-done.11.refs_3_), custom_call_target="tpu_custom_call" | custom-call | flops 1 | bytes 1 | tf_op jit(solution)/shard_map/pallas_call | solution.py:226
  121.4 3.2 %collective-permute-start.13 = (bf16[256,2304]{1,0:T(8,128)(2,1)}, bf16[256,2304]{1,0:T(8,128)(2,1)S(1)}, u32[]{:S(2)}, u32[]{:S(2)}) collective-permute-start(bf16[256,2304]{1,0:T(8,128)(2,1)} %get-tuple-element.24), channel_id=1, source_target_pairs={{0,6},{2,0},{4,2},{6,4},{1,7},{3,1},{5,3},{7,5},{8,14},{10,8},{12,... | collective-permute-start | bytes 3538952 | tf_op jit(solution)/shard_map/ppermute | solution.py:275
  124.7 13.6 %reduce-scatter.2.cloned.1.call-done.refs_2_ = bf16[128,2304]{1,0:T(8,128)(2,1)} async-done(((bf16[1024,2304]{1,0:T(8,128)(2,1)}), bf16[128,2304]{1,0:T(8,128)(2,1)}) %reduce-scatter.2.cloned.1.call-update) | async-done | bytes 589840 | tf_op jit(solution)/shard_map/reduce_scatter | solution.py:311
  140.0 4.9 %collective-permute-start.14 = (bf16[64,2304]{1,0:T(8,128)(2,1)}, bf16[64,2304]{1,0:T(8,128)(2,1)}, u32[]{:S(2)}, u32[]{:S(2)}) collective-permute-start(bf16[64,2304]{1,0:T(8,128)(2,1)} %slice.4), channel_id=1, source_target_pairs={{0,1},{1,0},{2,3},{3,2},{4,5},{5,4},{6,7},{7,6},{8,9},{9,8},{10,11... | collective-permute-start | bytes 884744 | tf_op jit(solution)/shard_map/ppermute | solution.py:275
  145.4 2.7 %add_convert_fusion.refs_1_ = bf16[256,2304]{1,0:T(8,128)(2,1)} fusion(bf16[256,2304]{1,0:T(8,128)(2,1)S(1)} %collective-permute-done.13, bf16[256,2304]{1,0:T(8,128)(2,1)S(1)} %collective-permute-done.12, bf16[256,2304]{1,0:T(8,128)(2,1)} %get-tuple-element.19), kind=kLoop, calls=%fused_computation | loop fusion | flops 3538944 | bytes 4718592 | tf_op jit(solution)/shard_map/convert_element_type | solution.py:221
  148.1 2.6 %shard_map.70.refs_0_ = bf16[512,512]{1,0:T(8,128)(2,1)} custom-call(bf16[8,512,256]{2,1,0:T(8,128)(2,1)} %all-to-all-done.refs_0_), custom_call_target="tpu_custom_call" | custom-call | flops 1 | bytes 1 | tf_op jit(solution)/shard_map/pallas_call | solution.py:226
  150.7 5.5 %collective-permute-done.14.refs_3_ = bf16[64,2304]{1,0:T(8,128)(2,1)} collective-permute-done((bf16[64,2304]{1,0:T(8,128)(2,1)}, bf16[64,2304]{1,0:T(8,128)(2,1)}, u32[]{:S(2)}, u32[]{:S(2)}) %collective-permute-start.14) | collective-permute-done | bytes 294944 | tf_op jit(solution)/shard_map/ppermute | solution.py:275
  (37 shorter events, 18.2 us)
Async XLA Ops:
  7.2 65.4 %all-gather.3.cloned.1.call-start = ((), (), s32[]{:S(2)}) async-start(), calls=%async_computation.4 | async-start | bytes 2654208 | tf_op jit(solution)/shard_map/all_gather | solution.py:283
  9.6 32.4 %collective-permute-start.1 = (bf16[128,2304]{1,0:T(8,128)(2,1)}, bf16[128,2304]{1,0:T(8,128)(2,1)}, u32[]{:S(2)}, u32[]{:S(2)}) collective-permute-start(bf16[128,2304]{1,0:T(8,128)(2,1)} %get-tuple-element.15.refs_5_.refs_1_), channel_id=1, source_target_pairs={{0,6},{2,0},{4,2},{6,4},{1,7},{3,1},{5,3},{7,5},{8,14},{10,8},{12,... | collective-permute-start | bytes 1769480 | tf_op jit(solution)/shard_map/ppermute | solution.py:275
  12.4 34.5 %collective-permute-start = (bf16[128,2304]{1,0:T(8,128)(2,1)}, bf16[128,2304]{1,0:T(8,128)(2,1)}, u32[]{:S(2)}, u32[]{:S(2)}) collective-permute-start(bf16[128,2304]{1,0:T(8,128)(2,1)} %get-tuple-element.14.refs_4_.refs_0_), channel_id=1, source_target_pairs={{0,2},{2,4},{4,6},{6,0},{1,3},{3,5},{5,7},{7,1},{8,10},{10,12},{12... | collective-permute-start | bytes 1769480 | tf_op jit(solution)/shard_map/ppermute | solution.py:275
  12.4 23.8 %collective-permute-start.2 = (bf16[64,2304]{1,0:T(8,128)(2,1)}, bf16[64,2304]{1,0:T(8,128)(2,1)}, u32[]{:S(2)}, u32[]{:S(2)}) collective-permute-start(bf16[64,2304]{1,0:T(8,128)(2,1)} %bitcast.14), channel_id=1, source_target_pairs={{0,1},{1,0},{2,3},{3,2},{4,5},{5,4},{6,7},{7,6},{8,9},{9,8},{10,11... | collective-permute-start | bytes 884744 | tf_op jit(solution)/shard_map/ppermute | solution.py:275
  21.3 5.4 %copy-start = (bf16[128,2304]{1,0:T(8,128)(2,1)S(1)}, bf16[128,2304]{1,0:T(8,128)(2,1)}, u32[]{:S(2)}) copy-start(bf16[128,2304]{1,0:T(8,128)(2,1)} %get-tuple-element.14.refs_4_.refs_0_) | copy-start | bytes 1769476
  21.3 61.1 %all-to-all-start.1 = ((bf16[8,512,256]{2,1,0:T(8,128)(2,1)}), bf16[8,512,256]{2,1,0:T(8,128)(2,1)}, u32[]{:S(2)}, u32[]{:S(2)}) async-start(bf16[8,512,256]{2,1,0:T(8,128)(2,1)} %shard_map.71), calls=%async_computation.1 | async-start | bytes 4194304 | tf_op jit(solution)/shard_map/all_to_all | solution.py:285
  27.5 21.3 %copy-start.1 = (bf16[128,2304]{1,0:T(8,128)(2,1)S(1)}, bf16[128,2304]{1,0:T(8,128)(2,1)}, u32[]{:S(2)}) copy-start(bf16[128,2304]{1,0:T(8,128)(2,1)} %get-tuple-element.15.refs_5_.refs_1_) | copy-start | bytes 1769476
  36.2 13.5 %collective-permute-start.3 = (bf16[64,2304]{1,0:T(8,128)(2,1)}, bf16[64,2304]{1,0:T(8,128)(2,1)}, u32[]{:S(2)}, u32[]{:S(2)}) collective-permute-start(bf16[64,2304]{1,0:T(8,128)(2,1)} %collective-permute-done.2.refs_2_), channel_id=1, source_target_pairs={{0,64},{64,128},{128,192},{192,0},{1,65},{65,129},{129,193},{193,1... | collective-permute-start | bytes 884744 | tf_op jit(solution)/shard_map/ppermute | solution.py:275
  37.7 16.1 %collective-permute-start.4 = (bf16[64,2304]{1,0:T(8,128)(2,1)}, bf16[64,2304]{1,0:T(8,128)(2,1)}, u32[]{:S(2)}, u32[]{:S(2)}) collective-permute-start(bf16[64,2304]{1,0:T(8,128)(2,1)} %collective-permute-done.2.refs_2_), channel_id=1, source_target_pairs={{0,128},{64,192},{128,0},{192,64},{1,129},{65,193},{129,1},{193,65... | collective-permute-start | bytes 884744 | tf_op jit(solution)/shard_map/ppermute | solution.py:275
  40.6 13.2 %collective-permute-start.5 = (bf16[64,2304]{1,0:T(8,128)(2,1)}, bf16[64,2304]{1,0:T(8,128)(2,1)}, u32[]{:S(2)}, u32[]{:S(2)}) collective-permute-start(bf16[64,2304]{1,0:T(8,128)(2,1)} %collective-permute-done.2.refs_2_), channel_id=1, source_target_pairs={{0,192},{64,0},{128,64},{192,128},{1,193},{65,1},{129,65},{193,129... | collective-permute-start | bytes 884744 | tf_op jit(solution)/shard_map/ppermute | solution.py:275
  43.9 22.5 %collective-permute-start.9 = (bf16[256,2304]{1,0:T(8,128)(2,1)}, bf16[256,2304]{1,0:T(8,128)(2,1)}, u32[]{:S(2)}, u32[]{:S(2)}) collective-permute-start(bf16[256,2304]{1,0:T(8,128)(2,1)} %constant_dynamic-update-slice_fusion.2.refs_1_), channel_id=1, source_target_pairs={{0,6},{2,0},{4,2},{6,4},{1,7},{3,1},{5,3},{7,5},{8,14},{10,8},{12,... | collective-permute-start | bytes 3538952 | tf_op jit(solution)/shard_map/ppermute | solution.py:275
  49.7 22.9 %collective-permute-start.8 = (bf16[256,2304]{1,0:T(8,128)(2,1)}, bf16[256,2304]{1,0:T(8,128)(2,1)}, u32[]{:S(2)}, u32[]{:S(2)}) collective-permute-start(bf16[256,2304]{1,0:T(8,128)(2,1)} %constant_dynamic-update-slice_fusion.refs_0_), channel_id=1, source_target_pairs={{0,2},{2,4},{4,6},{6,0},{1,3},{3,5},{5,7},{7,1},{8,10},{10,12},{12... | collective-permute-start | bytes 3538952 | tf_op jit(solution)/shard_map/ppermute | solution.py:275
  56.2 2.3 %collective-permute-start.6 = (bf16[128,2304]{1,0:T(8,128)(2,1)}, bf16[128,2304]{1,0:T(8,128)(2,1)}, u32[]{:S(2)}, u32[]{:S(2)}) collective-permute-start(bf16[128,2304]{1,0:T(8,128)(2,1)} %get-tuple-element.16.refs_0_.refs_3_.refs_7_), channel_id=1, source_target_pairs={{0,32},{32,0},{1,33},{33,1},{2,34},{34,2},{3,35},{35,3},{4,36},{36... | collective-permute-start | bytes 1769480 | tf_op jit(solution)/shard_map/ppermute | solution.py:275
  56.2 3.2 %collective-permute-start.7 = (bf16[128,2304]{1,0:T(8,128)(2,1)}, bf16[128,2304]{1,0:T(8,128)(2,1)}, u32[]{:S(2)}, u32[]{:S(2)}) collective-permute-start(bf16[128,2304]{1,0:T(8,128)(2,1)} %get-tuple-element.17.refs_2_.refs_5_.refs_9_), channel_id=1, source_target_pairs={{0,32},{32,0},{1,33},{33,1},{2,34},{34,2},{3,35},{35,3},{4,36},{36... | collective-permute-start | bytes 1769480 | tf_op jit(solution)/shard_map/ppermute | solution.py:275
  82.4 65.7 %all-to-all-start = ((bf16[8,512,256]{2,1,0:T(8,128)(2,1)}), bf16[8,512,256]{2,1,0:T(8,128)(2,1)}, u32[]{:S(2)}, u32[]{:S(2)}) async-start(bf16[8,512,256]{2,1,0:T(8,128)(2,1)} %shard_map.69._), calls=%async_computation | async-start | bytes 4194304 | tf_op jit(solution)/shard_map/all_to_all | solution.py:303
  90.0 48.3 %reduce-scatter.2.cloned.1.call-start = ((), (), s32[]{:S(2)}) async-start(), calls=%async_computation.3 | async-start | bytes 5308416 | tf_op jit(solution)/shard_map/reduce_scatter | solution.py:311
  105.7 12.1 %collective-permute-start.10 = (bf16[128,2304]{1,0:T(8,128)(2,1)}, bf16[128,2304]{1,0:T(8,128)(2,1)}, u32[]{:S(2)}, u32[]{:S(2)}) collective-permute-start(bf16[128,2304]{1,0:T(8,128)(2,1)} %get-tuple-element.18._), channel_id=1, source_target_pairs={{0,2},{2,4},{4,6},{6,0},{1,3},{3,5},{5,7},{7,1},{8,10},{10,12},{12... | collective-permute-start | bytes 1769480 | tf_op jit(solution)/shard_map/ppermute | solution.py:275
  105.7 12.1 %collective-permute-start.11 = (bf16[128,2304]{1,0:T(8,128)(2,1)}, bf16[128,2304]{1,0:T(8,128)(2,1)}, u32[]{:S(2)}, u32[]{:S(2)}) collective-permute-start(bf16[128,2304]{1,0:T(8,128)(2,1)} %get-tuple-element.22), channel_id=1, source_target_pairs={{0,6},{2,0},{4,2},{6,4},{1,7},{3,1},{5,3},{7,5},{8,14},{10,8},{12,... | collective-permute-start | bytes 1769480 | tf_op jit(solution)/shard_map/ppermute | solution.py:275
  121.4 24.0 %collective-permute-start.12 = (bf16[256,2304]{1,0:T(8,128)(2,1)}, bf16[256,2304]{1,0:T(8,128)(2,1)S(1)}, u32[]{:S(2)}, u32[]{:S(2)}) collective-permute-start(bf16[256,2304]{1,0:T(8,128)(2,1)} %get-tuple-element.23), channel_id=1, source_target_pairs={{0,2},{2,4},{4,6},{6,0},{1,3},{3,5},{5,7},{7,1},{8,10},{10,12},{12... | collective-permute-start | bytes 3538952 | tf_op jit(solution)/shard_map/ppermute | solution.py:275
  121.4 24.0 %collective-permute-start.13 = (bf16[256,2304]{1,0:T(8,128)(2,1)}, bf16[256,2304]{1,0:T(8,128)(2,1)S(1)}, u32[]{:S(2)}, u32[]{:S(2)}) collective-permute-start(bf16[256,2304]{1,0:T(8,128)(2,1)} %get-tuple-element.24), channel_id=1, source_target_pairs={{0,6},{2,0},{4,2},{6,4},{1,7},{3,1},{5,3},{7,5},{8,14},{10,8},{12,... | collective-permute-start | bytes 3538952 | tf_op jit(solution)/shard_map/ppermute | solution.py:275
  140.0 16.3 %collective-permute-start.14 = (bf16[64,2304]{1,0:T(8,128)(2,1)}, bf16[64,2304]{1,0:T(8,128)(2,1)}, u32[]{:S(2)}, u32[]{:S(2)}) collective-permute-start(bf16[64,2304]{1,0:T(8,128)(2,1)} %slice.4), channel_id=1, source_target_pairs={{0,1},{1,0},{2,3},{3,2},{4,5},{5,4},{6,7},{7,6},{8,9},{9,8},{10,11... | collective-permute-start | bytes 884744 | tf_op jit(solution)/shard_map/ppermute | solution.py:275
Sparse Core Ops, SparseCore 0:
  12.5 36.0 all-gather.2
  99.6 38.6 reduce-scatter.1

commit v15 on v12

--- a/solution.py
+++ b/solution.py
@@ -34,41 +34,26 @@
     return [(i, (i + step) % size) for i in range(size)]
 
 
-def dequantize_kernel(scales, quantized, top, bottom):
+def prepare_kernel(scales, quantized, inputs, top, bottom, split):
     for r, half in enumerate((top, bottom)):
         for c in range(scales.shape[1]):
             lanes = pl.ds(c * BLOCK, BLOCK)
             block = quantized[pl.ds(r * BLOCK, BLOCK), lanes].astype(F32)
             half[:, lanes] = (block * scales[r, c]).astype(BF)
-
-
-def dequantize(scales, quantized):
-    half = (BLOCK, quantized.shape[1])
-    return pl.pallas_call(
-        dequantize_kernel,
-        out_shape=[jax.ShapeDtypeStruct(half, BF)] * 2,
-        in_specs=[SCALAR, whole(quantized.shape)],
-        out_specs=[whole(half)] * 2,
-        compiler_params=params(),
-        cost_estimate=cost(1, 1),
-    )(scales, quantized)
-
-
-def split_kernel(inputs, split):
     for at in range(8):
         split[at] = inputs[:, at % 2 * 256 : at % 2 * 256 + 256]
 
 
-def split_units(inputs):
-    shape = (8, 512, 256)
-    return pl.pallas_call(
-        split_kernel,
-        out_shape=jax.ShapeDtypeStruct(shape, BF),
-        in_specs=[whole(inputs.shape)],
-        out_specs=whole(shape),
+def prepare(scales, quantized, inputs):
+    shapes = [(BLOCK, quantized.shape[1])] * 2 + [(8, 512, 256)]
+    return pl.pallas_call(
+        prepare_kernel,
+        out_shape=[jax.ShapeDtypeStruct(shape, BF) for shape in shapes],
+        in_specs=[SCALAR, whole(quantized.shape), whole(inputs.shape)],
+        out_specs=[whole(shape) for shape in shapes],
         compiler_params=params(),
         cost_estimate=cost(1, 1),
-    )(inputs)
+    )(scales, quantized, inputs)
 
 
 PRODUCT = cost(1, 1)
@@ -286,10 +271,9 @@
     F = qweight.shape[1]
 
     near = lax.all_gather(grad_out[0], ("y", "k"), axis=0, tiled=True)
-    split = split_units(inputs[0])
+    top, bottom, split = prepare(scales, qweight, inputs[0])
     panel = lax.all_to_all(split, ("zl", "zh"), 0, 0, tiled=True)
 
-    top, bottom = dequantize(scales, qweight)
     top_up, bottom_down = shift(top, "x", 1), shift(bottom, "x", -1)
     far = shift(grad_out[0], "zh", 1)
     far = [far] + [shift(far, "y", e) for e in (1, 2, 3)]

time: 165 us -> 166 us (level)
  waiting for transfers between devices: 52.1 us -> 54.5 us
  Pallas kernels: 53.4 us -> 51.7 us
    ppermute x15, waiting for transfers between devices: 39.1 us -> 40.9 us  [shift(): return lax.ppermute(array, axis, ring(lax.axis_size(axis), step))]
    pallas_call x2 -> x1, Pallas kernels: 4.94 us -> 3.29 us  [prepare(): pl.pallas_call(prepare_kernel, out_shape=[jax.ShapeDtypeStruct(shape, BF)...]
  transfers between devices with their start and end apart: 19 -> 19, of which waited for: 12 -> 12; matrix products, arithmetic and copies ran while one was open for 3% -> 3% of each run, Pallas kernels for 31% -> 30%
where the time goes in v15:
time: 166 us; the launch traced here: 165 us
  waiting for transfers between devices  54.5 us (33%)
  Pallas kernels  51.7 us (31%)
  starting transfers between devices  40 us (24%)
  between operations  14.1 us (8%)
  other arithmetic  3.26 us (2%)
  local copies, waits for them, and re-layouts  1.69 us (1%)
    ppermute x15, waiting for transfers between devices, shift(): return lax.ppermute(array, axis, ring(lax.axis_size(axis), step))  40.9 us
    ppermute x15, starting transfers between devices, shift(): return lax.ppermute(array, axis, ring(lax.axis_size(axis), step))  26.7 us
    pallas_call x2, Pallas kernels, weight_grad(): pl.pallas_call(functools.partial(weight_grad_kernel, len(offsets)), grid_...  15.5 us
    pallas_call x5, Pallas kernels, local(): pl.pallas_call(lambda *refs: kernel(*refs[len(after):]), out_shape=[jax.S...  13.6 us
    reduce_scatter x1, waiting for transfers between devices, per_device(): lax.psum_scatter(product, ('y', 'k'), scatter_dimension=0, tiled=True)  12.9 us
    pallas_call x1, Pallas kernels, backward(): pl.pallas_call(backward_kernel, grid=(2,), out_shape=jax.ShapeDtypeStruct...  9.86 us
    pallas_call x1, Pallas kernels, forward(): pl.pallas_call(forward_kernel, grid=(width // tile,), out_shape=jax.Shape...  9.53 us
    all_to_all x1, starting transfers between devices, per_device(): sums = lax.all_to_all(sums, ('zl', 'zh'), 0, 0, tiled=True)  8.07 us
  transfers between devices with their start and end apart: 19, of which 12 were waited for; matrix products, arithmetic and copies ran while one was open for 3% of the time, Pallas kernels for 30%

profile of v15, /device:TPU:32, one launch (start us, length us, event | category | flops | bytes accessed | tf_op | source)
XLA Modules:
  0.0 165.2 jit_solution(11653097707060516050)
XLA Ops:
  7.9 3.3 %shard_map.67 = (bf16[128,2304]{1,0:T(8,128)(2,1)}, bf16[128,2304]{1,0:T(8,128)(2,1)}, bf16[8,512,256]{2,1,0:T(8,128)(2,1)}) custom-call(f32[2,18]{1,0:T(2,128)} %scales.1, bf16[256,2304]{1,0:T(8,128)(2,1)} %quantized.1, bf16[512,512]{1,0:T(8,128)(2,1)} %bitcast.13), custom_call_target="tpu_custom_call" | custom-call | flops 1 | bytes 1 | tf_op jit(solution)/shard_map/pallas_call | solution.py:49
  14.4 6.3 %collective-permute-start.2 = (bf16[64,2304]{1,0:T(8,128)(2,1)}, bf16[64,2304]{1,0:T(8,128)(2,1)}, u32[]{:S(2)}, u32[]{:S(2)}) collective-permute-start(bf16[64,2304]{1,0:T(8,128)(2,1)} %bitcast.14), channel_id=1, source_target_pairs={{0,1},{1,0},{2,3},{3,2},{4,5},{5,4},{6,7},{7,6},{8,9},{9,8},{10,11... | collective-permute-start | bytes 884744 | tf_op jit(solution)/shard_map/ppermute | solution.py:265
  20.7 5.2 %all-to-all-start.1 = ((bf16[8,512,256]{2,1,0:T(8,128)(2,1)}), bf16[8,512,256]{2,1,0:T(8,128)(2,1)}, u32[]{:S(2)}, u32[]{:S(2)}) async-start(bf16[8,512,256]{2,1,0:T(8,128)(2,1)} %get-tuple-element.23), calls=%async_computation.1 | async-start | bytes 4194304 | tf_op jit(solution)/shard_map/all_to_all | solution.py:275
  25.9 12.7 %collective-permute-done.2.refs_1_ = bf16[64,2304]{1,0:T(8,128)(2,1)} collective-permute-done((bf16[64,2304]{1,0:T(8,128)(2,1)}, bf16[64,2304]{1,0:T(8,128)(2,1)}, u32[]{:S(2)}, u32[]{:S(2)}) %collective-permute-start.2) | collective-permute-done | bytes 294944 | tf_op jit(solution)/shard_map/ppermute | solution.py:265
  38.7 3.0 %collective-permute-start.5 = (bf16[64,2304]{1,0:T(8,128)(2,1)}, bf16[64,2304]{1,0:T(8,128)(2,1)}, u32[]{:S(2)}, u32[]{:S(2)}) collective-permute-start(bf16[64,2304]{1,0:T(8,128)(2,1)} %collective-permute-done.2.refs_1_), channel_id=1, source_target_pairs={{0,192},{64,0},{128,64},{192,128},{1,193},{65,1},{129,65},{193,129... | collective-permute-start | bytes 884744 | tf_op jit(solution)/shard_map/ppermute | solution.py:265
  43.3 3.1 %shard_map.68 = (bf16[256,2304]{1,0:T(8,128)(2,1)}, bf16[256,2304]{1,0:T(8,128)(2,1)}) custom-call(bf16[128,2304]{1,0:T(8,128)(2,1)} %get-tuple-element.17.refs_0_.refs_4_, bf16[128,2304]{1,0:T(8,128)(2,1)} %get-tuple-element.18.refs_1_.refs_5_, bf16[128,2304]{1,0:T(8,128)(2,1)} %collective-permute-done.refs_2_.refs_6_, ...), custom_call_target="tpu_custom_call" | custom-call | flops 1 | bytes 1 | tf_op jit(solution)/shard_map/pallas_call | solution.py:211
  50.6 2.8 %collective-permute-done.3.refs_2_ = bf16[64,2304]{1,0:T(8,128)(2,1)} collective-permute-done((bf16[64,2304]{1,0:T(8,128)(2,1)}, bf16[64,2304]{1,0:T(8,128)(2,1)}, u32[]{:S(2)}, u32[]{:S(2)}) %collective-permute-start.3) | collective-permute-done | bytes 294944 | tf_op jit(solution)/shard_map/ppermute | solution.py:265
  53.4 2.3 %shard_map.69 = (bf16[128,2304]{1,0:T(8,128)(2,1)}, bf16[128,2304]{1,0:T(8,128)(2,1)}) custom-call(bf16[256,2304]{1,0:T(8,128)(2,1)} %get-tuple-element.19.refs_0_, bf16[64,2304]{1,0:T(8,128)(2,1)} %collective-permute-done.2.refs_1_, bf16[64,2304]{1,0:T(8,128)(2,1)} %collective-permute-done.3.refs_2_, bf16[64,2304]{1,0:T(8,128)(2,1)} %collective-permute-done.4.refs_3_, ...), custom_call_target="tpu_custom_call" | custom-call | flops 28000000000 | bytes 1 | tf_op jit(solution)/shard_map/pallas_call | solution.py:211
  58.9 8.8 %collective-permute-done.9.refs_8_.refs_4_ = bf16[256,2304]{1,0:T(8,128)(2,1)} collective-permute-done((bf16[256,2304]{1,0:T(8,128)(2,1)}, bf16[256,2304]{1,0:T(8,128)(2,1)}, u32[]{:S(2)}, u32[]{:S(2)}) %collective-permute-start.9) | collective-permute-done | bytes 1179680 | tf_op jit(solution)/shard_map/ppermute | solution.py:265
  67.6 2.5 %collective-permute-done.8.refs_7_.refs_3_ = bf16[256,2304]{1,0:T(8,128)(2,1)} collective-permute-done((bf16[256,2304]{1,0:T(8,128)(2,1)}, bf16[256,2304]{1,0:T(8,128)(2,1)}, u32[]{:S(2)}, u32[]{:S(2)}) %collective-permute-start.8) | collective-permute-done | bytes 1179680 | tf_op jit(solution)/shard_map/ppermute | solution.py:265
  70.1 9.9 %shard_map.70._ = bf16[8,512,256]{2,1,0:T(8,128)(2,1)} custom-call(s32[4]{0:T(128)} %pad_add_fusion.place, bf16[512,2304]{1,0:T(8,128)(2,1)} %bitcast.9, bf16[128,2304]{1,0:T(8,128)(2,1)} %get-tuple-element.20.refs_0_.refs_3_.refs_7_, bf16[128,2304]{1,0:T(8,128)(2,1)} %collective-permute-done.6.refs_1_.refs_4_.refs_8_, ...), custom_call_target="tpu_custom_call" | custom-call | flops 1 | bytes 1 | tf_op jit(solution)/shard_map/pallas_call | solution.py:189
  80.0 8.1 %all-to-all-start = ((bf16[8,512,256]{2,1,0:T(8,128)(2,1)}), bf16[8,512,256]{2,1,0:T(8,128)(2,1)}, u32[]{:S(2)}, u32[]{:S(2)}) async-start(bf16[8,512,256]{2,1,0:T(8,128)(2,1)} %shard_map.70._), calls=%async_computation | async-start | bytes 4194304 | tf_op jit(solution)/shard_map/all_to_all | solution.py:293
  88.1 9.5 %shard_map.72._ = bf16[1024,2304]{1,0:T(8,128)(2,1)} custom-call(s32[4]{0:T(128)} %pad_add_fusion.place, bf16[8,512,256]{2,1,0:T(8,128)(2,1)} %shard_map.70._, bf16[8,512,256]{2,1,0:T(8,128)(2,1)} %all-to-all-done.1.panel.refs_0_.refs_1_.refs_2_.refs_3_.refs_4_.refs_5_, bf16[128,2304]{1,0:T(8,128)(2,1)} %get-tuple-element.17.refs_0_.refs_4_, ...), custom_call_target="tpu_custom_call" | custom-call | flops 1 | bytes 1 | tf_op jit(solution)/shard_map/pallas_call | solution.py:95
  97.6 6.3 %shard_map.73 = (bf16[128,2304]{1,0:T(8,128)(2,1)}, bf16[128,2304]{1,0:T(8,128)(2,1)}) custom-call(s32[4]{0:T(128)} %pad_add_fusion.place, bf16[1024,2304]{1,0:T(8,128)(2,1)} %shard_map.72._, bf16[8,512,256]{2,1,0:T(8,128)(2,1)} %all-to-all-done.1.panel.refs_0_.refs_1_.refs_2_.refs_3_.refs_4_.refs_5_, ...), custom_call_target="tpu_custom_call" | custom-call | flops 1 | bytes 1 | tf_op jit(solution)/shard_map/pallas_call | solution.py:148
  105.9 9.2 %shard_map.74 = (bf16[256,2304]{1,0:T(8,128)(2,1)}, bf16[256,2304]{1,0:T(8,128)(2,1)}, bf16[256,2304]{1,0:T(8,128)(2,1)}) custom-call(s32[4]{0:T(128)} %pad_add_fusion.place, bf16[128,2304]{1,0:T(8,128)(2,1)} %get-tuple-element.24._, bf16[8,512,256]{2,1,0:T(8,128)(2,1)} %all-to-all-done.1.panel.refs_0_.refs_1_.refs_2_.refs_3_.refs_4_.refs_5_, ...), custom_call_target="tpu_custom_call" | custom-call | flops 999999995904 | bytes 1 | tf_op jit(solution)/shard_map/pallas_call | solution.py:148
  116.3 2.5 %collective-permute-done.10.refs_2_ = bf16[128,2304]{1,0:T(8,128)(2,1)} collective-permute-done((bf16[128,2304]{1,0:T(8,128)(2,1)}, bf16[128,2304]{1,0:T(8,128)(2,1)}, u32[]{:S(2)}, u32[]{:S(2)}) %collective-permute-start.10) | collective-permute-done | bytes 589856 | tf_op jit(solution)/shard_map/ppermute | solution.py:265
  118.7 3.6 %shard_map.75 = (bf16[256,2304]{1,0:T(8,128)(2,1)}, bf16[256,2304]{1,0:T(8,128)(2,1)}) custom-call(bf16[256,2304]{1,0:T(8,128)(2,1)} %get-tuple-element.26.refs_0_, bf16[256,2304]{1,0:T(8,128)(2,1)} %get-tuple-element.27.refs_1_, bf16[128,2304]{1,0:T(8,128)(2,1)} %collective-permute-done.10.refs_2_, bf16[128,2304]{1,0:T(8,128)(2,1)} %collective-permute-done.11.refs_3_), custom_call_target="tpu_custom_call" | custom-call | flops 1 | bytes 1 | tf_op jit(solution)/shard_map/pallas_call | solution.py:211
  122.4 3.2 %collective-permute-start.13 = (bf16[256,2304]{1,0:T(8,128)(2,1)}, bf16[256,2304]{1,0:T(8,128)(2,1)S(1)}, u32[]{:S(2)}, u32[]{:S(2)}) collective-permute-start(bf16[256,2304]{1,0:T(8,128)(2,1)} %get-tuple-element.30), channel_id=1, source_target_pairs={{0,6},{2,0},{4,2},{6,4},{1,7},{3,1},{5,3},{7,5},{8,14},{10,8},{12,... | collective-permute-start | bytes 3538952 | tf_op jit(solution)/shard_map/ppermute | solution.py:265
  125.6 12.9 %reduce-scatter.2.cloned.1.call-done.refs_2_ = bf16[128,2304]{1,0:T(8,128)(2,1)} async-done(((bf16[1024,2304]{1,0:T(8,128)(2,1)}), bf16[128,2304]{1,0:T(8,128)(2,1)}) %reduce-scatter.2.cloned.1.call-update) | async-done | bytes 589840 | tf_op jit(solution)/shard_map/reduce_scatter | solution.py:301
  140.1 4.7 %collective-permute-start.14 = (bf16[64,2304]{1,0:T(8,128)(2,1)}, bf16[64,2304]{1,0:T(8,128)(2,1)}, u32[]{:S(2)}, u32[]{:S(2)}) collective-permute-start(bf16[64,2304]{1,0:T(8,128)(2,1)} %slice.4), channel_id=1, source_target_pairs={{0,1},{1,0},{2,3},{3,2},{4,5},{5,4},{6,7},{7,6},{8,9},{9,8},{10,11... | collective-permute-start | bytes 884744 | tf_op jit(solution)/shard_map/ppermute | solution.py:265
  144.9 3.7 %collective-permute-done.12 = bf16[256,2304]{1,0:T(8,128)(2,1)S(1)} collective-permute-done((bf16[256,2304]{1,0:T(8,128)(2,1)}, bf16[256,2304]{1,0:T(8,128)(2,1)S(1)}, u32[]{:S(2)}, u32[]{:S(2)}) %collective-permute-start.12) | collective-permute-done | bytes 1179680 | tf_op jit(solution)/shard_map/ppermute | solution.py:265
  148.6 2.7 %add_convert_fusion.refs_1_ = bf16[256,2304]{1,0:T(8,128)(2,1)} fusion(bf16[256,2304]{1,0:T(8,128)(2,1)S(1)} %collective-permute-done.13, bf16[256,2304]{1,0:T(8,128)(2,1)S(1)} %collective-permute-done.12, bf16[256,2304]{1,0:T(8,128)(2,1)} %get-tuple-element.25), kind=kLoop, calls=%fused_computation | loop fusion | flops 3538944 | bytes 4718592 | tf_op jit(solution)/shard_map/convert_element_type | solution.py:206
  151.3 2.6 %shard_map.71.refs_0_ = bf16[512,512]{1,0:T(8,128)(2,1)} custom-call(bf16[8,512,256]{2,1,0:T(8,128)(2,1)} %all-to-all-done.refs_0_), custom_call_target="tpu_custom_call" | custom-call | flops 1 | bytes 1 | tf_op jit(solution)/shard_map/pallas_call | solution.py:211
  153.9 2.5 %collective-permute-done.14.refs_3_ = bf16[64,2304]{1,0:T(8,128)(2,1)} collective-permute-done((bf16[64,2304]{1,0:T(8,128)(2,1)}, bf16[64,2304]{1,0:T(8,128)(2,1)}, u32[]{:S(2)}, u32[]{:S(2)}) %collective-permute-start.14) | collective-permute-done | bytes 294944 | tf_op jit(solution)/shard_map/ppermute | solution.py:265
  (29 shorter events, 19.8 us)
Async XLA Ops:
  7.2 63.0 %all-gather.3.cloned.1.call-start = ((), (), s32[]{:S(2)}) async-start(), calls=%async_computation.4 | async-start | bytes 2654208 | tf_op jit(solution)/shard_map/all_gather | solution.py:273
  11.2 32.1 %collective-permute-start = (bf16[128,2304]{1,0:T(8,128)(2,1)}, bf16[128,2304]{1,0:T(8,128)(2,1)}, u32[]{:S(2)}, u32[]{:S(2)}) collective-permute-start(bf16[128,2304]{1,0:T(8,128)(2,1)} %get-tuple-element.17.refs_0_.refs_4_), channel_id=1, source_target_pairs={{0,2},{2,4},{4,6},{6,0},{1,3},{3,5},{5,7},{7,1},{8,10},{10,12},{12... | collective-permute-start | bytes 1769480 | tf_op jit(solution)/shard_map/ppermute | solution.py:265
  12.7 30.6 %collective-permute-start.1 = (bf16[128,2304]{1,0:T(8,128)(2,1)}, bf16[128,2304]{1,0:T(8,128)(2,1)}, u32[]{:S(2)}, u32[]{:S(2)}) collective-permute-start(bf16[128,2304]{1,0:T(8,128)(2,1)} %get-tuple-element.18.refs_1_.refs_5_), channel_id=1, source_target_pairs={{0,6},{2,0},{4,2},{6,4},{1,7},{3,1},{5,3},{7,5},{8,14},{10,8},{12,... | collective-permute-start | bytes 1769480 | tf_op jit(solution)/shard_map/ppermute | solution.py:265
  14.4 24.2 %collective-permute-start.2 = (bf16[64,2304]{1,0:T(8,128)(2,1)}, bf16[64,2304]{1,0:T(8,128)(2,1)}, u32[]{:S(2)}, u32[]{:S(2)}) collective-permute-start(bf16[64,2304]{1,0:T(8,128)(2,1)} %bitcast.14), channel_id=1, source_target_pairs={{0,1},{1,0},{2,3},{3,2},{4,5},{5,4},{6,7},{7,6},{8,9},{9,8},{10,11... | collective-permute-start | bytes 884744 | tf_op jit(solution)/shard_map/ppermute | solution.py:265
  20.7 59.3 %all-to-all-start.1 = ((bf16[8,512,256]{2,1,0:T(8,128)(2,1)}), bf16[8,512,256]{2,1,0:T(8,128)(2,1)}, u32[]{:S(2)}, u32[]{:S(2)}) async-start(bf16[8,512,256]{2,1,0:T(8,128)(2,1)} %get-tuple-element.23), calls=%async_computation.1 | async-start | bytes 4194304 | tf_op jit(solution)/shard_map/all_to_all | solution.py:275
  38.7 11.9 %collective-permute-start.5 = (bf16[64,2304]{1,0:T(8,128)(2,1)}, bf16[64,2304]{1,0:T(8,128)(2,1)}, u32[]{:S(2)}, u32[]{:S(2)}) collective-permute-start(bf16[64,2304]{1,0:T(8,128)(2,1)} %collective-permute-done.2.refs_1_), channel_id=1, source_target_pairs={{0,192},{64,0},{128,64},{192,128},{1,193},{65,1},{129,65},{193,129... | collective-permute-start | bytes 884744 | tf_op jit(solution)/shard_map/ppermute | solution.py:265
  41.7 8.9 %collective-permute-start.4 = (bf16[64,2304]{1,0:T(8,128)(2,1)}, bf16[64,2304]{1,0:T(8,128)(2,1)}, u32[]{:S(2)}, u32[]{:S(2)}) collective-permute-start(bf16[64,2304]{1,0:T(8,128)(2,1)} %collective-permute-done.2.refs_1_), channel_id=1, source_target_pairs={{0,128},{64,192},{128,0},{192,64},{1,129},{65,193},{129,1},{193,65... | collective-permute-start | bytes 884744 | tf_op jit(solution)/shard_map/ppermute | solution.py:265
  42.3 11.1 %collective-permute-start.3 = (bf16[64,2304]{1,0:T(8,128)(2,1)}, bf16[64,2304]{1,0:T(8,128)(2,1)}, u32[]{:S(2)}, u32[]{:S(2)}) collective-permute-start(bf16[64,2304]{1,0:T(8,128)(2,1)} %collective-permute-done.2.refs_1_), channel_id=1, source_target_pairs={{0,64},{64,128},{128,192},{192,0},{1,65},{65,129},{129,193},{193,1... | collective-permute-start | bytes 884744 | tf_op jit(solution)/shard_map/ppermute | solution.py:265
  46.4 21.2 %collective-permute-start.9 = (bf16[256,2304]{1,0:T(8,128)(2,1)}, bf16[256,2304]{1,0:T(8,128)(2,1)}, u32[]{:S(2)}, u32[]{:S(2)}) collective-permute-start(bf16[256,2304]{1,0:T(8,128)(2,1)} %get-tuple-element.22), channel_id=1, source_target_pairs={{0,6},{2,0},{4,2},{6,4},{1,7},{3,1},{5,3},{7,5},{8,14},{10,8},{12,... | collective-permute-start | bytes 3538952 | tf_op jit(solution)/shard_map/ppermute | solution.py:265
  47.9 22.2 %collective-permute-start.8 = (bf16[256,2304]{1,0:T(8,128)(2,1)}, bf16[256,2304]{1,0:T(8,128)(2,1)}, u32[]{:S(2)}, u32[]{:S(2)}) collective-permute-start(bf16[256,2304]{1,0:T(8,128)(2,1)} %get-tuple-element.19.refs_0_), channel_id=1, source_target_pairs={{0,2},{2,4},{4,6},{6,0},{1,3},{3,5},{5,7},{7,1},{8,10},{10,12},{12... | collective-permute-start | bytes 3538952 | tf_op jit(solution)/shard_map/ppermute | solution.py:265
  55.7 2.3 %collective-permute-start.6 = (bf16[128,2304]{1,0:T(8,128)(2,1)}, bf16[128,2304]{1,0:T(8,128)(2,1)}, u32[]{:S(2)}, u32[]{:S(2)}) collective-permute-start(bf16[128,2304]{1,0:T(8,128)(2,1)} %get-tuple-element.20.refs_0_.refs_3_.refs_7_), channel_id=1, source_target_pairs={{0,32},{32,0},{1,33},{33,1},{2,34},{34,2},{3,35},{35,3},{4,36},{36... | collective-permute-start | bytes 1769480 | tf_op jit(solution)/shard_map/ppermute | solution.py:265
  55.7 3.2 %collective-permute-start.7 = (bf16[128,2304]{1,0:T(8,128)(2,1)}, bf16[128,2304]{1,0:T(8,128)(2,1)}, u32[]{:S(2)}, u32[]{:S(2)}) collective-permute-start(bf16[128,2304]{1,0:T(8,128)(2,1)} %get-tuple-element.21.refs_2_.refs_5_.refs_9_), channel_id=1, source_target_pairs={{0,32},{32,0},{1,33},{33,1},{2,34},{34,2},{3,35},{35,3},{4,36},{36... | collective-permute-start | bytes 1769480 | tf_op jit(solution)/shard_map/ppermute | solution.py:265
  80.0 71.3 %all-to-all-start = ((bf16[8,512,256]{2,1,0:T(8,128)(2,1)}), bf16[8,512,256]{2,1,0:T(8,128)(2,1)}, u32[]{:S(2)}, u32[]{:S(2)}) async-start(bf16[8,512,256]{2,1,0:T(8,128)(2,1)} %shard_map.70._), calls=%async_computation | async-start | bytes 4194304 | tf_op jit(solution)/shard_map/all_to_all | solution.py:293
  88.1 50.4 %reduce-scatter.2.cloned.1.call-start = ((), (), s32[]{:S(2)}) async-start(), calls=%async_computation.3 | async-start | bytes 5308416 | tf_op jit(solution)/shard_map/reduce_scatter | solution.py:301
  103.9 12.4 %collective-permute-start.11 = (bf16[128,2304]{1,0:T(8,128)(2,1)}, bf16[128,2304]{1,0:T(8,128)(2,1)}, u32[]{:S(2)}, u32[]{:S(2)}) collective-permute-start(bf16[128,2304]{1,0:T(8,128)(2,1)} %get-tuple-element.28), channel_id=1, source_target_pairs={{0,6},{2,0},{4,2},{6,4},{1,7},{3,1},{5,3},{7,5},{8,14},{10,8},{12,... | collective-permute-start | bytes 1769480 | tf_op jit(solution)/shard_map/ppermute | solution.py:265
  104.2 14.6 %collective-permute-start.10 = (bf16[128,2304]{1,0:T(8,128)(2,1)}, bf16[128,2304]{1,0:T(8,128)(2,1)}, u32[]{:S(2)}, u32[]{:S(2)}) collective-permute-start(bf16[128,2304]{1,0:T(8,128)(2,1)} %get-tuple-element.24._), channel_id=1, source_target_pairs={{0,2},{2,4},{4,6},{6,0},{1,3},{3,5},{5,7},{7,1},{8,10},{10,12},{12... | collective-permute-start | bytes 1769480 | tf_op jit(solution)/shard_map/ppermute | solution.py:265
  122.4 26.2 %collective-permute-start.12 = (bf16[256,2304]{1,0:T(8,128)(2,1)}, bf16[256,2304]{1,0:T(8,128)(2,1)S(1)}, u32[]{:S(2)}, u32[]{:S(2)}) collective-permute-start(bf16[256,2304]{1,0:T(8,128)(2,1)} %get-tuple-element.29), channel_id=1, source_target_pairs={{0,2},{2,4},{4,6},{6,0},{1,3},{3,5},{5,7},{7,1},{8,10},{10,12},{12... | collective-permute-start | bytes 3538952 | tf_op jit(solution)/shard_map/ppermute | solution.py:265
  122.4 26.2 %collective-permute-start.13 = (bf16[256,2304]{1,0:T(8,128)(2,1)}, bf16[256,2304]{1,0:T(8,128)(2,1)S(1)}, u32[]{:S(2)}, u32[]{:S(2)}) collective-permute-start(bf16[256,2304]{1,0:T(8,128)(2,1)} %get-tuple-element.30), channel_id=1, source_target_pairs={{0,6},{2,0},{4,2},{6,4},{1,7},{3,1},{5,3},{7,5},{8,14},{10,8},{12,... | collective-permute-start | bytes 3538952 | tf_op jit(solution)/shard_map/ppermute | solution.py:265
  140.1 16.3 %collective-permute-start.14 = (bf16[64,2304]{1,0:T(8,128)(2,1)}, bf16[64,2304]{1,0:T(8,128)(2,1)}, u32[]{:S(2)}, u32[]{:S(2)}) collective-permute-start(bf16[64,2304]{1,0:T(8,128)(2,1)} %slice.4), channel_id=1, source_target_pairs={{0,1},{1,0},{2,3},{3,2},{4,5},{5,4},{6,7},{7,6},{8,9},{9,8},{10,11... | collective-permute-start | bytes 884744 | tf_op jit(solution)/shard_map/ppermute | solution.py:265
Sparse Core Ops, SparseCore 0:
  9.8 31.4 all-gather.2
  97.7 40.6 reduce-scatter.1
